TPU v7x, 32 devices: a whole 2x2x4 slice. The times are simulated.
32 devices in a mesh: dp: 2 (over core), ctx: 4 (over z), mp: 4 (over y, x).
Axes of the slice: x: 2, y: 2, z: 4, core: 2. Of those that a mesh axis runs over, the one named last changes fastest.
Arguments:
- image_states: bfloat16 [2, 1024, 8192], P('dp', 'ctx', 'mp'), may hold values from -6 to 6
- place_index: int32 [2, 1024], P('dp'), may hold values from 0 to 2047, as said below
- doc_ids: int32 [2, 2048], P('dp'), may hold values from 0 to 15, never falling along the last dimension, each value on 1 to 512 neighbouring positions
- queries: bfloat16 [2, 2048, 4096], P('dp', 'ctx', 'mp'), may hold values from -160 to 160
- text_kv: bfloat16 [2, 2048, 1024], P('dp', 'ctx', 'mp'), may hold values from -5.5 to 5.5
- kv_weight: bfloat16 [4, 8192, 256], P('mp'), may hold values from -0.0625 to 0.0625
- d_out: bfloat16 [2, 2048, 4096], P('dp', 'ctx', 'mp'), may hold values from -6 to 6
Outputs:
- attn_out: bfloat16 [2, 2048, 4096], P('dp', 'ctx', 'mp')
- image_grad: bfloat16 [2, 1024, 8192], P('dp', 'ctx', 'mp')
- kv_weight_grad: float32 [4, 8192, 256], P('mp', 'ctx')
Inputs may be any that keep to these rules, and one draw needn't show every extreme that they name: `place_index`: images are whole blocks of 16 image tokens, consecutive in a vision rank's order and placed on 16 consecutive positions aligned to 16; every context shard of 512 positions holds exactly 256 image tokens; no position gets two image tokens; at most 64 image tokens of one vision rank lie in one context shard, and in every draw some vision rank places exactly 64 in some shard.
All inputs are finite; a program needn't handle non-finite values.
Results may differ from a plain program's by a relative error of at most 0.0085.
Values may be sent and summed in bfloat16 or wider, within the bound.
No kernel may reach another device: no remote copies, remote signals or barrier semaphores. Data moves between devices by JAX's collectives and lax.ppermute only.
A program may use at most 128 MiB of HBM per device.

v0:
```python
import jax
import jax.numpy as jnp
from jax import lax
from jax.sharding import PartitionSpec as P

IMGTOK = 16


def shifted_2(block, axis, distance):
    devices = range(lax.axis_size(axis))
    route = [(i - distance, i) for i in devices if i - distance in devices]
    return lax.ppermute(block, axis, route)


def routing_tables(place_row, shard_index, image_dev, capacity, ctx_dev, rank_count):
    dest_shard = place_row // ctx_dev
    by_source = dest_shard.reshape(rank_count, image_dev)
    onehot = (
        by_source[:, :, None] == jnp.arange(rank_count, dtype=jnp.int32)[None, None, :]
    ).astype(jnp.int32)
    running = jnp.cumsum(onehot, axis=1) - 1
    slot_index = jnp.sum(running * onehot, axis=2).reshape(-1)
    source_rank = jnp.arange(rank_count * image_dev, dtype=jnp.int32) // image_dev
    send_flat = dest_shard * capacity + slot_index
    recv_flat = source_rank * capacity + slot_index
    is_mine = dest_shard == shard_index
    local_pos = place_row % ctx_dev
    image_marks = (
        jnp.zeros((ctx_dev,), jnp.int32)
        .at[jnp.where(is_mine, local_pos, ctx_dev)]
        .set(1, mode="drop")
    )
    compact_of_pos = jnp.cumsum(image_marks) - 1
    compact = jnp.where(is_mine, compact_of_pos[local_pos], image_dev)
    recv_of_compact = jnp.zeros((image_dev,), jnp.int32).at[compact].set(recv_flat, mode="drop")
    image_pos = jnp.nonzero(image_marks, size=image_dev)[0].astype(jnp.int32)
    own_slots = lax.dynamic_slice_in_dim(send_flat, shard_index * image_dev, image_dev)
    return (own_slots, recv_of_compact, image_pos)


def per_device(image_states, place_index, doc_ids, queries, text_kv, kv_weight, d_out):
    rank_count = lax.axis_size("ctx")
    shard_index = lax.axis_index("ctx")
    ctx_dev = queries.shape[1]
    image_dev = image_states.shape[1]
    head_size = kv_weight.shape[2] // 2
    group_size = queries.shape[2] // head_size
    capacity = IMGTOK * ((image_dev // IMGTOK + rank_count - 1) // rank_count)
    own_slots, recv_of_compact, image_pos = routing_tables(
        place_index[0], shard_index, image_dev, capacity, ctx_dev, rank_count
    )
    weights = kv_weight[0]
    own_states = image_states[0]
    holder = (
        jnp.zeros((rank_count * capacity, own_states.shape[1]), own_states.dtype)
        .at[own_slots]
        .set(own_states)
    )
    arrived = lax.all_to_all(
        holder.reshape(rank_count, capacity, own_states.shape[1]),
        "ctx",
        split_axis=0,
        concat_axis=0,
        tiled=True,
    )
    state_rows = lax.all_gather(
        arrived.reshape(rank_count * capacity, arrived.shape[2])[recv_of_compact],
        "mp",
        axis=1,
        tiled=True,
    )
    image_kv = jnp.dot(state_rows, weights, preferred_element_type=jnp.float32).astype(jnp.bfloat16)
    kv_local = text_kv[0].at[image_pos].set(image_kv)
    earlier = shifted_2(kv_local, "ctx", 1)
    key_window = jnp.concatenate([earlier, kv_local], axis=0)
    key_part = key_window[:, :head_size]
    value_part = key_window[:, head_size:]
    all_docs = doc_ids[0]
    own_docs = lax.dynamic_slice_in_dim(all_docs, shard_index * ctx_dev, ctx_dev)
    prior_docs = lax.dynamic_slice_in_dim(
        all_docs, jnp.maximum(shard_index - 1, 0) * ctx_dev, ctx_dev
    )
    prior_docs = jnp.where(shard_index > 0, prior_docs, -1)
    key_docs = jnp.concatenate([prior_docs, own_docs], axis=0)
    query_pos = jnp.arange(ctx_dev, dtype=jnp.int32)
    key_pos = jnp.arange(2 * ctx_dev, dtype=jnp.int32) - ctx_dev
    allowed = (key_pos[None, :] <= query_pos[:, None]) & (key_docs[None, :] == own_docs[:, None])
    score_scale = head_size ** (-0.5)
    query_heads = queries[0].reshape(ctx_dev, group_size, head_size).transpose(1, 0, 2)
    grad_heads = d_out[0].reshape(ctx_dev, group_size, head_size).transpose(1, 0, 2)

    def one_head(running_sums, head_inputs):
        query_head, grad_head = head_inputs
        scores = (
            lax.dot_general(
                query_head, key_part, (((1,), (1,)), ((), ())), preferred_element_type=jnp.float32
            )
            * score_scale
        )
        scores = jnp.where(allowed, scores, -1e30)
        shifted = jnp.exp(scores - jnp.max(scores, axis=1, keepdims=True))
        shifted = jnp.where(allowed, shifted, 0.0)
        attention = shifted / jnp.sum(shifted, axis=1, keepdims=True)
        attention_low = attention.astype(jnp.bfloat16)
        context = jnp.dot(attention_low, value_part, preferred_element_type=jnp.float32)
        grad_attention = lax.dot_general(
            grad_head, value_part, (((1,), (1,)), ((), ())), preferred_element_type=jnp.float32
        )
        row_delta = jnp.sum(grad_head.astype(jnp.float32) * context, axis=1, keepdims=True)
        grad_scores = (attention * (grad_attention - row_delta)).astype(jnp.bfloat16)
        key_grad = running_sums[0] + score_scale * lax.dot_general(
            grad_scores, query_head, (((0,), (0,)), ((), ())), preferred_element_type=jnp.float32
        )
        value_grad = running_sums[1] + lax.dot_general(
            attention_low, grad_head, (((0,), (0,)), ((), ())), preferred_element_type=jnp.float32
        )
        return ((key_grad, value_grad), context.astype(jnp.bfloat16))

    zero_grads = jnp.zeros((2 * ctx_dev, head_size), jnp.float32)
    (key_grad, value_grad), outputs = lax.scan(
        one_head, (zero_grads, zero_grads), (query_heads, grad_heads)
    )
    attn_out = outputs.transpose(1, 0, 2).reshape(ctx_dev, group_size * head_size)
    kv_grad = jnp.concatenate([key_grad, value_grad], axis=1)
    later = shifted_2(kv_grad[:ctx_dev], "ctx", -1)
    total_grad = kv_grad[ctx_dev:] + later
    grad_low = total_grad[image_pos].astype(jnp.bfloat16)
    partial_value = lax.dot_general(
        grad_low, weights, (((1,), (1,)), ((), ())), preferred_element_type=jnp.float32
    )
    grad_rows = lax.psum_scatter(partial_value, "mp", scatter_dimension=1, tiled=True).astype(
        jnp.bfloat16
    )
    holder = (
        jnp.zeros((rank_count * capacity, grad_rows.shape[1]), grad_rows.dtype)
        .at[recv_of_compact]
        .set(grad_rows)
    )
    back = lax.all_to_all(
        holder.reshape(rank_count, capacity, grad_rows.shape[1]),
        "ctx",
        split_axis=0,
        concat_axis=0,
        tiled=True,
    )
    image_grad = back.reshape(rank_count * capacity, back.shape[2])[own_slots]
    weight_share = lax.psum_scatter(
        lax.dot_general(
            state_rows, grad_low, (((0,), (0,)), ((), ())), preferred_element_type=jnp.float32
        ),
        "ctx",
        scatter_dimension=0,
        tiled=True,
    )
    weight_grad = lax.psum(weight_share, "dp")
    return (attn_out[None], image_grad[None], weight_grad[None])


def solution(mesh):
    in_specs = (
        P("dp", "ctx", "mp"),
        P("dp", None),
        P("dp", None),
        P("dp", "ctx", "mp"),
        P("dp", "ctx", "mp"),
        P("mp", None, None),
        P("dp", "ctx", "mp"),
    )
    out_specs = (P("dp", "ctx", "mp"), P("dp", "ctx", "mp"), P("mp", "ctx", None))
    return jax.shard_map(
        per_device, mesh=mesh, in_specs=in_specs, out_specs=out_specs, check_vma=False
    )
```

profile of v0, /device:TPU:0, one launch (start us, length us, event | category | flops | bytes accessed | tf_op | source)
XLA Modules:
  0.0 515.1 jit_solution(12511965188491713041)
XLA Ops:
  8.0 4.8 reduce-window.39
  16.0 3.1 scatter_custom_fusion.2
  19.1 6.3 %all-to-all-start = ((bf16[4,64,2048]{2,1,0:T(8,128)(2,1)}), bf16[4,64,2048]{2,1,0:T(8,128)(2,1)S(1)}, u32[]{:S(2)}, u32[]{:S(2)}) async-start(bf16[4,64,2048]{2,1,0:T(8,128)(2,1)} %bitcast.16), calls=%async_computation | async-start | bytes 2097152 | tf_op jit(solution)/shard_map/all_to_all | solution.py:59
  25.5 4.3 scatter_custom_fusion
  30.5 6.9 %gather_fusion = s32[1024]{0:T(1024)S(1)} fusion(s32[512]{0:T(512)S(1)} %add_bitcast_fusion, s32[1024]{0:T(1024)S(1)} %broadcast_clamp_fusion), kind=kCustom, calls=%fused_computation | custom fusion | bytes 12288 | tf_op jit(solution)/shard_map/gather | solution.py:34
  37.3 4.3 scatter_custom_fusion.3
  41.7 9.5 %all-to-all-done = bf16[4,64,2048]{2,1,0:T(8,128)(2,1)S(1)} async-done(((bf16[4,64,2048]{2,1,0:T(8,128)(2,1)}), bf16[4,64,2048]{2,1,0:T(8,128)(2,1)S(1)}, u32[]{:S(2)}, u32[]{:S(2)}) %all-to-all-start) | async-done | bytes 1048608 | tf_op jit(solution)/shard_map/all_to_all | solution.py:59
  54.8 4.1 scatter_custom_fusion.1
  60.2 45.3 %all-gather.3.cloned.1.call-done = bf16[256,8192]{1,0:T(8,128)(2,1)} async-done(((bf16[256,2048]{1,0:T(8,128)(2,1)}), bf16[256,8192]{1,0:T(8,128)(2,1)}) %all-gather.3.cloned.1.call-update) | async-done | bytes 4194320 | tf_op jit(solution)/shard_map/all_gather | solution.py:66
  105.5 4.7 fusion.32
  111.9 4.1 collective-permute-start
  122.6 86.2 %while.15 = (s32[]{:T(128)}, f32[1024,128]{1,0:T(8,128)}, f32[1024,128]{1,0:T(8,128)}, bf16[8,512,128]{1,2,0:T(8,128)(2,1)}, bf16[8,512,128]{1,2,0:T(8,128)(2,1)...) while((s32[]{:T(128)}, f32[1024,128]{1,0:T(8,128)}, ...), condition=%wide.region_19.20_spmd.clone, body=%wide.region_15.19_spmd.clone.sunk | while | flops 686160384 | bytes 18659980 | solution.py:120
  149.5 2.7 fusion.95
  160.4 2.7 fusion.95
  171.2 2.7 fusion.95
  212.3 14.2 %collective-permute-done.1 = f32[512,256]{1,0:T(8,128)S(1)} collective-permute-done((f32[512,256]{1,0:T(8,128)S(1)}, f32[512,256]{1,0:T(8,128)S(1)}, u32[]{:S(2)}, u32[]{:S(2)}) %collective-permute-start.1) | collective-permute-done | bytes 524320 | tf_op jit(solution)/shard_map/ppermute | solution.py:12
  227.8 6.7 %fusion.66 = f32[8192,256]{1,0:T(8,128)} fusion(bf16[256,8192]{1,0:T(8,128)(2,1)} %all-gather.3.cloned.1.call-done, bf16[256,256]{1,0:T(8,128)(2,1)S(1)} %gather_fusion.2), kind=kOutput, calls=%fused_computation.140 | convolution fusion | flops 1073741824 | bytes 12713984 | tf_op jit(solution)/shard_map/dot_general | solution.py:148
  234.6 7.1 %fusion.28 = f32[256,8192]{1,0:T(8,128)} fusion(bf16[1,8192,256]{2,1,0:T(8,128)(2,1)} %param.14, bf16[256,256]{1,0:T(8,128)(2,1)S(1)} %gather_fusion.2), kind=kOutput, calls=%fused_computation.41 | convolution fusion | flops 1073741824 | bytes 12713984 | tf_op jit(solution)/shard_map/dot_general | solution.py:128
  241.7 136.8 %reduce-scatter.5.cloned.1.call-done = f32[2048,256]{1,0:T(8,128)} async-done(((f32[8192,256]{1,0:T(8,128)}), f32[2048,256]{1,0:T(8,128)}) %reduce-scatter.5.cloned.1.call-update) | async-done | bytes 2097168 | tf_op jit(solution)/shard_map/reduce_scatter | solution.py:147
  378.5 90.2 %reduce-scatter.3.cloned.1.call-done = f32[256,2048]{1,0:T(8,128)} async-done(((f32[256,8192]{1,0:T(8,128)}), f32[256,2048]{1,0:T(8,128)}) %reduce-scatter.3.cloned.1.call-update) | async-done | bytes 2097168 | tf_op jit(solution)/shard_map/reduce_scatter | solution.py:131
  468.7 4.2 scatter_custom_fusion.5
  472.9 4.6 all-to-all-start.1
  478.9 24.3 %all-to-all-done.1 = bf16[4,64,2048]{2,1,0:T(8,128)(2,1)S(1)} async-done(((bf16[4,64,2048]{2,1,0:T(8,128)(2,1)}), bf16[4,64,2048]{2,1,0:T(8,128)(2,1)S(1)}, u32[]{:S(2)}, u32[]{:S(2)}) %all-to-all-start.1) | async-done | bytes 1048608 | tf_op jit(solution)/shard_map/all_to_all | solution.py:139
  505.5 3.0 copy.42
  (143 shorter events, 104.1 us)
Async XLA Ops:
  7.2 8.8 %copy-start = (bf16[1,256,2048]{2,1,0:T(8,128)(2,1)S(1)}, bf16[1,256,2048]{2,1,0:T(8,128)(2,1)}, u32[]{:S(2)}) copy-start(bf16[1,256,2048]{2,1,0:T(8,128)(2,1)} %param.9) | copy-start | bytes 3145732
  16.0 9.5 %copy-start.5 = (s32[1,1024]{1,0:T(1,128)S(1)}, s32[1,1024]{1,0:T(1,128)}, u32[]{:S(2)}) copy-start(s32[1,1024]{1,0:T(1,128)} %param.10) | copy-start | bytes 12292
  19.1 32.0 %all-to-all-start = ((bf16[4,64,2048]{2,1,0:T(8,128)(2,1)}), bf16[4,64,2048]{2,1,0:T(8,128)(2,1)S(1)}, u32[]{:S(2)}, u32[]{:S(2)}) async-start(bf16[4,64,2048]{2,1,0:T(8,128)(2,1)} %bitcast.16), calls=%async_computation | async-start | bytes 2097152 | tf_op jit(solution)/shard_map/all_to_all | solution.py:59
  25.5 80.1 %all-gather.3.cloned.1.call-start = ((), (), s32[]{:S(2)}) async-start(), calls=%async_computation.7 | async-start | bytes 5242880 | tf_op jit(solution)/shard_map/all_gather | solution.py:66
  53.5 325.0 %reduce-scatter.5.cloned.1.call-start = ((), (), s32[]{:S(2)}) async-start(), calls=%async_computation.5 | async-start | bytes 10485760 | tf_op jit(solution)/shard_map/reduce_scatter | solution.py:147
  60.2 50.0 %copy-start.1 = (bf16[1,512,256]{2,1,0:T(8,128)(2,1)S(1)}, bf16[1,512,256]{2,1,0:T(8,128)(2,1)}, u32[]{:S(2)}) copy-start(bf16[1,512,256]{2,1,0:T(8,128)(2,1)} %param.13) | copy-start | bytes 786436
  110.2 5.8 %copy-start.2 = (bf16[1,512,1024]{2,1,0:T(8,128)(2,1)S(1)}, bf16[1,512,1024]{2,1,0:T(8,128)(2,1)}, u32[]{:S(2)}) copy-start(bf16[1,512,1024]{2,1,0:T(8,128)(2,1)} %param.12) | copy-start | bytes 3145732
  110.2 7.1 %copy-start.3 = (bf16[1,512,1024]{2,1,0:T(8,128)(2,1)S(1)}, bf16[1,512,1024]{2,1,0:T(8,128)(2,1)}, u32[]{:S(2)}) copy-start(bf16[1,512,1024]{2,1,0:T(8,128)(2,1)} %param.15) | copy-start | bytes 3145732
  111.9 8.9 %collective-permute-start = (bf16[512,256]{1,0:T(8,128)(2,1)S(1)}, bf16[512,256]{1,0:T(8,128)(2,1)}, u32[]{:S(2)}, u32[]{:S(2)}) collective-permute-start(bf16[512,256]{1,0:T(8,128)(2,1)S(1)} %scatter_fusion), channel_id=1, source_target_pairs={{0,4},{4,8},{8,12},{1,5},{5,9},{9,13},{2,6},{6,10},{10,14},{3,7},{... | collective-permute-start | bytes 786440 | tf_op jit(solution)/shard_map/ppermute | solution.py:12
  116.0 2.6 copy-start.6
  211.0 15.5 %collective-permute-start.1 = (f32[512,256]{1,0:T(8,128)S(1)}, f32[512,256]{1,0:T(8,128)S(1)}, u32[]{:S(2)}, u32[]{:S(2)}) collective-permute-start(f32[512,256]{1,0:T(8,128)S(1)} %slice.64), channel_id=1, source_target_pairs={{4,0},{8,4},{12,8},{5,1},{9,5},{13,9},{6,2},{10,6},{14,10},{7,3},{... | collective-permute-start | bytes 1572872 | tf_op jit(solution)/shard_map/ppermute | solution.py:12
  234.5 234.2 %reduce-scatter.3.cloned.1.call-start = ((), (), s32[]{:S(2)}) async-start(), calls=%async_computation.4 | async-start | bytes 10485760 | tf_op jit(solution)/shard_map/reduce_scatter | solution.py:131
  241.7 263.9 %all-reduce.2.cloned.1.call-start = ((), (), s32[]{:S(2)}) async-start(), calls=%async_computation.6 | async-start | bytes 4194304 | tf_op jit(solution)/shard_map/psum | solution.py:155
  378.5 99.0 %copy-start.4 = (bf16[8,512,128]{1,2,0:T(8,128)(2,1)S(1)}, bf16[8,512,128]{1,2,0:T(8,128)(2,1)}, u32[]{:S(2)}) copy-start(bf16[8,512,128]{1,2,0:T(8,128)(2,1)} %get-tuple-element.52) | copy-start | bytes 3145732
  472.9 30.3 %all-to-all-start.1 = ((bf16[4,64,2048]{2,1,0:T(8,128)(2,1)}), bf16[4,64,2048]{2,1,0:T(8,128)(2,1)S(1)}, u32[]{:S(2)}, u32[]{:S(2)}) async-start(bf16[4,64,2048]{2,1,0:T(8,128)(2,1)} %bitcast.30), calls=%async_computation.2 | async-start | bytes 2097152 | tf_op jit(solution)/shard_map/all_to_all | solution.py:139
Sparse Core Ops, SparseCore 0:
  53.7 51.8 all-gather.2
  234.7 143.7 reduce-scatter.4
  381.6 87.1 reduce-scatter.2
  471.1 21.1 all-reduce.1
where the time goes:
time: 516 us; the launch traced here: 515 us
  waiting for transfers between devices  323 us (63%)
  matrix products  84.9 us (16%)
  local copies, waits for them, and re-layouts  43.8 us (8%)
  other arithmetic  33.2 us (6%)
  starting transfers between devices  16.5 us (3%)
  between operations  14 us (3%)
    reduce_scatter x1, waiting for transfers between devices, per_device(): lax.psum_scatter(lax.dot_general(state_rows, grad_low, (((0,), (0,)), (()...  137 us
    reduce_scatter x1, waiting for transfers between devices, per_device(): lax.psum_scatter(partial_value, 'mp', scatter_dimension=1, tiled=True)  90.2 us
    all_gather x1, waiting for transfers between devices, per_device(): lax.all_gather(arrived.reshape(rank_count * capacity, arrived.shape[2])[r...  45.3 us
    all_to_all x1, waiting for transfers between devices, per_device(): lax.all_to_all(holder.reshape(rank_count, capacity, grad_rows.shape[1]),...  24.3 us
    dot_general x8, matrix products, one_head(): lax.dot_general(grad_scores, query_head, (((0,), (0,)), ((), ())), prefer...  21.7 us
    dot_general x8, matrix products, one_head(): lax.dot_general(attention_low, grad_head, (((0,), (0,)), ((), ())), prefe...  19 us
    ppermute x2, waiting for transfers between devices, shifted_2(): return lax.ppermute(block, axis, route)  16.4 us
    dot_general x8, matrix products, one_head(): lax.dot_general(query_head, key_part, (((1,), (1,)), ((), ())), preferred...  14.5 us
  transfers between devices with their start and end apart: 8, of which 7 were waited for; matrix products, arithmetic and copies ran while one was open for 8% of the time, Pallas kernels for 0%

commit v1 on v0

v1 whole, which is shorter than its diff:
```python
import functools

import jax
import jax.numpy as jnp
from jax import lax
from jax.experimental import pallas as pl
from jax.experimental.pallas import tpu as pltpu
from jax.sharding import PartitionSpec as P

IMGTOK = 16
QTILE = 128
LOG2E = 1.4426950408889634
VMEM = 56 * 1024 * 1024

NN = (((1,), (0,)), ((), ()))
NT = (((1,), (1,)), ((), ()))
TN = (((0,), (0,)), ((), ()))


def dot(a, b, dims):
    return lax.dot_general(a, b, dims, preferred_element_type=jnp.float32)


def params():
    return pltpu.CompilerParams(vmem_limit_bytes=VMEM)


def shift(block, axis, distance):
    devices = range(lax.axis_size(axis))
    route = [(i - distance, i) for i in devices if i - distance in devices]
    return lax.ppermute(block, axis, route)


def swap(block, axis):
    count = lax.axis_size(axis)
    return lax.ppermute(block, axis, [(i, count - 1 - i) for i in range(count)])


def exchange(blocks, axis):
    return lax.all_to_all(blocks, axis, split_axis=0, concat_axis=0, tiled=True)


def rows16(start):
    return pl.ds(pl.multiple_of(start * IMGTOK, IMGTOK), IMGTOK)


def project_body(d_ref, s_ref, near_ref, far_ref, out_ref):
    half = near_ref.shape[1]
    d = d_ref[0]
    near = s_ref[:, pl.ds(pl.multiple_of(d * half, half), half)]
    far = s_ref[:, pl.ds(pl.multiple_of((1 - d) * half, half), half)]
    out_ref[0] = dot(near, near_ref[0], NN) + dot(far, far_ref[0], NN)


def project(d, states, near, far):
    heads, half, width = near.shape
    rows = states.shape[0]
    return pl.pallas_call(
        project_body,
        grid_spec=pltpu.PrefetchScalarGridSpec(
            num_scalar_prefetch=1,
            grid=(heads,),
            in_specs=[
                pl.BlockSpec(states.shape, lambda h, d: (0, 0)),
                pl.BlockSpec((1, half, width), lambda h, d: (h, 0, 0)),
                pl.BlockSpec((1, half, width), lambda h, d: (h, 0, 0)),
            ],
            out_specs=pl.BlockSpec((1, rows, width), lambda h, d: (h, 0, 0)),
        ),
        out_shape=jax.ShapeDtypeStruct((heads, rows, width), jnp.float32),
        compiler_params=params(),
    )(d, states, near, far)


def pack_body(per_shard, c_ref, place_ref, part_ref, out_ref, rounded, count):
    shards = out_ref.shape[0]
    total = part_ref[0]
    for m in range(1, part_ref.shape[0]):
        total = total + part_ref[m]
    rounded[...] = total.astype(jnp.bfloat16)
    out_ref[...] = jnp.zeros_like(out_ref)
    for s in range(shards):
        count[s] = 0
    images = rounded.shape[0] // IMGTOK
    c = c_ref[0]

    def step(i, carry):
        dest = place_ref[c * images + i] // per_shard
        slot = count[dest]
        count[dest] = slot + 1
        block = rounded[rows16(i), :]
        out_ref[dest, 0, rows16(slot), :] = block

        @pl.when(dest + 1 < shards)
        def _():
            out_ref[dest + 1, 1, rows16(slot), :] = block

        return carry

    lax.fori_loop(0, images, step, 0)


def pack(c, place, parts, shards, capacity, per_shard):
    _, rows, width = parts.shape
    smem = pl.BlockSpec(memory_space=pltpu.SMEM)
    vmem = pl.BlockSpec(memory_space=pltpu.VMEM)
    return pl.pallas_call(
        functools.partial(pack_body, per_shard),
        in_specs=[smem, smem, vmem],
        out_specs=vmem,
        out_shape=jax.ShapeDtypeStruct((shards, 2, capacity, width), jnp.bfloat16),
        scratch_shapes=[
            pltpu.VMEM((rows, width), jnp.bfloat16),
            pltpu.SMEM((shards,), jnp.int32),
        ],
        compiler_params=params(),
    )(c, place, parts)


def attention_body(
    per_shard,
    images,
    c_ref,
    place_ref,
    start_ref,
    q_ref,
    g_ref,
    own_ref,
    prior_ref,
    image_ref,
    out_ref,
    own_grad_ref,
    prior_grad_ref,
    window,
    probs,
    grads,
    total,
):
    t = pl.program_id(0)
    c = c_ref[0]
    rows = own_ref.shape[0]
    hd = own_ref.shape[1] // 2
    blocks = place_ref.shape[0]
    span = rows + QTILE
    heads = q_ref.shape[1] // hd
    scale = hd ** (-0.5)

    @pl.when(t == 0)
    def _():
        window[:rows, :] = prior_ref[...]
        window[rows:, :] = own_ref[...]
        total[...] = jnp.zeros_like(total)

        def step(b, carry):
            n_own, n_prior = carry
            rank = b // images
            fresh = b % images == 0
            n_own = jnp.where(fresh, 0, n_own)
            n_prior = jnp.where(fresh, 0, n_prior)
            at = place_ref[b] - (c - 1) * per_shard
            is_prior = (at >= 0) & (at < per_shard)
            is_own = (at >= per_shard) & (at < 2 * per_shard)

            @pl.when(is_own)
            def _():
                window[rows16(at), :] = image_ref[rank, 0, rows16(n_own), :]

            @pl.when(is_prior)
            def _():
                window[rows16(at), :] = image_ref[rank, 1, rows16(n_prior), :]

            return n_own + is_own.astype(jnp.int32), n_prior + is_prior.astype(jnp.int32)

        lax.fori_loop(0, blocks, step, (jnp.int32(0), jnp.int32(0)))

    first = pl.multiple_of(t * QTILE, QTILE)
    keys = window[pl.ds(first, span), :hd]
    values = window[pl.ds(first, span), hd:]
    values_t = values.T
    key_pos = lax.broadcasted_iota(jnp.int32, (span, QTILE), 0) + first
    query_pos = lax.broadcasted_iota(jnp.int32, (span, QTILE), 1) + (first + rows)
    allowed = (key_pos <= query_pos) & (key_pos >= start_ref[...])
    bias = jnp.where(allowed, 0.0, -1e30)
    bias = jnp.concatenate([bias, bias], axis=1)

    def stack(ref, a, b):
        return jnp.concatenate([ref[:, h * hd : (h + 1) * hd] for h in range(a, b)], axis=0)

    for h in range(0, heads, 2):
        query = stack(q_ref, h, h + 2)
        grad = stack(g_ref, h, h + 2)
        scores = dot(keys, query, NT) * (scale * LOG2E) + bias
        top = jnp.max(scores, axis=0, keepdims=True)
        e = jnp.exp2(scores - top)
        p = e * (1.0 / jnp.sum(e, axis=0, keepdims=True))
        low = p.astype(jnp.bfloat16)
        context_t = dot(values_t, low, NN)
        grad_p = dot(values, grad, NT)
        grad_t = grad.astype(jnp.float32).T
        delta = jnp.sum(grad_t * context_t, axis=0, keepdims=True)
        ds = (p * (grad_p - delta)).astype(jnp.bfloat16)
        context = context_t.T.astype(jnp.bfloat16)
        out_ref[:, h * hd : (h + 1) * hd] = context[:QTILE]
        out_ref[:, (h + 1) * hd : (h + 2) * hd] = context[QTILE:]
        probs[:, h * QTILE : (h + 2) * QTILE] = low
        grads[:, h * QTILE : (h + 2) * QTILE] = ds
    total[pl.ds(first, span), :hd] += dot(grads[...], stack(q_ref, 0, heads), NN)
    total[pl.ds(first, span), hd:] += dot(probs[...], stack(g_ref, 0, heads), NN)

    @pl.when(t == pl.num_programs(0) - 1)
    def _():
        total[:, :hd] = total[:, :hd] * scale
        prior_grad_ref[...] = jnp.zeros_like(prior_grad_ref)

        def step(b, carry):
            n_own, n_prior = carry
            at = place_ref[b] - (c - 1) * per_shard
            is_prior = (at >= 0) & (at < per_shard)
            is_own = (at >= per_shard) & (at < 2 * per_shard)

            @pl.when(is_own)
            def _():
                own_grad_ref[rows16(n_own), :] = total[rows16(at), :]

            @pl.when(is_prior)
            def _():
                prior_grad_ref[rows16(n_prior), :] = total[rows16(at), :]

            return n_own + is_own.astype(jnp.int32), n_prior + is_prior.astype(jnp.int32)

        lax.fori_loop(0, blocks, step, (jnp.int32(0), jnp.int32(0)))


def attention(c, place, start, queries, d_out, own, prior, image, images, per_shard, image_rows):
    rows, width = own.shape
    cols = queries.shape[1]
    tiles = rows // QTILE
    span = rows + QTILE
    head_rows = cols // (width // 2) * QTILE
    whole = lambda a: pl.BlockSpec(a.shape, lambda t, *_: (0,) * a.ndim)
    tile = pl.BlockSpec((QTILE, cols), lambda t, *_: (t, 0))
    grad = jax.ShapeDtypeStruct((image_rows, width), jnp.float32)
    return pl.pallas_call(
        functools.partial(attention_body, per_shard, images),
        grid_spec=pltpu.PrefetchScalarGridSpec(
            num_scalar_prefetch=2,
            grid=(tiles,),
            in_specs=[
                pl.BlockSpec((1, QTILE), lambda t, *_: (0, t)),
                tile,
                tile,
                whole(own),
                whole(prior),
                whole(image),
            ],
            out_specs=[tile, whole(grad), whole(grad)],
            scratch_shapes=[
                pltpu.VMEM((2 * rows, width), jnp.bfloat16),
                pltpu.VMEM((span, head_rows), jnp.bfloat16),
                pltpu.VMEM((span, head_rows), jnp.bfloat16),
                pltpu.VMEM((2 * rows, width), jnp.float32),
            ],
        ),
        out_shape=[jax.ShapeDtypeStruct((rows, cols), jnp.bfloat16), grad, grad],
        compiler_params=params(),
    )(c, place, start, queries, d_out, own, prior, image)


def reorder_body(per_shard, images, c_ref, place_ref, g_ref, out_ref, mine_ref, count):
    shards = g_ref.shape[0]
    for s in range(shards):
        count[s] = 0
    c = c_ref[0]

    def step(b, carry):
        dest = place_ref[b] // per_shard
        slot = count[dest]
        count[dest] = slot + 1
        out_ref[rows16(b), :] = g_ref[dest, rows16(slot), :]
        return carry

    lax.fori_loop(0, place_ref.shape[0], step, 0)
    rows = mine_ref.shape[1]
    mine = out_ref[pl.ds(pl.multiple_of(c * rows, IMGTOK), rows), :]
    for m in range(mine_ref.shape[0]):
        mine_ref[m] = mine


def reorder(c, place, gathered, copies, per_shard, images):
    shards, rows, width = gathered.shape
    smem = pl.BlockSpec(memory_space=pltpu.SMEM)
    vmem = pl.BlockSpec(memory_space=pltpu.VMEM)
    return pl.pallas_call(
        functools.partial(reorder_body, per_shard, images),
        in_specs=[smem, smem, vmem],
        out_specs=[vmem, vmem],
        out_shape=[
            jax.ShapeDtypeStruct((shards * rows, width), gathered.dtype),
            jax.ShapeDtypeStruct((copies, rows, width), gathered.dtype),
        ],
        scratch_shapes=[pltpu.SMEM((shards,), jnp.int32)],
        compiler_params=params(),
    )(c, place, gathered)


def weight_body(s_ref, g_ref, out_ref):
    out_ref[...] = dot(s_ref[0], g_ref[...], TN)


def weight_term(states, grad):
    parts, rows, cols = states.shape
    width = grad.shape[1]
    return pl.pallas_call(
        weight_body,
        grid=(parts,),
        in_specs=[
            pl.BlockSpec((1, rows, cols), lambda k: (k, 0, 0)),
            pl.BlockSpec((rows, width), lambda k: (0, 0)),
        ],
        out_specs=pl.BlockSpec((cols, width), lambda k: (k, 0)),
        out_shape=jax.ShapeDtypeStruct((parts * cols, width), jnp.float32),
        compiler_params=params(),
    )(states, grad)


def image_body(d_ref, g_ref, near_ref, far_ref, out_ref):
    j = pl.program_id(0)
    heads, cols, _ = near_ref.shape
    half = out_ref.shape[1] // 2
    d = d_ref[0]
    for ref, side in ((near_ref, d), (far_ref, 1 - d)):
        total = dot(g_ref[0], ref[0], NT)
        for h in range(1, heads):
            total = total + dot(g_ref[h], ref[h], NT)
        at = pl.multiple_of(side * half + j * cols, cols)
        out_ref[:, pl.ds(at, cols)] = total.astype(out_ref.dtype)


def image_term(d, grad, near, far):
    heads, half, width = near.shape
    rows = grad.shape[1]
    tiles = 4
    side = pl.BlockSpec((heads, half // tiles, width), lambda j, d: (0, j, 0))
    return pl.pallas_call(
        image_body,
        grid_spec=pltpu.PrefetchScalarGridSpec(
            num_scalar_prefetch=1,
            grid=(tiles,),
            in_specs=[pl.BlockSpec(grad.shape, lambda j, d: (0, 0, 0)), side, side],
            out_specs=pl.BlockSpec((rows, 2 * half), lambda j, d: (0, 0)),
        ),
        out_shape=jax.ShapeDtypeStruct((rows, 2 * half), jnp.bfloat16),
        compiler_params=params(),
    )(d, grad, near, far)


def per_device(image_states, place_index, doc_ids, queries, text_kv, kv_weight, d_out):
    ranks = lax.axis_size("ctx")
    mps = lax.axis_size("mp")
    c = lax.axis_index("ctx")
    d = lax.axis_index("dp")
    rows = queries.shape[1]
    states = image_states[0]
    image_rows, feats = states.shape
    images = image_rows // IMGTOK
    per_shard = rows // IMGTOK
    capacity = IMGTOK * ((images + ranks - 1) // ranks)
    weights = kv_weight[0]
    width = weights.shape[1]
    c1 = jnp.reshape(c, (1,)).astype(jnp.int32)
    d1 = jnp.reshape(d, (1,)).astype(jnp.int32)
    place = place_index[0, ::IMGTOK] // IMGTOK

    halves = weights.reshape(mps, 2, feats // 2, width)
    mine = lax.dynamic_index_in_dim(halves, d, axis=1, keepdims=False)
    near = exchange(mine, "mp")
    far = swap(near, "dp")

    sub = feats * mps // ranks // mps
    per_mp = ranks // mps
    pieces = states.reshape(image_rows, per_mp, mps, sub).transpose(2, 0, 1, 3)
    pieces = exchange(pieces, "mp")
    pieces = pieces.transpose(0, 2, 1, 3).reshape(ranks, image_rows, sub)
    pieces = exchange(pieces, "ctx").reshape(ranks * image_rows, sub)
    all_states = lax.all_gather(pieces, "mp", axis=0)

    prior_text = shift(text_kv[0], "ctx", 1)
    docs = doc_ids[0]
    own_docs = lax.dynamic_slice_in_dim(docs, c * rows, rows)
    prior_docs = lax.dynamic_slice_in_dim(docs, jnp.maximum(c - 1, 0) * rows, rows)
    prior_docs = jnp.where(c > 0, prior_docs, -1)
    key_docs = jnp.concatenate([prior_docs, own_docs])
    start = jnp.sum((key_docs[:, None] < own_docs[None, :]).astype(jnp.int32), axis=0)[None]

    parts = exchange(project(d1, states, near, far), "mp")
    packed = pack(c1, place, parts, ranks, capacity, per_shard)
    image = exchange(packed, "ctx")
    attn_out, own_grad, prior_grad = attention(
        c1, place, start, queries[0], d_out[0], text_kv[0], prior_text, image,
        images, per_shard, image_rows,
    )
    grad = (own_grad + shift(prior_grad, "ctx", -1)).astype(jnp.bfloat16)
    gathered = exchange(jnp.broadcast_to(grad, (ranks,) + grad.shape), "ctx")
    by_rank, mine = reorder(c1, place, gathered, mps, per_shard, images)
    head_grad = exchange(mine, "mp")
    image_grad = image_term(d1, head_grad, near, far)
    term = weight_term(all_states, by_rank)
    weight_grad = term + swap(term, "dp")
    return (attn_out[None], image_grad[None], weight_grad[None])


def solution(mesh):
    in_specs = (
        P("dp", "ctx", "mp"),
        P("dp", None),
        P("dp", None),
        P("dp", "ctx", "mp"),
        P("dp", "ctx", "mp"),
        P("mp", None, None),
        P("dp", "ctx", "mp"),
    )
    out_specs = (P("dp", "ctx", "mp"), P("dp", "ctx", "mp"), P("mp", "ctx", None))
    return jax.shard_map(
        per_device, mesh=mesh, in_specs=in_specs, out_specs=out_specs, check_vma=False
    )
```

time: 516 us -> 238 us (0.46)
  waiting for transfers between devices: 323 us -> 66 us
  blocking collectives: 0 us -> 88.3 us
  matrix products: 84.9 us -> 0 us
  Pallas kernels: 0 us -> 39.2 us
  local copies, waits for them, and re-layouts: 43.8 us -> 8.69 us
  other arithmetic: 33.2 us -> 4.05 us
    reduce_scatter x2 -> x0, waiting for transfers between devices: 227 us -> none  [the longest x1 137 us: per_device(): lax.psum_scatter(lax.dot_general(state_rows, grad_low, (((0,), (0,)), (()...]
    all_to_all x0 -> x4, blocking collectives: none -> 88.3 us  [exchange(): return lax.all_to_all(blocks, axis, split_axis=0, concat_axis=0, tiled=True)]
    dot_general x35 -> x0, matrix products: 84.9 us -> none  [the longest x8 21.7 us: one_head(): lax.dot_general(grad_scores, query_head, (((0,), (0,)), ((), ())), prefer...]
    all_gather x1, waiting for transfers between devices: 45.3 us -> 0.01 us  [per_device(): all_states = lax.all_gather(pieces, 'mp', axis=0)]
    pallas_call x0 -> x6, Pallas kernels: none -> 39.2 us  [the longest x1 18 us: attention(): pl.pallas_call(functools.partial(attention_body, per_shard, images), grid...]
    scatter x4 -> x0, local copies, waits for them, and re-layouts: 13.4 us -> none  [the longest x1 4.3 us: routing_tables(): jnp.zeros((image_dev,), jnp.int32).at[compact].set(recv_flat, mode='drop')]
    all_to_all x2 -> x3, waiting for transfers between devices: 33.8 us -> 46.5 us  [exchange(): return lax.all_to_all(blocks, axis, split_axis=0, concat_axis=0, tiled=True)]
    gather x4 -> x0, local copies, waits for them, and re-layouts: 12.7 us -> none  [the longest x1 6.86 us: routing_tables(): compact = jnp.where(is_mine, compact_of_pos[local_pos], image_dev)]
  transfers between devices with their start and end apart: 8 -> 8, of which waited for: 7 -> 5; matrix products, arithmetic and copies ran while one was open for 8% -> 2% of each run, Pallas kernels for 0% -> 14%
where the time goes in v1:
time: 238 us
  blocking collectives  88.3 us (37%)
  waiting for transfers between devices  66 us (28%)
  Pallas kernels  39.2 us (16%)
  starting transfers between devices  17.1 us (7%)
  between operations  14.1 us (6%)
  local copies, waits for them, and re-layouts  8.69 us (4%)
  other arithmetic  4.05 us (2%)
    all_to_all x4, blocking collectives, exchange(): return lax.all_to_all(blocks, axis, split_axis=0, concat_axis=0, tiled=True)  88.3 us
    all_to_all x3, waiting for transfers between devices, exchange(): return lax.all_to_all(blocks, axis, split_axis=0, concat_axis=0, tiled=True)  46.5 us
    pallas_call x1, Pallas kernels, attention(): pl.pallas_call(functools.partial(attention_body, per_shard, images), grid...  18 us
    ppermute x2, waiting for transfers between devices, shift(): return lax.ppermute(block, axis, route)  15.3 us
    all_to_all x3, starting transfers between devices, exchange(): return lax.all_to_all(blocks, axis, split_axis=0, concat_axis=0, tiled=True)  11.9 us
    unnamed x21, local copies, waits for them, and re-layouts  5.54 us
    pallas_call x1, Pallas kernels, weight_term(): pl.pallas_call(weight_body, grid=(parts,), in_specs=[pl.BlockSpec((1, row...  5.33 us
    pallas_call x1, Pallas kernels, image_term(): pl.pallas_call(image_body, grid_spec=pltpu.PrefetchScalarGridSpec(num_sca...  5.24 us
  transfers between devices with their start and end apart: 8, of which 5 were waited for; matrix products, arithmetic and copies ran while one was open for 2% of the time, Pallas kernels for 14%

profile of v1, /device:TPU:0, one launch (start us, length us, event | category | flops | bytes accessed | tf_op | source)
XLA Modules:
  0.0 237.5 jit_solution(3773368690426125936)
XLA Ops:
  7.2 1.5 copy.17
  9.2 19.2 %all_to_all.35 = bf16[4,256,1,512]{3,1,2,0:T(8,128)(2,1)} all-to-all(bf16[4,256,1,512]{3,1,2,0:T(8,128)(2,1)S(1)} %copy.18), channel_id=1, replica_groups=mesh['dp'=2,'ctx'=4,'mp'=4] {'mp'}, dimensions={0} | all-to-all | bytes 2097152 | tf_op jit(solution)/shard_map/all_to_all | solution.py:40
  28.4 4.9 %all-to-all-start.6 = ((bf16[4,256,512]{2,1,0:T(8,128)(2,1)}), bf16[4,256,512]{2,1,0:T(8,128)(2,1)S(1)}, u32[]{:S(2)}, u32[]{:S(2)}) async-start(bf16[4,256,512]{2,1,0:T(8,128)(2,1)} %bitcast.16), calls=%async_computation.6 | async-start | bytes 2097152 | tf_op jit(solution)/shard_map/all_to_all | solution.py:40
  33.3 24.2 %all-to-all-done.6 = bf16[4,256,512]{2,1,0:T(8,128)(2,1)S(1)} async-done(((bf16[4,256,512]{2,1,0:T(8,128)(2,1)}), bf16[4,256,512]{2,1,0:T(8,128)(2,1)S(1)}, u32[]{:S(2)}, u32[]{:S(2)}) %all-to-all-start.6) | async-done | bytes 1048608 | tf_op jit(solution)/shard_map/all_to_all | solution.py:40
  58.5 1.7 dynamic-slice_bitcast_fusion
  60.2 38.6 %all_to_all.36.near_ref = bf16[4,1024,256]{2,1,0:T(8,128)(2,1)S(1)} all-to-all(bf16[4,1024,256]{2,1,0:T(8,128)(2,1)S(1)} %dynamic-slice_bitcast_fusion), channel_id=1, replica_groups=mesh['dp'=2,'ctx'=4,'mp'=4] {'mp'}, dimensions={0} | all-to-all | bytes 4194304 | tf_op jit(solution)/shard_map/all_to_all | solution.py:40
  98.8 4.2 %collective-permute-done.1.far_ref = bf16[4,1024,256]{2,1,0:T(8,128)(2,1)S(1)} collective-permute-done((bf16[4,1024,256]{2,1,0:T(8,128)(2,1)S(1)}, bf16[4,1024,256]{2,1,0:T(8,128)(2,1)S(1)}, u32[]{:S(2)}, u32[]{:S(2)}) %collective-permute-start.1) | collective-permute-done | bytes 2097184 | tf_op jit(solution)/shard_map/ppermute | solution.py:36
  102.9 1.3 copy-done.1
  104.3 5.1 %shard_map.94 = f32[4,256,256]{2,1,0:T(8,128)} custom-call(s32[1]{0:T(128)} %bitcast.8.d_ref, bf16[256,2048]{1,0:T(8,128)(2,1)} %bitcast.31, bf16[4,1024,256]{2,1,0:T(8,128)(2,1)} %copy-done, bf16[4,1024,256]{2,1,0:T(8,128)(2,1)} %copy-done.1), custom_call_target="tpu_custom_call" | custom-call | tf_op jit(solution)/shard_map/pallas_call | solution.py:58
  109.4 3.6 %all-to-all-start.1 = ((f32[4,256,256]{2,1,0:T(8,128)}), f32[4,256,256]{2,1,0:T(8,128)S(1)}, u32[]{:S(2)}, u32[]{:S(2)}) async-start(f32[4,256,256]{2,1,0:T(8,128)} %shard_map.94), calls=%async_computation.1 | async-start | bytes 2097152 | tf_op jit(solution)/shard_map/all_to_all | solution.py:40
  114.5 22.3 %all-to-all-done.1.part_ref = f32[4,256,256]{2,1,0:T(8,128)S(1)} async-done(((f32[4,256,256]{2,1,0:T(8,128)}), f32[4,256,256]{2,1,0:T(8,128)S(1)}, u32[]{:S(2)}, u32[]{:S(2)}) %all-to-all-start.1) | async-done | bytes 1048608 | tf_op jit(solution)/shard_map/all_to_all | solution.py:40
  137.8 2.4 shard_map.95
  140.1 3.4 %all-to-all-start.2 = ((bf16[4,2,64,256]{3,2,1,0:T(8,128)(2,1)}), bf16[4,2,64,256]{3,2,1,0:T(8,128)(2,1)S(1)}, u32[]{:S(2)}, u32[]{:S(2)}) async-start(bf16[4,2,64,256]{3,2,1,0:T(8,128)(2,1)} %shard_map.95), calls=%async_computation.2 | async-start | bytes 524288 | tf_op jit(solution)/shard_map/all_to_all | solution.py:40
  143.6 3.9 %collective-permute-start = (bf16[512,256]{1,0:T(8,128)(2,1)S(1)}, bf16[512,256]{1,0:T(8,128)(2,1)S(1)}, u32[]{:S(2)}, u32[]{:S(2)}) collective-permute-start(bf16[512,256]{1,0:T(8,128)(2,1)S(1)} %bitcast.39), channel_id=1, source_target_pairs={{0,4},{4,8},{8,12},{1,5},{5,9},{9,13},{2,6},{6,10},{10,14},{3,7},{... | collective-permute-start | bytes 786440 | tf_op jit(solution)/shard_map/ppermute | solution.py:31
  148.4 5.5 %collective-permute-done.prior_ref = bf16[512,256]{1,0:T(8,128)(2,1)S(1)} collective-permute-done((bf16[512,256]{1,0:T(8,128)(2,1)S(1)}, bf16[512,256]{1,0:T(8,128)(2,1)S(1)}, u32[]{:S(2)}, u32[]{:S(2)}) %collective-permute-start) | collective-permute-done | bytes 262176 | tf_op jit(solution)/shard_map/ppermute | solution.py:31
  154.7 18.0 %shard_map.96 = (bf16[512,1024]{1,0:T(8,128)(2,1)}, f32[256,256]{1,0:T(8,128)}, f32[256,256]{1,0:T(8,128)}) custom-call(s32[1]{0:T(128)} %bitcast.c_ref, s32[64]{0:T(128)} %and_select_fusion.place_ref, s32[1,512]{1,0:T(1,128)} %bitcast.42, bf16[512,1024]{1,0:T(8,128)(2,1)} %bitcast.34, bf16[512,1024]{1,0:T(8,128)(2,1)} %bitcast.35, ...), custom_call_target="tpu_custom_call" | custom-call | tf_op jit(solution)/shard_map/pallas_call | solution.py:243
  172.7 1.3 collective-permute-start.2
  174.0 9.8 %collective-permute-done.2 = f32[256,256]{1,0:T(8,128)S(1)} collective-permute-done((f32[256,256]{1,0:T(8,128)}, f32[256,256]{1,0:T(8,128)S(1)}, u32[]{:S(2)}, u32[]{:S(2)}) %collective-permute-start.2) | collective-permute-done | bytes 262176 | tf_op jit(solution)/shard_map/ppermute | solution.py:31
  184.8 17.9 %all_to_all.37.g_ref = bf16[4,256,256]{2,1,0:T(8,128)(2,1)} all-to-all(bf16[4,256,256]{2,1,0:T(8,128)(2,1)S(1)} %broadcast_in_dim.24), channel_id=1, replica_groups=mesh['dp'=2,'ctx'=4,'mp'=4] {'ctx'}, dimensions={0} | all-to-all | bytes 1048576 | tf_op jit(solution)/shard_map/all_to_all | solution.py:40
  202.7 3.2 %shard_map.97 = (bf16[1024,256]{1,0:T(8,128)(2,1)}, bf16[4,256,256]{2,1,0:T(8,128)(2,1)}) custom-call(s32[1]{0:T(128)} %bitcast.c_ref, s32[64]{0:T(128)} %and_select_fusion.place_ref, bf16[4,256,256]{2,1,0:T(8,128)(2,1)} %all_to_all.37.g_ref), custom_call_target="tpu_custom_call" | custom-call | tf_op jit(solution)/shard_map/pallas_call | solution.py:293
  205.9 5.3 %shard_map.99 = f32[2048,256]{1,0:T(8,128)} custom-call(bf16[4,1024,512]{2,1,0:T(8,128)(2,1)} %all-gather.2.cloned.1.call-done.s_ref, bf16[1024,256]{1,0:T(8,128)(2,1)} %get-tuple-element.12.g_ref), custom_call_target="tpu_custom_call" | custom-call | tf_op jit(solution)/shard_map/pallas_call | solution.py:313
  211.3 12.6 %all_to_all.38.g_ref = bf16[4,256,256]{2,1,0:T(8,128)(2,1)} all-to-all(bf16[4,256,256]{2,1,0:T(8,128)(2,1)S(1)} %copy-done.6), channel_id=1, replica_groups=mesh['dp'=2,'ctx'=4,'mp'=4] {'mp'}, dimensions={0} | all-to-all | bytes 1048576 | tf_op jit(solution)/shard_map/all_to_all | solution.py:40
  223.8 5.2 %shard_map.98 = bf16[256,2048]{1,0:T(8,128)(2,1)} custom-call(s32[1]{0:T(128)} %bitcast.8.d_ref, bf16[4,256,256]{2,1,0:T(8,128)(2,1)} %all_to_all.38.g_ref, bf16[4,1024,256]{2,1,0:T(8,128)(2,1)} %copy-done, bf16[4,1024,256]{2,1,0:T(8,128)(2,1)} %copy-done.1), custom_call_target="tpu_custom_call" | custom-call | tf_op jit(solution)/shard_map/pallas_call | solution.py:344
  229.1 1.6 add_bitcast_fusion
  (34 shorter events, 6.6 us)
Async XLA Ops:
  28.4 29.1 %all-to-all-start.6 = ((bf16[4,256,512]{2,1,0:T(8,128)(2,1)}), bf16[4,256,512]{2,1,0:T(8,128)(2,1)S(1)}, u32[]{:S(2)}, u32[]{:S(2)}) async-start(bf16[4,256,512]{2,1,0:T(8,128)(2,1)} %bitcast.16), calls=%async_computation.6 | async-start | bytes 2097152 | tf_op jit(solution)/shard_map/all_to_all | solution.py:40
  33.3 172.6 %all-gather.2.cloned.1.call-start = ((), (), s32[]{:S(2)}) async-start(), calls=%async_computation.7 | async-start | bytes 5242880 | tf_op jit(solution)/shard_map/all_gather | solution.py:385
  57.5 1.0 copy-start.3
  98.8 4.2 %copy-start = (bf16[4,1024,256]{2,1,0:T(8,128)(2,1)}, bf16[4,1024,256]{2,1,0:T(8,128)(2,1)S(1)}, u32[]{:S(2)}) copy-start(bf16[4,1024,256]{2,1,0:T(8,128)(2,1)S(1)} %all_to_all.36.near_ref) | copy-start | bytes 6291460
  98.8 4.2 %collective-permute-start.1 = (bf16[4,1024,256]{2,1,0:T(8,128)(2,1)S(1)}, bf16[4,1024,256]{2,1,0:T(8,128)(2,1)S(1)}, u32[]{:S(2)}, u32[]{:S(2)}) collective-permute-start(bf16[4,1024,256]{2,1,0:T(8,128)(2,1)S(1)} %all_to_all.36.near_ref), channel_id=1, source_target_pairs={{0,16},{16,0},{1,17},{17,1},{2,18},{18,2},{3,19},{19,3},{4,20},{20... | collective-permute-start | bytes 6291464 | tf_op jit(solution)/shard_map/ppermute | solution.py:36
  102.9 1.3 copy-start.1
  109.4 34.2 %copy-start.7 = (bf16[1,512,256]{2,1,0:T(8,128)(2,1)S(1)}, bf16[1,512,256]{2,1,0:T(8,128)(2,1)}, u32[]{:S(2)}) copy-start(bf16[1,512,256]{2,1,0:T(8,128)(2,1)} %param.11) | copy-start | bytes 786436
  109.4 38.1 %copy-start.9 = (s32[1,2048]{1,0:T(1,128)S(1)}, s32[1,2048]{1,0:T(1,128)}, u32[]{:S(2)}) copy-start(s32[1,2048]{1,0:T(1,128)} %param.9) | copy-start | bytes 24580
  109.4 27.4 %all-to-all-start.1 = ((f32[4,256,256]{2,1,0:T(8,128)}), f32[4,256,256]{2,1,0:T(8,128)S(1)}, u32[]{:S(2)}, u32[]{:S(2)}) async-start(f32[4,256,256]{2,1,0:T(8,128)} %shard_map.94), calls=%async_computation.1 | async-start | bytes 2097152 | tf_op jit(solution)/shard_map/all_to_all | solution.py:40
  136.8 1.0 copy-start.4
  140.1 13.8 %all-to-all-start.2 = ((bf16[4,2,64,256]{3,2,1,0:T(8,128)(2,1)}), bf16[4,2,64,256]{3,2,1,0:T(8,128)(2,1)S(1)}, u32[]{:S(2)}, u32[]{:S(2)}) async-start(bf16[4,2,64,256]{3,2,1,0:T(8,128)(2,1)} %shard_map.95), calls=%async_computation.2 | async-start | bytes 524288 | tf_op jit(solution)/shard_map/all_to_all | solution.py:40
  143.6 10.3 %collective-permute-start = (bf16[512,256]{1,0:T(8,128)(2,1)S(1)}, bf16[512,256]{1,0:T(8,128)(2,1)S(1)}, u32[]{:S(2)}, u32[]{:S(2)}) collective-permute-start(bf16[512,256]{1,0:T(8,128)(2,1)S(1)} %bitcast.39), channel_id=1, source_target_pairs={{0,4},{4,8},{8,12},{1,5},{5,9},{9,13},{2,6},{6,10},{10,14},{3,7},{... | collective-permute-start | bytes 786440 | tf_op jit(solution)/shard_map/ppermute | solution.py:31
  153.9 0.7 copy-start.8
  153.9 0.8 copy-start.5
  172.7 11.1 %collective-permute-start.2 = (f32[256,256]{1,0:T(8,128)}, f32[256,256]{1,0:T(8,128)S(1)}, u32[]{:S(2)}, u32[]{:S(2)}) collective-permute-start(f32[256,256]{1,0:T(8,128)} %get-tuple-element.10), channel_id=1, source_target_pairs={{4,0},{8,4},{12,8},{5,1},{9,5},{13,9},{6,2},{10,6},{14,10},{7,3},{... | collective-permute-start | bytes 786440 | tf_op jit(solution)/shard_map/ppermute | solution.py:31
  205.9 5.3 %copy-start.6 = (bf16[4,256,256]{2,1,0:T(8,128)(2,1)S(1)}, bf16[4,256,256]{2,1,0:T(8,128)(2,1)}, u32[]{:S(2)}) copy-start(bf16[4,256,256]{2,1,0:T(8,128)(2,1)} %get-tuple-element.11) | copy-start | bytes 1572868
  211.3 17.8 %collective-permute-start.3 = (f32[2048,256]{1,0:T(8,128)}, f32[2048,256]{1,0:T(8,128)S(1)}, u32[]{:S(2)}, u32[]{:S(2)}) collective-permute-start(f32[2048,256]{1,0:T(8,128)} %shard_map.99), channel_id=1, source_target_pairs={{0,16},{16,0},{1,17},{17,1},{2,18},{18,2},{3,19},{19,3},{4,20},{20... | collective-permute-start | bytes 6291464 | tf_op jit(solution)/shard_map/ppermute | solution.py:36
  223.8 5.2 %copy-start.2 = (f32[2048,256]{1,0:T(8,128)S(1)}, f32[2048,256]{1,0:T(8,128)}, u32[]{:S(2)}) copy-start(f32[2048,256]{1,0:T(8,128)} %shard_map.99) | copy-start | bytes 6291460
Sparse Core Ops, SparseCore 0:
  58.6 78.5 all-gather.1

commit v2 on v1

--- a/solution.py
+++ b/solution.py
@@ -10,7 +10,7 @@
 IMGTOK = 16
 QTILE = 128
 LOG2E = 1.4426950408889634
-VMEM = 56 * 1024 * 1024
+VMEM = 24 * 1024 * 1024
 
 NN = (((1,), (0,)), ((), ()))
 NT = (((1,), (1,)), ((), ()))
@@ -23,6 +23,10 @@
 
 def params():
     return pltpu.CompilerParams(vmem_limit_bytes=VMEM)
+
+
+def cost(flops, moved):
+    return pl.CostEstimate(flops=int(flops), bytes_accessed=int(moved), transcendentals=0)
 
 
 def shift(block, axis, distance):
@@ -40,43 +44,43 @@
     return lax.all_to_all(blocks, axis, split_axis=0, concat_axis=0, tiled=True)
 
 
+def trade(block, axis, step):
+    count = lax.axis_size(axis)
+    return lax.ppermute(block, axis, [(i, i ^ step) for i in range(count)])
+
+
 def rows16(start):
     return pl.ds(pl.multiple_of(start * IMGTOK, IMGTOK), IMGTOK)
 
 
 def project_body(d_ref, s_ref, near_ref, far_ref, out_ref):
-    half = near_ref.shape[1]
+    half = near_ref.shape[0]
     d = d_ref[0]
     near = s_ref[:, pl.ds(pl.multiple_of(d * half, half), half)]
     far = s_ref[:, pl.ds(pl.multiple_of((1 - d) * half, half), half)]
-    out_ref[0] = dot(near, near_ref[0], NN) + dot(far, far_ref[0], NN)
+    out_ref[...] = dot(near, near_ref[...], NN) + dot(far, far_ref[...], NN)
 
 
 def project(d, states, near, far):
-    heads, half, width = near.shape
+    half, width = near.shape
     rows = states.shape[0]
+    vmem = pl.BlockSpec(memory_space=pltpu.VMEM)
     return pl.pallas_call(
         project_body,
-        grid_spec=pltpu.PrefetchScalarGridSpec(
-            num_scalar_prefetch=1,
-            grid=(heads,),
-            in_specs=[
-                pl.BlockSpec(states.shape, lambda h, d: (0, 0)),
-                pl.BlockSpec((1, half, width), lambda h, d: (h, 0, 0)),
-                pl.BlockSpec((1, half, width), lambda h, d: (h, 0, 0)),
-            ],
-            out_specs=pl.BlockSpec((1, rows, width), lambda h, d: (h, 0, 0)),
-        ),
-        out_shape=jax.ShapeDtypeStruct((heads, rows, width), jnp.float32),
+        in_specs=[pl.BlockSpec(memory_space=pltpu.SMEM), vmem, vmem, vmem],
+        out_specs=vmem,
+        out_shape=jax.ShapeDtypeStruct((rows, width), jnp.float32),
+        cost_estimate=cost(4 * rows * half * width, 4 * states.size),
         compiler_params=params(),
     )(d, states, near, far)
 
 
-def pack_body(per_shard, c_ref, place_ref, part_ref, out_ref, rounded, count):
+def pack_body(per_shard, c_ref, place_ref, *refs):
+    *part_refs, out_ref, rounded, count = refs
     shards = out_ref.shape[0]
-    total = part_ref[0]
-    for m in range(1, part_ref.shape[0]):
-        total = total + part_ref[m]
+    total = part_refs[0][...]
+    for ref in part_refs[1:]:
+        total = total + ref[...]
     rounded[...] = total.astype(jnp.bfloat16)
     out_ref[...] = jnp.zeros_like(out_ref)
     for s in range(shards):
@@ -101,20 +105,21 @@
 
 
 def pack(c, place, parts, shards, capacity, per_shard):
-    _, rows, width = parts.shape
+    rows, width = parts[0].shape
     smem = pl.BlockSpec(memory_space=pltpu.SMEM)
     vmem = pl.BlockSpec(memory_space=pltpu.VMEM)
     return pl.pallas_call(
         functools.partial(pack_body, per_shard),
-        in_specs=[smem, smem, vmem],
+        in_specs=[smem, smem] + [vmem] * len(parts),
         out_specs=vmem,
         out_shape=jax.ShapeDtypeStruct((shards, 2, capacity, width), jnp.bfloat16),
         scratch_shapes=[
             pltpu.VMEM((rows, width), jnp.bfloat16),
             pltpu.SMEM((shards,), jnp.int32),
         ],
-        compiler_params=params(),
-    )(c, place, parts)
+        cost_estimate=cost(0, parts[0].size * 4 * 6),
+        compiler_params=params(),
+    )(c, place, *parts)
 
 
 def attention_body(
@@ -262,6 +267,7 @@
             ],
         ),
         out_shape=[jax.ShapeDtypeStruct((rows, cols), jnp.bfloat16), grad, grad],
+        cost_estimate=cost(2 * 20 * cols * span * rows, 4 * queries.size * 2),
         compiler_params=params(),
     )(c, place, start, queries, d_out, own, prior, image)
 
@@ -280,13 +286,11 @@
         return carry
 
     lax.fori_loop(0, place_ref.shape[0], step, 0)
-    rows = mine_ref.shape[1]
-    mine = out_ref[pl.ds(pl.multiple_of(c * rows, IMGTOK), rows), :]
-    for m in range(mine_ref.shape[0]):
-        mine_ref[m] = mine
-
-
-def reorder(c, place, gathered, copies, per_shard, images):
+    rows = mine_ref.shape[0]
+    mine_ref[...] = out_ref[pl.ds(pl.multiple_of(c * rows, IMGTOK), rows), :]
+
+
+def reorder(c, place, gathered, per_shard, images):
     shards, rows, width = gathered.shape
     smem = pl.BlockSpec(memory_space=pltpu.SMEM)
     vmem = pl.BlockSpec(memory_space=pltpu.VMEM)
@@ -296,62 +300,76 @@
         out_specs=[vmem, vmem],
         out_shape=[
             jax.ShapeDtypeStruct((shards * rows, width), gathered.dtype),
-            jax.ShapeDtypeStruct((copies, rows, width), gathered.dtype),
+            jax.ShapeDtypeStruct((rows, width), gathered.dtype),
         ],
         scratch_shapes=[pltpu.SMEM((shards,), jnp.int32)],
+        cost_estimate=cost(0, gathered.size * 2 * 4),
         compiler_params=params(),
     )(c, place, gathered)
 
 
-def weight_body(s_ref, g_ref, out_ref):
-    out_ref[...] = dot(s_ref[0], g_ref[...], TN)
-
-
-def weight_term(states, grad):
+def weight_body(mixed, s_ref, g_ref, out_ref):
+    k = pl.program_id(0)
+    ranks, rows, _ = g_ref.shape
+    if not mixed:
+        out_ref[...] = dot(s_ref[0], g_ref[...].reshape(ranks * rows, -1), TN)
+        return
+    grad = jnp.concatenate([g_ref[k ^ s] for s in range(ranks)], axis=0)
+    out_ref[...] = dot(s_ref[0], grad, TN)
+
+
+def weight_term(states, grad, mixed):
     parts, rows, cols = states.shape
-    width = grad.shape[1]
-    return pl.pallas_call(
-        weight_body,
+    width = grad.shape[2]
+    return pl.pallas_call(
+        functools.partial(weight_body, mixed),
         grid=(parts,),
         in_specs=[
             pl.BlockSpec((1, rows, cols), lambda k: (k, 0, 0)),
-            pl.BlockSpec((rows, width), lambda k: (0, 0)),
+            pl.BlockSpec(grad.shape, lambda k: (0, 0, 0)),
         ],
         out_specs=pl.BlockSpec((cols, width), lambda k: (k, 0)),
         out_shape=jax.ShapeDtypeStruct((parts * cols, width), jnp.float32),
+        cost_estimate=cost(2 * states.size * width, states.size * 4),
         compiler_params=params(),
     )(states, grad)
 
 
-def image_body(d_ref, g_ref, near_ref, far_ref, out_ref):
+def image_body(d_ref, *refs):
+    out_ref = refs[-1]
+    heads = (len(refs) - 1) // 3
+    grads, sides = refs[:heads], (refs[heads : 2 * heads], refs[2 * heads : -1])
     j = pl.program_id(0)
-    heads, cols, _ = near_ref.shape
+    cols = sides[0][0].shape[0]
     half = out_ref.shape[1] // 2
     d = d_ref[0]
-    for ref, side in ((near_ref, d), (far_ref, 1 - d)):
-        total = dot(g_ref[0], ref[0], NT)
+    for refs_of, side in zip(sides, (d, 1 - d)):
+        total = dot(grads[0][...], refs_of[0][...], NT)
         for h in range(1, heads):
-            total = total + dot(g_ref[h], ref[h], NT)
+            total = total + dot(grads[h][...], refs_of[h][...], NT)
         at = pl.multiple_of(side * half + j * cols, cols)
         out_ref[:, pl.ds(at, cols)] = total.astype(out_ref.dtype)
 
 
-def image_term(d, grad, near, far):
-    heads, half, width = near.shape
-    rows = grad.shape[1]
+def image_term(d, grads, near, far):
+    heads = len(near)
+    half, width = near[0].shape
+    rows = grads[0].shape[0]
     tiles = 4
-    side = pl.BlockSpec((heads, half // tiles, width), lambda j, d: (0, j, 0))
+    side = pl.BlockSpec((half // tiles, width), lambda j, d: (j, 0))
+    grad = pl.BlockSpec((rows, width), lambda j, d: (0, 0))
     return pl.pallas_call(
         image_body,
         grid_spec=pltpu.PrefetchScalarGridSpec(
             num_scalar_prefetch=1,
             grid=(tiles,),
-            in_specs=[pl.BlockSpec(grad.shape, lambda j, d: (0, 0, 0)), side, side],
+            in_specs=[grad] * heads + [side] * (2 * heads),
             out_specs=pl.BlockSpec((rows, 2 * half), lambda j, d: (0, 0)),
         ),
         out_shape=jax.ShapeDtypeStruct((rows, 2 * half), jnp.bfloat16),
-        compiler_params=params(),
-    )(d, grad, near, far)
+        cost_estimate=cost(4 * heads * near[0].size * rows, 4 * heads * near[0].size * 2),
+        compiler_params=params(),
+    )(d, *grads, *near, *far)
 
 
 def per_device(image_states, place_index, doc_ids, queries, text_kv, kv_weight, d_out):
@@ -371,18 +389,15 @@
     d1 = jnp.reshape(d, (1,)).astype(jnp.int32)
     place = place_index[0, ::IMGTOK] // IMGTOK
 
-    halves = weights.reshape(mps, 2, feats // 2, width)
-    mine = lax.dynamic_index_in_dim(halves, d, axis=1, keepdims=False)
-    near = exchange(mine, "mp")
-    far = swap(near, "dp")
-
-    sub = feats * mps // ranks // mps
-    per_mp = ranks // mps
-    pieces = states.reshape(image_rows, per_mp, mps, sub).transpose(2, 0, 1, 3)
-    pieces = exchange(pieces, "mp")
-    pieces = pieces.transpose(0, 2, 1, 3).reshape(ranks, image_rows, sub)
-    pieces = exchange(pieces, "ctx").reshape(ranks * image_rows, sub)
-    all_states = lax.all_gather(pieces, "mp", axis=0)
+    m = lax.axis_index("mp")
+    steps = range(mps)
+
+    half = feats // 2
+    near = [
+        lax.dynamic_slice_in_dim(weights, (m ^ s) * feats + d * half, half) for s in steps
+    ]
+    near = [trade(near[s], "mp", s) if s else near[0] for s in steps]
+    far = [swap(near[s], "dp") for s in steps]
 
     prior_text = shift(text_kv[0], "ctx", 1)
     docs = doc_ids[0]
@@ -392,7 +407,29 @@
     key_docs = jnp.concatenate([prior_docs, own_docs])
     start = jnp.sum((key_docs[:, None] < own_docs[None, :]).astype(jnp.int32), axis=0)[None]
 
-    parts = exchange(project(d1, states, near, far), "mp")
+    sub = feats // (ranks // mps) // mps
+    mixed = ranks == mps
+    *near, states_late, prior_text, start, place = lax.optimization_barrier(
+        (*near, states, prior_text, start, place)
+    )
+    if mixed:
+        pieces = []
+        for s in steps:
+            piece = lax.dynamic_slice_in_dim(states_late, (c ^ s) * sub, sub, axis=1)
+            route = [
+                (i * mps + j, j * mps + (i ^ s)) for i in range(ranks) for j in range(mps)
+            ]
+            pieces.append(lax.ppermute(piece, ("ctx", "mp"), route))
+        pieces = jnp.concatenate(pieces, axis=0)
+    else:
+        pieces = states_late.reshape(image_rows, ranks // mps, mps, sub).transpose(2, 0, 1, 3)
+        pieces = exchange(pieces, "mp")
+        pieces = pieces.transpose(0, 2, 1, 3).reshape(ranks, image_rows, sub)
+        pieces = exchange(pieces, "ctx").reshape(ranks * image_rows, sub)
+    all_states = lax.all_gather(pieces, "mp", axis=0)
+
+    parts = [project(d1, states, near[s], far[s]) for s in steps]
+    parts = [trade(parts[s], "mp", s) if s else parts[0] for s in steps]
     packed = pack(c1, place, parts, ranks, capacity, per_shard)
     image = exchange(packed, "ctx")
     attn_out, own_grad, prior_grad = attention(
@@ -401,10 +438,10 @@
     )
     grad = (own_grad + shift(prior_grad, "ctx", -1)).astype(jnp.bfloat16)
     gathered = exchange(jnp.broadcast_to(grad, (ranks,) + grad.shape), "ctx")
-    by_rank, mine = reorder(c1, place, gathered, mps, per_shard, images)
-    head_grad = exchange(mine, "mp")
+    by_rank, mine = reorder(c1, place, gathered, per_shard, images)
+    head_grad = [trade(mine, "mp", s) if s else mine for s in steps]
+    term = weight_term(all_states, by_rank.reshape(ranks, image_rows, width), mixed)
     image_grad = image_term(d1, head_grad, near, far)
-    term = weight_term(all_states, by_rank)
     weight_grad = term + swap(term, "dp")
     return (attn_out[None], image_grad[None], weight_grad[None])
 

time: 238 us -> 211 us (0.89)
  blocking collectives: 88.3 us -> 26 us
  waiting for transfers between devices: 66 us -> 106 us
  Pallas kernels: 39.2 us -> 26.7 us
  starting transfers between devices: 17.1 us -> 28.4 us
  local copies, waits for them, and re-layouts: 8.69 us -> 6 us
    ppermute x0 -> x13, waiting for transfers between devices: none -> 95.2 us  [the longest x4 58.8 us: per_device(): pieces.append(lax.ppermute(piece, ('ctx', 'mp'), route))]
    all_to_all x4 -> x2, blocking collectives: 88.3 us -> 26 us  [exchange(): return lax.all_to_all(blocks, axis, split_axis=0, concat_axis=0, tiled=True)]
    all_to_all x3 -> x0, waiting for transfers between devices: 46.5 us -> none  [exchange(): return lax.all_to_all(blocks, axis, split_axis=0, concat_axis=0, tiled=True)]
    ppermute x0 -> x13, starting transfers between devices: none -> 21.3 us  [the longest x9 15 us: trade(): return lax.ppermute(block, axis, [(i, i ^ step) for i in range(count)])]
    all_to_all x3 -> x0, starting transfers between devices: 11.9 us -> none  [exchange(): return lax.all_to_all(blocks, axis, split_axis=0, concat_axis=0, tiled=True)]
    pallas_call x2 -> x5, Pallas kernels: 10.4 us -> 3.81 us  [the longest x1 2 us: weight_term(): pl.pallas_call(functools.partial(weight_body, mixed), grid=(parts,), in_s...]
    ppermute x2, waiting for transfers between devices: 15.3 us -> 9.8 us  [shift(): return lax.ppermute(block, axis, route)]
    unnamed x21 -> x28, local copies, waits for them, and re-layouts: 5.54 us -> 2.24 us
  transfers between devices with their start and end apart: 8 -> 21, of which waited for: 5 -> 12; matrix products, arithmetic and copies ran while one was open for 2% -> 1% of each run, Pallas kernels for 14% -> 12%
where the time goes in v2:
time: 211 us; the launch traced here: 210 us
  waiting for transfers between devices  106 us (50%)
  starting transfers between devices  28.4 us (13%)
  Pallas kernels  26.7 us (13%)
  blocking collectives  26 us (12%)
  between operations  14.3 us (7%)
  local copies, waits for them, and re-layouts  6 us (3%)
  other arithmetic  2.98 us (1%)
    ppermute x4, waiting for transfers between devices, per_device(): pieces.append(lax.ppermute(piece, ('ctx', 'mp'), route))  58.8 us
    ppermute x9, waiting for transfers between devices, trade(): return lax.ppermute(block, axis, [(i, i ^ step) for i in range(count)])  36.4 us
    all_to_all x2, blocking collectives, exchange(): return lax.all_to_all(blocks, axis, split_axis=0, concat_axis=0, tiled=True)  26 us
    pallas_call x1, Pallas kernels, attention(): pl.pallas_call(functools.partial(attention_body, per_shard, images), grid...  17.3 us
    ppermute x9, starting transfers between devices, trade(): return lax.ppermute(block, axis, [(i, i ^ step) for i in range(count)])  15 us
    ppermute x2, waiting for transfers between devices, shift(): return lax.ppermute(block, axis, route)  9.8 us
    ppermute x4, starting transfers between devices, per_device(): pieces.append(lax.ppermute(piece, ('ctx', 'mp'), route))  6.29 us
    ppermute x2, starting transfers between devices, shift(): return lax.ppermute(block, axis, route)  5.92 us
  transfers between devices with their start and end apart: 21, of which 12 were waited for; matrix products, arithmetic and copies ran while one was open for 1% of the time, Pallas kernels for 12%

profile of v2, /device:TPU:0, one launch (start us, length us, event | category | flops | bytes accessed | tf_op | source)
XLA Modules:
  0.0 210.4 jit_solution(15238901848743903882)
XLA Ops:
  7.3 2.8 %dynamic-slice_bitcast_fusion = (bf16[1024,256]{1,0:T(8,128)(2,1)}, bf16[1024,256]{1,0:T(8,128)(2,1)}, bf16[1024,256]{1,0:T(8,128)(2,1)S(1)}, bf16[1024,256]{1,0:T(8,128)(2,1)}) fusion(bf16[1,8192,256]{2,1,0:T(8,128)(2,1)} %param.12, s32[]{:T(128)S(6)} %select_n.47, s32[]{:T(128)S(6)} %select_n.45, s32[]{:T(128)S(6)} %select_n.44, s32[]{:T(128)S(6)} %select_n.46), kind=kLoop, calls=%fused_computation.3 | loop fusion | bytes 4194320 | tf_op jit(solution)/shard_map/dynamic_slice | solution.py:397
  10.1 2.9 %collective-permute-start = (bf16[1024,256]{1,0:T(8,128)(2,1)}, bf16[1024,256]{1,0:T(8,128)(2,1)S(1)}, u32[]{:S(2)}, u32[]{:S(2)}) collective-permute-start(bf16[1024,256]{1,0:T(8,128)(2,1)} %get-tuple-element.30), channel_id=1, source_target_pairs={{0,1},{1,0},{2,3},{3,2},{4,5},{5,4},{6,7},{7,6},{8,9},{9,8},{10,11... | collective-permute-start | bytes 1572872 | tf_op jit(solution)/shard_map/ppermute | solution.py:49
  14.5 4.6 %collective-permute-start.3 = (bf16[512,256]{1,0:T(8,128)(2,1)S(1)}, bf16[512,256]{1,0:T(8,128)(2,1)}, u32[]{:S(2)}, u32[]{:S(2)}) collective-permute-start(bf16[512,256]{1,0:T(8,128)(2,1)S(1)} %bitcast.41), channel_id=1, source_target_pairs={{0,4},{4,8},{8,12},{1,5},{5,9},{9,13},{2,6},{6,10},{10,14},{3,7},{... | collective-permute-start | bytes 786440 | tf_op jit(solution)/shard_map/ppermute | solution.py:35
  20.4 2.8 %collective-permute-done.3.prior_ref = bf16[512,256]{1,0:T(8,128)(2,1)} collective-permute-done((bf16[512,256]{1,0:T(8,128)(2,1)S(1)}, bf16[512,256]{1,0:T(8,128)(2,1)}, u32[]{:S(2)}, u32[]{:S(2)}) %collective-permute-start.3) | collective-permute-done | bytes 262176 | tf_op jit(solution)/shard_map/ppermute | solution.py:35
  23.2 2.8 %collective-permute-done.near_ref.refs_5_ = bf16[1024,256]{1,0:T(8,128)(2,1)S(1)} collective-permute-done((bf16[1024,256]{1,0:T(8,128)(2,1)}, bf16[1024,256]{1,0:T(8,128)(2,1)S(1)}, u32[]{:S(2)}, u32[]{:S(2)}) %collective-permute-start) | collective-permute-done | bytes 524320 | tf_op jit(solution)/shard_map/ppermute | solution.py:49
  26.0 11.9 %collective-permute-done.1.near_ref.refs_6_ = bf16[1024,256]{1,0:T(8,128)(2,1)S(1)} collective-permute-done((bf16[1024,256]{1,0:T(8,128)(2,1)}, bf16[1024,256]{1,0:T(8,128)(2,1)S(1)}, u32[]{:S(2)}, u32[]{:S(2)}) %collective-permute-start.1) | collective-permute-done | bytes 524320 | tf_op jit(solution)/shard_map/ppermute | solution.py:49
  39.5 2.6 %collective-permute-start.17 = (bf16[256,512]{1,0:T(8,128)(2,1)S(1)}, bf16[256,512]{1,0:T(8,128)(2,1)S(1)}, u32[]{:S(2)}, u32[]{:S(2)}) collective-permute-start(bf16[256,512]{1,0:T(8,128)(2,1)S(1)} %get-tuple-element.35), channel_id=1, source_target_pairs={{0,2},{1,6},{2,10},{3,14},{4,3},{5,7},{6,11},{7,15},{8,0},{9,4},{1... | collective-permute-start | bytes 786440 | tf_op jit(solution)/shard_map/ppermute | solution.py:422
  44.2 4.9 %collective-permute-done.18 = bf16[256,512]{1,0:T(8,128)(2,1)S(1)} collective-permute-done((bf16[256,512]{1,0:T(8,128)(2,1)S(1)}, bf16[256,512]{1,0:T(8,128)(2,1)S(1)}, u32[]{:S(2)}, u32[]{:S(2)}) %collective-permute-start.18) | collective-permute-done | bytes 262176 | tf_op jit(solution)/shard_map/ppermute | solution.py:422
  49.1 26.0 %collective-permute-done.17 = bf16[256,512]{1,0:T(8,128)(2,1)S(1)} collective-permute-done((bf16[256,512]{1,0:T(8,128)(2,1)S(1)}, bf16[256,512]{1,0:T(8,128)(2,1)S(1)}, u32[]{:S(2)}, u32[]{:S(2)}) %collective-permute-start.17) | collective-permute-done | bytes 262176 | tf_op jit(solution)/shard_map/ppermute | solution.py:422
  75.2 27.9 %collective-permute-done.16 = bf16[256,512]{1,0:T(8,128)(2,1)S(1)} collective-permute-done((bf16[256,512]{1,0:T(8,128)(2,1)S(1)}, bf16[256,512]{1,0:T(8,128)(2,1)S(1)}, u32[]{:S(2)}, u32[]{:S(2)}) %collective-permute-start.16) | collective-permute-done | bytes 262176 | tf_op jit(solution)/shard_map/ppermute | solution.py:422
  106.6 5.2 %collective-permute-start.6 = (f32[256,256]{1,0:T(8,128)S(1)}, f32[256,256]{1,0:T(8,128)S(1)}, u32[]{:S(2)}, u32[]{:S(2)}) collective-permute-start(f32[256,256]{1,0:T(8,128)S(1)} %shard_map.95), channel_id=1, source_target_pairs={{0,1},{1,0},{2,3},{3,2},{4,5},{5,4},{6,7},{7,6},{8,9},{9,8},{10,11... | collective-permute-start | bytes 786440 | tf_op jit(solution)/shard_map/ppermute | solution.py:49
  112.8 1.7 collective-permute-start.10
  115.0 4.3 %collective-permute-done.6.refs_1_ = f32[256,256]{1,0:T(8,128)S(1)} collective-permute-done((f32[256,256]{1,0:T(8,128)S(1)}, f32[256,256]{1,0:T(8,128)S(1)}, u32[]{:S(2)}, u32[]{:S(2)}) %collective-permute-start.6) | collective-permute-done | bytes 262176 | tf_op jit(solution)/shard_map/ppermute | solution.py:49
  119.4 11.8 %collective-permute-done.8.refs_2_ = f32[256,256]{1,0:T(8,128)S(1)} collective-permute-done((f32[256,256]{1,0:T(8,128)S(1)}, f32[256,256]{1,0:T(8,128)S(1)}, u32[]{:S(2)}, u32[]{:S(2)}) %collective-permute-start.8) | collective-permute-done | bytes 262176 | tf_op jit(solution)/shard_map/ppermute | solution.py:49
  132.1 13.2 %all_to_all.10.image_ref = bf16[4,2,64,256]{3,2,1,0:T(8,128)(2,1)S(1)} all-to-all(bf16[4,2,64,256]{3,2,1,0:T(8,128)(2,1)S(1)} %shard_map.98), channel_id=1, replica_groups=mesh['dp'=2,'ctx'=4,'mp'=4] {'ctx'}, dimensions={0} | all-to-all | bytes 524288 | tf_op jit(solution)/shard_map/all_to_all | solution.py:44
  145.3 17.3 %shard_map.99 = (bf16[512,1024]{1,0:T(8,128)(2,1)}, f32[256,256]{1,0:T(8,128)S(1)}, f32[256,256]{1,0:T(8,128)S(1)}) custom-call(s32[1]{0:T(128)} %bitcast.c_ref, s32[64]{0:T(128)S(1)} %and_select_fusion.place_ref, s32[1,512]{1,0:T(1,128)S(1)} %bitcast.38, bf16[512,1024]{1,0:T(8,128)(2,1)S(1)} %bitcast.39, bf16[512,1024]{1,0:T(8,128)(2,1)S(1)} %bitcast.40, ...), custom_call_target="tpu_custom_call" | custom-call | flops 13421772800 | bytes 4194304 | tf_op jit(solution)/shard_map/pallas_call | solution.py:248
  163.9 7.0 %collective-permute-done.11 = f32[256,256]{1,0:T(8,128)S(1)} collective-permute-done((f32[256,256]{1,0:T(8,128)S(1)}, f32[256,256]{1,0:T(8,128)S(1)}, u32[]{:S(2)}, u32[]{:S(2)}) %collective-permute-start.11) | collective-permute-done | bytes 262176 | tf_op jit(solution)/shard_map/ppermute | solution.py:35
  171.0 12.8 %all_to_all.11.g_ref = bf16[4,256,256]{2,1,0:T(8,128)(2,1)S(1)} all-to-all(bf16[4,256,256]{2,1,0:T(8,128)(2,1)S(1)} %broadcast_in_dim.24), channel_id=1, replica_groups=mesh['dp'=2,'ctx'=4,'mp'=4] {'ctx'}, dimensions={0} | all-to-all | bytes 1048576 | tf_op jit(solution)/shard_map/all_to_all | solution.py:44
  185.5 2.2 %copy-done.1 = bf16[4096,512]{1,0:T(8,128)(2,1)S(1)} copy-done((bf16[4096,512]{1,0:T(8,128)(2,1)S(1)}, bf16[4096,512]{1,0:T(8,128)(2,1)}, u32[]{:S(2)}) %copy-start.1) | copy-done | bytes 4194328
  187.7 2.0 shard_map.102
  191.1 2.3 %collective-permute-start.14 = (bf16[256,256]{1,0:T(8,128)(2,1)S(1)}, bf16[256,256]{1,0:T(8,128)(2,1)S(1)}, u32[]{:S(2)}, u32[]{:S(2)}) collective-permute-start(bf16[256,256]{1,0:T(8,128)(2,1)S(1)} %get-tuple-element.26.refs_0_), channel_id=1, source_target_pairs={{0,3},{1,2},{2,1},{3,0},{4,7},{5,6},{6,5},{7,4},{8,11},{9,10},{10,... | collective-permute-start | bytes 393224 | tf_op jit(solution)/shard_map/ppermute | solution.py:49
  193.3 2.8 %collective-permute-done.12.refs_1_ = bf16[256,256]{1,0:T(8,128)(2,1)S(1)} collective-permute-done((bf16[256,256]{1,0:T(8,128)(2,1)S(1)}, bf16[256,256]{1,0:T(8,128)(2,1)S(1)}, u32[]{:S(2)}, u32[]{:S(2)}) %collective-permute-start.12) | collective-permute-done | bytes 131104 | tf_op jit(solution)/shard_map/ppermute | solution.py:49
  196.2 2.8 %collective-permute-done.13.refs_2_ = bf16[256,256]{1,0:T(8,128)(2,1)S(1)} collective-permute-done((bf16[256,256]{1,0:T(8,128)(2,1)S(1)}, bf16[256,256]{1,0:T(8,128)(2,1)S(1)}, u32[]{:S(2)}, u32[]{:S(2)}) %collective-permute-start.13) | collective-permute-done | bytes 131104 | tf_op jit(solution)/shard_map/ppermute | solution.py:49
  199.0 2.9 %shard_map.101 = bf16[256,2048]{1,0:T(8,128)(2,1)} custom-call(s32[1]{0:T(128)} %bitcast.13.d_ref, bf16[256,256]{1,0:T(8,128)(2,1)S(1)} %get-tuple-element.26.refs_0_, bf16[256,256]{1,0:T(8,128)(2,1)S(1)} %collective-permute-done.12.refs_1_, bf16[256,256]{1,0:T(8,128)(2,1)S(1)} %collective-permute-done.13.refs_2_, ...), custom_call_target="tpu_custom_call" | custom-call | flops 1073741824 | bytes 8388608 | tf_op jit(solution)/shard_map/pallas_call | solution.py:361
  (69 shorter events, 18.4 us)
Async XLA Ops:
  7.2 178.3 %all-gather.3.cloned.1.call-start = ((), (), s32[]{:S(2)}) async-start(), calls=%async_computation.2 | async-start | bytes 5242880 | tf_op jit(solution)/shard_map/all_gather | solution.py:429
  10.1 15.9 %collective-permute-start = (bf16[1024,256]{1,0:T(8,128)(2,1)}, bf16[1024,256]{1,0:T(8,128)(2,1)S(1)}, u32[]{:S(2)}, u32[]{:S(2)}) collective-permute-start(bf16[1024,256]{1,0:T(8,128)(2,1)} %get-tuple-element.30), channel_id=1, source_target_pairs={{0,1},{1,0},{2,3},{3,2},{4,5},{5,4},{6,7},{7,6},{8,9},{9,8},{10,11... | collective-permute-start | bytes 1572872 | tf_op jit(solution)/shard_map/ppermute | solution.py:49
  13.0 24.8 %collective-permute-start.1 = (bf16[1024,256]{1,0:T(8,128)(2,1)}, bf16[1024,256]{1,0:T(8,128)(2,1)S(1)}, u32[]{:S(2)}, u32[]{:S(2)}) collective-permute-start(bf16[1024,256]{1,0:T(8,128)(2,1)} %get-tuple-element.32), channel_id=1, source_target_pairs={{0,2},{1,3},{2,0},{3,1},{4,6},{5,7},{6,4},{7,5},{8,10},{9,11},{10,... | collective-permute-start | bytes 1572872 | tf_op jit(solution)/shard_map/ppermute | solution.py:49
  14.5 23.3 %collective-permute-start.2 = (bf16[1024,256]{1,0:T(8,128)(2,1)}, bf16[1024,256]{1,0:T(8,128)(2,1)S(1)}, u32[]{:S(2)}, u32[]{:S(2)}) collective-permute-start(bf16[1024,256]{1,0:T(8,128)(2,1)} %get-tuple-element.29), channel_id=1, source_target_pairs={{0,3},{1,2},{2,1},{3,0},{4,7},{5,6},{6,5},{7,4},{8,11},{9,10},{10,... | collective-permute-start | bytes 1572872 | tf_op jit(solution)/shard_map/ppermute | solution.py:49
  14.5 8.7 %collective-permute-start.3 = (bf16[512,256]{1,0:T(8,128)(2,1)S(1)}, bf16[512,256]{1,0:T(8,128)(2,1)}, u32[]{:S(2)}, u32[]{:S(2)}) collective-permute-start(bf16[512,256]{1,0:T(8,128)(2,1)S(1)} %bitcast.41), channel_id=1, source_target_pairs={{0,4},{4,8},{8,12},{1,5},{5,9},{9,13},{2,6},{6,10},{10,14},{3,7},{... | collective-permute-start | bytes 786440 | tf_op jit(solution)/shard_map/ppermute | solution.py:35
  37.9 11.2 %collective-permute-start.18 = (bf16[256,512]{1,0:T(8,128)(2,1)S(1)}, bf16[256,512]{1,0:T(8,128)(2,1)S(1)}, u32[]{:S(2)}, u32[]{:S(2)}) collective-permute-start(bf16[256,512]{1,0:T(8,128)(2,1)S(1)} %get-tuple-element.34), channel_id=1, source_target_pairs={{0,3},{1,7},{2,11},{3,15},{4,2},{5,6},{6,10},{7,14},{8,1},{9,5},{1... | collective-permute-start | bytes 786440 | tf_op jit(solution)/shard_map/ppermute | solution.py:422
  39.5 35.7 %collective-permute-start.17 = (bf16[256,512]{1,0:T(8,128)(2,1)S(1)}, bf16[256,512]{1,0:T(8,128)(2,1)S(1)}, u32[]{:S(2)}, u32[]{:S(2)}) collective-permute-start(bf16[256,512]{1,0:T(8,128)(2,1)S(1)} %get-tuple-element.35), channel_id=1, source_target_pairs={{0,2},{1,6},{2,10},{3,14},{4,3},{5,7},{6,11},{7,15},{8,0},{9,4},{1... | collective-permute-start | bytes 786440 | tf_op jit(solution)/shard_map/ppermute | solution.py:422
  42.1 61.0 %collective-permute-start.16 = (bf16[256,512]{1,0:T(8,128)(2,1)S(1)}, bf16[256,512]{1,0:T(8,128)(2,1)S(1)}, u32[]{:S(2)}, u32[]{:S(2)}) collective-permute-start(bf16[256,512]{1,0:T(8,128)(2,1)S(1)} %get-tuple-element.36), channel_id=1, source_target_pairs={{0,1},{1,5},{2,9},{3,13},{4,0},{5,4},{6,8},{7,12},{8,3},{9,7},{10,... | collective-permute-start | bytes 786440 | tf_op jit(solution)/shard_map/ppermute | solution.py:422
  43.6 59.5 %collective-permute-start.15 = (bf16[256,512]{1,0:T(8,128)(2,1)S(1)}, bf16[256,512]{1,0:T(8,128)(2,1)S(1)}, u32[]{:S(2)}, u32[]{:S(2)}) collective-permute-start(bf16[256,512]{1,0:T(8,128)(2,1)S(1)} %get-tuple-element.33), channel_id=1, source_target_pairs={{0,0},{1,4},{2,8},{3,12},{4,1},{5,5},{6,9},{7,13},{8,2},{9,6},{10,... | collective-permute-start | bytes 786440 | tf_op jit(solution)/shard_map/ppermute | solution.py:422
  104.1 2.0 collective-permute-start.5
  104.2 7.6 %collective-permute-start.7 = (bf16[1024,256]{1,0:T(8,128)(2,1)S(1)}, bf16[1024,256]{1,0:T(8,128)(2,1)S(1)}, u32[]{:S(2)}, u32[]{:S(2)}) collective-permute-start(bf16[1024,256]{1,0:T(8,128)(2,1)S(1)} %collective-permute-done.1.near_ref.refs_6_), channel_id=1, source_target_pairs={{0,16},{16,0},{1,17},{17,1},{2,18},{18,2},{3,19},{19,3},{4,20},{20... | collective-permute-start | bytes 1572872 | tf_op jit(solution)/shard_map/ppermute | solution.py:40
  104.7 7.6 %collective-permute-start.9 = (bf16[1024,256]{1,0:T(8,128)(2,1)S(1)}, bf16[1024,256]{1,0:T(8,128)(2,1)S(1)}, u32[]{:S(2)}, u32[]{:S(2)}) collective-permute-start(bf16[1024,256]{1,0:T(8,128)(2,1)S(1)} %collective-permute-done.2.near_ref.refs_7_), channel_id=1, source_target_pairs={{0,16},{16,0},{1,17},{17,1},{2,18},{18,2},{3,19},{19,3},{4,20},{20... | collective-permute-start | bytes 1572872 | tf_op jit(solution)/shard_map/ppermute | solution.py:40
  104.8 9.8 %collective-permute-start.4 = (bf16[1024,256]{1,0:T(8,128)(2,1)S(1)}, bf16[1024,256]{1,0:T(8,128)(2,1)S(1)}, u32[]{:S(2)}, u32[]{:S(2)}) collective-permute-start(bf16[1024,256]{1,0:T(8,128)(2,1)S(1)} %get-tuple-element.19.near_ref.refs_4_), channel_id=1, source_target_pairs={{0,16},{16,0},{1,17},{17,1},{2,18},{18,2},{3,19},{19,3},{4,20},{20... | collective-permute-start | bytes 1572872 | tf_op jit(solution)/shard_map/ppermute | solution.py:40
  106.6 12.8 %collective-permute-start.6 = (f32[256,256]{1,0:T(8,128)S(1)}, f32[256,256]{1,0:T(8,128)S(1)}, u32[]{:S(2)}, u32[]{:S(2)}) collective-permute-start(f32[256,256]{1,0:T(8,128)S(1)} %shard_map.95), channel_id=1, source_target_pairs={{0,1},{1,0},{2,3},{3,2},{4,5},{5,4},{6,7},{7,6},{8,9},{9,8},{10,11... | collective-permute-start | bytes 786440 | tf_op jit(solution)/shard_map/ppermute | solution.py:49
  112.3 18.9 %collective-permute-start.8 = (f32[256,256]{1,0:T(8,128)S(1)}, f32[256,256]{1,0:T(8,128)S(1)}, u32[]{:S(2)}, u32[]{:S(2)}) collective-permute-start(f32[256,256]{1,0:T(8,128)S(1)} %shard_map.96), channel_id=1, source_target_pairs={{0,2},{1,3},{2,0},{3,1},{4,6},{5,7},{6,4},{7,5},{8,10},{9,11},{10,... | collective-permute-start | bytes 786440 | tf_op jit(solution)/shard_map/ppermute | solution.py:49
  112.8 32.5 %copy-start.10 = (bf16[1,512,1024]{2,1,0:T(8,128)(2,1)S(1)}, bf16[1,512,1024]{2,1,0:T(8,128)(2,1)}, u32[]{:S(2)}) copy-start(bf16[1,512,1024]{2,1,0:T(8,128)(2,1)} %param.10) | copy-start | bytes 3145732
  112.8 32.5 %copy-start.11 = (bf16[1,512,1024]{2,1,0:T(8,128)(2,1)S(1)}, bf16[1,512,1024]{2,1,0:T(8,128)(2,1)}, u32[]{:S(2)}) copy-start(bf16[1,512,1024]{2,1,0:T(8,128)(2,1)} %param.13) | copy-start | bytes 3145732
  112.8 18.3 %collective-permute-start.10 = (f32[256,256]{1,0:T(8,128)S(1)}, f32[256,256]{1,0:T(8,128)S(1)}, u32[]{:S(2)}, u32[]{:S(2)}) collective-permute-start(f32[256,256]{1,0:T(8,128)S(1)} %shard_map.97), channel_id=1, source_target_pairs={{0,3},{1,2},{2,1},{3,0},{4,7},{5,6},{6,5},{7,4},{8,11},{9,10},{10,... | collective-permute-start | bytes 786440 | tf_op jit(solution)/shard_map/ppermute | solution.py:49
  114.6 30.7 %copy-start.8 = (bf16[1024,256]{1,0:T(8,128)(2,1)}, bf16[1024,256]{1,0:T(8,128)(2,1)S(1)}, u32[]{:S(2)}) copy-start(bf16[1024,256]{1,0:T(8,128)(2,1)S(1)} %collective-permute-done.4.far_ref.refs_8_) | copy-start | bytes 1572868
  162.6 8.3 %collective-permute-start.11 = (f32[256,256]{1,0:T(8,128)S(1)}, f32[256,256]{1,0:T(8,128)S(1)}, u32[]{:S(2)}, u32[]{:S(2)}) collective-permute-start(f32[256,256]{1,0:T(8,128)S(1)} %get-tuple-element.25), channel_id=1, source_target_pairs={{4,0},{8,4},{12,8},{5,1},{9,5},{13,9},{6,2},{10,6},{14,10},{7,3},{... | collective-permute-start | bytes 786440 | tf_op jit(solution)/shard_map/ppermute | solution.py:35
  189.7 12.2 %collective-permute-start.19 = (f32[2048,256]{1,0:T(8,128)S(1)}, f32[2048,256]{1,0:T(8,128)S(1)}, u32[]{:S(2)}, u32[]{:S(2)}) collective-permute-start(f32[2048,256]{1,0:T(8,128)S(1)} %shard_map.102), channel_id=1, source_target_pairs={{0,16},{16,0},{1,17},{17,1},{2,18},{18,2},{3,19},{19,3},{4,20},{20... | collective-permute-start | bytes 6291464 | tf_op jit(solution)/shard_map/ppermute | solution.py:40
  189.8 6.4 %collective-permute-start.12 = (bf16[256,256]{1,0:T(8,128)(2,1)S(1)}, bf16[256,256]{1,0:T(8,128)(2,1)S(1)}, u32[]{:S(2)}, u32[]{:S(2)}) collective-permute-start(bf16[256,256]{1,0:T(8,128)(2,1)S(1)} %get-tuple-element.26.refs_0_), channel_id=1, source_target_pairs={{0,1},{1,0},{2,3},{3,2},{4,5},{5,4},{6,7},{7,6},{8,9},{9,8},{10,11... | collective-permute-start | bytes 393224 | tf_op jit(solution)/shard_map/ppermute | solution.py:49
  190.6 8.4 %collective-permute-start.13 = (bf16[256,256]{1,0:T(8,128)(2,1)S(1)}, bf16[256,256]{1,0:T(8,128)(2,1)S(1)}, u32[]{:S(2)}, u32[]{:S(2)}) collective-permute-start(bf16[256,256]{1,0:T(8,128)(2,1)S(1)} %get-tuple-element.26.refs_0_), channel_id=1, source_target_pairs={{0,2},{1,3},{2,0},{3,1},{4,6},{5,7},{6,4},{7,5},{8,10},{9,11},{10,... | collective-permute-start | bytes 393224 | tf_op jit(solution)/shard_map/ppermute | solution.py:49
  191.1 7.9 %collective-permute-start.14 = (bf16[256,256]{1,0:T(8,128)(2,1)S(1)}, bf16[256,256]{1,0:T(8,128)(2,1)S(1)}, u32[]{:S(2)}, u32[]{:S(2)}) collective-permute-start(bf16[256,256]{1,0:T(8,128)(2,1)S(1)} %get-tuple-element.26.refs_0_), channel_id=1, source_target_pairs={{0,3},{1,2},{2,1},{3,0},{4,7},{5,6},{6,5},{7,4},{8,11},{9,10},{10,... | collective-permute-start | bytes 393224 | tf_op jit(solution)/shard_map/ppermute | solution.py:49
  (11 other events, 107.0 us)
Sparse Core Ops, SparseCore 0:
  104.3 64.4 all-gather.2

commit v3 on v2

--- a/solution.py
+++ b/solution.py
@@ -9,6 +9,7 @@
 
 IMGTOK = 16
 QTILE = 128
+SPANS = (2, 3)
 LOG2E = 1.4426950408889634
 VMEM = 24 * 1024 * 1024
 
@@ -53,34 +54,38 @@
     return pl.ds(pl.multiple_of(start * IMGTOK, IMGTOK), IMGTOK)
 
 
-def project_body(d_ref, s_ref, near_ref, far_ref, out_ref):
-    half = near_ref.shape[0]
+def project_body(d_ref, m_ref, s_ref, own_near, near_ref, own_far, far_ref, out_ref):
+    half = own_near.shape[0]
     d = d_ref[0]
+    m = m_ref[0]
     near = s_ref[:, pl.ds(pl.multiple_of(d * half, half), half)]
     far = s_ref[:, pl.ds(pl.multiple_of((1 - d) * half, half), half)]
-    out_ref[...] = dot(near, near_ref[...], NN) + dot(far, far_ref[...], NN)
-
-
-def project(d, states, near, far):
-    half, width = near.shape
+    for h in range(out_ref.shape[0]):
+        near_w = near_ref[h - 1] if h else own_near[...]
+        far_w = far_ref[h - 1] if h else own_far[...]
+        out_ref[m ^ h] = dot(near, near_w, NN) + dot(far, far_w, NN)
+
+
+def project(d, m, states, own_near, near, own_far, far):
+    others, half, width = near.shape
     rows = states.shape[0]
+    smem = pl.BlockSpec(memory_space=pltpu.SMEM)
     vmem = pl.BlockSpec(memory_space=pltpu.VMEM)
     return pl.pallas_call(
         project_body,
-        in_specs=[pl.BlockSpec(memory_space=pltpu.SMEM), vmem, vmem, vmem],
+        in_specs=[smem, smem] + [vmem] * 5,
         out_specs=vmem,
-        out_shape=jax.ShapeDtypeStruct((rows, width), jnp.float32),
-        cost_estimate=cost(4 * rows * half * width, 4 * states.size),
-        compiler_params=params(),
-    )(d, states, near, far)
-
-
-def pack_body(per_shard, c_ref, place_ref, *refs):
-    *part_refs, out_ref, rounded, count = refs
+        out_shape=jax.ShapeDtypeStruct((others + 1, rows, width), jnp.float32),
+        cost_estimate=cost(4 * (others + 1) * rows * half * width, 8 * near.size),
+        compiler_params=params(),
+    )(d, m, states, own_near, near, own_far, far)
+
+
+def pack_body(per_shard, c_ref, place_ref, part_ref, out_ref, rounded, count):
     shards = out_ref.shape[0]
-    total = part_refs[0][...]
-    for ref in part_refs[1:]:
-        total = total + ref[...]
+    total = part_ref[0]
+    for m in range(1, part_ref.shape[0]):
+        total = total + part_ref[m]
     rounded[...] = total.astype(jnp.bfloat16)
     out_ref[...] = jnp.zeros_like(out_ref)
     for s in range(shards):
@@ -105,21 +110,21 @@
 
 
 def pack(c, place, parts, shards, capacity, per_shard):
-    rows, width = parts[0].shape
+    _, rows, width = parts.shape
     smem = pl.BlockSpec(memory_space=pltpu.SMEM)
     vmem = pl.BlockSpec(memory_space=pltpu.VMEM)
     return pl.pallas_call(
         functools.partial(pack_body, per_shard),
-        in_specs=[smem, smem] + [vmem] * len(parts),
+        in_specs=[smem, smem, vmem],
         out_specs=vmem,
         out_shape=jax.ShapeDtypeStruct((shards, 2, capacity, width), jnp.bfloat16),
         scratch_shapes=[
             pltpu.VMEM((rows, width), jnp.bfloat16),
             pltpu.SMEM((shards,), jnp.int32),
         ],
-        cost_estimate=cost(0, parts[0].size * 4 * 6),
-        compiler_params=params(),
-    )(c, place, *parts)
+        cost_estimate=cost(0, parts.size * 6),
+        compiler_params=params(),
+    )(c, place, parts)
 
 
 def attention_body(
@@ -127,6 +132,7 @@
     images,
     c_ref,
     place_ref,
+    first_ref,
     start_ref,
     q_ref,
     g_ref,
@@ -146,7 +152,6 @@
     rows = own_ref.shape[0]
     hd = own_ref.shape[1] // 2
     blocks = place_ref.shape[0]
-    span = rows + QTILE
     heads = q_ref.shape[1] // hd
     scale = hd ** (-0.5)
 
@@ -178,39 +183,68 @@
 
         lax.fori_loop(0, blocks, step, (jnp.int32(0), jnp.int32(0)))
 
-    first = pl.multiple_of(t * QTILE, QTILE)
-    keys = window[pl.ds(first, span), :hd]
-    values = window[pl.ds(first, span), hd:]
-    values_t = values.T
-    key_pos = lax.broadcasted_iota(jnp.int32, (span, QTILE), 0) + first
-    query_pos = lax.broadcasted_iota(jnp.int32, (span, QTILE), 1) + (first + rows)
-    allowed = (key_pos <= query_pos) & (key_pos >= start_ref[...])
-    bias = jnp.where(allowed, 0.0, -1e30)
-    bias = jnp.concatenate([bias, bias], axis=1)
+    first = t * QTILE
 
     def stack(ref, a, b):
         return jnp.concatenate([ref[:, h * hd : (h + 1) * hd] for h in range(a, b)], axis=0)
 
-    for h in range(0, heads, 2):
-        query = stack(q_ref, h, h + 2)
-        grad = stack(g_ref, h, h + 2)
-        scores = dot(keys, query, NT) * (scale * LOG2E) + bias
-        top = jnp.max(scores, axis=0, keepdims=True)
-        e = jnp.exp2(scores - top)
-        p = e * (1.0 / jnp.sum(e, axis=0, keepdims=True))
-        low = p.astype(jnp.bfloat16)
-        context_t = dot(values_t, low, NN)
-        grad_p = dot(values, grad, NT)
-        grad_t = grad.astype(jnp.float32).T
-        delta = jnp.sum(grad_t * context_t, axis=0, keepdims=True)
-        ds = (p * (grad_p - delta)).astype(jnp.bfloat16)
-        context = context_t.T.astype(jnp.bfloat16)
-        out_ref[:, h * hd : (h + 1) * hd] = context[:QTILE]
-        out_ref[:, (h + 1) * hd : (h + 2) * hd] = context[QTILE:]
-        probs[:, h * QTILE : (h + 2) * QTILE] = low
-        grads[:, h * QTILE : (h + 2) * QTILE] = ds
-    total[pl.ds(first, span), :hd] += dot(grads[...], stack(q_ref, 0, heads), NN)
-    total[pl.ds(first, span), hd:] += dot(probs[...], stack(g_ref, 0, heads), NN)
+    def tile(span):
+        base = pl.multiple_of(first + (full - span), QTILE)
+        keys = window[pl.ds(base, span), :hd]
+        values = window[pl.ds(base, span), hd:]
+        values_t = values.T
+        key_pos = lax.broadcasted_iota(jnp.int32, (span, QTILE), 0) + base
+        query_pos = lax.broadcasted_iota(jnp.int32, (span, QTILE), 1) + (first + rows)
+        allowed = (key_pos <= query_pos) & (key_pos >= start_ref[...])
+        bias = jnp.where(allowed, 0.0, -1e30)
+        bias = jnp.concatenate([bias, bias], axis=1)
+
+        def products(h):
+            query = stack(q_ref, h, h + 2)
+            grad = stack(g_ref, h, h + 2)
+            return dot(keys, query, NT), dot(values, grad, NT)
+
+        def softmax(h, scores):
+            scores = scores * (scale * LOG2E) + bias
+            top = jnp.max(scores, axis=0, keepdims=True)
+            e = jnp.exp2(scores - top)
+            p = e * (1.0 / jnp.sum(e, axis=0, keepdims=True))
+            low = p.astype(jnp.bfloat16)
+            probs[:span, h * QTILE : (h + 2) * QTILE] = low
+            return p, dot(values_t, low, NN)
+
+        def backward(h, p, grad_p, context_t):
+            grad_t = stack(g_ref, h, h + 2).astype(jnp.float32).T
+            delta = jnp.sum(grad_t * context_t, axis=0, keepdims=True)
+            ds = (p * (grad_p - delta)).astype(jnp.bfloat16)
+            context = context_t.T.astype(jnp.bfloat16)
+            out_ref[:, h * hd : (h + 1) * hd] = context[:QTILE]
+            out_ref[:, (h + 1) * hd : (h + 2) * hd] = context[QTILE:]
+            grads[:span, h * QTILE : (h + 2) * QTILE] = ds
+
+        pairs = heads // 2
+        first_stage, second_stage = {}, {}
+        for i in range(pairs + 2):
+            if i < pairs:
+                first_stage[i] = products(2 * i)
+            if 1 <= i <= pairs:
+                scores, grad_p = first_stage.pop(i - 1)
+                second_stage[i - 1] = (grad_p, *softmax(2 * (i - 1), scores))
+            if i >= 2:
+                grad_p, p, context_t = second_stage.pop(i - 2)
+                backward(2 * (i - 2), p, grad_p, context_t)
+        total[pl.ds(base, span), :hd] += dot(grads[:span, :], stack(q_ref, 0, heads), NN)
+        total[pl.ds(base, span), hd:] += dot(probs[:span, :], stack(g_ref, 0, heads), NN)
+
+    full = rows + QTILE
+    need = full - (first_ref[t] - first)
+    below = 0
+    for span in sorted({min(b * QTILE, full) for b in SPANS} | {full}):
+        lower, below = below, span
+
+        @pl.when((need > lower) & (need <= span))
+        def _():
+            tile(span)
 
     @pl.when(t == pl.num_programs(0) - 1)
     def _():
@@ -248,7 +282,7 @@
     return pl.pallas_call(
         functools.partial(attention_body, per_shard, images),
         grid_spec=pltpu.PrefetchScalarGridSpec(
-            num_scalar_prefetch=2,
+            num_scalar_prefetch=3,
             grid=(tiles,),
             in_specs=[
                 pl.BlockSpec((1, QTILE), lambda t, *_: (0, t)),
@@ -269,7 +303,7 @@
         out_shape=[jax.ShapeDtypeStruct((rows, cols), jnp.bfloat16), grad, grad],
         cost_estimate=cost(2 * 20 * cols * span * rows, 4 * queries.size * 2),
         compiler_params=params(),
-    )(c, place, start, queries, d_out, own, prior, image)
+    )(c, place, start[0, ::QTILE], start, queries, d_out, own, prior, image)
 
 
 def reorder_body(per_shard, images, c_ref, place_ref, g_ref, out_ref, mine_ref, count):
@@ -308,68 +342,70 @@
     )(c, place, gathered)
 
 
-def weight_body(mixed, s_ref, g_ref, out_ref):
-    k = pl.program_id(0)
-    ranks, rows, _ = g_ref.shape
-    if not mixed:
-        out_ref[...] = dot(s_ref[0], g_ref[...].reshape(ranks * rows, -1), TN)
-        return
-    grad = jnp.concatenate([g_ref[k ^ s] for s in range(ranks)], axis=0)
+def weight_body(mixed, c_ref, s_ref, g_ref, out_ref):
+    ranks, rows, width = g_ref.shape
+    c = c_ref[0]
+    if mixed:
+        grad = jnp.concatenate([g_ref[c ^ s] for s in range(ranks)], axis=0)
+    else:
+        grad = g_ref[...].reshape(ranks * rows, width)
     out_ref[...] = dot(s_ref[0], grad, TN)
 
 
-def weight_term(states, grad, mixed):
+def weight_term(c, states, grad, mixed):
     parts, rows, cols = states.shape
     width = grad.shape[2]
     return pl.pallas_call(
         functools.partial(weight_body, mixed),
-        grid=(parts,),
-        in_specs=[
-            pl.BlockSpec((1, rows, cols), lambda k: (k, 0, 0)),
-            pl.BlockSpec(grad.shape, lambda k: (0, 0, 0)),
-        ],
-        out_specs=pl.BlockSpec((cols, width), lambda k: (k, 0)),
+        grid_spec=pltpu.PrefetchScalarGridSpec(
+            num_scalar_prefetch=1,
+            grid=(parts,),
+            in_specs=[
+                pl.BlockSpec((1, rows, cols), lambda k, c: (k, 0, 0)),
+                pl.BlockSpec(grad.shape, lambda k, c: (0, 0, 0)),
+            ],
+            out_specs=pl.BlockSpec((cols, width), lambda k, c: (k, 0)),
+        ),
         out_shape=jax.ShapeDtypeStruct((parts * cols, width), jnp.float32),
         cost_estimate=cost(2 * states.size * width, states.size * 4),
         compiler_params=params(),
-    )(states, grad)
+    )(c, states, grad)
 
 
 def image_body(d_ref, *refs):
-    out_ref = refs[-1]
-    heads = (len(refs) - 1) // 3
-    grads, sides = refs[:heads], (refs[heads : 2 * heads], refs[2 * heads : -1])
+    own_near, near_ref, own_far, far_ref, out_ref = refs[-5:]
+    grads = refs[:-5]
     j = pl.program_id(0)
-    cols = sides[0][0].shape[0]
+    cols = own_near.shape[0]
     half = out_ref.shape[1] // 2
     d = d_ref[0]
-    for refs_of, side in zip(sides, (d, 1 - d)):
-        total = dot(grads[0][...], refs_of[0][...], NT)
-        for h in range(1, heads):
-            total = total + dot(grads[h][...], refs_of[h][...], NT)
+    for own, others, side in ((own_near, near_ref, d), (own_far, far_ref, 1 - d)):
+        total = dot(grads[0][...], own[...], NT)
+        for h in range(1, len(grads)):
+            total = total + dot(grads[h][...], others[h - 1], NT)
         at = pl.multiple_of(side * half + j * cols, cols)
         out_ref[:, pl.ds(at, cols)] = total.astype(out_ref.dtype)
 
 
-def image_term(d, grads, near, far):
-    heads = len(near)
-    half, width = near[0].shape
+def image_term(d, grads, own_near, near, own_far, far):
+    others, half, width = near.shape
     rows = grads[0].shape[0]
     tiles = 4
-    side = pl.BlockSpec((half // tiles, width), lambda j, d: (j, 0))
+    own = pl.BlockSpec((half // tiles, width), lambda j, d: (j, 0))
+    side = pl.BlockSpec((others, half // tiles, width), lambda j, d: (0, j, 0))
     grad = pl.BlockSpec((rows, width), lambda j, d: (0, 0))
     return pl.pallas_call(
         image_body,
         grid_spec=pltpu.PrefetchScalarGridSpec(
             num_scalar_prefetch=1,
             grid=(tiles,),
-            in_specs=[grad] * heads + [side] * (2 * heads),
+            in_specs=[grad] * len(grads) + [own, side] * 2,
             out_specs=pl.BlockSpec((rows, 2 * half), lambda j, d: (0, 0)),
         ),
         out_shape=jax.ShapeDtypeStruct((rows, 2 * half), jnp.bfloat16),
-        cost_estimate=cost(4 * heads * near[0].size * rows, 4 * heads * near[0].size * 2),
-        compiler_params=params(),
-    )(d, *grads, *near, *far)
+        cost_estimate=cost(4 * len(grads) * half * width * rows, 8 * near.size),
+        compiler_params=params(),
+    )(d, *grads, own_near, near, own_far, far)
 
 
 def per_device(image_states, place_index, doc_ids, queries, text_kv, kv_weight, d_out):
@@ -390,14 +426,15 @@
     place = place_index[0, ::IMGTOK] // IMGTOK
 
     m = lax.axis_index("mp")
-    steps = range(mps)
+    m1 = jnp.reshape(m, (1,)).astype(jnp.int32)
+    steps = range(1, mps)
 
     half = feats // 2
-    near = [
-        lax.dynamic_slice_in_dim(weights, (m ^ s) * feats + d * half, half) for s in steps
-    ]
-    near = [trade(near[s], "mp", s) if s else near[0] for s in steps]
-    far = [swap(near[s], "dp") for s in steps]
+
+    def slab(source, head, side):
+        return lax.dynamic_slice_in_dim(source, head * feats + side * half, half)
+
+    near = [trade(slab(weights, m ^ s, d), "mp", s) for s in steps]
 
     prior_text = shift(text_kv[0], "ctx", 1)
     docs = doc_ids[0]
@@ -409,28 +446,26 @@
 
     sub = feats // (ranks // mps) // mps
     mixed = ranks == mps
-    *near, states_late, prior_text, start, place = lax.optimization_barrier(
-        (*near, states, prior_text, start, place)
+    pieces = states.reshape(image_rows, ranks // mps, mps, sub).transpose(2, 0, 1, 3)
+    pieces = exchange(pieces, "mp")
+    pieces = pieces.transpose(0, 2, 1, 3).reshape(ranks, image_rows, sub)
+    *near, pieces, weights_late, prior_text, start, place = lax.optimization_barrier(
+        (*near, pieces, weights, prior_text, start, place)
     )
     if mixed:
-        pieces = []
-        for s in steps:
-            piece = lax.dynamic_slice_in_dim(states_late, (c ^ s) * sub, sub, axis=1)
-            route = [
-                (i * mps + j, j * mps + (i ^ s)) for i in range(ranks) for j in range(mps)
-            ]
-            pieces.append(lax.ppermute(piece, ("ctx", "mp"), route))
-        pieces = jnp.concatenate(pieces, axis=0)
+        moved = [lax.dynamic_index_in_dim(pieces, c ^ s, keepdims=False) for s in range(ranks)]
+        moved = [trade(moved[s], "ctx", s) if s else moved[0] for s in range(ranks)]
     else:
-        pieces = states_late.reshape(image_rows, ranks // mps, mps, sub).transpose(2, 0, 1, 3)
-        pieces = exchange(pieces, "mp")
-        pieces = pieces.transpose(0, 2, 1, 3).reshape(ranks, image_rows, sub)
-        pieces = exchange(pieces, "ctx").reshape(ranks * image_rows, sub)
-    all_states = lax.all_gather(pieces, "mp", axis=0)
-
-    parts = [project(d1, states, near[s], far[s]) for s in steps]
-    parts = [trade(parts[s], "mp", s) if s else parts[0] for s in steps]
+        moved = [exchange(pieces, "ctx").reshape(ranks * image_rows, sub)]
+
+    near = jnp.stack(near)
+    far = swap(near, "dp")
+    own_near = slab(weights_late, m, d)
+    own_far = slab(weights_late, m, 1 - d)
+    parts = exchange(project(d1, m1, states, own_near, near, own_far, far), "mp")
     packed = pack(c1, place, parts, ranks, capacity, per_shard)
+    packed, *moved = lax.optimization_barrier((packed, *moved))
+    all_states = lax.all_gather(jnp.concatenate(moved, axis=0), "mp", axis=0)
     image = exchange(packed, "ctx")
     attn_out, own_grad, prior_grad = attention(
         c1, place, start, queries[0], d_out[0], text_kv[0], prior_text, image,
@@ -439,9 +474,9 @@
     grad = (own_grad + shift(prior_grad, "ctx", -1)).astype(jnp.bfloat16)
     gathered = exchange(jnp.broadcast_to(grad, (ranks,) + grad.shape), "ctx")
     by_rank, mine = reorder(c1, place, gathered, per_shard, images)
-    head_grad = [trade(mine, "mp", s) if s else mine for s in steps]
-    term = weight_term(all_states, by_rank.reshape(ranks, image_rows, width), mixed)
-    image_grad = image_term(d1, head_grad, near, far)
+    head_grad = [mine] + [trade(mine, "mp", s) for s in steps]
+    term = weight_term(c1, all_states, by_rank.reshape(ranks, image_rows, width), mixed)
+    image_grad = image_term(d1, head_grad, own_near, near, own_far, far)
     weight_grad = term + swap(term, "dp")
     return (attn_out[None], image_grad[None], weight_grad[None])
 

time: 211 us -> 179 us (0.85)
  waiting for transfers between devices: 106 us -> 67.4 us
  local copies, waits for them, and re-layouts: 6 us -> 21.2 us
  blocking collectives: 26 us -> 16.5 us
  Pallas kernels: 26.7 us -> 22.6 us
  other arithmetic: 2.98 us -> 5.62 us
    ppermute x4 -> x0, waiting for transfers between devices: 58.8 us -> none  [per_device(): pieces.append(lax.ppermute(piece, ('ctx', 'mp'), route))]
    all_to_all x0 -> x3, waiting for transfers between devices: none -> 30.5 us  [exchange(): return lax.all_to_all(blocks, axis, split_axis=0, concat_axis=0, tiled=True)]
    all_to_all x0 -> x3, starting transfers between devices: none -> 13.2 us  [exchange(): return lax.all_to_all(blocks, axis, split_axis=0, concat_axis=0, tiled=True)]
    unnamed x28 -> x33, local copies, waits for them, and re-layouts: 2.24 us -> 14 us
    all_to_all x2 -> x1, blocking collectives: 26 us -> 16.5 us  [exchange(): return lax.all_to_all(blocks, axis, split_axis=0, concat_axis=0, tiled=True)]
    ppermute x9, waiting for transfers between devices: 36.4 us -> 27.9 us  [trade(): return lax.ppermute(block, axis, [(i, i ^ step) for i in range(count)])]
    ppermute x4 -> x0, starting transfers between devices: 6.29 us -> none  [per_device(): pieces.append(lax.ppermute(piece, ('ctx', 'mp'), route))]
    pallas_call x1, Pallas kernels: 17.3 us -> 12.2 us  [attention(): pl.pallas_call(functools.partial(attention_body, per_shard, images), grid...]
  transfers between devices with their start and end apart: 21 -> 17, of which waited for: 12 -> 11; matrix products, arithmetic and copies ran while one was open for 1% -> 4% of each run, Pallas kernels for 12% -> 11%
where the time goes in v3:
time: 179 us; the launch traced here: 177 us
  waiting for transfers between devices  67.4 us (38%)
  starting transfers between devices  29.8 us (17%)
  Pallas kernels  22.6 us (13%)
  local copies, waits for them, and re-layouts  21.2 us (12%)
  blocking collectives  16.5 us (9%)
  between operations  14.2 us (8%)
  other arithmetic  5.62 us (3%)
    all_to_all x3, waiting for transfers between devices, exchange(): return lax.all_to_all(blocks, axis, split_axis=0, concat_axis=0, tiled=True)  30.5 us
    ppermute x9, waiting for transfers between devices, trade(): return lax.ppermute(block, axis, [(i, i ^ step) for i in range(count)])  27.9 us
    all_to_all x1, blocking collectives, exchange(): return lax.all_to_all(blocks, axis, split_axis=0, concat_axis=0, tiled=True)  16.5 us
    unnamed x33, local copies, waits for them, and re-layouts  14 us
    all_to_all x3, starting transfers between devices, exchange(): return lax.all_to_all(blocks, axis, split_axis=0, concat_axis=0, tiled=True)  13.2 us
    pallas_call x1, Pallas kernels, attention(): pl.pallas_call(functools.partial(attention_body, per_shard, images), grid...  12.2 us
    ppermute x9, starting transfers between devices, trade(): return lax.ppermute(block, axis, [(i, i ^ step) for i in range(count)])  11.6 us
    ppermute x2, waiting for transfers between devices, shift(): return lax.ppermute(block, axis, route)  6.97 us
  transfers between devices with their start and end apart: 17, of which 11 were waited for; matrix products, arithmetic and copies ran while one was open for 4% of the time, Pallas kernels for 11%

profile of v3, /device:TPU:0, one launch (start us, length us, event | category | flops | bytes accessed | tf_op | source)
XLA Modules:
  0.0 177.4 jit_solution(9545937675148948282)
XLA Ops:
  7.2 2.3 %copy.18 = bf16[1,256,2048]{1,2,0:T(8,128)(2,1)} copy(bf16[1,256,2048]{2,1,0:T(8,128)(2,1)} %param.7) | data formatting | bytes 2097152 | tf_op args[0]
  9.5 5.2 %all-to-all-start = ((bf16[4,256,1,512]{1,3,2,0:T(8,128)(2,1)}), bf16[4,256,1,512]{1,3,2,0:T(8,128)(2,1)S(1)}, u32[]{:S(2)}, u32[]{:S(2)}) async-start(bf16[4,256,1,512]{1,3,2,0:T(8,128)(2,1)} %bitcast.6), calls=%async_computation | async-start | bytes 2097152 | tf_op jit(solution)/shard_map/all_to_all | solution.py:45
  14.6 3.6 %collective-permute-start.3 = (bf16[512,256]{1,0:T(8,128)(2,1)S(1)}, bf16[512,256]{1,0:T(8,128)(2,1)S(1)}, u32[]{:S(2)}, u32[]{:S(2)}) collective-permute-start(bf16[512,256]{1,0:T(8,128)(2,1)S(1)} %bitcast.56), channel_id=1, source_target_pairs={{0,4},{4,8},{8,12},{1,5},{5,9},{9,13},{2,6},{6,10},{10,14},{3,7},{... | collective-permute-start | bytes 786440 | tf_op jit(solution)/shard_map/ppermute | solution.py:36
  19.8 3.0 %collective-permute-start.2 = (bf16[1024,256]{1,0:T(8,128)(2,1)S(1)}, bf16[1024,256]{1,0:T(8,128)(2,1)}, u32[]{:S(2)}, u32[]{:S(2)}) collective-permute-start(bf16[1024,256]{1,0:T(8,128)(2,1)S(1)} %get-tuple-element.41), channel_id=1, source_target_pairs={{0,3},{1,2},{2,1},{3,0},{4,7},{5,6},{6,5},{7,4},{8,11},{9,10},{10,... | collective-permute-start | bytes 1572872 | tf_op jit(solution)/shard_map/ppermute | solution.py:50
  24.6 14.5 %all-to-all-done = bf16[4,256,1,512]{1,3,2,0:T(8,128)(2,1)S(1)} async-done(((bf16[4,256,1,512]{1,3,2,0:T(8,128)(2,1)}), bf16[4,256,1,512]{1,3,2,0:T(8,128)(2,1)S(1)}, u32[]{:S(2)}, u32[]{:S(2)}) %all-to-all-start) | async-done | bytes 1048608 | tf_op jit(solution)/shard_map/all_to_all | solution.py:45
  42.0 8.8 %collective-permute-done.1 = bf16[1024,256]{1,0:T(8,128)(2,1)} collective-permute-done((bf16[1024,256]{1,0:T(8,128)(2,1)S(1)}, bf16[1024,256]{1,0:T(8,128)(2,1)}, u32[]{:S(2)}, u32[]{:S(2)}) %collective-permute-start.1) | collective-permute-done | bytes 524320 | tf_op jit(solution)/shard_map/ppermute | solution.py:50
  53.9 2.0 %collective-permute-done.4.far_ref.refs_7_ = bf16[3,1024,256]{2,1,0:T(8,128)(2,1)S(1)} collective-permute-done((bf16[3,1024,256]{2,1,0:T(8,128)(2,1)S(1)}, bf16[3,1024,256]{2,1,0:T(8,128)(2,1)S(1)}, u32[]{:S(2)}, u32[]{:S(2)}) %collective-permute-start.4) | collective-permute-done | bytes 1572896 | tf_op jit(solution)/shard_map/ppermute | solution.py:41
  59.8 4.2 %all-to-all-start.1 = ((f32[4,256,256]{2,1,0:T(8,128)}), f32[4,256,256]{2,1,0:T(8,128)}, u32[]{:S(2)}, u32[]{:S(2)}) async-start(f32[4,256,256]{2,1,0:T(8,128)} %copy-done.6), calls=%async_computation.1 | async-start | bytes 2097152 | tf_op jit(solution)/shard_map/all_to_all | solution.py:45
  64.1 2.1 %dynamic-slice_bitcast_fusion.3 = (bf16[256,512]{1,0:T(8,128)(2,1)}, bf16[256,512]{1,0:T(8,128)(2,1)}, bf16[256,512]{1,0:T(8,128)(2,1)}, bf16[256,512]{1,0:T(8,128)(2,1)S(1)}) fusion(bf16[4,256,512]{2,1,0:T(8,128)(2,1)} %bitcast.59, s32[]{:T(128)S(6)} %select_n.64, s32[]{:T(128)S(6)} %select_n.63, s32[]{:T(128)S(6)} %select_n.62, s32[]{:T(128)S(6)} %select_n.61), kind=kLoop, calls=%fused_computation.8 | loop fusion | bytes 2097168 | tf_op jit(solution)/shard_map/jit(dynamic_index_in_dim)/squeeze | solution.py:456
  66.2 3.7 %collective-permute-start.7 = (bf16[256,512]{1,0:T(8,128)(2,1)}, bf16[256,512]{1,0:T(8,128)(2,1)}, u32[]{:S(2)}, u32[]{:S(2)}) collective-permute-start(bf16[256,512]{1,0:T(8,128)(2,1)} %get-tuple-element.44), channel_id=1, source_target_pairs={{0,12},{4,8},{8,4},{12,0},{1,13},{5,9},{9,5},{13,1},{2,14},{6,10},... | collective-permute-start | bytes 786440 | tf_op jit(solution)/shard_map/ppermute | solution.py:50
  70.6 7.7 %all-to-all-done.1.part_ref = f32[4,256,256]{2,1,0:T(8,128)} async-done(((f32[4,256,256]{2,1,0:T(8,128)}), f32[4,256,256]{2,1,0:T(8,128)}, u32[]{:S(2)}, u32[]{:S(2)}) %all-to-all-start.1) | async-done | bytes 1048608 | tf_op jit(solution)/shard_map/all_to_all | solution.py:45
  78.3 2.4 %shard_map.95 = bf16[4,2,64,256]{3,2,1,0:T(8,128)(2,1)} custom-call(s32[1]{0:T(128)} %bitcast.c_ref, s32[64]{0:T(128)S(1)} %and_select_fusion.place_ref, f32[4,256,256]{2,1,0:T(8,128)} %all-to-all-done.1.part_ref), custom_call_target="tpu_custom_call" | custom-call | bytes 1572864 | tf_op jit(solution)/shard_map/pallas_call | solution.py:116
  80.7 12.1 %collective-permute-done.6 = bf16[256,512]{1,0:T(8,128)(2,1)} collective-permute-done((bf16[256,512]{1,0:T(8,128)(2,1)}, bf16[256,512]{1,0:T(8,128)(2,1)}, u32[]{:S(2)}, u32[]{:S(2)}) %collective-permute-start.6) | collective-permute-done | bytes 262176 | tf_op jit(solution)/shard_map/ppermute | solution.py:50
  92.8 2.1 %pad_maximum_fusion.1 = bf16[1024,512]{1,0:T(8,128)(2,1)} fusion(bf16[256,512]{1,0:T(8,128)(2,1)} %collective-permute-done.7, bf16[256,512]{1,0:T(8,128)(2,1)} %collective-permute-done.6, bf16[256,512]{1,0:T(8,128)(2,1)} %collective-permute-done.5, bf16[256,512]{1,0:T(8,128)(2,1)S(1)} %get-tuple-element.34), kind=kLoop, calls=%fused_computation.3 | loop fusion | flops 4194304 | bytes 2097152 | tf_op jit(solution)/shard_map/concatenate | solution.py:468
  94.9 3.8 %all-to-all-start.2 = ((bf16[4,2,64,256]{3,2,1,0:T(8,128)(2,1)}), bf16[4,2,64,256]{3,2,1,0:T(8,128)(2,1)S(1)}, u32[]{:S(2)}, u32[]{:S(2)}) async-start(bf16[4,2,64,256]{3,2,1,0:T(8,128)(2,1)} %shard_map.95), calls=%async_computation.2 | async-start | bytes 524288 | tf_op jit(solution)/shard_map/all_to_all | solution.py:45
  98.8 8.2 %all-to-all-done.2.image_ref = bf16[4,2,64,256]{3,2,1,0:T(8,128)(2,1)S(1)} async-done(((bf16[4,2,64,256]{3,2,1,0:T(8,128)(2,1)}), bf16[4,2,64,256]{3,2,1,0:T(8,128)(2,1)S(1)}, u32[]{:S(2)}, u32[]{:S(2)}) %all-to-all-start.2) | async-done | bytes 262176 | tf_op jit(solution)/shard_map/all_to_all | solution.py:45
  111.4 12.2 %shard_map.96 = (bf16[512,1024]{1,0:T(8,128)(2,1)}, f32[256,256]{1,0:T(8,128)S(1)}, f32[256,256]{1,0:T(8,128)S(1)}) custom-call(s32[1]{0:T(128)} %bitcast.c_ref, s32[64]{0:T(128)S(1)} %and_select_fusion.place_ref, s32[4]{0:T(128)S(1)} %bitcast.58, s32[1,512]{1,0:T(1,128)S(1)} %bitcast.53, bf16[512,1024]{1,0:T(8,128)(2,1)S(1)} %bitcast.54, ...), custom_call_target="tpu_custom_call" | custom-call | flops 13421772800 | bytes 4194304 | tf_op jit(solution)/shard_map/pallas_call | solution.py:282
  124.9 7.0 %collective-permute-done.8 = f32[256,256]{1,0:T(8,128)S(1)} collective-permute-done((f32[256,256]{1,0:T(8,128)S(1)}, f32[256,256]{1,0:T(8,128)S(1)}, u32[]{:S(2)}, u32[]{:S(2)}) %collective-permute-start.8) | collective-permute-done | bytes 262176 | tf_op jit(solution)/shard_map/ppermute | solution.py:36
  131.9 16.5 %all_to_all.20.g_ref = bf16[4,256,256]{2,1,0:T(8,128)(2,1)S(1)} all-to-all(bf16[4,256,256]{2,1,0:T(8,128)(2,1)S(1)} %broadcast_in_dim.24), channel_id=1, replica_groups=mesh['dp'=2,'ctx'=4,'mp'=4] {'ctx'}, dimensions={0} | all-to-all | bytes 1048576 | tf_op jit(solution)/shard_map/all_to_all | solution.py:45
  150.8 2.2 %copy-done.4 = bf16[4096,512]{1,0:T(8,128)(2,1)S(1)} copy-done((bf16[4096,512]{1,0:T(8,128)(2,1)S(1)}, bf16[4096,512]{1,0:T(8,128)(2,1)}, u32[]{:S(2)}) %copy-start.4) | copy-done | bytes 4194328
  156.2 2.1 %collective-permute-start.11 = (bf16[256,256]{1,0:T(8,128)(2,1)S(1)}, bf16[256,256]{1,0:T(8,128)(2,1)S(1)}, u32[]{:S(2)}, u32[]{:S(2)}) collective-permute-start(bf16[256,256]{1,0:T(8,128)(2,1)S(1)} %get-tuple-element.33.refs_0_), channel_id=1, source_target_pairs={{0,3},{1,2},{2,1},{3,0},{4,7},{5,6},{6,5},{7,4},{8,11},{9,10},{10,... | collective-permute-start | bytes 393224 | tf_op jit(solution)/shard_map/ppermute | solution.py:50
  159.7 3.7 %collective-permute-done.11.refs_3_ = bf16[256,256]{1,0:T(8,128)(2,1)S(1)} collective-permute-done((bf16[256,256]{1,0:T(8,128)(2,1)S(1)}, bf16[256,256]{1,0:T(8,128)(2,1)S(1)}, u32[]{:S(2)}, u32[]{:S(2)}) %collective-permute-start.11) | collective-permute-done | bytes 131104 | tf_op jit(solution)/shard_map/ppermute | solution.py:50
  163.4 2.4 %collective-permute-done.10.refs_2_ = bf16[256,256]{1,0:T(8,128)(2,1)S(1)} collective-permute-done((bf16[256,256]{1,0:T(8,128)(2,1)S(1)}, bf16[256,256]{1,0:T(8,128)(2,1)S(1)}, u32[]{:S(2)}, u32[]{:S(2)}) %collective-permute-start.10) | collective-permute-done | bytes 131104 | tf_op jit(solution)/shard_map/ppermute | solution.py:50
  165.8 3.2 %shard_map.98 = bf16[256,2048]{1,0:T(8,128)(2,1)} custom-call(s32[1]{0:T(128)} %bitcast.17.d_ref, bf16[256,256]{1,0:T(8,128)(2,1)S(1)} %get-tuple-element.33.refs_0_, bf16[256,256]{1,0:T(8,128)(2,1)S(1)} %collective-permute-done.9.refs_1_, bf16[256,256]{1,0:T(8,128)(2,1)S(1)} %collective-permute-done.10.refs_2_, ...), custom_call_target="tpu_custom_call" | custom-call | flops 1073741824 | bytes 6291456 | tf_op jit(solution)/shard_map/pallas_call | solution.py:397
  (66 shorter events, 28.3 us)
Async XLA Ops:
  7.2 7.5 %copy-start.11 = (bf16[1,512,256]{2,1,0:T(8,128)(2,1)S(1)}, bf16[1,512,256]{2,1,0:T(8,128)(2,1)}, u32[]{:S(2)}) copy-start(bf16[1,512,256]{2,1,0:T(8,128)(2,1)} %param.11) | copy-start | bytes 786436
  9.5 29.6 %all-to-all-start = ((bf16[4,256,1,512]{1,3,2,0:T(8,128)(2,1)}), bf16[4,256,1,512]{1,3,2,0:T(8,128)(2,1)S(1)}, u32[]{:S(2)}, u32[]{:S(2)}) async-start(bf16[4,256,1,512]{1,3,2,0:T(8,128)(2,1)} %bitcast.6), calls=%async_computation | async-start | bytes 2097152 | tf_op jit(solution)/shard_map/all_to_all | solution.py:45
  14.6 8.8 %copy-start.15 = (s32[1,2048]{1,0:T(1,128)S(1)}, s32[1,2048]{1,0:T(1,128)}, u32[]{:S(2)}) copy-start(s32[1,2048]{1,0:T(1,128)} %param.9) | copy-start | bytes 24580
  14.6 25.8 %collective-permute-start.3 = (bf16[512,256]{1,0:T(8,128)(2,1)S(1)}, bf16[512,256]{1,0:T(8,128)(2,1)S(1)}, u32[]{:S(2)}, u32[]{:S(2)}) collective-permute-start(bf16[512,256]{1,0:T(8,128)(2,1)S(1)} %bitcast.56), channel_id=1, source_target_pairs={{0,4},{4,8},{8,12},{1,5},{5,9},{9,13},{2,6},{6,10},{10,14},{3,7},{... | collective-permute-start | bytes 786440 | tf_op jit(solution)/shard_map/ppermute | solution.py:36
  19.8 22.2 %collective-permute-start.2 = (bf16[1024,256]{1,0:T(8,128)(2,1)S(1)}, bf16[1024,256]{1,0:T(8,128)(2,1)}, u32[]{:S(2)}, u32[]{:S(2)}) collective-permute-start(bf16[1024,256]{1,0:T(8,128)(2,1)S(1)} %get-tuple-element.41), channel_id=1, source_target_pairs={{0,3},{1,2},{2,1},{3,0},{4,7},{5,6},{6,5},{7,4},{8,11},{9,10},{10,... | collective-permute-start | bytes 1572872 | tf_op jit(solution)/shard_map/ppermute | solution.py:50
  22.8 28.1 %collective-permute-start.1 = (bf16[1024,256]{1,0:T(8,128)(2,1)S(1)}, bf16[1024,256]{1,0:T(8,128)(2,1)}, u32[]{:S(2)}, u32[]{:S(2)}) collective-permute-start(bf16[1024,256]{1,0:T(8,128)(2,1)S(1)} %get-tuple-element.42), channel_id=1, source_target_pairs={{0,2},{1,3},{2,0},{3,1},{4,6},{5,7},{6,4},{7,5},{8,10},{9,11},{10,... | collective-permute-start | bytes 1572872 | tf_op jit(solution)/shard_map/ppermute | solution.py:50
  23.3 27.6 %collective-permute-start = (bf16[1024,256]{1,0:T(8,128)(2,1)S(1)}, bf16[1024,256]{1,0:T(8,128)(2,1)}, u32[]{:S(2)}, u32[]{:S(2)}) collective-permute-start(bf16[1024,256]{1,0:T(8,128)(2,1)S(1)} %get-tuple-element.43), channel_id=1, source_target_pairs={{0,1},{1,0},{2,3},{3,2},{4,5},{5,4},{6,7},{7,6},{8,9},{9,8},{10,11... | collective-permute-start | bytes 1572872 | tf_op jit(solution)/shard_map/ppermute | solution.py:50
  52.4 3.5 %collective-permute-start.4 = (bf16[3,1024,256]{2,1,0:T(8,128)(2,1)S(1)}, bf16[3,1024,256]{2,1,0:T(8,128)(2,1)S(1)}, u32[]{:S(2)}, u32[]{:S(2)}) collective-permute-start(bf16[3,1024,256]{2,1,0:T(8,128)(2,1)S(1)} %pad_maximum_fusion.near_ref.refs_5_), channel_id=1, source_target_pairs={{0,16},{16,0},{1,17},{17,1},{2,18},{18,2},{3,19},{19,3},{4,20},{20... | collective-permute-start | bytes 4718600 | tf_op jit(solution)/shard_map/ppermute | solution.py:41
  52.5 3.4 %copy-start.5 = (bf16[1,256,2048]{2,1,0:T(8,128)(2,1)S(1)}, bf16[1,256,2048]{2,1,0:T(8,128)(2,1)}, u32[]{:S(2)}) copy-start(bf16[1,256,2048]{2,1,0:T(8,128)(2,1)} %param.7) | copy-start | bytes 3145732
  59.8 18.5 %all-to-all-start.1 = ((f32[4,256,256]{2,1,0:T(8,128)}), f32[4,256,256]{2,1,0:T(8,128)}, u32[]{:S(2)}, u32[]{:S(2)}) async-start(f32[4,256,256]{2,1,0:T(8,128)} %copy-done.6), calls=%async_computation.1 | async-start | bytes 2097152 | tf_op jit(solution)/shard_map/all_to_all | solution.py:45
  64.0 86.8 %all-gather.3.cloned.1.call-start = ((), (), s32[]{:S(2)}) async-start(), calls=%async_computation.4 | async-start | bytes 5242880 | tf_op jit(solution)/shard_map/all_gather | solution.py:468
  66.2 14.5 %collective-permute-start.7 = (bf16[256,512]{1,0:T(8,128)(2,1)}, bf16[256,512]{1,0:T(8,128)(2,1)}, u32[]{:S(2)}, u32[]{:S(2)}) collective-permute-start(bf16[256,512]{1,0:T(8,128)(2,1)} %get-tuple-element.44), channel_id=1, source_target_pairs={{0,12},{4,8},{8,4},{12,0},{1,13},{5,9},{9,5},{13,1},{2,14},{6,10},... | collective-permute-start | bytes 786440 | tf_op jit(solution)/shard_map/ppermute | solution.py:50
  69.8 22.9 %collective-permute-start.6 = (bf16[256,512]{1,0:T(8,128)(2,1)}, bf16[256,512]{1,0:T(8,128)(2,1)}, u32[]{:S(2)}, u32[]{:S(2)}) collective-permute-start(bf16[256,512]{1,0:T(8,128)(2,1)} %get-tuple-element.45), channel_id=1, source_target_pairs={{0,8},{4,12},{8,0},{12,4},{1,9},{5,13},{9,1},{13,5},{2,10},{6,14},... | collective-permute-start | bytes 786440 | tf_op jit(solution)/shard_map/ppermute | solution.py:50
  69.8 22.9 %collective-permute-start.5 = (bf16[256,512]{1,0:T(8,128)(2,1)}, bf16[256,512]{1,0:T(8,128)(2,1)}, u32[]{:S(2)}, u32[]{:S(2)}) collective-permute-start(bf16[256,512]{1,0:T(8,128)(2,1)} %get-tuple-element.46), channel_id=1, source_target_pairs={{0,4},{4,0},{8,12},{12,8},{1,5},{5,1},{9,13},{13,9},{2,6},{6,2},{1... | collective-permute-start | bytes 786440 | tf_op jit(solution)/shard_map/ppermute | solution.py:50
  94.9 12.1 %all-to-all-start.2 = ((bf16[4,2,64,256]{3,2,1,0:T(8,128)(2,1)}), bf16[4,2,64,256]{3,2,1,0:T(8,128)(2,1)S(1)}, u32[]{:S(2)}, u32[]{:S(2)}) async-start(bf16[4,2,64,256]{3,2,1,0:T(8,128)(2,1)} %shard_map.95), calls=%async_computation.2 | async-start | bytes 524288 | tf_op jit(solution)/shard_map/all_to_all | solution.py:45
  107.0 1.2 copy-start.9
  123.6 8.3 %collective-permute-start.8 = (f32[256,256]{1,0:T(8,128)S(1)}, f32[256,256]{1,0:T(8,128)S(1)}, u32[]{:S(2)}, u32[]{:S(2)}) collective-permute-start(f32[256,256]{1,0:T(8,128)S(1)} %get-tuple-element.32), channel_id=1, source_target_pairs={{4,0},{8,4},{12,8},{5,1},{9,5},{13,9},{6,2},{10,6},{14,10},{7,3},{... | collective-permute-start | bytes 786440 | tf_op jit(solution)/shard_map/ppermute | solution.py:36
  150.8 2.2 %copy-start.4 = (bf16[4096,512]{1,0:T(8,128)(2,1)S(1)}, bf16[4096,512]{1,0:T(8,128)(2,1)}, u32[]{:S(2)}) copy-start(bf16[4096,512]{1,0:T(8,128)(2,1)} %all-gather.3.cloned.1.call-done) | copy-start | bytes 12582916
  154.1 11.7 %copy-start.1 = (bf16[1024,256]{1,0:T(8,128)(2,1)S(1)}, bf16[1024,256]{1,0:T(8,128)(2,1)}, u32[]{:S(2)}) copy-start(bf16[1024,256]{1,0:T(8,128)(2,1)} %copy-done) | copy-start | bytes 1572868
  154.1 11.7 %copy-start.3 = (bf16[1024,256]{1,0:T(8,128)(2,1)S(1)}, bf16[1024,256]{1,0:T(8,128)(2,1)}, u32[]{:S(2)}) copy-start(bf16[1024,256]{1,0:T(8,128)(2,1)} %copy-done.2) | copy-start | bytes 1572868
  156.1 12.9 %collective-permute-start.12 = (f32[2048,256]{1,0:T(8,128)S(1)}, f32[2048,256]{1,0:T(8,128)S(1)}, u32[]{:S(2)}, u32[]{:S(2)}) collective-permute-start(f32[2048,256]{1,0:T(8,128)S(1)} %shard_map.99), channel_id=1, source_target_pairs={{0,16},{16,0},{1,17},{17,1},{2,18},{18,2},{3,19},{19,3},{4,20},{20... | collective-permute-start | bytes 6291464 | tf_op jit(solution)/shard_map/ppermute | solution.py:41
  156.2 7.3 %collective-permute-start.11 = (bf16[256,256]{1,0:T(8,128)(2,1)S(1)}, bf16[256,256]{1,0:T(8,128)(2,1)S(1)}, u32[]{:S(2)}, u32[]{:S(2)}) collective-permute-start(bf16[256,256]{1,0:T(8,128)(2,1)S(1)} %get-tuple-element.33.refs_0_), channel_id=1, source_target_pairs={{0,3},{1,2},{2,1},{3,0},{4,7},{5,6},{6,5},{7,4},{8,11},{9,10},{10,... | collective-permute-start | bytes 393224 | tf_op jit(solution)/shard_map/ppermute | solution.py:50
  158.2 7.5 %collective-permute-start.10 = (bf16[256,256]{1,0:T(8,128)(2,1)S(1)}, bf16[256,256]{1,0:T(8,128)(2,1)S(1)}, u32[]{:S(2)}, u32[]{:S(2)}) collective-permute-start(bf16[256,256]{1,0:T(8,128)(2,1)S(1)} %get-tuple-element.33.refs_0_), channel_id=1, source_target_pairs={{0,2},{1,3},{2,0},{3,1},{4,6},{5,7},{6,4},{7,5},{8,10},{9,11},{10,... | collective-permute-start | bytes 393224 | tf_op jit(solution)/shard_map/ppermute | solution.py:50
  158.8 7.0 %collective-permute-start.9 = (bf16[256,256]{1,0:T(8,128)(2,1)S(1)}, bf16[256,256]{1,0:T(8,128)(2,1)S(1)}, u32[]{:S(2)}, u32[]{:S(2)}) collective-permute-start(bf16[256,256]{1,0:T(8,128)(2,1)S(1)} %get-tuple-element.33.refs_0_), channel_id=1, source_target_pairs={{0,1},{1,0},{2,3},{3,2},{4,5},{5,4},{6,7},{7,6},{8,9},{9,8},{10,11... | collective-permute-start | bytes 393224 | tf_op jit(solution)/shard_map/ppermute | solution.py:50
  (9 other events, 8.3 us)
Sparse Core Ops, SparseCore 0:
  95.1 52.8 all-gather.2

commit v4 on v3

--- a/solution.py
+++ b/solution.py
@@ -54,40 +54,37 @@
     return pl.ds(pl.multiple_of(start * IMGTOK, IMGTOK), IMGTOK)
 
 
-def project_body(d_ref, m_ref, s_ref, own_near, near_ref, own_far, far_ref, out_ref):
-    half = own_near.shape[0]
+def project_body(d_ref, s_ref, near_ref, far_ref, out_ref):
+    half = near_ref.shape[0]
     d = d_ref[0]
-    m = m_ref[0]
     near = s_ref[:, pl.ds(pl.multiple_of(d * half, half), half)]
     far = s_ref[:, pl.ds(pl.multiple_of((1 - d) * half, half), half)]
-    for h in range(out_ref.shape[0]):
-        near_w = near_ref[h - 1] if h else own_near[...]
-        far_w = far_ref[h - 1] if h else own_far[...]
-        out_ref[m ^ h] = dot(near, near_w, NN) + dot(far, far_w, NN)
-
-
-def project(d, m, states, own_near, near, own_far, far):
-    others, half, width = near.shape
+    out_ref[...] = dot(near, near_ref[...], NN) + dot(far, far_ref[...], NN)
+
+
+def project(d, states, near, far):
+    half, width = near.shape
     rows = states.shape[0]
-    smem = pl.BlockSpec(memory_space=pltpu.SMEM)
     vmem = pl.BlockSpec(memory_space=pltpu.VMEM)
     return pl.pallas_call(
         project_body,
-        in_specs=[smem, smem] + [vmem] * 5,
+        in_specs=[pl.BlockSpec(memory_space=pltpu.SMEM), vmem, vmem, vmem],
         out_specs=vmem,
-        out_shape=jax.ShapeDtypeStruct((others + 1, rows, width), jnp.float32),
-        cost_estimate=cost(4 * (others + 1) * rows * half * width, 8 * near.size),
+        out_shape=jax.ShapeDtypeStruct((rows, width), jnp.float32),
+        cost_estimate=cost(4 * rows * half * width, 4 * states.size),
         compiler_params=params(),
-    )(d, m, states, own_near, near, own_far, far)
-
-
-def pack_body(per_shard, c_ref, place_ref, part_ref, out_ref, rounded, count):
-    shards = out_ref.shape[0]
-    total = part_ref[0]
-    for m in range(1, part_ref.shape[0]):
-        total = total + part_ref[m]
+    )(d, states, near, far)
+
+
+def pack_body(per_shard, terms, c_ref, place_ref, *refs):
+    part_refs, out_refs = refs[:terms], refs[terms:-3]
+    rounded, sorted_ref, count = refs[-3:]
+    shards = sorted_ref.shape[0]
+    total = part_refs[0][...]
+    for ref in part_refs[1:]:
+        total = total + ref[...]
     rounded[...] = total.astype(jnp.bfloat16)
-    out_ref[...] = jnp.zeros_like(out_ref)
+    sorted_ref[...] = jnp.zeros_like(sorted_ref)
     for s in range(shards):
         count[s] = 0
     images = rounded.shape[0] // IMGTOK
@@ -98,33 +95,44 @@
         slot = count[dest]
         count[dest] = slot + 1
         block = rounded[rows16(i), :]
-        out_ref[dest, 0, rows16(slot), :] = block
+        sorted_ref[dest, 0, rows16(slot), :] = block
 
         @pl.when(dest + 1 < shards)
         def _():
-            out_ref[dest + 1, 1, rows16(slot), :] = block
+            sorted_ref[dest + 1, 1, rows16(slot), :] = block
 
         return carry
 
     lax.fori_loop(0, images, step, 0)
-
-
-def pack(c, place, parts, shards, capacity, per_shard):
-    _, rows, width = parts.shape
+    if len(out_refs) == 1:
+        out_refs[0][...] = sorted_ref[...]
+    else:
+        for u, ref in enumerate(out_refs):
+            ref[...] = sorted_ref[c ^ u]
+
+
+def pack(c, place, parts, shards, capacity, per_shard, mixed):
+    rows, width = parts[0].shape
     smem = pl.BlockSpec(memory_space=pltpu.SMEM)
     vmem = pl.BlockSpec(memory_space=pltpu.VMEM)
+    shape = (2, capacity, width)
+    if mixed:
+        out = [jax.ShapeDtypeStruct(shape, jnp.bfloat16)] * shards
+    else:
+        out = [jax.ShapeDtypeStruct((shards,) + shape, jnp.bfloat16)]
     return pl.pallas_call(
-        functools.partial(pack_body, per_shard),
-        in_specs=[smem, smem, vmem],
-        out_specs=vmem,
-        out_shape=jax.ShapeDtypeStruct((shards, 2, capacity, width), jnp.bfloat16),
+        functools.partial(pack_body, per_shard, len(parts)),
+        in_specs=[smem, smem] + [vmem] * len(parts),
+        out_specs=[vmem] * len(out),
+        out_shape=out,
         scratch_shapes=[
             pltpu.VMEM((rows, width), jnp.bfloat16),
+            pltpu.VMEM((shards,) + shape, jnp.bfloat16),
             pltpu.SMEM((shards,), jnp.int32),
         ],
-        cost_estimate=cost(0, parts.size * 6),
+        cost_estimate=cost(0, parts[0].size * 4 * 6),
         compiler_params=params(),
-    )(c, place, parts)
+    )(c, place, *parts)
 
 
 def attention_body(
@@ -138,15 +146,10 @@
     g_ref,
     own_ref,
     prior_ref,
-    image_ref,
-    out_ref,
-    own_grad_ref,
-    prior_grad_ref,
-    window,
-    probs,
-    grads,
-    total,
+    *refs,
 ):
+    image_refs = refs[:-8]
+    out_ref, own_grad_ref, prior_grad_ref, window, probs, grads, total, image_ref = refs[-8:]
     t = pl.program_id(0)
     c = c_ref[0]
     rows = own_ref.shape[0]
@@ -160,6 +163,11 @@
         window[:rows, :] = prior_ref[...]
         window[rows:, :] = own_ref[...]
         total[...] = jnp.zeros_like(total)
+        if len(image_refs) == 1:
+            image_ref[...] = image_refs[0][...]
+        else:
+            for u, ref in enumerate(image_refs):
+                image_ref[c ^ u] = ref[...]
 
         def step(b, carry):
             n_own, n_prior = carry
@@ -263,7 +271,7 @@
 
             @pl.when(is_prior)
             def _():
-                prior_grad_ref[rows16(n_prior), :] = total[rows16(at), :]
+                prior_grad_ref[rows16(n_prior), :] = total[rows16(at), :].astype(jnp.bfloat16)
 
             return n_own + is_own.astype(jnp.int32), n_prior + is_prior.astype(jnp.int32)
 
@@ -271,6 +279,7 @@
 
 
 def attention(c, place, start, queries, d_out, own, prior, image, images, per_shard, image_rows):
+    ranks = len(image) if len(image) > 1 else image[0].shape[0]
     rows, width = own.shape
     cols = queries.shape[1]
     tiles = rows // QTILE
@@ -279,6 +288,7 @@
     whole = lambda a: pl.BlockSpec(a.shape, lambda t, *_: (0,) * a.ndim)
     tile = pl.BlockSpec((QTILE, cols), lambda t, *_: (t, 0))
     grad = jax.ShapeDtypeStruct((image_rows, width), jnp.float32)
+    prior_grad = jax.ShapeDtypeStruct((image_rows, width), jnp.bfloat16)
     return pl.pallas_call(
         functools.partial(attention_body, per_shard, images),
         grid_spec=pltpu.PrefetchScalarGridSpec(
@@ -290,7 +300,7 @@
                 tile,
                 whole(own),
                 whole(prior),
-                whole(image),
+                *map(whole, image),
             ],
             out_specs=[tile, whole(grad), whole(grad)],
             scratch_shapes=[
@@ -298,16 +308,24 @@
                 pltpu.VMEM((span, head_rows), jnp.bfloat16),
                 pltpu.VMEM((span, head_rows), jnp.bfloat16),
                 pltpu.VMEM((2 * rows, width), jnp.float32),
+                pltpu.VMEM((ranks,) + image[0].shape[-3:], jnp.bfloat16),
             ],
         ),
-        out_shape=[jax.ShapeDtypeStruct((rows, cols), jnp.bfloat16), grad, grad],
+        out_shape=[jax.ShapeDtypeStruct((rows, cols), jnp.bfloat16), grad, prior_grad],
         cost_estimate=cost(2 * 20 * cols * span * rows, 4 * queries.size * 2),
         compiler_params=params(),
-    )(c, place, start[0, ::QTILE], start, queries, d_out, own, prior, image)
-
-
-def reorder_body(per_shard, images, c_ref, place_ref, g_ref, out_ref, mine_ref, count):
+    )(c, place, start[0, ::QTILE], start, queries, d_out, own, prior, *image)
+
+
+def reorder_body(per_shard, images, c_ref, place_ref, *refs):
+    grad_refs = refs[:-4]
+    out_ref, mine_ref, g_ref, count = refs[-4:]
     shards = g_ref.shape[0]
+    if len(grad_refs) == 1:
+        g_ref[...] = grad_refs[0][...]
+    else:
+        for u, ref in enumerate(grad_refs):
+            g_ref[c_ref[0] ^ u] = ref[...]
     for s in range(shards):
         count[s] = 0
     c = c_ref[0]
@@ -324,88 +342,103 @@
     mine_ref[...] = out_ref[pl.ds(pl.multiple_of(c * rows, IMGTOK), rows), :]
 
 
-def reorder(c, place, gathered, per_shard, images):
-    shards, rows, width = gathered.shape
+def reorder(c, place, gathered, per_shard, images, shards):
+    rows, width = gathered[0].shape[-2:]
+    dtype = gathered[0].dtype
     smem = pl.BlockSpec(memory_space=pltpu.SMEM)
     vmem = pl.BlockSpec(memory_space=pltpu.VMEM)
     return pl.pallas_call(
         functools.partial(reorder_body, per_shard, images),
-        in_specs=[smem, smem, vmem],
+        in_specs=[smem, smem] + [vmem] * len(gathered),
         out_specs=[vmem, vmem],
         out_shape=[
-            jax.ShapeDtypeStruct((shards * rows, width), gathered.dtype),
-            jax.ShapeDtypeStruct((rows, width), gathered.dtype),
+            jax.ShapeDtypeStruct((shards * rows, width), dtype),
+            jax.ShapeDtypeStruct((rows, width), dtype),
         ],
-        scratch_shapes=[pltpu.SMEM((shards,), jnp.int32)],
-        cost_estimate=cost(0, gathered.size * 2 * 4),
+        scratch_shapes=[
+            pltpu.VMEM((shards, rows, width), dtype),
+            pltpu.SMEM((shards,), jnp.int32),
+        ],
+        cost_estimate=cost(0, shards * rows * width * 8),
         compiler_params=params(),
-    )(c, place, gathered)
-
-
-def weight_body(mixed, c_ref, s_ref, g_ref, out_ref):
+    )(c, place, *gathered)
+
+
+def weight_body(mixed, c_ref, *refs):
+    *state_refs, g_ref, out_ref = refs
     ranks, rows, width = g_ref.shape
     c = c_ref[0]
-    if mixed:
-        grad = jnp.concatenate([g_ref[c ^ s] for s in range(ranks)], axis=0)
-    else:
-        grad = g_ref[...].reshape(ranks * rows, width)
-    out_ref[...] = dot(s_ref[0], grad, TN)
+    total = None
+    done = 0
+    for ref in state_refs:
+        count = ref.shape[1] // rows
+        if mixed:
+            grad = [g_ref[c ^ s] for s in range(done, done + count)]
+            grad = jnp.concatenate(grad, axis=0)
+        else:
+            grad = g_ref[...].reshape(ranks * rows, width)
+        done += count
+        term = dot(ref[0], grad, TN)
+        total = term if total is None else total + term
+    out_ref[...] = total
 
 
 def weight_term(c, states, grad, mixed):
-    parts, rows, cols = states.shape
+    parts, _, cols = states[0].shape
     width = grad.shape[2]
+    size = sum(a.size for a in states)
     return pl.pallas_call(
         functools.partial(weight_body, mixed),
         grid_spec=pltpu.PrefetchScalarGridSpec(
             num_scalar_prefetch=1,
             grid=(parts,),
             in_specs=[
-                pl.BlockSpec((1, rows, cols), lambda k, c: (k, 0, 0)),
+                *[pl.BlockSpec((1,) + a.shape[1:], lambda k, c: (k, 0, 0)) for a in states],
                 pl.BlockSpec(grad.shape, lambda k, c: (0, 0, 0)),
             ],
             out_specs=pl.BlockSpec((cols, width), lambda k, c: (k, 0)),
         ),
         out_shape=jax.ShapeDtypeStruct((parts * cols, width), jnp.float32),
-        cost_estimate=cost(2 * states.size * width, states.size * 4),
+        cost_estimate=cost(2 * size * width, size * 4),
         compiler_params=params(),
-    )(c, states, grad)
+    )(c, *states, grad)
 
 
 def image_body(d_ref, *refs):
-    own_near, near_ref, own_far, far_ref, out_ref = refs[-5:]
-    grads = refs[:-5]
+    out_ref = refs[-1]
+    heads = (len(refs) - 1) // 3
+    grads, near, far = refs[:heads], refs[heads : 2 * heads], refs[2 * heads : -1]
     j = pl.program_id(0)
-    cols = own_near.shape[0]
+    cols = near[0].shape[0]
     half = out_ref.shape[1] // 2
     d = d_ref[0]
-    for own, others, side in ((own_near, near_ref, d), (own_far, far_ref, 1 - d)):
-        total = dot(grads[0][...], own[...], NT)
-        for h in range(1, len(grads)):
-            total = total + dot(grads[h][...], others[h - 1], NT)
+    for weights, side in ((near, d), (far, 1 - d)):
+        total = dot(grads[0][...], weights[0][...], NT)
+        for h in range(1, heads):
+            total = total + dot(grads[h][...], weights[h][...], NT)
         at = pl.multiple_of(side * half + j * cols, cols)
         out_ref[:, pl.ds(at, cols)] = total.astype(out_ref.dtype)
 
 
-def image_term(d, grads, own_near, near, own_far, far):
-    others, half, width = near.shape
+def image_term(d, grads, near, far):
+    heads = len(near)
+    half, width = near[0].shape
     rows = grads[0].shape[0]
     tiles = 4
-    own = pl.BlockSpec((half // tiles, width), lambda j, d: (j, 0))
-    side = pl.BlockSpec((others, half // tiles, width), lambda j, d: (0, j, 0))
+    side = pl.BlockSpec((half // tiles, width), lambda j, d: (j, 0))
     grad = pl.BlockSpec((rows, width), lambda j, d: (0, 0))
     return pl.pallas_call(
         image_body,
         grid_spec=pltpu.PrefetchScalarGridSpec(
             num_scalar_prefetch=1,
             grid=(tiles,),
-            in_specs=[grad] * len(grads) + [own, side] * 2,
+            in_specs=[grad] * heads + [side] * (2 * heads),
             out_specs=pl.BlockSpec((rows, 2 * half), lambda j, d: (0, 0)),
         ),
         out_shape=jax.ShapeDtypeStruct((rows, 2 * half), jnp.bfloat16),
-        cost_estimate=cost(4 * len(grads) * half * width * rows, 8 * near.size),
+        cost_estimate=cost(4 * heads * half * width * rows, 4 * heads * half * width * 2),
         compiler_params=params(),
-    )(d, *grads, own_near, near, own_far, far)
+    )(d, *grads, *near, *far)
 
 
 def per_device(image_states, place_index, doc_ids, queries, text_kv, kv_weight, d_out):
@@ -426,15 +459,18 @@
     place = place_index[0, ::IMGTOK] // IMGTOK
 
     m = lax.axis_index("mp")
-    m1 = jnp.reshape(m, (1,)).astype(jnp.int32)
     steps = range(1, mps)
+    mixed = ranks == mps
 
     half = feats // 2
 
     def slab(source, head, side):
         return lax.dynamic_slice_in_dim(source, head * feats + side * half, half)
 
-    near = [trade(slab(weights, m ^ s, d), "mp", s) for s in steps]
+    slabs = [slab(weights, m ^ s, d) for s in steps]
+    *slabs, states_late = lax.optimization_barrier((*slabs, states))
+    near = [trade(w, "mp", s) for w, s in zip(slabs, steps)]
+    far = [swap(w, "dp") for w in near]
 
     prior_text = shift(text_kv[0], "ctx", 1)
     docs = doc_ids[0]
@@ -445,38 +481,61 @@
     start = jnp.sum((key_docs[:, None] < own_docs[None, :]).astype(jnp.int32), axis=0)[None]
 
     sub = feats // (ranks // mps) // mps
-    mixed = ranks == mps
-    pieces = states.reshape(image_rows, ranks // mps, mps, sub).transpose(2, 0, 1, 3)
-    pieces = exchange(pieces, "mp")
-    pieces = pieces.transpose(0, 2, 1, 3).reshape(ranks, image_rows, sub)
-    *near, pieces, weights_late, prior_text, start, place = lax.optimization_barrier(
-        (*near, pieces, weights, prior_text, start, place)
-    )
     if mixed:
-        moved = [lax.dynamic_index_in_dim(pieces, c ^ s, keepdims=False) for s in range(ranks)]
-        moved = [trade(moved[s], "ctx", s) if s else moved[0] for s in range(ranks)]
+        source = states_late
+        pieces = [lax.dynamic_slice_in_dim(source, m * sub, sub, axis=1)]
+        for s in steps:
+            piece = lax.dynamic_slice_in_dim(source, (m ^ s) * sub, sub, axis=1)
+            pieces.append(trade(piece, "mp", s))
+        *near, pieces = lax.optimization_barrier((*near, jnp.stack(pieces)))
+        moved = [
+            lax.dynamic_index_in_dim(pieces, m ^ c ^ s, keepdims=False) for s in range(ranks)
+        ]
     else:
+        pieces = states.reshape(image_rows, ranks // mps, mps, sub).transpose(2, 0, 1, 3)
+        pieces = exchange(pieces, "mp")
+        pieces = pieces.transpose(0, 2, 1, 3).reshape(ranks, image_rows, sub)
         moved = [exchange(pieces, "ctx").reshape(ranks * image_rows, sub)]
 
-    near = jnp.stack(near)
-    far = swap(near, "dp")
-    own_near = slab(weights_late, m, d)
-    own_far = slab(weights_late, m, 1 - d)
-    parts = exchange(project(d1, m1, states, own_near, near, own_far, far), "mp")
-    packed = pack(c1, place, parts, ranks, capacity, per_shard)
-    packed, *moved = lax.optimization_barrier((packed, *moved))
-    all_states = lax.all_gather(jnp.concatenate(moved, axis=0), "mp", axis=0)
-    image = exchange(packed, "ctx")
+    weights_late, _ = lax.optimization_barrier((weights, near[-1]))
+    near = [slab(weights_late, m, d)] + near
+    far = [slab(weights_late, m, 1 - d)] + far
+    parts = [project(d1, states, near[s], far[s]) for s in range(mps)]
+    parts = [trade(parts[s], "mp", s) if s else parts[0] for s in range(mps)]
+    packed = pack(c1, place, parts, ranks, capacity, per_shard, mixed)
+    cut = ranks // 2
+    if mixed:
+        for s in range(1, cut):
+            moved[s] = trade(moved[s], "ctx", s)
+        moved[cut], _ = lax.optimization_barrier((moved[cut], packed[0]))
+        moved[cut] = trade(moved[cut], "ctx", cut)
+        image = [trade(packed[s], "ctx", s) if s else packed[0] for s in range(ranks)]
+        for s in range(cut + 1, ranks):
+            moved[s], *image = lax.optimization_barrier((moved[s], *image))
+            moved[s] = trade(moved[s], "ctx", s)
+        moved = [jnp.concatenate(moved[:cut], axis=0), jnp.concatenate(moved[cut:], axis=0)]
+    else:
+        image = [exchange(packed[0], "ctx")]
+    moved[0], _ = lax.optimization_barrier((moved[0], packed[0]))
+    all_states = [lax.all_gather(moved[0], "mp", axis=0)]
     attn_out, own_grad, prior_grad = attention(
         c1, place, start, queries[0], d_out[0], text_kv[0], prior_text, image,
         images, per_shard, image_rows,
     )
-    grad = (own_grad + shift(prior_grad, "ctx", -1)).astype(jnp.bfloat16)
-    gathered = exchange(jnp.broadcast_to(grad, (ranks,) + grad.shape), "ctx")
-    by_rank, mine = reorder(c1, place, gathered, per_shard, images)
+    if mixed:
+        moved[1], prior_grad = lax.optimization_barrier((moved[1], prior_grad))
+        all_states.append(lax.all_gather(moved[1], "mp", axis=0))
+    grad = own_grad + shift(prior_grad, "ctx", -1).astype(jnp.float32)
+    grad = grad.astype(jnp.bfloat16)
+    if mixed:
+        gathered = [trade(grad, "ctx", s) if s else grad for s in range(ranks)]
+    else:
+        gathered = [exchange(jnp.broadcast_to(grad, (ranks,) + grad.shape), "ctx")]
+    by_rank, mine = reorder(c1, place, gathered, per_shard, images, ranks)
     head_grad = [mine] + [trade(mine, "mp", s) for s in steps]
+    by_rank, *head_grad = lax.optimization_barrier((by_rank, *head_grad))
+    image_grad = image_term(d1, head_grad, near, far)
     term = weight_term(c1, all_states, by_rank.reshape(ranks, image_rows, width), mixed)
-    image_grad = image_term(d1, head_grad, own_near, near, own_far, far)
     weight_grad = term + swap(term, "dp")
     return (attn_out[None], image_grad[None], weight_grad[None])
 

time: 179 us -> 168 us (0.939)
  blocking collectives: 16.5 us -> 0 us
  starting transfers between devices: 29.8 us -> 39.6 us
  local copies, waits for them, and re-layouts: 21.2 us -> 12.3 us
  Pallas kernels: 22.6 us -> 27.8 us
    all_to_all x3 -> x0, waiting for transfers between devices: 30.5 us -> none  [exchange(): return lax.all_to_all(blocks, axis, split_axis=0, concat_axis=0, tiled=True)]
    ppermute x9 -> x21, waiting for transfers between devices: 27.9 us -> 54 us  [trade(): return lax.ppermute(block, axis, [(i, i ^ step) for i in range(count)])]
    ppermute x9 -> x21, starting transfers between devices: 11.6 us -> 35.1 us  [trade(): return lax.ppermute(block, axis, [(i, i ^ step) for i in range(count)])]
    all_to_all x1 -> x0, blocking collectives: 16.5 us -> none  [exchange(): return lax.all_to_all(blocks, axis, split_axis=0, concat_axis=0, tiled=True)]
    all_to_all x3 -> x0, starting transfers between devices: 13.2 us -> none  [exchange(): return lax.all_to_all(blocks, axis, split_axis=0, concat_axis=0, tiled=True)]
    unnamed x33 -> x26, local copies, waits for them, and re-layouts: 14 us -> 5.67 us
    all_gather x1 -> x2, waiting for transfers between devices: 0.01 us -> 8.11 us  [the longest x1 8.1 us: per_device(): all_states.append(lax.all_gather(moved[1], 'mp', axis=0))]
    pallas_call x2 -> x5, Pallas kernels: 3.65 us -> 7.55 us  [the longest x4 5.98 us: project(): pl.pallas_call(project_body, in_specs=[pl.BlockSpec(memory_space=pltpu.SM...]
  transfers between devices with their start and end apart: 17 -> 29, of which waited for: 11 -> 13; matrix products, arithmetic and copies ran while one was open for 4% -> 5% of each run, Pallas kernels for 11% -> 14%
where the time goes in v4:
time: 168 us
  waiting for transfers between devices  67.7 us (40%)
  starting transfers between devices  39.6 us (24%)
  Pallas kernels  27.8 us (17%)
  between operations  14.3 us (9%)
  local copies, waits for them, and re-layouts  12.3 us (7%)
  other arithmetic  5.83 us (3%)
    ppermute x21, waiting for transfers between devices, trade(): return lax.ppermute(block, axis, [(i, i ^ step) for i in range(count)])  54 us
    ppermute x21, starting transfers between devices, trade(): return lax.ppermute(block, axis, [(i, i ^ step) for i in range(count)])  35.1 us
    pallas_call x1, Pallas kernels, attention(): pl.pallas_call(functools.partial(attention_body, per_shard, images), grid...  12.2 us
    all_gather x1, waiting for transfers between devices, per_device(): all_states.append(lax.all_gather(moved[1], 'mp', axis=0))  8.1 us
    pallas_call x4, Pallas kernels, project(): pl.pallas_call(project_body, in_specs=[pl.BlockSpec(memory_space=pltpu.SM...  5.98 us
    unnamed x26, local copies, waits for them, and re-layouts  5.67 us
    ppermute x2, waiting for transfers between devices, shift(): return lax.ppermute(block, axis, route)  5.56 us
    pallas_call x1, Pallas kernels, image_term(): pl.pallas_call(image_body, grid_spec=pltpu.PrefetchScalarGridSpec(num_sca...  4.43 us
  transfers between devices with their start and end apart: 29, of which 13 were waited for; matrix products, arithmetic and copies ran while one was open for 5% of the time, Pallas kernels for 14%

profile of v4, /device:TPU:0, one launch (start us, length us, event | category | flops | bytes accessed | tf_op | source)
XLA Modules:
  0.0 167.5 jit_solution(17063265046533819722)
XLA Ops:
  7.2 2.5 %dynamic-slice_bitcast_fusion = (bf16[1024,256]{1,0:T(8,128)(2,1)}, bf16[1024,256]{1,0:T(8,128)(2,1)}, bf16[1024,256]{1,0:T(8,128)(2,1)S(1)}) fusion(bf16[1,8192,256]{2,1,0:T(8,128)(2,1)} %param.12, s32[]{:T(128)S(6)} %select_n.70, s32[]{:T(128)S(6)} %select_n.69, s32[]{:T(128)S(6)} %select_n.68), kind=kLoop, calls=%fused_computation.5 | loop fusion | bytes 3145740 | tf_op jit(solution)/shard_map/dynamic_slice | solution.py:468
  9.8 2.9 %collective-permute-start.1 = (bf16[1024,256]{1,0:T(8,128)(2,1)S(1)}, bf16[1024,256]{1,0:T(8,128)(2,1)S(1)}, u32[]{:S(2)}, u32[]{:S(2)}) collective-permute-start(bf16[1024,256]{1,0:T(8,128)(2,1)S(1)} %get-tuple-element.35), channel_id=1, source_target_pairs={{0,1},{1,0},{2,3},{3,2},{4,5},{5,4},{6,7},{7,6},{8,9},{9,8},{10,11... | collective-permute-start | bytes 1572872 | tf_op jit(solution)/shard_map/ppermute | solution.py:50
  15.1 2.9 %collective-permute-start.6 = (bf16[256,512]{1,0:T(8,128)(2,1)S(1)}, bf16[256,512]{1,0:T(8,128)(2,1)S(1)}, u32[]{:S(2)}, u32[]{:S(2)}) collective-permute-start(bf16[256,512]{1,0:T(8,128)(2,1)S(1)} %get-tuple-element.77), channel_id=1, source_target_pairs={{0,3},{1,2},{2,1},{3,0},{4,7},{5,6},{6,5},{7,4},{8,11},{9,10},{10,... | collective-permute-start | bytes 786440 | tf_op jit(solution)/shard_map/ppermute | solution.py:50
  18.5 24.2 %collective-permute-done.6 = bf16[256,512]{1,0:T(8,128)(2,1)S(1)} collective-permute-done((bf16[256,512]{1,0:T(8,128)(2,1)S(1)}, bf16[256,512]{1,0:T(8,128)(2,1)S(1)}, u32[]{:S(2)}, u32[]{:S(2)}) %collective-permute-start.6) | collective-permute-done | bytes 262176 | tf_op jit(solution)/shard_map/ppermute | solution.py:50
  45.8 3.0 %collective-permute-done.5 = bf16[256,512]{1,0:T(8,128)(2,1)} collective-permute-done((bf16[256,512]{1,0:T(8,128)(2,1)}, bf16[256,512]{1,0:T(8,128)(2,1)}, u32[]{:S(2)}, u32[]{:S(2)}) %collective-permute-start.5) | collective-permute-done | bytes 262176 | tf_op jit(solution)/shard_map/ppermute | solution.py:50
  56.7 2.2 %shard_map.96 = f32[256,256]{1,0:T(8,128)} custom-call(s32[1]{0:T(128)} %bitcast.18.d_ref, bf16[256,2048]{1,0:T(8,128)(2,1)S(1)} %bitcast.47, bf16[1024,256]{1,0:T(8,128)(2,1)S(1)} %collective-permute-done.2.near_ref.refs_6_, bf16[1024,256]{1,0:T(8,128)(2,1)} %collective-permute-done.9.far_ref.refs_10_), custom_call_target="tpu_custom_call" | custom-call | flops 268435456 | bytes 2097152 | tf_op jit(solution)/shard_map/pallas_call | solution.py:69
  59.4 2.2 %shard_map.97 = f32[256,256]{1,0:T(8,128)} custom-call(s32[1]{0:T(128)} %bitcast.18.d_ref, bf16[256,2048]{1,0:T(8,128)(2,1)S(1)} %bitcast.48, bf16[1024,256]{1,0:T(8,128)(2,1)S(1)} %collective-permute-done.3.near_ref.refs_7_, bf16[1024,256]{1,0:T(8,128)(2,1)} %collective-permute-done.11.far_ref.refs_11_), custom_call_target="tpu_custom_call" | custom-call | flops 268435456 | bytes 2097152 | tf_op jit(solution)/shard_map/pallas_call | solution.py:69
  64.9 1.8 %pad_maximum_fusion.2 = bf16[512,512]{1,0:T(8,128)(2,1)} fusion(bf16[256,512]{1,0:T(8,128)(2,1)} %collective-permute-done.25, bf16[256,512]{1,0:T(8,128)(2,1)S(1)} %copy-done.10), kind=kLoop, calls=%fused_computation.4 | loop fusion | flops 1048576 | bytes 1048576 | tf_op jit(solution)/shard_map/concatenate | solution.py:516
  66.7 4.3 %collective-permute-done.10.refs_2_ = f32[256,256]{1,0:T(8,128)} collective-permute-done((f32[256,256]{1,0:T(8,128)}, f32[256,256]{1,0:T(8,128)}, u32[]{:S(2)}, u32[]{:S(2)}) %collective-permute-start.10) | collective-permute-done | bytes 262176 | tf_op jit(solution)/shard_map/ppermute | solution.py:50
  72.7 2.4 %collective-permute-start = (bf16[512,256]{1,0:T(8,128)(2,1)S(1)}, bf16[512,256]{1,0:T(8,128)(2,1)S(1)}, u32[]{:S(2)}, u32[]{:S(2)}) collective-permute-start(bf16[512,256]{1,0:T(8,128)(2,1)S(1)} %bitcast.57), channel_id=1, source_target_pairs={{0,4},{4,8},{8,12},{1,5},{5,9},{9,13},{2,6},{6,10},{10,14},{3,7},{... | collective-permute-start | bytes 786440 | tf_op jit(solution)/shard_map/ppermute | solution.py:36
  75.1 2.8 %collective-permute-start.13 = (bf16[2,64,256]{2,1,0:T(8,128)(2,1)S(1)}, bf16[2,64,256]{2,1,0:T(8,128)(2,1)S(1)}, u32[]{:S(2)}, u32[]{:S(2)}) collective-permute-start(bf16[2,64,256]{2,1,0:T(8,128)(2,1)S(1)} %get-tuple-element.45), channel_id=1, source_target_pairs={{0,4},{4,0},{8,12},{12,8},{1,5},{5,1},{9,13},{13,9},{2,6},{6,2},{1... | collective-permute-start | bytes 196616 | tf_op jit(solution)/shard_map/ppermute | solution.py:50
  77.8 2.4 %collective-permute-start.15 = (bf16[2,64,256]{2,1,0:T(8,128)(2,1)S(1)}, bf16[2,64,256]{2,1,0:T(8,128)(2,1)S(1)}, u32[]{:S(2)}, u32[]{:S(2)}) collective-permute-start(bf16[2,64,256]{2,1,0:T(8,128)(2,1)S(1)} %get-tuple-element.47), channel_id=1, source_target_pairs={{0,12},{4,8},{8,4},{12,0},{1,13},{5,9},{9,5},{13,1},{2,14},{6,10},... | collective-permute-start | bytes 196616 | tf_op jit(solution)/shard_map/ppermute | solution.py:50
  81.6 8.8 %collective-permute-done.14.refs_2_ = bf16[2,64,256]{2,1,0:T(8,128)(2,1)S(1)} collective-permute-done((bf16[2,64,256]{2,1,0:T(8,128)(2,1)S(1)}, bf16[2,64,256]{2,1,0:T(8,128)(2,1)S(1)}, u32[]{:S(2)}, u32[]{:S(2)}) %collective-permute-start.14) | collective-permute-done | bytes 65568 | tf_op jit(solution)/shard_map/ppermute | solution.py:50
  90.4 6.5 %collective-permute-start.17 = (bf16[256,512]{1,0:T(8,128)(2,1)}, bf16[256,512]{1,0:T(8,128)(2,1)S(1)}, u32[]{:S(2)}, u32[]{:S(2)}) collective-permute-start(bf16[256,512]{1,0:T(8,128)(2,1)} %get-tuple-element.55), channel_id=1, source_target_pairs={{0,12},{4,8},{8,4},{12,0},{1,13},{5,9},{9,5},{13,1},{2,14},{6,10},... | collective-permute-start | bytes 786440 | tf_op jit(solution)/shard_map/ppermute | solution.py:50
  99.4 12.2 %shard_map.99 = (bf16[512,1024]{1,0:T(8,128)(2,1)}, f32[256,256]{1,0:T(8,128)S(1)}, bf16[256,256]{1,0:T(8,128)(2,1)S(1)}) custom-call(s32[1]{0:T(128)} %bitcast.c_ref, s32[64]{0:T(128)S(1)} %and_select_fusion.place_ref, s32[4]{0:T(128)S(1)} %bitcast.59, s32[1,512]{1,0:T(1,128)S(1)} %bitcast.54, bf16[512,1024]{1,0:T(8,128)(2,1)S(1)} %bitcast.55, ...), custom_call_target="tpu_custom_call" | custom-call | flops 13421772800 | bytes 4194304 | tf_op jit(solution)/shard_map/pallas_call | solution.py:292
  113.7 5.6 %collective-permute-done.18 = bf16[256,256]{1,0:T(8,128)(2,1)S(1)} collective-permute-done((bf16[256,256]{1,0:T(8,128)(2,1)S(1)}, bf16[256,256]{1,0:T(8,128)(2,1)S(1)}, u32[]{:S(2)}, u32[]{:S(2)}) %collective-permute-start.18) | collective-permute-done | bytes 131104 | tf_op jit(solution)/shard_map/ppermute | solution.py:36
  121.6 2.2 %collective-permute-start.21 = (bf16[256,256]{1,0:T(8,128)(2,1)S(1)}, bf16[256,256]{1,0:T(8,128)(2,1)S(1)}, u32[]{:S(2)}, u32[]{:S(2)}) collective-permute-start(bf16[256,256]{1,0:T(8,128)(2,1)S(1)} %add_convert_fusion.refs_0_), channel_id=1, source_target_pairs={{0,12},{4,8},{8,4},{12,0},{1,13},{5,9},{9,5},{13,1},{2,14},{6,10},... | collective-permute-start | bytes 393224 | tf_op jit(solution)/shard_map/ppermute | solution.py:50
  125.9 2.9 %collective-permute-done.21.refs_3_ = bf16[256,256]{1,0:T(8,128)(2,1)S(1)} collective-permute-done((bf16[256,256]{1,0:T(8,128)(2,1)S(1)}, bf16[256,256]{1,0:T(8,128)(2,1)S(1)}, u32[]{:S(2)}, u32[]{:S(2)}) %collective-permute-start.21) | collective-permute-done | bytes 131104 | tf_op jit(solution)/shard_map/ppermute | solution.py:50
  128.8 1.7 shard_map.100
  135.5 3.7 %collective-permute-done.23.refs_2_ = bf16[256,256]{1,0:T(8,128)(2,1)S(1)} collective-permute-done((bf16[256,256]{1,0:T(8,128)(2,1)S(1)}, bf16[256,256]{1,0:T(8,128)(2,1)S(1)}, u32[]{:S(2)}, u32[]{:S(2)}) %collective-permute-start.23) | collective-permute-done | bytes 131104 | tf_op jit(solution)/shard_map/ppermute | solution.py:50
  139.2 2.1 %collective-permute-done.24.refs_3_ = bf16[256,256]{1,0:T(8,128)(2,1)S(1)} collective-permute-done((bf16[256,256]{1,0:T(8,128)(2,1)S(1)}, bf16[256,256]{1,0:T(8,128)(2,1)S(1)}, u32[]{:S(2)}, u32[]{:S(2)}) %collective-permute-start.24) | collective-permute-done | bytes 131104 | tf_op jit(solution)/shard_map/ppermute | solution.py:50
  141.3 8.1 %all-gather.7.cloned.1.call-done = bf16[2048,512]{1,0:T(8,128)(2,1)} async-done(((bf16[512,512]{1,0:T(8,128)(2,1)}), bf16[2048,512]{1,0:T(8,128)(2,1)}) %all-gather.7.cloned.1.call-update) | async-done | bytes 2097168 | tf_op jit(solution)/shard_map/all_gather | solution.py:527
  152.6 2.0 %shard_map.102 = f32[2048,256]{1,0:T(8,128)S(1)} custom-call(s32[1]{0:T(128)} %bitcast.c_ref, bf16[4,512,512]{2,1,0:T(8,128)(2,1)S(1)} %bitcast.50, bf16[4,512,512]{2,1,0:T(8,128)(2,1)S(1)} %bitcast.51, bf16[4,256,256]{2,1,0:T(8,128)(2,1)S(1)} %bitcast.52), custom_call_target="tpu_custom_call" | custom-call | flops 1073741824 | bytes 8388608 | tf_op jit(solution)/shard_map/pallas_call | solution.py:390
  154.7 4.4 %shard_map.101 = bf16[256,2048]{1,0:T(8,128)(2,1)} custom-call(s32[1]{0:T(128)} %bitcast.18.d_ref, bf16[256,256]{1,0:T(8,128)(2,1)S(1)} %get-tuple-element.60.refs_0_, bf16[256,256]{1,0:T(8,128)(2,1)S(1)} %collective-permute-done.22.refs_1_, bf16[256,256]{1,0:T(8,128)(2,1)S(1)} %collective-permute-done.23.refs_2_, ...), custom_call_target="tpu_custom_call" | custom-call | flops 1073741824 | bytes 8388608 | tf_op jit(solution)/shard_map/pallas_call | solution.py:430
  (86 shorter events, 39.4 us)
Async XLA Ops:
  7.2 134.1 %all-gather.5.cloned.1.call-start = ((), (), s32[]{:S(2)}) async-start(), calls=%async_computation | async-start | bytes 2621440 | tf_op jit(solution)/shard_map/all_gather | solution.py:520
  9.8 34.5 %collective-permute-start.1 = (bf16[1024,256]{1,0:T(8,128)(2,1)S(1)}, bf16[1024,256]{1,0:T(8,128)(2,1)S(1)}, u32[]{:S(2)}, u32[]{:S(2)}) collective-permute-start(bf16[1024,256]{1,0:T(8,128)(2,1)S(1)} %get-tuple-element.35), channel_id=1, source_target_pairs={{0,1},{1,0},{2,3},{3,2},{4,5},{5,4},{6,7},{7,6},{8,9},{9,8},{10,11... | collective-permute-start | bytes 1572872 | tf_op jit(solution)/shard_map/ppermute | solution.py:50
  12.7 32.5 %collective-permute-start.2 = (bf16[1024,256]{1,0:T(8,128)(2,1)}, bf16[1024,256]{1,0:T(8,128)(2,1)S(1)}, u32[]{:S(2)}, u32[]{:S(2)}) collective-permute-start(bf16[1024,256]{1,0:T(8,128)(2,1)} %get-tuple-element.36), channel_id=1, source_target_pairs={{0,2},{1,3},{2,0},{3,1},{4,6},{5,7},{6,4},{7,5},{8,10},{9,11},{10,... | collective-permute-start | bytes 1572872 | tf_op jit(solution)/shard_map/ppermute | solution.py:50
  14.2 31.5 %collective-permute-start.3 = (bf16[1024,256]{1,0:T(8,128)(2,1)}, bf16[1024,256]{1,0:T(8,128)(2,1)S(1)}, u32[]{:S(2)}, u32[]{:S(2)}) collective-permute-start(bf16[1024,256]{1,0:T(8,128)(2,1)} %get-tuple-element.37), channel_id=1, source_target_pairs={{0,3},{1,2},{2,1},{3,0},{4,7},{5,6},{6,5},{7,4},{8,11},{9,10},{10,... | collective-permute-start | bytes 1572872 | tf_op jit(solution)/shard_map/ppermute | solution.py:50
  15.1 27.7 %collective-permute-start.6 = (bf16[256,512]{1,0:T(8,128)(2,1)S(1)}, bf16[256,512]{1,0:T(8,128)(2,1)S(1)}, u32[]{:S(2)}, u32[]{:S(2)}) collective-permute-start(bf16[256,512]{1,0:T(8,128)(2,1)S(1)} %get-tuple-element.77), channel_id=1, source_target_pairs={{0,3},{1,2},{2,1},{3,0},{4,7},{5,6},{6,5},{7,4},{8,11},{9,10},{10,... | collective-permute-start | bytes 786440 | tf_op jit(solution)/shard_map/ppermute | solution.py:50
  18.0 30.8 %collective-permute-start.5 = (bf16[256,512]{1,0:T(8,128)(2,1)}, bf16[256,512]{1,0:T(8,128)(2,1)}, u32[]{:S(2)}, u32[]{:S(2)}) collective-permute-start(bf16[256,512]{1,0:T(8,128)(2,1)} %get-tuple-element.78), channel_id=1, source_target_pairs={{0,2},{1,3},{2,0},{3,1},{4,6},{5,7},{6,4},{7,5},{8,10},{9,11},{10,... | collective-permute-start | bytes 786440 | tf_op jit(solution)/shard_map/ppermute | solution.py:50
  42.8 7.4 %collective-permute-start.4 = (bf16[256,512]{1,0:T(8,128)(2,1)}, bf16[256,512]{1,0:T(8,128)(2,1)}, u32[]{:S(2)}, u32[]{:S(2)}) collective-permute-start(bf16[256,512]{1,0:T(8,128)(2,1)} %get-tuple-element.79), channel_id=1, source_target_pairs={{0,1},{1,0},{2,3},{3,2},{4,5},{5,4},{6,7},{7,6},{8,9},{9,8},{10,11... | collective-permute-start | bytes 786440 | tf_op jit(solution)/shard_map/ppermute | solution.py:50
  44.3 9.8 %collective-permute-start.7 = (bf16[1024,256]{1,0:T(8,128)(2,1)S(1)}, bf16[1024,256]{1,0:T(8,128)(2,1)S(1)}, u32[]{:S(2)}, u32[]{:S(2)}) collective-permute-start(bf16[1024,256]{1,0:T(8,128)(2,1)S(1)} %collective-permute-done.1.near_ref.refs_5_), channel_id=1, source_target_pairs={{0,16},{16,0},{1,17},{17,1},{2,18},{18,2},{3,19},{19,3},{4,20},{20... | collective-permute-start | bytes 1572872 | tf_op jit(solution)/shard_map/ppermute | solution.py:41
  45.2 11.5 %collective-permute-start.9 = (bf16[1024,256]{1,0:T(8,128)(2,1)S(1)}, bf16[1024,256]{1,0:T(8,128)(2,1)}, u32[]{:S(2)}, u32[]{:S(2)}) collective-permute-start(bf16[1024,256]{1,0:T(8,128)(2,1)S(1)} %collective-permute-done.2.near_ref.refs_6_), channel_id=1, source_target_pairs={{0,16},{16,0},{1,17},{17,1},{2,18},{18,2},{3,19},{19,3},{4,20},{20... | collective-permute-start | bytes 1572872 | tf_op jit(solution)/shard_map/ppermute | solution.py:41
  45.7 13.7 %collective-permute-start.11 = (bf16[1024,256]{1,0:T(8,128)(2,1)S(1)}, bf16[1024,256]{1,0:T(8,128)(2,1)}, u32[]{:S(2)}, u32[]{:S(2)}) collective-permute-start(bf16[1024,256]{1,0:T(8,128)(2,1)S(1)} %collective-permute-done.3.near_ref.refs_7_), channel_id=1, source_target_pairs={{0,16},{16,0},{1,17},{17,1},{2,18},{18,2},{3,19},{19,3},{4,20},{20... | collective-permute-start | bytes 1572872 | tf_op jit(solution)/shard_map/ppermute | solution.py:41
  52.5 12.4 %collective-permute-start.25 = (bf16[256,512]{1,0:T(8,128)(2,1)}, bf16[256,512]{1,0:T(8,128)(2,1)}, u32[]{:S(2)}, u32[]{:S(2)}) collective-permute-start(bf16[256,512]{1,0:T(8,128)(2,1)} %get-tuple-element.73), channel_id=1, source_target_pairs={{0,4},{4,0},{8,12},{12,8},{1,5},{5,1},{9,13},{13,9},{2,6},{6,2},{1... | collective-permute-start | bytes 786440 | tf_op jit(solution)/shard_map/ppermute | solution.py:50
  55.2 11.5 %collective-permute-start.8 = (f32[256,256]{1,0:T(8,128)}, f32[256,256]{1,0:T(8,128)}, u32[]{:S(2)}, u32[]{:S(2)}) collective-permute-start(f32[256,256]{1,0:T(8,128)} %shard_map.95), channel_id=1, source_target_pairs={{0,1},{1,0},{2,3},{3,2},{4,5},{5,4},{6,7},{7,6},{8,9},{9,8},{10,11... | collective-permute-start | bytes 786440 | tf_op jit(solution)/shard_map/ppermute | solution.py:50
  58.9 12.1 %collective-permute-start.10 = (f32[256,256]{1,0:T(8,128)}, f32[256,256]{1,0:T(8,128)}, u32[]{:S(2)}, u32[]{:S(2)}) collective-permute-start(f32[256,256]{1,0:T(8,128)} %shard_map.96), channel_id=1, source_target_pairs={{0,2},{1,3},{2,0},{3,1},{4,6},{5,7},{6,4},{7,5},{8,10},{9,11},{10,... | collective-permute-start | bytes 786440 | tf_op jit(solution)/shard_map/ppermute | solution.py:50
  61.6 9.4 %collective-permute-start.12 = (f32[256,256]{1,0:T(8,128)}, f32[256,256]{1,0:T(8,128)}, u32[]{:S(2)}, u32[]{:S(2)}) collective-permute-start(f32[256,256]{1,0:T(8,128)} %shard_map.97), channel_id=1, source_target_pairs={{0,3},{1,2},{2,1},{3,0},{4,7},{5,6},{6,5},{7,4},{8,11},{9,10},{10,... | collective-permute-start | bytes 786440 | tf_op jit(solution)/shard_map/ppermute | solution.py:50
  72.6 76.8 %all-gather.7.cloned.1.call-start = ((), (), s32[]{:S(2)}) async-start(), calls=%async_computation.1 | async-start | bytes 2621440 | tf_op jit(solution)/shard_map/all_gather | solution.py:527
  72.7 24.3 %collective-permute-start = (bf16[512,256]{1,0:T(8,128)(2,1)S(1)}, bf16[512,256]{1,0:T(8,128)(2,1)S(1)}, u32[]{:S(2)}, u32[]{:S(2)}) collective-permute-start(bf16[512,256]{1,0:T(8,128)(2,1)S(1)} %bitcast.57), channel_id=1, source_target_pairs={{0,4},{4,8},{8,12},{1,5},{5,9},{9,13},{2,6},{6,10},{10,14},{3,7},{... | collective-permute-start | bytes 786440 | tf_op jit(solution)/shard_map/ppermute | solution.py:36
  77.8 12.6 %collective-permute-start.14 = (bf16[2,64,256]{2,1,0:T(8,128)(2,1)S(1)}, bf16[2,64,256]{2,1,0:T(8,128)(2,1)S(1)}, u32[]{:S(2)}, u32[]{:S(2)}) collective-permute-start(bf16[2,64,256]{2,1,0:T(8,128)(2,1)S(1)} %get-tuple-element.46), channel_id=1, source_target_pairs={{0,8},{4,12},{8,0},{12,4},{1,9},{5,13},{9,1},{13,5},{2,10},{6,14},... | collective-permute-start | bytes 196616 | tf_op jit(solution)/shard_map/ppermute | solution.py:50
  77.8 12.6 %collective-permute-start.15 = (bf16[2,64,256]{2,1,0:T(8,128)(2,1)S(1)}, bf16[2,64,256]{2,1,0:T(8,128)(2,1)S(1)}, u32[]{:S(2)}, u32[]{:S(2)}) collective-permute-start(bf16[2,64,256]{2,1,0:T(8,128)(2,1)S(1)} %get-tuple-element.47), channel_id=1, source_target_pairs={{0,12},{4,8},{8,4},{12,0},{1,13},{5,9},{9,5},{13,1},{2,14},{6,10},... | collective-permute-start | bytes 196616 | tf_op jit(solution)/shard_map/ppermute | solution.py:50
  80.7 30.9 %collective-permute-start.16 = (bf16[256,512]{1,0:T(8,128)(2,1)}, bf16[256,512]{1,0:T(8,128)(2,1)S(1)}, u32[]{:S(2)}, u32[]{:S(2)}) collective-permute-start(bf16[256,512]{1,0:T(8,128)(2,1)} %get-tuple-element.54), channel_id=1, source_target_pairs={{0,8},{4,12},{8,0},{12,4},{1,9},{5,13},{9,1},{13,5},{2,10},{6,14},... | collective-permute-start | bytes 786440 | tf_op jit(solution)/shard_map/ppermute | solution.py:50
  90.4 21.2 %collective-permute-start.17 = (bf16[256,512]{1,0:T(8,128)(2,1)}, bf16[256,512]{1,0:T(8,128)(2,1)S(1)}, u32[]{:S(2)}, u32[]{:S(2)}) collective-permute-start(bf16[256,512]{1,0:T(8,128)(2,1)} %get-tuple-element.55), channel_id=1, source_target_pairs={{0,12},{4,8},{8,4},{12,0},{1,13},{5,9},{9,5},{13,1},{2,14},{6,10},... | collective-permute-start | bytes 786440 | tf_op jit(solution)/shard_map/ppermute | solution.py:50
  112.4 6.9 %collective-permute-start.18 = (bf16[256,256]{1,0:T(8,128)(2,1)S(1)}, bf16[256,256]{1,0:T(8,128)(2,1)S(1)}, u32[]{:S(2)}, u32[]{:S(2)}) collective-permute-start(bf16[256,256]{1,0:T(8,128)(2,1)S(1)} %get-tuple-element.57), channel_id=1, source_target_pairs={{4,0},{8,4},{12,8},{5,1},{9,5},{13,9},{6,2},{10,6},{14,10},{7,3},{... | collective-permute-start | bytes 393224 | tf_op jit(solution)/shard_map/ppermute | solution.py:36
  121.6 7.2 %collective-permute-start.21 = (bf16[256,256]{1,0:T(8,128)(2,1)S(1)}, bf16[256,256]{1,0:T(8,128)(2,1)S(1)}, u32[]{:S(2)}, u32[]{:S(2)}) collective-permute-start(bf16[256,256]{1,0:T(8,128)(2,1)S(1)} %add_convert_fusion.refs_0_), channel_id=1, source_target_pairs={{0,12},{4,8},{8,4},{12,0},{1,13},{5,9},{9,5},{13,1},{2,14},{6,10},... | collective-permute-start | bytes 393224 | tf_op jit(solution)/shard_map/ppermute | solution.py:50
  131.5 7.8 %collective-permute-start.23 = (bf16[256,256]{1,0:T(8,128)(2,1)S(1)}, bf16[256,256]{1,0:T(8,128)(2,1)S(1)}, u32[]{:S(2)}, u32[]{:S(2)}) collective-permute-start(bf16[256,256]{1,0:T(8,128)(2,1)S(1)} %get-tuple-element.60.refs_0_), channel_id=1, source_target_pairs={{0,2},{1,3},{2,0},{3,1},{4,6},{5,7},{6,4},{7,5},{8,10},{9,11},{10,... | collective-permute-start | bytes 393224 | tf_op jit(solution)/shard_map/ppermute | solution.py:50
  132.8 8.5 %collective-permute-start.24 = (bf16[256,256]{1,0:T(8,128)(2,1)S(1)}, bf16[256,256]{1,0:T(8,128)(2,1)S(1)}, u32[]{:S(2)}, u32[]{:S(2)}) collective-permute-start(bf16[256,256]{1,0:T(8,128)(2,1)S(1)} %get-tuple-element.60.refs_0_), channel_id=1, source_target_pairs={{0,3},{1,2},{2,1},{3,0},{4,7},{5,6},{6,5},{7,4},{8,11},{9,10},{10,... | collective-permute-start | bytes 393224 | tf_op jit(solution)/shard_map/ppermute | solution.py:50
  (18 other events, 85.6 us)
Sparse Core Ops, SparseCore 0:
  72.7 33.8 all-gather.4
  112.6 36.7 all-gather.6

commit v5 on v4

--- a/solution.py
+++ b/solution.py
@@ -54,36 +54,42 @@
     return pl.ds(pl.multiple_of(start * IMGTOK, IMGTOK), IMGTOK)
 
 
-def project_body(d_ref, s_ref, near_ref, far_ref, out_ref):
-    half = near_ref.shape[0]
-    d = d_ref[0]
-    near = s_ref[:, pl.ds(pl.multiple_of(d * half, half), half)]
-    far = s_ref[:, pl.ds(pl.multiple_of((1 - d) * half, half), half)]
-    out_ref[...] = dot(near, near_ref[...], NN) + dot(far, far_ref[...], NN)
-
-
-def project(d, states, near, far):
-    half, width = near.shape
-    rows = states.shape[0]
-    vmem = pl.BlockSpec(memory_space=pltpu.VMEM)
+def project_body(m_ref, *refs):
+    *pairs, out_ref = refs
+    count = len(pairs) // 2
+    total = dot(pairs[0][...], pairs[count][...], NN)
+    for k in range(1, count):
+        total = total + dot(pairs[k][...], pairs[count + k][...], NN)
+    out_ref[...] = total
+
+
+def project(m, blocks, weights):
+    rows, feats = blocks[0].shape
+    width = weights.shape[1]
+    block = pl.BlockSpec((rows, feats), lambda i, m: (0, 0))
+    chunk = lambda k: pl.BlockSpec((feats, width), lambda i, m: (m[0] ^ k, 0))
     return pl.pallas_call(
         project_body,
-        in_specs=[pl.BlockSpec(memory_space=pltpu.SMEM), vmem, vmem, vmem],
-        out_specs=vmem,
+        grid_spec=pltpu.PrefetchScalarGridSpec(
+            num_scalar_prefetch=1,
+            grid=(1,),
+            in_specs=[block] * len(blocks) + [chunk(k) for k in range(len(blocks))],
+            out_specs=pl.BlockSpec((rows, width), lambda i, m: (0, 0)),
+        ),
         out_shape=jax.ShapeDtypeStruct((rows, width), jnp.float32),
-        cost_estimate=cost(4 * rows * half * width, 4 * states.size),
-        compiler_params=params(),
-    )(d, states, near, far)
-
-
-def pack_body(per_shard, terms, c_ref, place_ref, *refs):
-    part_refs, out_refs = refs[:terms], refs[terms:-3]
+        cost_estimate=cost(2 * len(blocks) * rows * feats * width, 4 * len(blocks) * feats * width),
+        compiler_params=params(),
+    )(m, *blocks, *[weights] * len(blocks))
+
+
+def pack_body(per_shard, m_ref, c_ref, place_ref, low_ref, high_ref, weight_ref, part_ref, *refs):
+    out_refs = refs[:-3]
     rounded, sorted_ref, count = refs[-3:]
     shards = sorted_ref.shape[0]
-    total = part_refs[0][...]
-    for ref in part_refs[1:]:
-        total = total + ref[...]
-    rounded[...] = total.astype(jnp.bfloat16)
+    half = low_ref.shape[0]
+    for at, ref in ((0, low_ref), (half, high_ref)):
+        term = dot(ref[...], weight_ref[...], NN)
+        rounded[at : at + half, :] = (part_ref[at : at + half, :] + term).astype(jnp.bfloat16)
     sorted_ref[...] = jnp.zeros_like(sorted_ref)
     for s in range(shards):
         count[s] = 0
@@ -111,28 +117,74 @@
             ref[...] = sorted_ref[c ^ u]
 
 
-def pack(c, place, parts, shards, capacity, per_shard, mixed):
-    rows, width = parts[0].shape
-    smem = pl.BlockSpec(memory_space=pltpu.SMEM)
-    vmem = pl.BlockSpec(memory_space=pltpu.VMEM)
+def pack(m, c, place, low, high, weights, part, shards, capacity, per_shard, mixed):
+    rows, width = part.shape
+    feats = low.shape[1]
+    whole = lambda a: pl.BlockSpec(a.shape, lambda i, *_: (0,) * len(a.shape))
     shape = (2, capacity, width)
     if mixed:
         out = [jax.ShapeDtypeStruct(shape, jnp.bfloat16)] * shards
     else:
         out = [jax.ShapeDtypeStruct((shards,) + shape, jnp.bfloat16)]
     return pl.pallas_call(
-        functools.partial(pack_body, per_shard, len(parts)),
-        in_specs=[smem, smem] + [vmem] * len(parts),
+        functools.partial(pack_body, per_shard),
+        grid_spec=pltpu.PrefetchScalarGridSpec(
+            num_scalar_prefetch=3,
+            grid=(1,),
+            in_specs=[
+                whole(low),
+                whole(high),
+                pl.BlockSpec((feats, width), lambda i, m, *_: (m[0] ^ 3, 0)),
+                whole(part),
+            ],
+            out_specs=[whole(a) for a in out],
+            scratch_shapes=[
+                pltpu.VMEM((rows, width), jnp.bfloat16),
+                pltpu.VMEM((shards,) + shape, jnp.bfloat16),
+                pltpu.SMEM((shards,), jnp.int32),
+            ],
+        ),
+        out_shape=out,
+        cost_estimate=cost(2 * rows * feats * width, part.size * 16),
+        compiler_params=params(),
+    )(m, c, place, low, high, weights, part)
+
+
+def slices_body(m_ref, c_ref, own_ref, x_ref, y_ref, low_ref, high_ref, kept_ref, *out_refs):
+    m = m_ref[0]
+    c = c_ref[0]
+    sub = out_refs[0].shape[1]
+    half = low_ref.shape[0]
+    for u, ref in enumerate((kept_ref,) + out_refs):
+        at = pl.ds(0, ref.shape[1]) if u == 0 else pl.ds(pl.multiple_of(m * sub, sub), sub)
+        which = m ^ c ^ u
+        for k, source in enumerate((own_ref, x_ref, y_ref)):
+
+            @pl.when(which == k)
+            def _():
+                ref[...] = source[:, at]
+
+        @pl.when(which == 3)
+        def _():
+            ref[:half, :] = low_ref[:, at]
+            ref[half:, :] = high_ref[:, at]
+
+
+def slices(m, c, blocks, sub):
+    rows, feats = blocks[0].shape
+    smem = pl.BlockSpec(memory_space=pltpu.SMEM)
+    vmem = pl.BlockSpec(memory_space=pltpu.VMEM)
+    dtype = blocks[0].dtype
+    out = [jax.ShapeDtypeStruct((rows, feats), dtype)]
+    out += [jax.ShapeDtypeStruct((rows, sub), dtype)] * 3
+    return pl.pallas_call(
+        slices_body,
+        in_specs=[smem, smem] + [vmem] * len(blocks),
         out_specs=[vmem] * len(out),
         out_shape=out,
-        scratch_shapes=[
-            pltpu.VMEM((rows, width), jnp.bfloat16),
-            pltpu.VMEM((shards,) + shape, jnp.bfloat16),
-            pltpu.SMEM((shards,), jnp.int32),
-        ],
-        cost_estimate=cost(0, parts[0].size * 4 * 6),
-        compiler_params=params(),
-    )(c, place, *parts)
+        cost_estimate=cost(0, rows * feats * 16),
+        compiler_params=params(),
+    )(m, c, *blocks)
 
 
 def attention_body(
@@ -368,40 +420,35 @@
     *state_refs, g_ref, out_ref = refs
     ranks, rows, width = g_ref.shape
     c = c_ref[0]
-    total = None
-    done = 0
-    for ref in state_refs:
-        count = ref.shape[1] // rows
-        if mixed:
-            grad = [g_ref[c ^ s] for s in range(done, done + count)]
-            grad = jnp.concatenate(grad, axis=0)
-        else:
-            grad = g_ref[...].reshape(ranks * rows, width)
-        done += count
-        term = dot(ref[0], grad, TN)
-        total = term if total is None else total + term
-    out_ref[...] = total
-
-
-def weight_term(c, states, grad, mixed):
-    parts, _, cols = states[0].shape
-    width = grad.shape[2]
-    size = sum(a.size for a in states)
-    return pl.pallas_call(
-        functools.partial(weight_body, mixed),
+    if mixed:
+        total = dot(state_refs[0][...], g_ref[c], TN)
+        grad = jnp.concatenate([g_ref[c ^ s] for s in range(1, ranks)], axis=0)
+        out_ref[...] = total + dot(state_refs[1][0], grad, TN)
+    else:
+        grad = g_ref[...].reshape(ranks * rows, width)
+        out_ref[...] = dot(state_refs[0][0], grad, TN)
+
+
+def weight_term(c, kept, states, grad):
+    parts, count, cols = states.shape
+    _, rows, width = grad.shape
+    specs = [pl.BlockSpec((1, count, cols), lambda k, c: (k, 0, 0))]
+    arrays = [states]
+    if kept is not None:
+        specs.insert(0, pl.BlockSpec((rows, cols), lambda k, c: (0, k)))
+        arrays.insert(0, kept)
+    return pl.pallas_call(
+        functools.partial(weight_body, kept is not None),
         grid_spec=pltpu.PrefetchScalarGridSpec(
             num_scalar_prefetch=1,
             grid=(parts,),
-            in_specs=[
-                *[pl.BlockSpec((1,) + a.shape[1:], lambda k, c: (k, 0, 0)) for a in states],
-                pl.BlockSpec(grad.shape, lambda k, c: (0, 0, 0)),
-            ],
+            in_specs=specs + [pl.BlockSpec(grad.shape, lambda k, c: (0, 0, 0))],
             out_specs=pl.BlockSpec((cols, width), lambda k, c: (k, 0)),
         ),
         out_shape=jax.ShapeDtypeStruct((parts * cols, width), jnp.float32),
-        cost_estimate=cost(2 * size * width, size * 4),
-        compiler_params=params(),
-    )(c, *states, grad)
+        cost_estimate=cost(2 * states.size * width, states.size * 4),
+        compiler_params=params(),
+    )(c, *arrays, grad)
 
 
 def image_body(d_ref, *refs):
@@ -459,18 +506,15 @@
     place = place_index[0, ::IMGTOK] // IMGTOK
 
     m = lax.axis_index("mp")
+    m1 = jnp.reshape(m, (1,)).astype(jnp.int32)
     steps = range(1, mps)
     mixed = ranks == mps
 
-    half = feats // 2
-
-    def slab(source, head, side):
-        return lax.dynamic_slice_in_dim(source, head * feats + side * half, half)
-
-    slabs = [slab(weights, m ^ s, d) for s in steps]
-    *slabs, states_late = lax.optimization_barrier((*slabs, states))
-    near = [trade(w, "mp", s) for w, s in zip(slabs, steps)]
-    far = [swap(w, "dp") for w in near]
+    x = trade(states, "mp", 1)
+    y = trade(states, "mp", 2)
+    low = trade(x[: image_rows // 2], "mp", 2)
+    high = trade(y[image_rows // 2 :], "mp", 1)
+    part = project(m1, [states, x, y], weights)
 
     prior_text = shift(text_kv[0], "ctx", 1)
     docs = doc_ids[0]
@@ -479,63 +523,61 @@
     prior_docs = jnp.where(c > 0, prior_docs, -1)
     key_docs = jnp.concatenate([prior_docs, own_docs])
     start = jnp.sum((key_docs[:, None] < own_docs[None, :]).astype(jnp.int32), axis=0)[None]
-
-    sub = feats // (ranks // mps) // mps
+    low, high, prior_text, start, place = lax.optimization_barrier(
+        (low, high, prior_text, start, place)
+    )
+    packed = pack(
+        m1, c1, place, low, high, weights, part, ranks, capacity, per_shard, mixed
+    )
+
     if mixed:
-        source = states_late
-        pieces = [lax.dynamic_slice_in_dim(source, m * sub, sub, axis=1)]
-        for s in steps:
-            piece = lax.dynamic_slice_in_dim(source, (m ^ s) * sub, sub, axis=1)
-            pieces.append(trade(piece, "mp", s))
-        *near, pieces = lax.optimization_barrier((*near, jnp.stack(pieces)))
-        moved = [
-            lax.dynamic_index_in_dim(pieces, m ^ c ^ s, keepdims=False) for s in range(ranks)
-        ]
+        kept, *moved = slices(m1, c1, [states, x, y, low, high], feats // mps)
+        moved[1], moved[2], _ = lax.optimization_barrier((moved[1], moved[2], packed[0]))
+        far_slices = [trade(moved[1], "ctx", 2), trade(moved[2], "ctx", 3)]
+        image = [trade(packed[s], "ctx", s) if s else packed[0] for s in range(ranks)]
+        moved[0], weights_late, *image = lax.optimization_barrier((moved[0], weights, *image))
+        moved = [trade(moved[0], "ctx", 1)] + far_slices
     else:
-        pieces = states.reshape(image_rows, ranks // mps, mps, sub).transpose(2, 0, 1, 3)
-        pieces = exchange(pieces, "mp")
-        pieces = pieces.transpose(0, 2, 1, 3).reshape(ranks, image_rows, sub)
-        moved = [exchange(pieces, "ctx").reshape(ranks * image_rows, sub)]
-
-    weights_late, _ = lax.optimization_barrier((weights, near[-1]))
-    near = [slab(weights_late, m, d)] + near
-    far = [slab(weights_late, m, 1 - d)] + far
-    parts = [project(d1, states, near[s], far[s]) for s in range(mps)]
-    parts = [trade(parts[s], "mp", s) if s else parts[0] for s in range(mps)]
-    packed = pack(c1, place, parts, ranks, capacity, per_shard, mixed)
-    cut = ranks // 2
-    if mixed:
-        for s in range(1, cut):
-            moved[s] = trade(moved[s], "ctx", s)
-        moved[cut], _ = lax.optimization_barrier((moved[cut], packed[0]))
-        moved[cut] = trade(moved[cut], "ctx", cut)
-        image = [trade(packed[s], "ctx", s) if s else packed[0] for s in range(ranks)]
-        for s in range(cut + 1, ranks):
-            moved[s], *image = lax.optimization_barrier((moved[s], *image))
-            moved[s] = trade(moved[s], "ctx", s)
-        moved = [jnp.concatenate(moved[:cut], axis=0), jnp.concatenate(moved[cut:], axis=0)]
-    else:
+        kept = None
         image = [exchange(packed[0], "ctx")]
-    moved[0], _ = lax.optimization_barrier((moved[0], packed[0]))
-    all_states = [lax.all_gather(moved[0], "mp", axis=0)]
+        whole = lax.all_gather(states, "mp", axis=1, tiled=True)
+        moved = whole.reshape(image_rows, ranks, mps, -1)
+        moved = lax.dynamic_index_in_dim(moved, m, axis=2, keepdims=False).transpose(1, 0, 2)
+        moved = [exchange(moved, "ctx").reshape(ranks * image_rows, -1)]
+        weights_late, *image = lax.optimization_barrier((weights, *image))
+
+    half = feats // 2
+
+    def slab(head, side):
+        return lax.dynamic_slice_in_dim(weights_late, head * feats + side * half, half)
+
+    near = [trade(slab(m ^ s, d), "mp", s) for s in steps]
+
     attn_out, own_grad, prior_grad = attention(
         c1, place, start, queries[0], d_out[0], text_kv[0], prior_text, image,
         images, per_shard, image_rows,
     )
-    if mixed:
-        moved[1], prior_grad = lax.optimization_barrier((moved[1], prior_grad))
-        all_states.append(lax.all_gather(moved[1], "mp", axis=0))
+    prior_grad, near[0], near[-1], *moved = lax.optimization_barrier(
+        (prior_grad, near[0], near[-1], *moved)
+    )
+    all_states = lax.all_gather(jnp.concatenate(moved, axis=0), "mp", axis=0)
     grad = own_grad + shift(prior_grad, "ctx", -1).astype(jnp.float32)
     grad = grad.astype(jnp.bfloat16)
     if mixed:
         gathered = [trade(grad, "ctx", s) if s else grad for s in range(ranks)]
     else:
         gathered = [exchange(jnp.broadcast_to(grad, (ranks,) + grad.shape), "ctx")]
+    count = len(gathered)
+    both = lax.optimization_barrier((*gathered, *near))
+    gathered, near = both[:count], list(both[count:])
+    far = [slab(m, 1 - d)] + [swap(w, "dp") for w in near]
+    near = [slab(m, d)] + near
     by_rank, mine = reorder(c1, place, gathered, per_shard, images, ranks)
     head_grad = [mine] + [trade(mine, "mp", s) for s in steps]
-    by_rank, *head_grad = lax.optimization_barrier((by_rank, *head_grad))
+    by_rank, *both = lax.optimization_barrier((by_rank, *head_grad, *far))
+    head_grad, far = both[:mps], both[mps:]
     image_grad = image_term(d1, head_grad, near, far)
-    term = weight_term(c1, all_states, by_rank.reshape(ranks, image_rows, width), mixed)
+    term = weight_term(c1, kept, all_states, by_rank.reshape(ranks, image_rows, width))
     weight_grad = term + swap(term, "dp")
     return (attn_out[None], image_grad[None], weight_grad[None])
 

time: 168 us -> 157 us (0.935)
  Pallas kernels: 27.8 us -> 20.9 us
  local copies, waits for them, and re-layouts: 12.3 us -> 19.1 us
  starting transfers between devices: 39.6 us -> 33.5 us
  waiting for transfers between devices: 67.7 us -> 64.5 us
  other arithmetic: 5.83 us -> 3.62 us
    unnamed x26 -> x68, local copies, waits for them, and re-layouts: 5.67 us -> 15.2 us
    ppermute x21 -> x19, starting transfers between devices: 35.1 us -> 28.2 us  [trade(): return lax.ppermute(block, axis, [(i, i ^ step) for i in range(count)])]
    all_gather x2 -> x1, waiting for transfers between devices: 8.11 us -> 2.84 us  [per_device(): all_states = lax.all_gather(jnp.concatenate(moved, axis=0), 'mp', axis=0)]
    ppermute x2, waiting for transfers between devices: 5.56 us -> 9.11 us  [shift(): return lax.ppermute(block, axis, route)]
    pallas_call x6 -> x4, Pallas kernels: 9.53 us -> 6.18 us  [the longest x1 2.11 us: weight_term(): pl.pallas_call(functools.partial(weight_body, kept is not None), grid_spe...]
    ppermute x21 -> x19, waiting for transfers between devices: 54 us -> 51.4 us  [trade(): return lax.ppermute(block, axis, [(i, i ^ step) for i in range(count)])]
    pallas_call x1, Pallas kernels: 12.2 us -> 10.1 us  [attention(): pl.pallas_call(functools.partial(attention_body, per_shard, images), grid...]
    concatenate x2 -> x1, other arithmetic: 2.66 us -> 0.93 us  [per_device(): all_states = lax.all_gather(jnp.concatenate(moved, axis=0), 'mp', axis=0)]
  transfers between devices with their start and end apart: 29 -> 26, of which waited for: 13 -> 13; matrix products, arithmetic and copies ran while one was open for 5% -> 3% of each run, Pallas kernels for 14% -> 11%
where the time goes in v5:
time: 157 us; the launch traced here: 156 us
  waiting for transfers between devices  64.5 us (41%)
  starting transfers between devices  33.5 us (21%)
  Pallas kernels  20.9 us (13%)
  local copies, waits for them, and re-layouts  19.1 us (12%)
  between operations  14.4 us (9%)
  other arithmetic  3.62 us (2%)
    ppermute x19, waiting for transfers between devices, trade(): return lax.ppermute(block, axis, [(i, i ^ step) for i in range(count)])  51.4 us
    ppermute x19, starting transfers between devices, trade(): return lax.ppermute(block, axis, [(i, i ^ step) for i in range(count)])  28.2 us
    unnamed x68, local copies, waits for them, and re-layouts  15.2 us
    pallas_call x1, Pallas kernels, attention(): pl.pallas_call(functools.partial(attention_body, per_shard, images), grid...  10.1 us
    ppermute x2, waiting for transfers between devices, shift(): return lax.ppermute(block, axis, route)  9.11 us
    ppermute x2, starting transfers between devices, shift(): return lax.ppermute(block, axis, route)  4.77 us
  transfers between devices with their start and end apart: 26, of which 13 were waited for; matrix products, arithmetic and copies ran while one was open for 3% of the time, Pallas kernels for 11%

profile of v5, /device:TPU:0, one launch (start us, length us, event | category | flops | bytes accessed | tf_op | source)
XLA Modules:
  0.0 156.0 jit_solution(16354997083995822399)
XLA Ops:
  7.2 3.0 %collective-permute-start.2 = (bf16[256,2048]{1,0:T(8,128)(2,1)}, bf16[256,2048]{1,0:T(8,128)(2,1)S(1)}, u32[]{:S(2)}, u32[]{:S(2)}) collective-permute-start(bf16[256,2048]{1,0:T(8,128)(2,1)} %bitcast.31), channel_id=1, source_target_pairs={{0,2},{1,3},{2,0},{3,1},{4,6},{5,7},{6,4},{7,5},{8,10},{9,11},{10,... | collective-permute-start | bytes 3145736 | tf_op jit(solution)/shard_map/ppermute | solution.py:50
  11.7 3.5 %collective-permute-start.4 = (bf16[512,256]{1,0:T(8,128)(2,1)}, bf16[512,256]{1,0:T(8,128)(2,1)S(1)}, u32[]{:S(2)}, u32[]{:S(2)}) collective-permute-start(bf16[512,256]{1,0:T(8,128)(2,1)} %bitcast.41), channel_id=1, source_target_pairs={{0,4},{4,8},{8,12},{1,5},{5,9},{9,13},{2,6},{6,10},{10,14},{3,7},{... | collective-permute-start | bytes 786440 | tf_op jit(solution)/shard_map/ppermute | solution.py:36
  16.9 16.8 %collective-permute-done.2.y_ref.refs_2_ = bf16[256,2048]{1,0:T(8,128)(2,1)S(1)} collective-permute-done((bf16[256,2048]{1,0:T(8,128)(2,1)}, bf16[256,2048]{1,0:T(8,128)(2,1)S(1)}, u32[]{:S(2)}, u32[]{:S(2)}) %collective-permute-start.2) | collective-permute-done | bytes 1048608 | tf_op jit(solution)/shard_map/ppermute | solution.py:50
  33.7 1.8 %collective-permute-start.3 = (bf16[128,2048]{1,0:T(8,128)(2,1)S(1)}, bf16[128,2048]{1,0:T(8,128)(2,1)S(1)}, u32[]{:S(2)}, u32[]{:S(2)}) collective-permute-start(bf16[128,2048]{1,0:T(8,128)(2,1)S(1)} %slice.17), channel_id=1, source_target_pairs={{0,1},{1,0},{2,3},{3,2},{4,5},{5,4},{6,7},{7,6},{8,9},{9,8},{10,11... | collective-permute-start | bytes 1572872 | tf_op jit(solution)/shard_map/ppermute | solution.py:50
  37.4 2.2 %copy-done = bf16[1,8192,256]{2,1,0:T(8,128)(2,1)S(1)} copy-done((bf16[1,8192,256]{2,1,0:T(8,128)(2,1)S(1)}, bf16[1,8192,256]{2,1,0:T(8,128)(2,1)}, u32[]{:S(2)}) %copy-start) | copy-done | bytes 4194328
  40.6 6.2 %collective-permute-done.3.high_ref = bf16[128,2048]{1,0:T(8,128)(2,1)S(1)} collective-permute-done((bf16[128,2048]{1,0:T(8,128)(2,1)S(1)}, bf16[128,2048]{1,0:T(8,128)(2,1)S(1)}, u32[]{:S(2)}, u32[]{:S(2)}) %collective-permute-start.3) | collective-permute-done | bytes 524320 | tf_op jit(solution)/shard_map/ppermute | solution.py:50
  48.1 2.0 %shard_map.96 = (bf16[2,64,256]{2,1,0:T(8,128)(2,1)S(1)}, bf16[2,64,256]{2,1,0:T(8,128)(2,1)}, bf16[2,64,256]{2,1,0:T(8,128)(2,1)S(1)}, bf16[2,64,256]{2,1,0:T(8,128)(2,1)S(1)}) custom-call(s32[1]{0:T(128)} %bitcast.10.m_ref, s32[1]{0:T(128)} %bitcast.c_ref, s32[64]{0:T(128)S(1)} %and_select_fusion.place_ref, ...), custom_call_target="tpu_custom_call" | custom-call | flops 268435456 | bytes 1048576 | tf_op jit(solution)/shard_map/pallas_call | solution.py:129
  52.3 2.6 %collective-permute-start.6 = (bf16[2,64,256]{2,1,0:T(8,128)(2,1)S(1)}, bf16[2,64,256]{2,1,0:T(8,128)(2,1)S(1)}, u32[]{:S(2)}, u32[]{:S(2)}) collective-permute-start(bf16[2,64,256]{2,1,0:T(8,128)(2,1)S(1)} %get-tuple-element.59), channel_id=1, source_target_pairs={{0,8},{4,12},{8,0},{12,4},{1,9},{5,13},{9,1},{13,5},{2,10},{6,14},... | collective-permute-start | bytes 196616 | tf_op jit(solution)/shard_map/ppermute | solution.py:50
  59.3 1.7 %collective-permute-start.11 = (bf16[256,512]{1,0:T(8,128)(2,1)}, bf16[256,512]{1,0:T(8,128)(2,1)S(1)}, u32[]{:S(2)}, u32[]{:S(2)}) collective-permute-start(bf16[256,512]{1,0:T(8,128)(2,1)} %get-tuple-element.72), channel_id=1, source_target_pairs={{0,8},{4,12},{8,0},{12,4},{1,9},{5,13},{9,1},{13,5},{2,10},{6,14},... | collective-permute-start | bytes 786440 | tf_op jit(solution)/shard_map/ppermute | solution.py:50
  61.0 2.0 %collective-permute-start.12 = (bf16[256,512]{1,0:T(8,128)(2,1)}, bf16[256,512]{1,0:T(8,128)(2,1)S(1)}, u32[]{:S(2)}, u32[]{:S(2)}) collective-permute-start(bf16[256,512]{1,0:T(8,128)(2,1)} %get-tuple-element.73), channel_id=1, source_target_pairs={{0,12},{4,8},{8,4},{12,0},{1,13},{5,9},{9,5},{13,1},{2,14},{6,10},... | collective-permute-start | bytes 786440 | tf_op jit(solution)/shard_map/ppermute | solution.py:50
  63.6 2.9 %constant_dynamic-slice_fusion = (bf16[1024,256]{1,0:T(8,128)(2,1)S(1)}, bf16[1024,256]{1,0:T(8,128)(2,1)S(1)}, bf16[1024,256]{1,0:T(8,128)(2,1)}, bf16[1024,256]{1,0:T(8,128)(2,1)S(1)}, bf16[1024,256]{1,0:T(8,128)(2,1)S(1)}) fusion(bf16[8192,256]{1,0:T(8,128)(2,1)} %bitcast.26, s32[]{:T(128)S(6)} %select_n.47, s32[]{:T(128)S(6)} %select_n.46, ...), kind=kLoop, calls=%fused_computation.7 | loop fusion | bytes 5242900 | tf_op jit(solution)/shard_map/dynamic_slice | solution.py:552
  72.1 10.1 %shard_map.97 = (bf16[512,1024]{1,0:T(8,128)(2,1)}, f32[256,256]{1,0:T(8,128)S(1)}, bf16[256,256]{1,0:T(8,128)(2,1)S(1)}) custom-call(s32[1]{0:T(128)} %bitcast.c_ref, s32[64]{0:T(128)S(1)} %and_select_fusion.place_ref, s32[4]{0:T(128)S(1)} %bitcast.43, s32[1,512]{1,0:T(1,128)S(1)} %bitcast.38, bf16[512,1024]{1,0:T(8,128)(2,1)S(1)} %bitcast.39, ...), custom_call_target="tpu_custom_call" | custom-call | flops 13421772800 | bytes 4194304 | tf_op jit(solution)/shard_map/pallas_call | solution.py:344
  82.3 6.6 %collective-permute-done.8.refs_5_ = bf16[1024,256]{1,0:T(8,128)(2,1)S(1)} collective-permute-done((bf16[1024,256]{1,0:T(8,128)(2,1)S(1)}, bf16[1024,256]{1,0:T(8,128)(2,1)S(1)}, u32[]{:S(2)}, u32[]{:S(2)}) %collective-permute-start.8) | collective-permute-done | bytes 524320 | tf_op jit(solution)/shard_map/ppermute | solution.py:50
  91.8 9.1 %collective-permute-done.13 = bf16[256,256]{1,0:T(8,128)(2,1)S(1)} collective-permute-done((bf16[256,256]{1,0:T(8,128)(2,1)S(1)}, bf16[256,256]{1,0:T(8,128)(2,1)S(1)}, u32[]{:S(2)}, u32[]{:S(2)}) %collective-permute-start.13) | collective-permute-done | bytes 131104 | tf_op jit(solution)/shard_map/ppermute | solution.py:36
  101.0 2.7 %collective-permute-start.15 = (bf16[256,256]{1,0:T(8,128)(2,1)S(1)}, bf16[256,256]{1,0:T(8,128)(2,1)S(1)}, u32[]{:S(2)}, u32[]{:S(2)}) collective-permute-start(bf16[256,256]{1,0:T(8,128)(2,1)S(1)} %add_convert_fusion.refs_0_), channel_id=1, source_target_pairs={{0,8},{4,12},{8,0},{12,4},{1,9},{5,13},{9,1},{13,5},{2,10},{6,14},... | collective-permute-start | bytes 393224 | tf_op jit(solution)/shard_map/ppermute | solution.py:50
  105.4 2.5 %collective-permute-done.16.refs_3_ = bf16[256,256]{1,0:T(8,128)(2,1)S(1)} collective-permute-done((bf16[256,256]{1,0:T(8,128)(2,1)S(1)}, bf16[256,256]{1,0:T(8,128)(2,1)S(1)}, u32[]{:S(2)}, u32[]{:S(2)}) %collective-permute-start.16) | collective-permute-done | bytes 131104 | tf_op jit(solution)/shard_map/ppermute | solution.py:50
  107.9 3.0 %collective-permute-done.15.refs_2_ = bf16[256,256]{1,0:T(8,128)(2,1)S(1)} collective-permute-done((bf16[256,256]{1,0:T(8,128)(2,1)S(1)}, bf16[256,256]{1,0:T(8,128)(2,1)S(1)}, u32[]{:S(2)}, u32[]{:S(2)}) %collective-permute-start.15) | collective-permute-done | bytes 131104 | tf_op jit(solution)/shard_map/ppermute | solution.py:50
  116.4 7.3 %collective-permute-done.20.refs_3_ = bf16[256,256]{1,0:T(8,128)(2,1)S(1)} collective-permute-done((bf16[256,256]{1,0:T(8,128)(2,1)S(1)}, bf16[256,256]{1,0:T(8,128)(2,1)S(1)}, u32[]{:S(2)}, u32[]{:S(2)}) %collective-permute-start.20) | collective-permute-done | bytes 131104 | tf_op jit(solution)/shard_map/ppermute | solution.py:50
  124.8 1.9 %collective-permute-done.19.refs_2_ = bf16[256,256]{1,0:T(8,128)(2,1)S(1)} collective-permute-done((bf16[256,256]{1,0:T(8,128)(2,1)S(1)}, bf16[256,256]{1,0:T(8,128)(2,1)S(1)}, u32[]{:S(2)}, u32[]{:S(2)}) %collective-permute-start.19) | collective-permute-done | bytes 131104 | tf_op jit(solution)/shard_map/ppermute | solution.py:50
  126.7 5.7 %collective-permute-done.18.refs_1_ = bf16[256,256]{1,0:T(8,128)(2,1)S(1)} collective-permute-done((bf16[256,256]{1,0:T(8,128)(2,1)S(1)}, bf16[256,256]{1,0:T(8,128)(2,1)S(1)}, u32[]{:S(2)}, u32[]{:S(2)}) %collective-permute-start.18) | collective-permute-done | bytes 131104 | tf_op jit(solution)/shard_map/ppermute | solution.py:50
  135.5 2.8 %all-gather.3.cloned.1.call-done = bf16[3072,512]{1,0:T(8,128)(2,1)} async-done(((bf16[768,512]{1,0:T(8,128)(2,1)}), bf16[3072,512]{1,0:T(8,128)(2,1)}) %all-gather.3.cloned.1.call-update) | async-done | bytes 3145744 | tf_op jit(solution)/shard_map/all_gather | solution.py:563
  138.3 1.9 %copy-done.2 = bf16[3072,512]{1,0:T(8,128)(2,1)S(1)} copy-done((bf16[3072,512]{1,0:T(8,128)(2,1)S(1)}, bf16[3072,512]{1,0:T(8,128)(2,1)}, u32[]{:S(2)}) %copy-start.2) | copy-done | bytes 3145752
  141.2 2.1 %shard_map.100 = f32[2048,256]{1,0:T(8,128)S(1)} custom-call(s32[1]{0:T(128)} %bitcast.c_ref, bf16[256,2048]{1,0:T(8,128)(2,1)S(1)} %copy-done.8, bf16[4,768,512]{2,1,0:T(8,128)(2,1)S(1)} %bitcast.35, bf16[4,256,256]{2,1,0:T(8,128)(2,1)S(1)} %bitcast.36), custom_call_target="tpu_custom_call" | custom-call | flops 805306368 | bytes 6291456 | tf_op jit(solution)/shard_map/pallas_call | solution.py:440
  143.5 2.9 %shard_map.99 = bf16[256,2048]{1,0:T(8,128)(2,1)} custom-call(s32[1]{0:T(128)} %bitcast.13.d_ref, bf16[256,256]{1,0:T(8,128)(2,1)S(1)} %get-tuple-element.86.refs_0_, bf16[256,256]{1,0:T(8,128)(2,1)S(1)} %copy-done.20, bf16[256,256]{1,0:T(8,128)(2,1)S(1)} %collective-permute-done.19.refs_2_, bf16[256,256]{1,0:T(8,128)(2,1)S(1)} %collective-permute-done.20.refs_3_, ...), custom_call_target="tpu_custom_call" | custom-call | flops 1073741824 | bytes 8388608 | tf_op jit(solution)/shard_map/pallas_call | solution.py:477
  (116 shorter events, 38.3 us)
Async XLA Ops:
  7.2 131.1 %all-gather.3.cloned.1.call-start = ((), (), s32[]{:S(2)}) async-start(), calls=%async_computation | async-start | bytes 3932160 | tf_op jit(solution)/shard_map/all_gather | solution.py:563
  7.2 26.4 %collective-permute-start.2 = (bf16[256,2048]{1,0:T(8,128)(2,1)}, bf16[256,2048]{1,0:T(8,128)(2,1)S(1)}, u32[]{:S(2)}, u32[]{:S(2)}) collective-permute-start(bf16[256,2048]{1,0:T(8,128)(2,1)} %bitcast.31), channel_id=1, source_target_pairs={{0,2},{1,3},{2,0},{3,1},{4,6},{5,7},{6,4},{7,5},{8,10},{9,11},{10,... | collective-permute-start | bytes 3145736 | tf_op jit(solution)/shard_map/ppermute | solution.py:50
  10.3 25.2 %collective-permute-start = (bf16[256,2048]{1,0:T(8,128)(2,1)}, bf16[256,2048]{1,0:T(8,128)(2,1)S(1)}, u32[]{:S(2)}, u32[]{:S(2)}) collective-permute-start(bf16[256,2048]{1,0:T(8,128)(2,1)} %bitcast.32), channel_id=1, source_target_pairs={{0,1},{1,0},{2,3},{3,2},{4,5},{5,4},{6,7},{7,6},{8,9},{9,8},{10,11... | collective-permute-start | bytes 3145736 | tf_op jit(solution)/shard_map/ppermute | solution.py:50
  11.7 28.8 %collective-permute-start.4 = (bf16[512,256]{1,0:T(8,128)(2,1)}, bf16[512,256]{1,0:T(8,128)(2,1)S(1)}, u32[]{:S(2)}, u32[]{:S(2)}) collective-permute-start(bf16[512,256]{1,0:T(8,128)(2,1)} %bitcast.41), channel_id=1, source_target_pairs={{0,4},{4,8},{8,12},{1,5},{5,9},{9,13},{2,6},{6,10},{10,14},{3,7},{... | collective-permute-start | bytes 786440 | tf_op jit(solution)/shard_map/ppermute | solution.py:36
  33.7 13.2 %collective-permute-start.3 = (bf16[128,2048]{1,0:T(8,128)(2,1)S(1)}, bf16[128,2048]{1,0:T(8,128)(2,1)S(1)}, u32[]{:S(2)}, u32[]{:S(2)}) collective-permute-start(bf16[128,2048]{1,0:T(8,128)(2,1)S(1)} %slice.17), channel_id=1, source_target_pairs={{0,1},{1,0},{2,3},{3,2},{4,5},{5,4},{6,7},{7,6},{8,9},{9,8},{10,11... | collective-permute-start | bytes 1572872 | tf_op jit(solution)/shard_map/ppermute | solution.py:50
  35.5 12.6 %collective-permute-start.1 = (bf16[128,2048]{1,0:T(8,128)(2,1)S(1)}, bf16[128,2048]{1,0:T(8,128)(2,1)S(1)}, u32[]{:S(2)}, u32[]{:S(2)}) collective-permute-start(bf16[128,2048]{1,0:T(8,128)(2,1)S(1)} %slice.16), channel_id=1, source_target_pairs={{0,2},{1,3},{2,0},{3,1},{4,6},{5,7},{6,4},{7,5},{8,10},{9,11},{10,... | collective-permute-start | bytes 1572872 | tf_op jit(solution)/shard_map/ppermute | solution.py:50
  50.7 12.3 %collective-permute-start.5 = (bf16[2,64,256]{2,1,0:T(8,128)(2,1)}, bf16[2,64,256]{2,1,0:T(8,128)(2,1)S(1)}, u32[]{:S(2)}, u32[]{:S(2)}) collective-permute-start(bf16[2,64,256]{2,1,0:T(8,128)(2,1)} %get-tuple-element.58), channel_id=1, source_target_pairs={{0,4},{4,0},{8,12},{12,8},{1,5},{5,1},{9,13},{13,9},{2,6},{6,2},{1... | collective-permute-start | bytes 196616 | tf_op jit(solution)/shard_map/ppermute | solution.py:50
  52.3 10.7 %collective-permute-start.6 = (bf16[2,64,256]{2,1,0:T(8,128)(2,1)S(1)}, bf16[2,64,256]{2,1,0:T(8,128)(2,1)S(1)}, u32[]{:S(2)}, u32[]{:S(2)}) collective-permute-start(bf16[2,64,256]{2,1,0:T(8,128)(2,1)S(1)} %get-tuple-element.59), channel_id=1, source_target_pairs={{0,8},{4,12},{8,0},{12,4},{1,9},{5,13},{9,1},{13,5},{2,10},{6,14},... | collective-permute-start | bytes 196616 | tf_op jit(solution)/shard_map/ppermute | solution.py:50
  54.9 8.1 %collective-permute-start.7 = (bf16[2,64,256]{2,1,0:T(8,128)(2,1)S(1)}, bf16[2,64,256]{2,1,0:T(8,128)(2,1)S(1)}, u32[]{:S(2)}, u32[]{:S(2)}) collective-permute-start(bf16[2,64,256]{2,1,0:T(8,128)(2,1)S(1)} %get-tuple-element.60), channel_id=1, source_target_pairs={{0,12},{4,8},{8,4},{12,0},{1,13},{5,9},{9,5},{13,1},{2,14},{6,10},... | collective-permute-start | bytes 196616 | tf_op jit(solution)/shard_map/ppermute | solution.py:50
  59.3 22.9 %collective-permute-start.11 = (bf16[256,512]{1,0:T(8,128)(2,1)}, bf16[256,512]{1,0:T(8,128)(2,1)S(1)}, u32[]{:S(2)}, u32[]{:S(2)}) collective-permute-start(bf16[256,512]{1,0:T(8,128)(2,1)} %get-tuple-element.72), channel_id=1, source_target_pairs={{0,8},{4,12},{8,0},{12,4},{1,9},{5,13},{9,1},{13,5},{2,10},{6,14},... | collective-permute-start | bytes 786440 | tf_op jit(solution)/shard_map/ppermute | solution.py:50
  61.0 21.2 %collective-permute-start.12 = (bf16[256,512]{1,0:T(8,128)(2,1)}, bf16[256,512]{1,0:T(8,128)(2,1)S(1)}, u32[]{:S(2)}, u32[]{:S(2)}) collective-permute-start(bf16[256,512]{1,0:T(8,128)(2,1)} %get-tuple-element.73), channel_id=1, source_target_pairs={{0,12},{4,8},{8,4},{12,0},{1,13},{5,9},{9,5},{13,1},{2,14},{6,10},... | collective-permute-start | bytes 786440 | tf_op jit(solution)/shard_map/ppermute | solution.py:50
  63.1 19.2 %collective-permute-start.10 = (bf16[256,512]{1,0:T(8,128)(2,1)}, bf16[256,512]{1,0:T(8,128)(2,1)S(1)}, u32[]{:S(2)}, u32[]{:S(2)}) collective-permute-start(bf16[256,512]{1,0:T(8,128)(2,1)} %get-tuple-element.69), channel_id=1, source_target_pairs={{0,4},{4,0},{8,12},{12,8},{1,5},{5,1},{9,13},{13,9},{2,6},{6,2},{1... | collective-permute-start | bytes 786440 | tf_op jit(solution)/shard_map/ppermute | solution.py:50
  66.5 15.8 %collective-permute-start.9 = (bf16[1024,256]{1,0:T(8,128)(2,1)S(1)}, bf16[1024,256]{1,0:T(8,128)(2,1)S(1)}, u32[]{:S(2)}, u32[]{:S(2)}) collective-permute-start(bf16[1024,256]{1,0:T(8,128)(2,1)S(1)} %get-tuple-element.102), channel_id=1, source_target_pairs={{0,3},{1,2},{2,1},{3,0},{4,7},{5,6},{6,5},{7,4},{8,11},{9,10},{10,... | collective-permute-start | bytes 1572872 | tf_op jit(solution)/shard_map/ppermute | solution.py:50
  68.1 20.9 %collective-permute-start.8 = (bf16[1024,256]{1,0:T(8,128)(2,1)S(1)}, bf16[1024,256]{1,0:T(8,128)(2,1)S(1)}, u32[]{:S(2)}, u32[]{:S(2)}) collective-permute-start(bf16[1024,256]{1,0:T(8,128)(2,1)S(1)} %get-tuple-element.103), channel_id=1, source_target_pairs={{0,1},{1,0},{2,3},{3,2},{4,5},{5,4},{6,7},{7,6},{8,9},{9,8},{10,11... | collective-permute-start | bytes 1572872 | tf_op jit(solution)/shard_map/ppermute | solution.py:50
  89.9 15.5 %collective-permute-start.17 = (bf16[1024,256]{1,0:T(8,128)(2,1)}, bf16[1024,256]{1,0:T(8,128)(2,1)S(1)}, u32[]{:S(2)}, u32[]{:S(2)}) collective-permute-start(bf16[1024,256]{1,0:T(8,128)(2,1)} %get-tuple-element.101), channel_id=1, source_target_pairs={{0,2},{1,3},{2,0},{3,1},{4,6},{5,7},{6,4},{7,5},{8,10},{9,11},{10,... | collective-permute-start | bytes 1572872 | tf_op jit(solution)/shard_map/ppermute | solution.py:50
  90.5 10.4 %collective-permute-start.13 = (bf16[256,256]{1,0:T(8,128)(2,1)S(1)}, bf16[256,256]{1,0:T(8,128)(2,1)S(1)}, u32[]{:S(2)}, u32[]{:S(2)}) collective-permute-start(bf16[256,256]{1,0:T(8,128)(2,1)S(1)} %get-tuple-element.74), channel_id=1, source_target_pairs={{4,0},{8,4},{12,8},{5,1},{9,5},{13,9},{6,2},{10,6},{14,10},{7,3},{... | collective-permute-start | bytes 393224 | tf_op jit(solution)/shard_map/ppermute | solution.py:36
  101.0 9.9 %collective-permute-start.15 = (bf16[256,256]{1,0:T(8,128)(2,1)S(1)}, bf16[256,256]{1,0:T(8,128)(2,1)S(1)}, u32[]{:S(2)}, u32[]{:S(2)}) collective-permute-start(bf16[256,256]{1,0:T(8,128)(2,1)S(1)} %add_convert_fusion.refs_0_), channel_id=1, source_target_pairs={{0,8},{4,12},{8,0},{12,4},{1,9},{5,13},{9,1},{13,5},{2,10},{6,14},... | collective-permute-start | bytes 393224 | tf_op jit(solution)/shard_map/ppermute | solution.py:50
  103.7 7.2 %collective-permute-start.14 = (bf16[256,256]{1,0:T(8,128)(2,1)S(1)}, bf16[256,256]{1,0:T(8,128)(2,1)S(1)}, u32[]{:S(2)}, u32[]{:S(2)}) collective-permute-start(bf16[256,256]{1,0:T(8,128)(2,1)S(1)} %add_convert_fusion.refs_0_), channel_id=1, source_target_pairs={{0,4},{4,0},{8,12},{12,8},{1,5},{5,1},{9,13},{13,9},{2,6},{6,2},{1... | collective-permute-start | bytes 393224 | tf_op jit(solution)/shard_map/ppermute | solution.py:50
  110.9 22.1 %collective-permute-start.21 = (bf16[1024,256]{1,0:T(8,128)(2,1)S(1)}, bf16[1024,256]{1,0:T(8,128)(2,1)S(1)}, u32[]{:S(2)}, u32[]{:S(2)}) collective-permute-start(bf16[1024,256]{1,0:T(8,128)(2,1)S(1)} %collective-permute-done.8.refs_5_), channel_id=1, source_target_pairs={{0,16},{16,0},{1,17},{17,1},{2,18},{18,2},{3,19},{19,3},{4,20},{20... | collective-permute-start | bytes 1572872 | tf_op jit(solution)/shard_map/ppermute | solution.py:41
  110.9 22.9 %collective-permute-start.22 = (bf16[1024,256]{1,0:T(8,128)(2,1)S(1)}, bf16[1024,256]{1,0:T(8,128)(2,1)S(1)}, u32[]{:S(2)}, u32[]{:S(2)}) collective-permute-start(bf16[1024,256]{1,0:T(8,128)(2,1)S(1)} %collective-permute-done.17.refs_6_), channel_id=1, source_target_pairs={{0,16},{16,0},{1,17},{17,1},{2,18},{18,2},{3,19},{19,3},{4,20},{20... | collective-permute-start | bytes 1572872 | tf_op jit(solution)/shard_map/ppermute | solution.py:41
  111.4 23.2 %collective-permute-start.23 = (bf16[1024,256]{1,0:T(8,128)(2,1)S(1)}, bf16[1024,256]{1,0:T(8,128)(2,1)S(1)}, u32[]{:S(2)}, u32[]{:S(2)}) collective-permute-start(bf16[1024,256]{1,0:T(8,128)(2,1)S(1)} %collective-permute-done.9.refs_7_), channel_id=1, source_target_pairs={{0,16},{16,0},{1,17},{17,1},{2,18},{18,2},{3,19},{19,3},{4,20},{20... | collective-permute-start | bytes 1572872 | tf_op jit(solution)/shard_map/ppermute | solution.py:41
  113.9 9.8 %collective-permute-start.20 = (bf16[256,256]{1,0:T(8,128)(2,1)S(1)}, bf16[256,256]{1,0:T(8,128)(2,1)S(1)}, u32[]{:S(2)}, u32[]{:S(2)}) collective-permute-start(bf16[256,256]{1,0:T(8,128)(2,1)S(1)} %get-tuple-element.86.refs_0_), channel_id=1, source_target_pairs={{0,3},{1,2},{2,1},{3,0},{4,7},{5,6},{6,5},{7,4},{8,11},{9,10},{10,... | collective-permute-start | bytes 393224 | tf_op jit(solution)/shard_map/ppermute | solution.py:50
  115.4 11.3 %collective-permute-start.19 = (bf16[256,256]{1,0:T(8,128)(2,1)S(1)}, bf16[256,256]{1,0:T(8,128)(2,1)S(1)}, u32[]{:S(2)}, u32[]{:S(2)}) collective-permute-start(bf16[256,256]{1,0:T(8,128)(2,1)S(1)} %get-tuple-element.86.refs_0_), channel_id=1, source_target_pairs={{0,2},{1,3},{2,0},{3,1},{4,6},{5,7},{6,4},{7,5},{8,10},{9,11},{10,... | collective-permute-start | bytes 393224 | tf_op jit(solution)/shard_map/ppermute | solution.py:50
  123.7 8.7 %collective-permute-start.18 = (bf16[256,256]{1,0:T(8,128)(2,1)S(1)}, bf16[256,256]{1,0:T(8,128)(2,1)S(1)}, u32[]{:S(2)}, u32[]{:S(2)}) collective-permute-start(bf16[256,256]{1,0:T(8,128)(2,1)S(1)} %get-tuple-element.86.refs_0_), channel_id=1, source_target_pairs={{0,1},{1,0},{2,3},{3,2},{4,5},{5,4},{6,7},{7,6},{8,9},{9,8},{10,11... | collective-permute-start | bytes 393224 | tf_op jit(solution)/shard_map/ppermute | solution.py:50
  (36 other events, 211.2 us)
Sparse Core Ops, SparseCore 0:
  90.0 48.2 all-gather.2

commit v6 on v5

--- a/solution.py
+++ b/solution.py
@@ -416,39 +416,87 @@
     )(c, place, *gathered)
 
 
-def weight_body(mixed, c_ref, *refs):
-    *state_refs, g_ref, out_ref = refs
-    ranks, rows, width = g_ref.shape
-    c = c_ref[0]
-    if mixed:
-        total = dot(state_refs[0][...], g_ref[c], TN)
-        grad = jnp.concatenate([g_ref[c ^ s] for s in range(1, ranks)], axis=0)
-        out_ref[...] = total + dot(state_refs[1][0], grad, TN)
-    else:
-        grad = g_ref[...].reshape(ranks * rows, width)
-        out_ref[...] = dot(state_refs[0][0], grad, TN)
-
-
-def weight_term(c, kept, states, grad):
-    parts, count, cols = states.shape
-    _, rows, width = grad.shape
-    specs = [pl.BlockSpec((1, count, cols), lambda k, c: (k, 0, 0))]
-    arrays = [states]
-    if kept is not None:
-        specs.insert(0, pl.BlockSpec((rows, cols), lambda k, c: (0, k)))
-        arrays.insert(0, kept)
-    return pl.pallas_call(
-        functools.partial(weight_body, kept is not None),
-        grid_spec=pltpu.PrefetchScalarGridSpec(
-            num_scalar_prefetch=1,
-            grid=(parts,),
-            in_specs=specs + [pl.BlockSpec(grad.shape, lambda k, c: (0, 0, 0))],
-            out_specs=pl.BlockSpec((cols, width), lambda k, c: (k, 0)),
-        ),
+def weight_body(s_ref, g_ref, out_ref):
+    out_ref[...] = dot(s_ref[0], g_ref[...], TN)
+
+
+def weight_term(states, grad):
+    parts, rows, cols = states.shape
+    width = grad.shape[1]
+    return pl.pallas_call(
+        weight_body,
+        grid=(parts,),
+        in_specs=[
+            pl.BlockSpec((1, rows, cols), lambda k: (k, 0, 0)),
+            pl.BlockSpec(grad.shape, lambda k: (0, 0)),
+        ],
+        out_specs=pl.BlockSpec((cols, width), lambda k: (k, 0)),
         out_shape=jax.ShapeDtypeStruct((parts * cols, width), jnp.float32),
         cost_estimate=cost(2 * states.size * width, states.size * 4),
         compiler_params=params(),
-    )(c, *arrays, grad)
+    )(states, grad)
+
+
+def slice_body(first, groups, m_ref, c_ref, kept_ref, g_ref, *refs):
+    out_ref = refs[-1]
+    ranks, rows, width = g_ref.shape
+    m = m_ref[0]
+    c = c_ref[0]
+    grad = jnp.concatenate([g_ref[c ^ u] for u in range(1, ranks)], axis=0)
+    cols = refs[0].shape[1]
+    state_refs = list(refs[:-1])
+    for k, count in enumerate(groups):
+        at = pl.multiple_of((m ^ (first + k)) * cols, cols)
+        total = dot(kept_ref[:, pl.ds(at, cols)], g_ref[c], TN)
+        done = 0
+        for ref in state_refs[:count]:
+            total = total + dot(ref[...], grad[done : done + ref.shape[0]], TN)
+            done += ref.shape[0]
+        state_refs = state_refs[count:]
+        out_ref[k] = total
+
+
+def slice_terms(first, groups, m, c, kept, grad, states):
+    cols = states[0].shape[1]
+    width = grad.shape[2]
+    smem = pl.BlockSpec(memory_space=pltpu.SMEM)
+    vmem = pl.BlockSpec(memory_space=pltpu.VMEM)
+    rows = grad.shape[0] * grad.shape[1]
+    return pl.pallas_call(
+        functools.partial(slice_body, first, groups),
+        in_specs=[smem, smem] + [vmem] * (2 + len(states)),
+        out_specs=vmem,
+        out_shape=jax.ShapeDtypeStruct((len(groups), cols, width), jnp.float32),
+        cost_estimate=cost(2 * rows * cols * width * len(groups), rows * cols * len(groups) * 4),
+        compiler_params=params(),
+    )(m, c, kept, grad, *states)
+
+
+def settle_body(m_ref, *refs):
+    out_ref = refs[-1]
+    m = m_ref[0]
+    half = (len(refs) - 1) // 2
+    k = 0
+    for own, other in zip(refs[:half], refs[half:-1]):
+        for i in range(own.shape[0]):
+            cols = own.shape[1]
+            at = pl.ds(pl.multiple_of((m ^ k) * cols, cols), cols)
+            out_ref[at, :] = own[i] + other[i]
+            k += 1
+
+
+def settle(m, own, other):
+    count = sum(a.shape[0] for a in own)
+    _, cols, width = own[0].shape
+    vmem = pl.BlockSpec(memory_space=pltpu.VMEM)
+    return pl.pallas_call(
+        settle_body,
+        in_specs=[pl.BlockSpec(memory_space=pltpu.SMEM)] + [vmem] * (2 * len(own)),
+        out_specs=vmem,
+        out_shape=jax.ShapeDtypeStruct((count * cols, width), jnp.float32),
+        cost_estimate=cost(0, count * cols * width * 12),
+        compiler_params=params(),
+    )(m, *own, *other)
 
 
 def image_body(d_ref, *refs):
@@ -530,55 +578,75 @@
         m1, c1, place, low, high, weights, part, ranks, capacity, per_shard, mixed
     )
 
+    half = feats // 2
+
+    def slab(head, side):
+        return lax.dynamic_slice_in_dim(weights_late, head * feats + side * half, half)
+
+    weights_late, _, _ = lax.optimization_barrier((weights, x, y))
+    slabs = [slab(m ^ s, d) for s in steps]
+    own_slabs = [slab(m, d), slab(m, 1 - d)]
+    *both, _ = lax.optimization_barrier((*slabs, *own_slabs, packed[0]))
+    slabs, own_slabs = both[: len(slabs)], both[len(slabs) :]
+    near = [None] * len(slabs)
+    near[0] = trade(slabs[0], "mp", 1)
+    near[2] = trade(slabs[2], "mp", 3)
+
     if mixed:
         kept, *moved = slices(m1, c1, [states, x, y, low, high], feats // mps)
-        moved[1], moved[2], _ = lax.optimization_barrier((moved[1], moved[2], packed[0]))
-        far_slices = [trade(moved[1], "ctx", 2), trade(moved[2], "ctx", 3)]
         image = [trade(packed[s], "ctx", s) if s else packed[0] for s in range(ranks)]
-        moved[0], weights_late, *image = lax.optimization_barrier((moved[0], weights, *image))
-        moved = [trade(moved[0], "ctx", 1)] + far_slices
+        both = lax.optimization_barrier((*moved, *image))
+        moved, image = both[: len(moved)], both[len(moved) :]
+        moved = [trade(moved[s - 1], "ctx", s) for s in range(1, ranks)]
     else:
-        kept = None
         image = [exchange(packed[0], "ctx")]
         whole = lax.all_gather(states, "mp", axis=1, tiled=True)
         moved = whole.reshape(image_rows, ranks, mps, -1)
         moved = lax.dynamic_index_in_dim(moved, m, axis=2, keepdims=False).transpose(1, 0, 2)
         moved = [exchange(moved, "ctx").reshape(ranks * image_rows, -1)]
-        weights_late, *image = lax.optimization_barrier((weights, *image))
-
-    half = feats // 2
-
-    def slab(head, side):
-        return lax.dynamic_slice_in_dim(weights_late, head * feats + side * half, half)
-
-    near = [trade(slab(m ^ s, d), "mp", s) for s in steps]
 
     attn_out, own_grad, prior_grad = attention(
         c1, place, start, queries[0], d_out[0], text_kv[0], prior_text, image,
         images, per_shard, image_rows,
     )
-    prior_grad, near[0], near[-1], *moved = lax.optimization_barrier(
-        (prior_grad, near[0], near[-1], *moved)
+    early = ranks // 2 if mixed else 1
+    prior_grad, slabs[1], near[0], near[2], *both = lax.optimization_barrier(
+        (prior_grad, slabs[1], near[0], near[2], *moved[:early])
     )
-    all_states = lax.all_gather(jnp.concatenate(moved, axis=0), "mp", axis=0)
+    moved = both + list(moved[early:])
+    near[1] = trade(slabs[1], "mp", 2)
+    far = [own_slabs[1], swap(near[0], "dp"), None, swap(near[2], "dp")]
     grad = own_grad + shift(prior_grad, "ctx", -1).astype(jnp.float32)
     grad = grad.astype(jnp.bfloat16)
+    grad, far[1], far[3], *moved = lax.optimization_barrier((grad, far[1], far[3], *moved))
     if mixed:
         gathered = [trade(grad, "ctx", s) if s else grad for s in range(ranks)]
+        base = jnp.concatenate(moved, axis=0)
+        cut = base.shape[0] // 2
+        base_x = trade(base, "mp", 1)
+        base_y = trade(base, "mp", 2)
+        base_low = trade(base_x[:cut], "mp", 2)
+        base_high = trade(base_y[cut:], "mp", 1)
     else:
         gathered = [exchange(jnp.broadcast_to(grad, (ranks,) + grad.shape), "ctx")]
-    count = len(gathered)
-    both = lax.optimization_barrier((*gathered, *near))
-    gathered, near = both[:count], list(both[count:])
-    far = [slab(m, 1 - d)] + [swap(w, "dp") for w in near]
-    near = [slab(m, d)] + near
+        all_states = lax.all_gather(moved[0], "mp", axis=0)
+    near[1], *gathered = lax.optimization_barrier((near[1], *gathered))
     by_rank, mine = reorder(c1, place, gathered, per_shard, images, ranks)
     head_grad = [mine] + [trade(mine, "mp", s) for s in steps]
-    by_rank, *both = lax.optimization_barrier((by_rank, *head_grad, *far))
-    head_grad, far = both[:mps], both[mps:]
+    by_rank, *head_grad = lax.optimization_barrier((by_rank, *head_grad))
+    far[2] = swap(near[1], "dp")
+    near = [own_slabs[0]] + near
     image_grad = image_term(d1, head_grad, near, far)
-    term = weight_term(c1, kept, all_states, by_rank.reshape(ranks, image_rows, width))
-    weight_grad = term + swap(term, "dp")
+    if mixed:
+        by_rank = by_rank.reshape(ranks, image_rows, width)
+        terms = [
+            slice_terms(0, (1, 1, 1), m1, c1, kept, by_rank, [base, base_x, base_y]),
+            slice_terms(3, (2,), m1, c1, kept, by_rank, [base_low, base_high]),
+        ]
+        weight_grad = settle(m1, terms, [swap(a, "dp") for a in terms])
+    else:
+        term = weight_term(all_states, by_rank)
+        weight_grad = term + swap(term, "dp")
     return (attn_out[None], image_grad[None], weight_grad[None])
 
 

time: 157 us -> 134 us (0.85)
  between operations: 14.4 us -> 0.94 us
  local copies, waits for them, and re-layouts: 19.1 us -> 6.95 us
  starting transfers between devices: 33.5 us -> 43.4 us
  waiting for transfers between devices: 64.5 us -> 59.2 us
  other arithmetic: 3.62 us -> 1.09 us
    unnamed x68 -> x28, local copies, waits for them, and re-layouts: 15.2 us -> 4.35 us
    ppermute x19 -> x23, starting transfers between devices: 28.2 us -> 37.8 us  [trade(): return lax.ppermute(block, axis, [(i, i ^ step) for i in range(count)])]
    ppermute x2, waiting for transfers between devices: 9.11 us -> 1.54 us  [shift(): return lax.ppermute(block, axis, route)]
    ppermute x19 -> x23, waiting for transfers between devices: 51.4 us -> 57.7 us  [trade(): return lax.ppermute(block, axis, [(i, i ^ step) for i in range(count)])]
    all_gather x1 -> x0, waiting for transfers between devices: 2.84 us -> none  [per_device(): all_states = lax.all_gather(jnp.concatenate(moved, axis=0), 'mp', axis=0)]
    broadcast_in_dim x1 -> x0, other arithmetic: 1.59 us -> none  [per_device(): return (attn_out[None], image_grad[None], weight_grad[None])]
  transfers between devices with their start and end apart: 26 -> 30, of which waited for: 13 -> 12; matrix products, arithmetic and copies ran while one was open for 3% -> 3% of each run, Pallas kernels for 11% -> 13%
where the time goes in v6:
time: 134 us
  waiting for transfers between devices  59.2 us (44%)
  starting transfers between devices  43.4 us (32%)
  Pallas kernels  22.4 us (17%)
  local copies, waits for them, and re-layouts  6.95 us (5%)
    ppermute x23, waiting for transfers between devices, trade(): return lax.ppermute(block, axis, [(i, i ^ step) for i in range(count)])  57.7 us
    ppermute x23, starting transfers between devices, trade(): return lax.ppermute(block, axis, [(i, i ^ step) for i in range(count)])  37.8 us
    pallas_call x1, Pallas kernels, attention(): pl.pallas_call(functools.partial(attention_body, per_shard, images), grid...  11.5 us
    ppermute x2, starting transfers between devices, shift(): return lax.ppermute(block, axis, route)  4.95 us
    unnamed x28, local copies, waits for them, and re-layouts  4.35 us
    pallas_call x1, Pallas kernels, image_term(): pl.pallas_call(image_body, grid_spec=pltpu.PrefetchScalarGridSpec(num_sca...  2.94 us
  transfers between devices with their start and end apart: 30, of which 12 were waited for; matrix products, arithmetic and copies ran while one was open for 3% of the time, Pallas kernels for 13%

profile of v6, /device:TPU:0, one launch (start us, length us, event | category | flops | bytes accessed | tf_op | source)
XLA Modules:
  0.0 134.0 jit_solution(8721213593114489447)
XLA Ops:
  0.6 3.0 %collective-permute-start.2 = (bf16[256,2048]{1,0:T(8,128)(2,1)}, bf16[256,2048]{1,0:T(8,128)(2,1)S(1)}, u32[]{:S(2)}, u32[]{:S(2)}) collective-permute-start(bf16[256,2048]{1,0:T(8,128)(2,1)} %bitcast.29), channel_id=1, source_target_pairs={{0,2},{1,3},{2,0},{3,1},{4,6},{5,7},{6,4},{7,5},{8,10},{9,11},{10,... | collective-permute-start | bytes 3145736 | tf_op jit(solution)/shard_map/ppermute | solution.py:50
  5.2 3.5 %collective-permute-start.4 = (bf16[512,256]{1,0:T(8,128)(2,1)}, bf16[512,256]{1,0:T(8,128)(2,1)S(1)}, u32[]{:S(2)}, u32[]{:S(2)}) collective-permute-start(bf16[512,256]{1,0:T(8,128)(2,1)} %bitcast.39), channel_id=1, source_target_pairs={{0,4},{4,8},{8,12},{1,5},{5,9},{9,13},{2,6},{6,10},{10,14},{3,7},{... | collective-permute-start | bytes 786440 | tf_op jit(solution)/shard_map/ppermute | solution.py:36
  10.3 16.7 %collective-permute-done.2.y_ref.refs_2_ = bf16[256,2048]{1,0:T(8,128)(2,1)S(1)} collective-permute-done((bf16[256,2048]{1,0:T(8,128)(2,1)}, bf16[256,2048]{1,0:T(8,128)(2,1)S(1)}, u32[]{:S(2)}, u32[]{:S(2)}) %collective-permute-start.2) | collective-permute-done | bytes 1048608 | tf_op jit(solution)/shard_map/ppermute | solution.py:50
  27.1 1.8 %collective-permute-start.3 = (bf16[128,2048]{1,0:T(8,128)(2,1)S(1)}, bf16[128,2048]{1,0:T(8,128)(2,1)S(1)}, u32[]{:S(2)}, u32[]{:S(2)}) collective-permute-start(bf16[128,2048]{1,0:T(8,128)(2,1)S(1)} %slice.25), channel_id=1, source_target_pairs={{0,1},{1,0},{2,3},{3,2},{4,5},{5,4},{6,7},{7,6},{8,9},{9,8},{10,11... | collective-permute-start | bytes 1572872 | tf_op jit(solution)/shard_map/ppermute | solution.py:50
  28.9 1.6 %collective-permute-start.1 = (bf16[128,2048]{1,0:T(8,128)(2,1)S(1)}, bf16[128,2048]{1,0:T(8,128)(2,1)S(1)}, u32[]{:S(2)}, u32[]{:S(2)}) collective-permute-start(bf16[128,2048]{1,0:T(8,128)(2,1)S(1)} %slice.24), channel_id=1, source_target_pairs={{0,2},{1,3},{2,0},{3,1},{4,6},{5,7},{6,4},{7,5},{8,10},{9,11},{10,... | collective-permute-start | bytes 1572872 | tf_op jit(solution)/shard_map/ppermute | solution.py:50
  30.8 2.2 %copy-done = bf16[1,8192,256]{2,1,0:T(8,128)(2,1)S(1)} copy-done((bf16[1,8192,256]{2,1,0:T(8,128)(2,1)S(1)}, bf16[1,8192,256]{2,1,0:T(8,128)(2,1)}, u32[]{:S(2)}) %copy-start) | copy-done | bytes 4194328
  34.0 6.3 %collective-permute-done.3.high_ref = bf16[128,2048]{1,0:T(8,128)(2,1)S(1)} collective-permute-done((bf16[128,2048]{1,0:T(8,128)(2,1)S(1)}, bf16[128,2048]{1,0:T(8,128)(2,1)S(1)}, u32[]{:S(2)}, u32[]{:S(2)}) %collective-permute-start.3) | collective-permute-done | bytes 524320 | tf_op jit(solution)/shard_map/ppermute | solution.py:50
  41.5 2.1 %shard_map.96 = (bf16[2,64,256]{2,1,0:T(8,128)(2,1)S(1)}, bf16[2,64,256]{2,1,0:T(8,128)(2,1)}, bf16[2,64,256]{2,1,0:T(8,128)(2,1)}, bf16[2,64,256]{2,1,0:T(8,128)(2,1)}) custom-call(s32[1]{0:T(128)} %bitcast.10.m_ref, s32[1]{0:T(128)} %bitcast.c_ref, s32[64]{0:T(128)S(1)} %and_select_fusion.place_ref, bf16[128,2048]{1,0:T(8,128)(2,1)S(1)} %collective-permute-done.1.low_ref, ...), custom_call_target="tpu_custom_call" | custom-call | flops 268435456 | bytes 1048576 | tf_op jit(solution)/shard_map/pallas_call | solution.py:129
  43.6 1.6 %collective-permute-start.5 = (bf16[2,64,256]{2,1,0:T(8,128)(2,1)}, bf16[2,64,256]{2,1,0:T(8,128)(2,1)S(1)}, u32[]{:S(2)}, u32[]{:S(2)}) collective-permute-start(bf16[2,64,256]{2,1,0:T(8,128)(2,1)} %get-tuple-element.65), channel_id=1, source_target_pairs={{0,4},{4,0},{8,12},{12,8},{1,5},{5,1},{9,13},{13,9},{2,6},{6,2},{1... | collective-permute-start | bytes 196616 | tf_op jit(solution)/shard_map/ppermute | solution.py:50
  45.1 2.6 %collective-permute-start.6 = (bf16[2,64,256]{2,1,0:T(8,128)(2,1)}, bf16[2,64,256]{2,1,0:T(8,128)(2,1)}, u32[]{:S(2)}, u32[]{:S(2)}) collective-permute-start(bf16[2,64,256]{2,1,0:T(8,128)(2,1)} %get-tuple-element.66), channel_id=1, source_target_pairs={{0,8},{4,12},{8,0},{12,4},{1,9},{5,13},{9,1},{13,5},{2,10},{6,14},... | collective-permute-start | bytes 196616 | tf_op jit(solution)/shard_map/ppermute | solution.py:50
  50.7 1.9 %collective-permute-start.9 = (bf16[1024,256]{1,0:T(8,128)(2,1)}, bf16[1024,256]{1,0:T(8,128)(2,1)S(1)}, u32[]{:S(2)}, u32[]{:S(2)}) collective-permute-start(bf16[1024,256]{1,0:T(8,128)(2,1)} %get-tuple-element.77), channel_id=1, source_target_pairs={{0,3},{1,2},{2,1},{3,0},{4,7},{5,6},{6,5},{7,4},{8,11},{9,10},{10,... | collective-permute-start | bytes 1572872 | tf_op jit(solution)/shard_map/ppermute | solution.py:50
  55.6 3.5 %collective-permute-start.11 = (bf16[256,512]{1,0:T(8,128)(2,1)S(1)}, bf16[256,512]{1,0:T(8,128)(2,1)S(1)}, u32[]{:S(2)}, u32[]{:S(2)}) collective-permute-start(bf16[256,512]{1,0:T(8,128)(2,1)S(1)} %get-tuple-element.79), channel_id=1, source_target_pairs={{0,8},{4,12},{8,0},{12,4},{1,9},{5,13},{9,1},{13,5},{2,10},{6,14},... | collective-permute-start | bytes 786440 | tf_op jit(solution)/shard_map/ppermute | solution.py:50
  59.1 11.5 %shard_map.97 = (bf16[512,1024]{1,0:T(8,128)(2,1)}, f32[256,256]{1,0:T(8,128)S(1)}, bf16[256,256]{1,0:T(8,128)(2,1)S(1)}) custom-call(s32[1]{0:T(128)} %bitcast.c_ref, s32[64]{0:T(128)S(1)} %and_select_fusion.place_ref, s32[4]{0:T(128)S(1)} %bitcast.41, s32[1,512]{1,0:T(1,128)S(1)} %bitcast.36, bf16[512,1024]{1,0:T(8,128)(2,1)S(1)} %bitcast.37, ...), custom_call_target="tpu_custom_call" | custom-call | flops 13421772800 | bytes 4194304 | tf_op jit(solution)/shard_map/pallas_call | solution.py:344
  70.6 2.2 %collective-permute-done.9.refs_7_ = bf16[1024,256]{1,0:T(8,128)(2,1)S(1)} collective-permute-done((bf16[1024,256]{1,0:T(8,128)(2,1)}, bf16[1024,256]{1,0:T(8,128)(2,1)S(1)}, u32[]{:S(2)}, u32[]{:S(2)}) %collective-permute-start.9) | collective-permute-done | bytes 524320 | tf_op jit(solution)/shard_map/ppermute | solution.py:50
  74.8 3.8 %collective-permute-start.16 = (bf16[256,512]{1,0:T(8,128)(2,1)S(1)}, bf16[256,512]{1,0:T(8,128)(2,1)S(1)}, u32[]{:S(2)}, u32[]{:S(2)}) collective-permute-start(bf16[256,512]{1,0:T(8,128)(2,1)S(1)} %get-tuple-element.87), channel_id=1, source_target_pairs={{0,12},{4,8},{8,4},{12,0},{1,13},{5,9},{9,5},{13,1},{2,14},{6,10},... | collective-permute-start | bytes 786440 | tf_op jit(solution)/shard_map/ppermute | solution.py:50
  80.6 6.9 %collective-permute-done.16 = bf16[256,512]{1,0:T(8,128)(2,1)S(1)} collective-permute-done((bf16[256,512]{1,0:T(8,128)(2,1)S(1)}, bf16[256,512]{1,0:T(8,128)(2,1)S(1)}, u32[]{:S(2)}, u32[]{:S(2)}) %collective-permute-start.16) | collective-permute-done | bytes 262176 | tf_op jit(solution)/shard_map/ppermute | solution.py:50
  90.2 5.4 %collective-permute-start.18 = (bf16[256,256]{1,0:T(8,128)(2,1)S(1)}, bf16[256,256]{1,0:T(8,128)(2,1)S(1)}, u32[]{:S(2)}, u32[]{:S(2)}) collective-permute-start(bf16[256,256]{1,0:T(8,128)(2,1)S(1)} %add_convert_fusion.refs_0_), channel_id=1, source_target_pairs={{0,8},{4,12},{8,0},{12,4},{1,9},{5,13},{9,1},{13,5},{2,10},{6,14},... | collective-permute-start | bytes 393224 | tf_op jit(solution)/shard_map/ppermute | solution.py:50
  96.3 8.0 %collective-permute-done.18.refs_2_ = bf16[256,256]{1,0:T(8,128)(2,1)S(1)} collective-permute-done((bf16[256,256]{1,0:T(8,128)(2,1)S(1)}, bf16[256,256]{1,0:T(8,128)(2,1)S(1)}, u32[]{:S(2)}, u32[]{:S(2)}) %collective-permute-start.18) | collective-permute-done | bytes 131104 | tf_op jit(solution)/shard_map/ppermute | solution.py:50
  104.4 1.7 %shard_map.98 = (bf16[1024,256]{1,0:T(8,128)(2,1)S(1)}, bf16[256,256]{1,0:T(8,128)(2,1)S(1)}) custom-call(s32[1]{0:T(128)} %bitcast.c_ref, s32[64]{0:T(128)S(1)} %and_select_fusion.place_ref, bf16[256,256]{1,0:T(8,128)(2,1)S(1)} %add_convert_fusion.refs_0_, bf16[256,256]{1,0:T(8,128)(2,1)S(1)} %collective-permute-done.17.refs_1_, ...), custom_call_target="tpu_custom_call" | custom-call | bytes 2097152 | tf_op jit(solution)/shard_map/pallas_call | solution.py:402
  106.1 2.0 %collective-permute-start.22 = (bf16[256,256]{1,0:T(8,128)(2,1)S(1)}, bf16[256,256]{1,0:T(8,128)(2,1)S(1)}, u32[]{:S(2)}, u32[]{:S(2)}) collective-permute-start(bf16[256,256]{1,0:T(8,128)(2,1)S(1)} %get-tuple-element.95.refs_0_), channel_id=1, source_target_pairs={{0,3},{1,2},{2,1},{3,0},{4,7},{5,6},{6,5},{7,4},{8,11},{9,10},{10,... | collective-permute-start | bytes 393224 | tf_op jit(solution)/shard_map/ppermute | solution.py:50
  109.6 3.7 %collective-permute-done.22.refs_3_ = bf16[256,256]{1,0:T(8,128)(2,1)S(1)} collective-permute-done((bf16[256,256]{1,0:T(8,128)(2,1)S(1)}, bf16[256,256]{1,0:T(8,128)(2,1)S(1)}, u32[]{:S(2)}, u32[]{:S(2)}) %collective-permute-start.22) | collective-permute-done | bytes 131104 | tf_op jit(solution)/shard_map/ppermute | solution.py:50
  113.3 1.9 %collective-permute-done.21.refs_2_ = bf16[256,256]{1,0:T(8,128)(2,1)S(1)} collective-permute-done((bf16[256,256]{1,0:T(8,128)(2,1)S(1)}, bf16[256,256]{1,0:T(8,128)(2,1)S(1)}, u32[]{:S(2)}, u32[]{:S(2)}) %collective-permute-start.21) | collective-permute-done | bytes 131104 | tf_op jit(solution)/shard_map/ppermute | solution.py:50
  118.9 9.1 %collective-permute-done.27.refs_1_ = bf16[384,512]{1,0:T(8,128)(2,1)S(1)} collective-permute-done((bf16[384,512]{1,0:T(8,128)(2,1)S(1)}, bf16[384,512]{1,0:T(8,128)(2,1)S(1)}, u32[]{:S(2)}, u32[]{:S(2)}) %collective-permute-start.27) | collective-permute-done | bytes 393248 | tf_op jit(solution)/shard_map/ppermute | solution.py:50
  129.6 2.9 %shard_map.99 = bf16[256,2048]{1,0:T(8,128)(2,1)} custom-call(s32[1]{0:T(128)} %bitcast.13.d_ref, bf16[256,256]{1,0:T(8,128)(2,1)S(1)} %get-tuple-element.95.refs_0_, bf16[256,256]{1,0:T(8,128)(2,1)S(1)} %collective-permute-done.20.refs_1_, bf16[256,256]{1,0:T(8,128)(2,1)S(1)} %collective-permute-done.21.refs_2_, ...), custom_call_target="tpu_custom_call" | custom-call | flops 1073741824 | bytes 8388608 | tf_op jit(solution)/shard_map/pallas_call | solution.py:525
  (86 shorter events, 27.3 us)
Async XLA Ops:
  0.6 26.4 %collective-permute-start.2 = (bf16[256,2048]{1,0:T(8,128)(2,1)}, bf16[256,2048]{1,0:T(8,128)(2,1)S(1)}, u32[]{:S(2)}, u32[]{:S(2)}) collective-permute-start(bf16[256,2048]{1,0:T(8,128)(2,1)} %bitcast.29), channel_id=1, source_target_pairs={{0,2},{1,3},{2,0},{3,1},{4,6},{5,7},{6,4},{7,5},{8,10},{9,11},{10,... | collective-permute-start | bytes 3145736 | tf_op jit(solution)/shard_map/ppermute | solution.py:50
  3.7 25.2 %collective-permute-start = (bf16[256,2048]{1,0:T(8,128)(2,1)}, bf16[256,2048]{1,0:T(8,128)(2,1)S(1)}, u32[]{:S(2)}, u32[]{:S(2)}) collective-permute-start(bf16[256,2048]{1,0:T(8,128)(2,1)} %bitcast.30), channel_id=1, source_target_pairs={{0,1},{1,0},{2,3},{3,2},{4,5},{5,4},{6,7},{7,6},{8,9},{9,8},{10,11... | collective-permute-start | bytes 3145736 | tf_op jit(solution)/shard_map/ppermute | solution.py:50
  5.2 28.8 %collective-permute-start.4 = (bf16[512,256]{1,0:T(8,128)(2,1)}, bf16[512,256]{1,0:T(8,128)(2,1)S(1)}, u32[]{:S(2)}, u32[]{:S(2)}) collective-permute-start(bf16[512,256]{1,0:T(8,128)(2,1)} %bitcast.39), channel_id=1, source_target_pairs={{0,4},{4,8},{8,12},{1,5},{5,9},{9,13},{2,6},{6,10},{10,14},{3,7},{... | collective-permute-start | bytes 786440 | tf_op jit(solution)/shard_map/ppermute | solution.py:36
  27.1 13.2 %collective-permute-start.3 = (bf16[128,2048]{1,0:T(8,128)(2,1)S(1)}, bf16[128,2048]{1,0:T(8,128)(2,1)S(1)}, u32[]{:S(2)}, u32[]{:S(2)}) collective-permute-start(bf16[128,2048]{1,0:T(8,128)(2,1)S(1)} %slice.25), channel_id=1, source_target_pairs={{0,1},{1,0},{2,3},{3,2},{4,5},{5,4},{6,7},{7,6},{8,9},{9,8},{10,11... | collective-permute-start | bytes 1572872 | tf_op jit(solution)/shard_map/ppermute | solution.py:50
  28.9 12.6 %collective-permute-start.1 = (bf16[128,2048]{1,0:T(8,128)(2,1)S(1)}, bf16[128,2048]{1,0:T(8,128)(2,1)S(1)}, u32[]{:S(2)}, u32[]{:S(2)}) collective-permute-start(bf16[128,2048]{1,0:T(8,128)(2,1)S(1)} %slice.24), channel_id=1, source_target_pairs={{0,2},{1,3},{2,0},{3,1},{4,6},{5,7},{6,4},{7,5},{8,10},{9,11},{10,... | collective-permute-start | bytes 1572872 | tf_op jit(solution)/shard_map/ppermute | solution.py:50
  43.6 11.3 %collective-permute-start.5 = (bf16[2,64,256]{2,1,0:T(8,128)(2,1)}, bf16[2,64,256]{2,1,0:T(8,128)(2,1)S(1)}, u32[]{:S(2)}, u32[]{:S(2)}) collective-permute-start(bf16[2,64,256]{2,1,0:T(8,128)(2,1)} %get-tuple-element.65), channel_id=1, source_target_pairs={{0,4},{4,0},{8,12},{12,8},{1,5},{5,1},{9,13},{13,9},{2,6},{6,2},{1... | collective-permute-start | bytes 196616 | tf_op jit(solution)/shard_map/ppermute | solution.py:50
  45.1 9.7 %collective-permute-start.6 = (bf16[2,64,256]{2,1,0:T(8,128)(2,1)}, bf16[2,64,256]{2,1,0:T(8,128)(2,1)}, u32[]{:S(2)}, u32[]{:S(2)}) collective-permute-start(bf16[2,64,256]{2,1,0:T(8,128)(2,1)} %get-tuple-element.66), channel_id=1, source_target_pairs={{0,8},{4,12},{8,0},{12,4},{1,9},{5,13},{9,1},{13,5},{2,10},{6,14},... | collective-permute-start | bytes 196616 | tf_op jit(solution)/shard_map/ppermute | solution.py:50
  49.6 21.1 %collective-permute-start.8 = (bf16[1024,256]{1,0:T(8,128)(2,1)}, bf16[1024,256]{1,0:T(8,128)(2,1)S(1)}, u32[]{:S(2)}, u32[]{:S(2)}) collective-permute-start(bf16[1024,256]{1,0:T(8,128)(2,1)} %get-tuple-element.76), channel_id=1, source_target_pairs={{0,1},{1,0},{2,3},{3,2},{4,5},{5,4},{6,7},{7,6},{8,9},{9,8},{10,11... | collective-permute-start | bytes 1572872 | tf_op jit(solution)/shard_map/ppermute | solution.py:50
  50.7 22.1 %collective-permute-start.9 = (bf16[1024,256]{1,0:T(8,128)(2,1)}, bf16[1024,256]{1,0:T(8,128)(2,1)S(1)}, u32[]{:S(2)}, u32[]{:S(2)}) collective-permute-start(bf16[1024,256]{1,0:T(8,128)(2,1)} %get-tuple-element.77), channel_id=1, source_target_pairs={{0,3},{1,2},{2,1},{3,0},{4,7},{5,6},{6,5},{7,4},{8,11},{9,10},{10,... | collective-permute-start | bytes 1572872 | tf_op jit(solution)/shard_map/ppermute | solution.py:50
  54.9 15.7 %collective-permute-start.10 = (bf16[256,512]{1,0:T(8,128)(2,1)S(1)}, bf16[256,512]{1,0:T(8,128)(2,1)S(1)}, u32[]{:S(2)}, u32[]{:S(2)}) collective-permute-start(bf16[256,512]{1,0:T(8,128)(2,1)S(1)} %get-tuple-element.78), channel_id=1, source_target_pairs={{0,4},{4,0},{8,12},{12,8},{1,5},{5,1},{9,13},{13,9},{2,6},{6,2},{1... | collective-permute-start | bytes 786440 | tf_op jit(solution)/shard_map/ppermute | solution.py:50
  55.6 15.0 %collective-permute-start.11 = (bf16[256,512]{1,0:T(8,128)(2,1)S(1)}, bf16[256,512]{1,0:T(8,128)(2,1)S(1)}, u32[]{:S(2)}, u32[]{:S(2)}) collective-permute-start(bf16[256,512]{1,0:T(8,128)(2,1)S(1)} %get-tuple-element.79), channel_id=1, source_target_pairs={{0,8},{4,12},{8,0},{12,4},{1,9},{5,13},{9,1},{13,5},{2,10},{6,14},... | collective-permute-start | bytes 786440 | tf_op jit(solution)/shard_map/ppermute | solution.py:50
  72.8 14.7 %collective-permute-start.14 = (bf16[1024,256]{1,0:T(8,128)(2,1)S(1)}, bf16[1024,256]{1,0:T(8,128)(2,1)S(1)}, u32[]{:S(2)}, u32[]{:S(2)}) collective-permute-start(bf16[1024,256]{1,0:T(8,128)(2,1)S(1)} %collective-permute-done.8.refs_5_), channel_id=1, source_target_pairs={{0,16},{16,0},{1,17},{17,1},{2,18},{18,2},{3,19},{19,3},{4,20},{20... | collective-permute-start | bytes 1572872 | tf_op jit(solution)/shard_map/ppermute | solution.py:41
  72.8 14.7 %collective-permute-start.15 = (bf16[1024,256]{1,0:T(8,128)(2,1)S(1)}, bf16[1024,256]{1,0:T(8,128)(2,1)S(1)}, u32[]{:S(2)}, u32[]{:S(2)}) collective-permute-start(bf16[1024,256]{1,0:T(8,128)(2,1)S(1)} %collective-permute-done.9.refs_7_), channel_id=1, source_target_pairs={{0,16},{16,0},{1,17},{17,1},{2,18},{18,2},{3,19},{19,3},{4,20},{20... | collective-permute-start | bytes 1572872 | tf_op jit(solution)/shard_map/ppermute | solution.py:41
  73.3 7.3 %collective-permute-start.13 = (bf16[256,256]{1,0:T(8,128)(2,1)S(1)}, bf16[256,256]{1,0:T(8,128)(2,1)S(1)}, u32[]{:S(2)}, u32[]{:S(2)}) collective-permute-start(bf16[256,256]{1,0:T(8,128)(2,1)S(1)} %get-tuple-element.82), channel_id=1, source_target_pairs={{4,0},{8,4},{12,8},{5,1},{9,5},{13,9},{6,2},{10,6},{14,10},{7,3},{... | collective-permute-start | bytes 393224 | tf_op jit(solution)/shard_map/ppermute | solution.py:36
  74.8 12.7 %collective-permute-start.16 = (bf16[256,512]{1,0:T(8,128)(2,1)S(1)}, bf16[256,512]{1,0:T(8,128)(2,1)S(1)}, u32[]{:S(2)}, u32[]{:S(2)}) collective-permute-start(bf16[256,512]{1,0:T(8,128)(2,1)S(1)} %get-tuple-element.87), channel_id=1, source_target_pairs={{0,12},{4,8},{8,4},{12,0},{1,13},{5,9},{9,5},{13,1},{2,14},{6,10},... | collective-permute-start | bytes 786440 | tf_op jit(solution)/shard_map/ppermute | solution.py:50
  78.5 17.1 %collective-permute-start.12 = (bf16[1024,256]{1,0:T(8,128)(2,1)S(1)}, bf16[1024,256]{1,0:T(8,128)(2,1)S(1)}, u32[]{:S(2)}, u32[]{:S(2)}) collective-permute-start(bf16[1024,256]{1,0:T(8,128)(2,1)S(1)} %copy-done.12), channel_id=1, source_target_pairs={{0,2},{1,3},{2,0},{3,1},{4,6},{5,7},{6,4},{7,5},{8,10},{9,11},{10,... | collective-permute-start | bytes 1572872 | tf_op jit(solution)/shard_map/ppermute | solution.py:50
  87.6 27.7 %collective-permute-start.25 = (bf16[768,512]{1,0:T(8,128)(2,1)S(1)}, bf16[768,512]{1,0:T(8,128)(2,1)S(1)}, u32[]{:S(2)}, u32[]{:S(2)}) collective-permute-start(bf16[768,512]{1,0:T(8,128)(2,1)S(1)} %constant_dynamic-update-slice_fusion.refs_0_), channel_id=1, source_target_pairs={{0,2},{1,3},{2,0},{3,1},{4,6},{5,7},{6,4},{7,5},{8,10},{9,11},{10,... | collective-permute-start | bytes 2359304 | tf_op jit(solution)/shard_map/ppermute | solution.py:50
  88.1 27.1 %collective-permute-start.24 = (bf16[768,512]{1,0:T(8,128)(2,1)S(1)}, bf16[768,512]{1,0:T(8,128)(2,1)S(1)}, u32[]{:S(2)}, u32[]{:S(2)}) collective-permute-start(bf16[768,512]{1,0:T(8,128)(2,1)S(1)} %constant_dynamic-update-slice_fusion.refs_0_), channel_id=1, source_target_pairs={{0,1},{1,0},{2,3},{3,2},{4,5},{5,4},{6,7},{7,6},{8,9},{9,8},{10,11... | collective-permute-start | bytes 2359304 | tf_op jit(solution)/shard_map/ppermute | solution.py:50
  90.2 14.2 %collective-permute-start.18 = (bf16[256,256]{1,0:T(8,128)(2,1)S(1)}, bf16[256,256]{1,0:T(8,128)(2,1)S(1)}, u32[]{:S(2)}, u32[]{:S(2)}) collective-permute-start(bf16[256,256]{1,0:T(8,128)(2,1)S(1)} %add_convert_fusion.refs_0_), channel_id=1, source_target_pairs={{0,8},{4,12},{8,0},{12,4},{1,9},{5,13},{9,1},{13,5},{2,10},{6,14},... | collective-permute-start | bytes 393224 | tf_op jit(solution)/shard_map/ppermute | solution.py:50
  95.6 8.8 %collective-permute-start.17 = (bf16[256,256]{1,0:T(8,128)(2,1)S(1)}, bf16[256,256]{1,0:T(8,128)(2,1)S(1)}, u32[]{:S(2)}, u32[]{:S(2)}) collective-permute-start(bf16[256,256]{1,0:T(8,128)(2,1)S(1)} %add_convert_fusion.refs_0_), channel_id=1, source_target_pairs={{0,4},{4,0},{8,12},{12,8},{1,5},{5,1},{9,13},{13,9},{2,6},{6,2},{1... | collective-permute-start | bytes 393224 | tf_op jit(solution)/shard_map/ppermute | solution.py:50
  116.3 16.2 %collective-permute-start.28 = (f32[3,512,256]{2,1,0:T(8,128)S(1)}, f32[3,512,256]{2,1,0:T(8,128)S(1)}, u32[]{:S(2)}, u32[]{:S(2)}) collective-permute-start(f32[3,512,256]{2,1,0:T(8,128)S(1)} %shard_map.100.refs_0_), channel_id=1, source_target_pairs={{0,16},{16,0},{1,17},{17,1},{2,18},{18,2},{3,19},{19,3},{4,20},{20... | collective-permute-start | bytes 4718600 | tf_op jit(solution)/shard_map/ppermute | solution.py:41
  116.4 11.6 %collective-permute-start.27 = (bf16[384,512]{1,0:T(8,128)(2,1)S(1)}, bf16[384,512]{1,0:T(8,128)(2,1)S(1)}, u32[]{:S(2)}, u32[]{:S(2)}) collective-permute-start(bf16[384,512]{1,0:T(8,128)(2,1)S(1)} %slice.27), channel_id=1, source_target_pairs={{0,1},{1,0},{2,3},{3,2},{4,5},{5,4},{6,7},{7,6},{8,9},{9,8},{10,11... | collective-permute-start | bytes 1179656 | tf_op jit(solution)/shard_map/ppermute | solution.py:50
  117.6 11.3 %collective-permute-start.26 = (bf16[384,512]{1,0:T(8,128)(2,1)S(1)}, bf16[384,512]{1,0:T(8,128)(2,1)S(1)}, u32[]{:S(2)}, u32[]{:S(2)}) collective-permute-start(bf16[384,512]{1,0:T(8,128)(2,1)S(1)} %slice.26), channel_id=1, source_target_pairs={{0,2},{1,3},{2,0},{3,1},{4,6},{5,7},{6,4},{7,5},{8,10},{9,11},{10,... | collective-permute-start | bytes 1179656 | tf_op jit(solution)/shard_map/ppermute | solution.py:50
  118.9 10.6 %collective-permute-start.23 = (bf16[1024,256]{1,0:T(8,128)(2,1)S(1)}, bf16[1024,256]{1,0:T(8,128)(2,1)S(1)}, u32[]{:S(2)}, u32[]{:S(2)}) collective-permute-start(bf16[1024,256]{1,0:T(8,128)(2,1)S(1)} %collective-permute-done.12.refs_6_), channel_id=1, source_target_pairs={{0,16},{16,0},{1,17},{17,1},{2,18},{18,2},{3,19},{19,3},{4,20},{20... | collective-permute-start | bytes 1572872 | tf_op jit(solution)/shard_map/ppermute | solution.py:41
  (19 other events, 146.1 us)

commit v7 on v6

--- a/solution.py
+++ b/solution.py
@@ -588,54 +588,55 @@
     own_slabs = [slab(m, d), slab(m, 1 - d)]
     *both, _ = lax.optimization_barrier((*slabs, *own_slabs, packed[0]))
     slabs, own_slabs = both[: len(slabs)], both[len(slabs) :]
-    near = [None] * len(slabs)
-    near[0] = trade(slabs[0], "mp", 1)
-    near[2] = trade(slabs[2], "mp", 3)
+    last = trade(slabs[2], "mp", 3)
 
     if mixed:
         kept, *moved = slices(m1, c1, [states, x, y, low, high], feats // mps)
+        moved[2], _ = lax.optimization_barrier((moved[2], packed[0]))
+        moved[2] = trade(moved[2], "ctx", 3)
         image = [trade(packed[s], "ctx", s) if s else packed[0] for s in range(ranks)]
-        both = lax.optimization_barrier((*moved, *image))
-        moved, image = both[: len(moved)], both[len(moved) :]
-        moved = [trade(moved[s - 1], "ctx", s) for s in range(1, ranks)]
+        moved[0], moved[1], slabs[0], slabs[1], *image = lax.optimization_barrier(
+            (moved[0], moved[1], slabs[0], slabs[1], *image)
+        )
+        moved = [trade(moved[0], "ctx", 1), trade(moved[1], "ctx", 2), moved[2]]
     else:
         image = [exchange(packed[0], "ctx")]
         whole = lax.all_gather(states, "mp", axis=1, tiled=True)
         moved = whole.reshape(image_rows, ranks, mps, -1)
         moved = lax.dynamic_index_in_dim(moved, m, axis=2, keepdims=False).transpose(1, 0, 2)
         moved = [exchange(moved, "ctx").reshape(ranks * image_rows, -1)]
+    near = [trade(slabs[0], "mp", 1), trade(slabs[1], "mp", 2), last]
 
     attn_out, own_grad, prior_grad = attention(
         c1, place, start, queries[0], d_out[0], text_kv[0], prior_text, image,
         images, per_shard, image_rows,
     )
-    early = ranks // 2 if mixed else 1
-    prior_grad, slabs[1], near[0], near[2], *both = lax.optimization_barrier(
-        (prior_grad, slabs[1], near[0], near[2], *moved[:early])
-    )
-    moved = both + list(moved[early:])
-    near[1] = trade(slabs[1], "mp", 2)
-    far = [own_slabs[1], swap(near[0], "dp"), None, swap(near[2], "dp")]
+    prior_grad, *both = lax.optimization_barrier((prior_grad, *near, *moved))
+    near, moved = both[: len(near)], both[len(near) :]
+    far = [own_slabs[1]] + [swap(w, "dp") for w in near]
     grad = own_grad + shift(prior_grad, "ctx", -1).astype(jnp.float32)
     grad = grad.astype(jnp.bfloat16)
-    grad, far[1], far[3], *moved = lax.optimization_barrier((grad, far[1], far[3], *moved))
     if mixed:
         gathered = [trade(grad, "ctx", s) if s else grad for s in range(ranks)]
         base = jnp.concatenate(moved, axis=0)
         cut = base.shape[0] // 2
         base_x = trade(base, "mp", 1)
         base_y = trade(base, "mp", 2)
-        base_low = trade(base_x[:cut], "mp", 2)
-        base_high = trade(base_y[cut:], "mp", 1)
     else:
         gathered = [exchange(jnp.broadcast_to(grad, (ranks,) + grad.shape), "ctx")]
         all_states = lax.all_gather(moved[0], "mp", axis=0)
-    near[1], *gathered = lax.optimization_barrier((near[1], *gathered))
+        base_x = base_y = all_states
+    base_x, base_y, *both = lax.optimization_barrier((base_x, base_y, *far, *gathered))
+    far, gathered = both[: len(far)], both[len(far) :]
     by_rank, mine = reorder(c1, place, gathered, per_shard, images, ranks)
     head_grad = [mine] + [trade(mine, "mp", s) for s in steps]
-    by_rank, *head_grad = lax.optimization_barrier((by_rank, *head_grad))
-    far[2] = swap(near[1], "dp")
-    near = [own_slabs[0]] + near
+    if mixed:
+        base_low = trade(base_x[:cut], "mp", 2)
+        base_high = trade(base_y[cut:], "mp", 1)
+        by_rank, base_low, base_high, *head_grad = lax.optimization_barrier(
+            (by_rank, base_low, base_high, *head_grad)
+        )
+    near = [own_slabs[0]] + list(near)
     image_grad = image_term(d1, head_grad, near, far)
     if mixed:
         by_rank = by_rank.reshape(ranks, image_rows, width)

time: 134 us -> 132 us (0.985); the launches traced: 134 us -> 133 us
  waiting for transfers between devices: 59.2 us -> 55 us
  local copies, waits for them, and re-layouts: 6.95 us -> 10.5 us
    ppermute x23, waiting for transfers between devices: 57.7 us -> 46.1 us  [trade(): return lax.ppermute(block, axis, [(i, i ^ step) for i in range(count)])]
    ppermute x2, waiting for transfers between devices: 1.54 us -> 6.59 us  [shift(): return lax.ppermute(block, axis, route)]
    ppermute x5, waiting for transfers between devices: 0.01 us -> 2.27 us  [swap(): return lax.ppermute(block, axis, [(i, count - 1 - i) for i in range(count)])]
    dynamic_slice x1, local copies, waits for them, and re-layouts: 1.52 us -> 2.89 us  [slab(): lax.dynamic_slice_in_dim(weights_late, head * feats + side * half, half)]
  transfers between devices with their start and end apart: 30 -> 30, of which waited for: 12 -> 12; matrix products, arithmetic and copies ran while one was open for 3% -> 4% of each run, Pallas kernels for 13% -> 13%
where the time goes in v7:
time: 132 us; the launch traced here: 133 us
  waiting for transfers between devices  55 us (42%)
  starting transfers between devices  43.8 us (33%)
  Pallas kernels  22.2 us (17%)
  local copies, waits for them, and re-layouts  10.5 us (8%)
    ppermute x23, waiting for transfers between devices, trade(): return lax.ppermute(block, axis, [(i, i ^ step) for i in range(count)])  46.1 us
    ppermute x23, starting transfers between devices, trade(): return lax.ppermute(block, axis, [(i, i ^ step) for i in range(count)])  37.5 us
    pallas_call x1, Pallas kernels, attention(): pl.pallas_call(functools.partial(attention_body, per_shard, images), grid...  11.2 us
    ppermute x2, waiting for transfers between devices, shift(): return lax.ppermute(block, axis, route)  6.59 us
    unnamed x28, local copies, waits for them, and re-layouts  5.6 us
    ppermute x2, starting transfers between devices, shift(): return lax.ppermute(block, axis, route)  5.09 us
    pallas_call x1, Pallas kernels, image_term(): pl.pallas_call(image_body, grid_spec=pltpu.PrefetchScalarGridSpec(num_sca...  2.92 us
    dynamic_slice x1, local copies, waits for them, and re-layouts, slab(): lax.dynamic_slice_in_dim(weights_late, head * feats + side * half, half)  2.89 us
  transfers between devices with their start and end apart: 30, of which 12 were waited for; matrix products, arithmetic and copies ran while one was open for 4% of the time, Pallas kernels for 13%

profile of v7, /device:TPU:0, one launch (start us, length us, event | category | flops | bytes accessed | tf_op | source)
XLA Modules:
  0.0 133.4 jit_solution(1411182884051737111)
XLA Ops:
  0.6 3.0 %collective-permute-start = (bf16[256,2048]{1,0:T(8,128)(2,1)}, bf16[256,2048]{1,0:T(8,128)(2,1)S(1)}, u32[]{:S(2)}, u32[]{:S(2)}) collective-permute-start(bf16[256,2048]{1,0:T(8,128)(2,1)} %bitcast.29), channel_id=1, source_target_pairs={{0,1},{1,0},{2,3},{3,2},{4,5},{5,4},{6,7},{7,6},{8,9},{9,8},{10,11... | collective-permute-start | bytes 3145736 | tf_op jit(solution)/shard_map/ppermute | solution.py:50
  5.2 3.5 %collective-permute-start.4 = (bf16[512,256]{1,0:T(8,128)(2,1)}, bf16[512,256]{1,0:T(8,128)(2,1)S(1)}, u32[]{:S(2)}, u32[]{:S(2)}) collective-permute-start(bf16[512,256]{1,0:T(8,128)(2,1)} %bitcast.39), channel_id=1, source_target_pairs={{0,4},{4,8},{8,12},{1,5},{5,9},{9,13},{2,6},{6,10},{10,14},{3,7},{... | collective-permute-start | bytes 786440 | tf_op jit(solution)/shard_map/ppermute | solution.py:36
  10.3 16.7 %collective-permute-done.x_ref.refs_1_ = bf16[256,2048]{1,0:T(8,128)(2,1)S(1)} collective-permute-done((bf16[256,2048]{1,0:T(8,128)(2,1)}, bf16[256,2048]{1,0:T(8,128)(2,1)S(1)}, u32[]{:S(2)}, u32[]{:S(2)}) %collective-permute-start) | collective-permute-done | bytes 1048608 | tf_op jit(solution)/shard_map/ppermute | solution.py:50
  27.1 1.8 %collective-permute-start.1 = (bf16[128,2048]{1,0:T(8,128)(2,1)S(1)}, bf16[128,2048]{1,0:T(8,128)(2,1)S(1)}, u32[]{:S(2)}, u32[]{:S(2)}) collective-permute-start(bf16[128,2048]{1,0:T(8,128)(2,1)S(1)} %slice.24), channel_id=1, source_target_pairs={{0,2},{1,3},{2,0},{3,1},{4,6},{5,7},{6,4},{7,5},{8,10},{9,11},{10,... | collective-permute-start | bytes 1572872 | tf_op jit(solution)/shard_map/ppermute | solution.py:50
  28.9 1.6 %collective-permute-start.3 = (bf16[128,2048]{1,0:T(8,128)(2,1)S(1)}, bf16[128,2048]{1,0:T(8,128)(2,1)S(1)}, u32[]{:S(2)}, u32[]{:S(2)}) collective-permute-start(bf16[128,2048]{1,0:T(8,128)(2,1)S(1)} %slice.25), channel_id=1, source_target_pairs={{0,1},{1,0},{2,3},{3,2},{4,5},{5,4},{6,7},{7,6},{8,9},{9,8},{10,11... | collective-permute-start | bytes 1572872 | tf_op jit(solution)/shard_map/ppermute | solution.py:50
  30.8 2.2 %copy-done = bf16[1,8192,256]{2,1,0:T(8,128)(2,1)S(1)} copy-done((bf16[1,8192,256]{2,1,0:T(8,128)(2,1)S(1)}, bf16[1,8192,256]{2,1,0:T(8,128)(2,1)}, u32[]{:S(2)}) %copy-start) | copy-done | bytes 4194328
  34.0 6.2 %collective-permute-done.1.low_ref = bf16[128,2048]{1,0:T(8,128)(2,1)S(1)} collective-permute-done((bf16[128,2048]{1,0:T(8,128)(2,1)S(1)}, bf16[128,2048]{1,0:T(8,128)(2,1)S(1)}, u32[]{:S(2)}, u32[]{:S(2)}) %collective-permute-start.1) | collective-permute-done | bytes 524320 | tf_op jit(solution)/shard_map/ppermute | solution.py:50
  46.2 3.6 %collective-permute-start.13 = (bf16[256,512]{1,0:T(8,128)(2,1)}, bf16[256,512]{1,0:T(8,128)(2,1)}, u32[]{:S(2)}, u32[]{:S(2)}) collective-permute-start(bf16[256,512]{1,0:T(8,128)(2,1)} %get-tuple-element.86), channel_id=1, source_target_pairs={{0,12},{4,8},{8,4},{12,0},{1,13},{5,9},{9,5},{13,1},{2,14},{6,10},... | collective-permute-start | bytes 786440 | tf_op jit(solution)/shard_map/ppermute | solution.py:50
  50.6 3.6 %collective-permute-start.7 = (bf16[2,64,256]{2,1,0:T(8,128)(2,1)S(1)}, bf16[2,64,256]{2,1,0:T(8,128)(2,1)}, u32[]{:S(2)}, u32[]{:S(2)}) collective-permute-start(bf16[2,64,256]{2,1,0:T(8,128)(2,1)S(1)} %get-tuple-element.73), channel_id=1, source_target_pairs={{0,12},{4,8},{8,4},{12,0},{1,13},{5,9},{9,5},{13,1},{2,14},{6,10},... | collective-permute-start | bytes 196616 | tf_op jit(solution)/shard_map/ppermute | solution.py:50
  54.2 2.9 %constant_dynamic-slice_fusion = (bf16[1024,256]{1,0:T(8,128)(2,1)S(1)}, bf16[1024,256]{1,0:T(8,128)(2,1)S(1)}, bf16[1024,256]{1,0:T(8,128)(2,1)}, bf16[1024,256]{1,0:T(8,128)(2,1)}, bf16[1024,256]{1,0:T(8,128)(2,1)}) fusion(bf16[8192,256]{1,0:T(8,128)(2,1)} %bitcast.24, s32[]{:T(128)S(6)} %select_n.47, s32[]{:T(128)S(6)} %select_n.46, s32[]{:T(128)S(6)} %select_n.45, ...), kind=kLoop, calls=%fused_computation.8 | loop fusion | bytes 5242900 | tf_op jit(solution)/shard_map/dynamic_slice | solution.py:584
  58.7 5.4 %collective-permute-done.6.refs_2_ = bf16[2,64,256]{2,1,0:T(8,128)(2,1)} collective-permute-done((bf16[2,64,256]{2,1,0:T(8,128)(2,1)}, bf16[2,64,256]{2,1,0:T(8,128)(2,1)}, u32[]{:S(2)}, u32[]{:S(2)}) %collective-permute-start.6) | collective-permute-done | bytes 65568 | tf_op jit(solution)/shard_map/ppermute | solution.py:50
  67.3 1.8 %collective-permute-start.12 = (bf16[256,512]{1,0:T(8,128)(2,1)}, bf16[256,512]{1,0:T(8,128)(2,1)S(1)}, u32[]{:S(2)}, u32[]{:S(2)}) collective-permute-start(bf16[256,512]{1,0:T(8,128)(2,1)} %copy-done.9), channel_id=1, source_target_pairs={{0,8},{4,12},{8,0},{12,4},{1,9},{5,13},{9,1},{13,5},{2,10},{6,14},... | collective-permute-start | bytes 786440 | tf_op jit(solution)/shard_map/ppermute | solution.py:50
  70.1 11.2 %shard_map.97 = (bf16[512,1024]{1,0:T(8,128)(2,1)}, f32[256,256]{1,0:T(8,128)S(1)}, bf16[256,256]{1,0:T(8,128)(2,1)S(1)}) custom-call(s32[1]{0:T(128)} %bitcast.c_ref, s32[64]{0:T(128)S(1)} %and_select_fusion.place_ref, s32[4]{0:T(128)S(1)} %bitcast.41, s32[1,512]{1,0:T(1,128)S(1)} %bitcast.36, bf16[512,1024]{1,0:T(8,128)(2,1)S(1)} %bitcast.37, ...), custom_call_target="tpu_custom_call" | custom-call | flops 13421772800 | bytes 4194304 | tf_op jit(solution)/shard_map/pallas_call | solution.py:344
  81.4 1.6 %collective-permute-start.19 = (bf16[256,256]{1,0:T(8,128)(2,1)S(1)}, bf16[256,256]{1,0:T(8,128)(2,1)S(1)}, u32[]{:S(2)}, u32[]{:S(2)}) collective-permute-start(bf16[256,256]{1,0:T(8,128)(2,1)S(1)} %get-tuple-element.95), channel_id=1, source_target_pairs={{4,0},{8,4},{12,8},{5,1},{9,5},{13,9},{6,2},{10,6},{14,10},{7,3},{... | collective-permute-start | bytes 393224 | tf_op jit(solution)/shard_map/ppermute | solution.py:36
  86.1 6.6 %collective-permute-done.19 = bf16[256,256]{1,0:T(8,128)(2,1)S(1)} collective-permute-done((bf16[256,256]{1,0:T(8,128)(2,1)S(1)}, bf16[256,256]{1,0:T(8,128)(2,1)S(1)}, u32[]{:S(2)}, u32[]{:S(2)}) %collective-permute-start.19) | collective-permute-done | bytes 131104 | tf_op jit(solution)/shard_map/ppermute | solution.py:36
  92.7 4.9 %collective-permute-start.20 = (bf16[256,256]{1,0:T(8,128)(2,1)S(1)}, bf16[256,256]{1,0:T(8,128)(2,1)S(1)}, u32[]{:S(2)}, u32[]{:S(2)}) collective-permute-start(bf16[256,256]{1,0:T(8,128)(2,1)S(1)} %add_convert_fusion.refs_0_), channel_id=1, source_target_pairs={{0,4},{4,0},{8,12},{12,8},{1,5},{5,1},{9,13},{13,9},{2,6},{6,2},{1... | collective-permute-start | bytes 393224 | tf_op jit(solution)/shard_map/ppermute | solution.py:50
  97.6 2.4 %collective-permute-start.22 = (bf16[256,256]{1,0:T(8,128)(2,1)S(1)}, bf16[256,256]{1,0:T(8,128)(2,1)S(1)}, u32[]{:S(2)}, u32[]{:S(2)}) collective-permute-start(bf16[256,256]{1,0:T(8,128)(2,1)S(1)} %add_convert_fusion.refs_0_), channel_id=1, source_target_pairs={{0,12},{4,8},{8,4},{12,0},{1,13},{5,9},{9,5},{13,1},{2,14},{6,10},... | collective-permute-start | bytes 393224 | tf_op jit(solution)/shard_map/ppermute | solution.py:50
  100.5 5.2 %collective-permute-done.21.refs_2_ = bf16[256,256]{1,0:T(8,128)(2,1)S(1)} collective-permute-done((bf16[256,256]{1,0:T(8,128)(2,1)S(1)}, bf16[256,256]{1,0:T(8,128)(2,1)S(1)}, u32[]{:S(2)}, u32[]{:S(2)}) %collective-permute-start.21) | collective-permute-done | bytes 131104 | tf_op jit(solution)/shard_map/ppermute | solution.py:50
  108.5 1.6 %collective-permute-start.23 = (bf16[384,512]{1,0:T(8,128)(2,1)S(1)}, bf16[384,512]{1,0:T(8,128)(2,1)S(1)}, u32[]{:S(2)}, u32[]{:S(2)}) collective-permute-start(bf16[384,512]{1,0:T(8,128)(2,1)S(1)} %slice.22), channel_id=1, source_target_pairs={{0,2},{1,3},{2,0},{3,1},{4,6},{5,7},{6,4},{7,5},{8,10},{9,11},{10,... | collective-permute-start | bytes 1179656 | tf_op jit(solution)/shard_map/ppermute | solution.py:50
  110.7 1.7 %shard_map.98 = (bf16[1024,256]{1,0:T(8,128)(2,1)S(1)}, bf16[256,256]{1,0:T(8,128)(2,1)S(1)}) custom-call(s32[1]{0:T(128)} %bitcast.c_ref, s32[64]{0:T(128)S(1)} %and_select_fusion.place_ref, bf16[256,256]{1,0:T(8,128)(2,1)S(1)} %add_convert_fusion.refs_0_, bf16[256,256]{1,0:T(8,128)(2,1)S(1)} %collective-permute-done.20.refs_1_, ...), custom_call_target="tpu_custom_call" | custom-call | bytes 2097152 | tf_op jit(solution)/shard_map/pallas_call | solution.py:402
  112.3 1.6 %collective-permute-start.25 = (bf16[256,256]{1,0:T(8,128)(2,1)S(1)}, bf16[256,256]{1,0:T(8,128)(2,1)S(1)}, u32[]{:S(2)}, u32[]{:S(2)}) collective-permute-start(bf16[256,256]{1,0:T(8,128)(2,1)S(1)} %get-tuple-element.104.refs_0_), channel_id=1, source_target_pairs={{0,1},{1,0},{2,3},{3,2},{4,5},{5,4},{6,7},{7,6},{8,9},{9,8},{10,11... | collective-permute-start | bytes 393224 | tf_op jit(solution)/shard_map/ppermute | solution.py:50
  115.9 9.0 %collective-permute-done.25.refs_1_ = bf16[256,256]{1,0:T(8,128)(2,1)S(1)} collective-permute-done((bf16[256,256]{1,0:T(8,128)(2,1)S(1)}, bf16[256,256]{1,0:T(8,128)(2,1)S(1)}, u32[]{:S(2)}, u32[]{:S(2)}) %collective-permute-start.25) | collective-permute-done | bytes 131104 | tf_op jit(solution)/shard_map/ppermute | solution.py:50
  124.9 1.6 %collective-permute-done.27.refs_3_ = bf16[256,256]{1,0:T(8,128)(2,1)S(1)} collective-permute-done((bf16[256,256]{1,0:T(8,128)(2,1)S(1)}, bf16[256,256]{1,0:T(8,128)(2,1)S(1)}, u32[]{:S(2)}, u32[]{:S(2)}) %collective-permute-start.27) | collective-permute-done | bytes 131104 | tf_op jit(solution)/shard_map/ppermute | solution.py:50
  128.8 2.9 %shard_map.99 = bf16[256,2048]{1,0:T(8,128)(2,1)} custom-call(s32[1]{0:T(128)} %bitcast.13.d_ref, bf16[256,256]{1,0:T(8,128)(2,1)S(1)} %get-tuple-element.104.refs_0_, bf16[256,256]{1,0:T(8,128)(2,1)S(1)} %collective-permute-done.25.refs_1_, bf16[256,256]{1,0:T(8,128)(2,1)S(1)} %collective-permute-done.26.refs_2_, ...), custom_call_target="tpu_custom_call" | custom-call | flops 1073741824 | bytes 8388608 | tf_op jit(solution)/shard_map/pallas_call | solution.py:525
  (86 shorter events, 29.9 us)
Async XLA Ops:
  0.6 26.4 %collective-permute-start = (bf16[256,2048]{1,0:T(8,128)(2,1)}, bf16[256,2048]{1,0:T(8,128)(2,1)S(1)}, u32[]{:S(2)}, u32[]{:S(2)}) collective-permute-start(bf16[256,2048]{1,0:T(8,128)(2,1)} %bitcast.29), channel_id=1, source_target_pairs={{0,1},{1,0},{2,3},{3,2},{4,5},{5,4},{6,7},{7,6},{8,9},{9,8},{10,11... | collective-permute-start | bytes 3145736 | tf_op jit(solution)/shard_map/ppermute | solution.py:50
  3.6 25.2 %collective-permute-start.2 = (bf16[256,2048]{1,0:T(8,128)(2,1)}, bf16[256,2048]{1,0:T(8,128)(2,1)S(1)}, u32[]{:S(2)}, u32[]{:S(2)}) collective-permute-start(bf16[256,2048]{1,0:T(8,128)(2,1)} %bitcast.30), channel_id=1, source_target_pairs={{0,2},{1,3},{2,0},{3,1},{4,6},{5,7},{6,4},{7,5},{8,10},{9,11},{10,... | collective-permute-start | bytes 3145736 | tf_op jit(solution)/shard_map/ppermute | solution.py:50
  5.2 28.9 %collective-permute-start.4 = (bf16[512,256]{1,0:T(8,128)(2,1)}, bf16[512,256]{1,0:T(8,128)(2,1)S(1)}, u32[]{:S(2)}, u32[]{:S(2)}) collective-permute-start(bf16[512,256]{1,0:T(8,128)(2,1)} %bitcast.39), channel_id=1, source_target_pairs={{0,4},{4,8},{8,12},{1,5},{5,9},{9,13},{2,6},{6,10},{10,14},{3,7},{... | collective-permute-start | bytes 786440 | tf_op jit(solution)/shard_map/ppermute | solution.py:36
  27.1 13.2 %collective-permute-start.1 = (bf16[128,2048]{1,0:T(8,128)(2,1)S(1)}, bf16[128,2048]{1,0:T(8,128)(2,1)S(1)}, u32[]{:S(2)}, u32[]{:S(2)}) collective-permute-start(bf16[128,2048]{1,0:T(8,128)(2,1)S(1)} %slice.24), channel_id=1, source_target_pairs={{0,2},{1,3},{2,0},{3,1},{4,6},{5,7},{6,4},{7,5},{8,10},{9,11},{10,... | collective-permute-start | bytes 1572872 | tf_op jit(solution)/shard_map/ppermute | solution.py:50
  28.9 12.6 %collective-permute-start.3 = (bf16[128,2048]{1,0:T(8,128)(2,1)S(1)}, bf16[128,2048]{1,0:T(8,128)(2,1)S(1)}, u32[]{:S(2)}, u32[]{:S(2)}) collective-permute-start(bf16[128,2048]{1,0:T(8,128)(2,1)S(1)} %slice.25), channel_id=1, source_target_pairs={{0,1},{1,0},{2,3},{3,2},{4,5},{5,4},{6,7},{7,6},{8,9},{9,8},{10,11... | collective-permute-start | bytes 1572872 | tf_op jit(solution)/shard_map/ppermute | solution.py:50
  46.2 21.1 %collective-permute-start.13 = (bf16[256,512]{1,0:T(8,128)(2,1)}, bf16[256,512]{1,0:T(8,128)(2,1)}, u32[]{:S(2)}, u32[]{:S(2)}) collective-permute-start(bf16[256,512]{1,0:T(8,128)(2,1)} %get-tuple-element.86), channel_id=1, source_target_pairs={{0,12},{4,8},{8,4},{12,0},{1,13},{5,9},{9,5},{13,1},{2,14},{6,10},... | collective-permute-start | bytes 786440 | tf_op jit(solution)/shard_map/ppermute | solution.py:50
  49.8 8.8 %collective-permute-start.5 = (bf16[2,64,256]{2,1,0:T(8,128)(2,1)}, bf16[2,64,256]{2,1,0:T(8,128)(2,1)}, u32[]{:S(2)}, u32[]{:S(2)}) collective-permute-start(bf16[2,64,256]{2,1,0:T(8,128)(2,1)} %copy-done.12), channel_id=1, source_target_pairs={{0,4},{4,0},{8,12},{12,8},{1,5},{5,1},{9,13},{13,9},{2,6},{6,2},{1... | collective-permute-start | bytes 196616 | tf_op jit(solution)/shard_map/ppermute | solution.py:50
  49.8 14.2 %collective-permute-start.6 = (bf16[2,64,256]{2,1,0:T(8,128)(2,1)}, bf16[2,64,256]{2,1,0:T(8,128)(2,1)}, u32[]{:S(2)}, u32[]{:S(2)}) collective-permute-start(bf16[2,64,256]{2,1,0:T(8,128)(2,1)} %copy-done.11), channel_id=1, source_target_pairs={{0,8},{4,12},{8,0},{12,4},{1,9},{5,13},{9,1},{13,5},{2,10},{6,14},... | collective-permute-start | bytes 196616 | tf_op jit(solution)/shard_map/ppermute | solution.py:50
  50.6 13.4 %collective-permute-start.7 = (bf16[2,64,256]{2,1,0:T(8,128)(2,1)S(1)}, bf16[2,64,256]{2,1,0:T(8,128)(2,1)}, u32[]{:S(2)}, u32[]{:S(2)}) collective-permute-start(bf16[2,64,256]{2,1,0:T(8,128)(2,1)S(1)} %get-tuple-element.73), channel_id=1, source_target_pairs={{0,12},{4,8},{8,4},{12,0},{1,13},{5,9},{9,5},{13,1},{2,14},{6,10},... | collective-permute-start | bytes 196616 | tf_op jit(solution)/shard_map/ppermute | solution.py:50
  57.2 24.1 %collective-permute-start.10 = (bf16[1024,256]{1,0:T(8,128)(2,1)}, bf16[1024,256]{1,0:T(8,128)(2,1)S(1)}, u32[]{:S(2)}, u32[]{:S(2)}) collective-permute-start(bf16[1024,256]{1,0:T(8,128)(2,1)} %get-tuple-element.82), channel_id=1, source_target_pairs={{0,3},{1,2},{2,1},{3,0},{4,7},{5,6},{6,5},{7,4},{8,11},{9,10},{10,... | collective-permute-start | bytes 1572872 | tf_op jit(solution)/shard_map/ppermute | solution.py:50
  64.1 17.2 %collective-permute-start.8 = (bf16[1024,256]{1,0:T(8,128)(2,1)}, bf16[1024,256]{1,0:T(8,128)(2,1)S(1)}, u32[]{:S(2)}, u32[]{:S(2)}) collective-permute-start(bf16[1024,256]{1,0:T(8,128)(2,1)} %get-tuple-element.80), channel_id=1, source_target_pairs={{0,1},{1,0},{2,3},{3,2},{4,5},{5,4},{6,7},{7,6},{8,9},{9,8},{10,11... | collective-permute-start | bytes 1572872 | tf_op jit(solution)/shard_map/ppermute | solution.py:50
  65.6 15.7 %collective-permute-start.9 = (bf16[1024,256]{1,0:T(8,128)(2,1)}, bf16[1024,256]{1,0:T(8,128)(2,1)S(1)}, u32[]{:S(2)}, u32[]{:S(2)}) collective-permute-start(bf16[1024,256]{1,0:T(8,128)(2,1)} %get-tuple-element.81), channel_id=1, source_target_pairs={{0,2},{1,3},{2,0},{3,1},{4,6},{5,7},{6,4},{7,5},{8,10},{9,11},{10,... | collective-permute-start | bytes 1572872 | tf_op jit(solution)/shard_map/ppermute | solution.py:50
  66.1 15.2 %collective-permute-start.11 = (bf16[256,512]{1,0:T(8,128)(2,1)}, bf16[256,512]{1,0:T(8,128)(2,1)S(1)}, u32[]{:S(2)}, u32[]{:S(2)}) collective-permute-start(bf16[256,512]{1,0:T(8,128)(2,1)} %copy-done.10), channel_id=1, source_target_pairs={{0,4},{4,0},{8,12},{12,8},{1,5},{5,1},{9,13},{13,9},{2,6},{6,2},{1... | collective-permute-start | bytes 786440 | tf_op jit(solution)/shard_map/ppermute | solution.py:50
  67.3 13.9 %collective-permute-start.12 = (bf16[256,512]{1,0:T(8,128)(2,1)}, bf16[256,512]{1,0:T(8,128)(2,1)S(1)}, u32[]{:S(2)}, u32[]{:S(2)}) collective-permute-start(bf16[256,512]{1,0:T(8,128)(2,1)} %copy-done.9), channel_id=1, source_target_pairs={{0,8},{4,12},{8,0},{12,4},{1,9},{5,13},{9,1},{13,5},{2,10},{6,14},... | collective-permute-start | bytes 786440 | tf_op jit(solution)/shard_map/ppermute | solution.py:50
  81.4 11.3 %collective-permute-start.19 = (bf16[256,256]{1,0:T(8,128)(2,1)S(1)}, bf16[256,256]{1,0:T(8,128)(2,1)S(1)}, u32[]{:S(2)}, u32[]{:S(2)}) collective-permute-start(bf16[256,256]{1,0:T(8,128)(2,1)S(1)} %get-tuple-element.95), channel_id=1, source_target_pairs={{4,0},{8,4},{12,8},{5,1},{9,5},{13,9},{6,2},{10,6},{14,10},{7,3},{... | collective-permute-start | bytes 393224 | tf_op jit(solution)/shard_map/ppermute | solution.py:36
  84.0 24.5 %collective-permute-start.14 = (bf16[768,512]{1,0:T(8,128)(2,1)S(1)}, bf16[768,512]{1,0:T(8,128)(2,1)S(1)}, u32[]{:S(2)}, u32[]{:S(2)}) collective-permute-start(bf16[768,512]{1,0:T(8,128)(2,1)S(1)} %constant_dynamic-update-slice_fusion.refs_0_), channel_id=1, source_target_pairs={{0,1},{1,0},{2,3},{3,2},{4,5},{5,4},{6,7},{7,6},{8,9},{9,8},{10,11... | collective-permute-start | bytes 2359304 | tf_op jit(solution)/shard_map/ppermute | solution.py:50
  85.1 23.3 %collective-permute-start.15 = (bf16[768,512]{1,0:T(8,128)(2,1)S(1)}, bf16[768,512]{1,0:T(8,128)(2,1)S(1)}, u32[]{:S(2)}, u32[]{:S(2)}) collective-permute-start(bf16[768,512]{1,0:T(8,128)(2,1)S(1)} %constant_dynamic-update-slice_fusion.refs_0_), channel_id=1, source_target_pairs={{0,2},{1,3},{2,0},{3,1},{4,6},{5,7},{6,4},{7,5},{8,10},{9,11},{10,... | collective-permute-start | bytes 2359304 | tf_op jit(solution)/shard_map/ppermute | solution.py:50
  97.6 8.2 %collective-permute-start.21 = (bf16[256,256]{1,0:T(8,128)(2,1)S(1)}, bf16[256,256]{1,0:T(8,128)(2,1)S(1)}, u32[]{:S(2)}, u32[]{:S(2)}) collective-permute-start(bf16[256,256]{1,0:T(8,128)(2,1)S(1)} %add_convert_fusion.refs_0_), channel_id=1, source_target_pairs={{0,8},{4,12},{8,0},{12,4},{1,9},{5,13},{9,1},{13,5},{2,10},{6,14},... | collective-permute-start | bytes 393224 | tf_op jit(solution)/shard_map/ppermute | solution.py:50
  97.6 8.2 %collective-permute-start.22 = (bf16[256,256]{1,0:T(8,128)(2,1)S(1)}, bf16[256,256]{1,0:T(8,128)(2,1)S(1)}, u32[]{:S(2)}, u32[]{:S(2)}) collective-permute-start(bf16[256,256]{1,0:T(8,128)(2,1)S(1)} %add_convert_fusion.refs_0_), channel_id=1, source_target_pairs={{0,12},{4,8},{8,4},{12,0},{1,13},{5,9},{9,5},{13,1},{2,14},{6,10},... | collective-permute-start | bytes 393224 | tf_op jit(solution)/shard_map/ppermute | solution.py:50
  108.5 18.1 %collective-permute-start.23 = (bf16[384,512]{1,0:T(8,128)(2,1)S(1)}, bf16[384,512]{1,0:T(8,128)(2,1)S(1)}, u32[]{:S(2)}, u32[]{:S(2)}) collective-permute-start(bf16[384,512]{1,0:T(8,128)(2,1)S(1)} %slice.22), channel_id=1, source_target_pairs={{0,2},{1,3},{2,0},{3,1},{4,6},{5,7},{6,4},{7,5},{8,10},{9,11},{10,... | collective-permute-start | bytes 1179656 | tf_op jit(solution)/shard_map/ppermute | solution.py:50
  110.1 16.5 %collective-permute-start.24 = (bf16[384,512]{1,0:T(8,128)(2,1)S(1)}, bf16[384,512]{1,0:T(8,128)(2,1)S(1)}, u32[]{:S(2)}, u32[]{:S(2)}) collective-permute-start(bf16[384,512]{1,0:T(8,128)(2,1)S(1)} %slice.23), channel_id=1, source_target_pairs={{0,1},{1,0},{2,3},{3,2},{4,5},{5,4},{6,7},{7,6},{8,9},{9,8},{10,11... | collective-permute-start | bytes 1179656 | tf_op jit(solution)/shard_map/ppermute | solution.py:50
  112.3 12.6 %collective-permute-start.25 = (bf16[256,256]{1,0:T(8,128)(2,1)S(1)}, bf16[256,256]{1,0:T(8,128)(2,1)S(1)}, u32[]{:S(2)}, u32[]{:S(2)}) collective-permute-start(bf16[256,256]{1,0:T(8,128)(2,1)S(1)} %get-tuple-element.104.refs_0_), channel_id=1, source_target_pairs={{0,1},{1,0},{2,3},{3,2},{4,5},{5,4},{6,7},{7,6},{8,9},{9,8},{10,11... | collective-permute-start | bytes 393224 | tf_op jit(solution)/shard_map/ppermute | solution.py:50
  113.9 11.1 %collective-permute-start.26 = (bf16[256,256]{1,0:T(8,128)(2,1)S(1)}, bf16[256,256]{1,0:T(8,128)(2,1)S(1)}, u32[]{:S(2)}, u32[]{:S(2)}) collective-permute-start(bf16[256,256]{1,0:T(8,128)(2,1)S(1)} %get-tuple-element.104.refs_0_), channel_id=1, source_target_pairs={{0,2},{1,3},{2,0},{3,1},{4,6},{5,7},{6,4},{7,5},{8,10},{9,11},{10,... | collective-permute-start | bytes 393224 | tf_op jit(solution)/shard_map/ppermute | solution.py:50
  114.4 12.2 %collective-permute-start.27 = (bf16[256,256]{1,0:T(8,128)(2,1)S(1)}, bf16[256,256]{1,0:T(8,128)(2,1)S(1)}, u32[]{:S(2)}, u32[]{:S(2)}) collective-permute-start(bf16[256,256]{1,0:T(8,128)(2,1)S(1)} %get-tuple-element.104.refs_0_), channel_id=1, source_target_pairs={{0,3},{1,2},{2,1},{3,0},{4,7},{5,6},{6,5},{7,4},{8,11},{9,10},{10,... | collective-permute-start | bytes 393224 | tf_op jit(solution)/shard_map/ppermute | solution.py:50
  (19 other events, 173.2 us)

commit v8 on v7

--- a/solution.py
+++ b/solution.py
@@ -54,32 +54,37 @@
     return pl.ds(pl.multiple_of(start * IMGTOK, IMGTOK), IMGTOK)
 
 
-def project_body(m_ref, *refs):
-    *pairs, out_ref = refs
-    count = len(pairs) // 2
-    total = dot(pairs[0][...], pairs[count][...], NN)
-    for k in range(1, count):
-        total = total + dot(pairs[k][...], pairs[count + k][...], NN)
+def project_body(m_ref, d_ref, own_ref, x_ref, y_ref, weight_ref, out_ref, *slab_refs):
+    m = m_ref[0]
+    d = d_ref[0]
+    feats = own_ref.shape[1]
+    half = slab_refs[0].shape[0]
+
+    def rows(k, at, count):
+        return pl.ds(pl.multiple_of((m ^ k) * feats + at, half), count)
+
+    total = dot(own_ref[...], weight_ref[rows(0, 0, feats), :], NN)
+    for k, ref in ((1, x_ref), (2, y_ref)):
+        total = total + dot(ref[...], weight_ref[rows(k, 0, feats), :], NN)
     out_ref[...] = total
-
-
-def project(m, blocks, weights):
+    for k, side, ref in zip((1, 2, 3, 0, 0), (d, d, d, d, 1 - d), slab_refs):
+        ref[...] = weight_ref[rows(k, side * half, half), :]
+
+
+def project(m, d, blocks, weights):
     rows, feats = blocks[0].shape
     width = weights.shape[1]
-    block = pl.BlockSpec((rows, feats), lambda i, m: (0, 0))
-    chunk = lambda k: pl.BlockSpec((feats, width), lambda i, m: (m[0] ^ k, 0))
+    smem = pl.BlockSpec(memory_space=pltpu.SMEM)
+    vmem = pl.BlockSpec(memory_space=pltpu.VMEM)
+    slab = jax.ShapeDtypeStruct((feats // 2, width), weights.dtype)
     return pl.pallas_call(
         project_body,
-        grid_spec=pltpu.PrefetchScalarGridSpec(
-            num_scalar_prefetch=1,
-            grid=(1,),
-            in_specs=[block] * len(blocks) + [chunk(k) for k in range(len(blocks))],
-            out_specs=pl.BlockSpec((rows, width), lambda i, m: (0, 0)),
-        ),
-        out_shape=jax.ShapeDtypeStruct((rows, width), jnp.float32),
-        cost_estimate=cost(2 * len(blocks) * rows * feats * width, 4 * len(blocks) * feats * width),
-        compiler_params=params(),
-    )(m, *blocks, *[weights] * len(blocks))
+        in_specs=[smem, smem] + [vmem] * 4,
+        out_specs=[vmem] * 6,
+        out_shape=[jax.ShapeDtypeStruct((rows, width), jnp.float32)] + [slab] * 5,
+        cost_estimate=cost(6 * rows * feats * width, 4 * weights.size),
+        compiler_params=params(),
+    )(m, d, *blocks, weights)
 
 
 def pack_body(per_shard, m_ref, c_ref, place_ref, low_ref, high_ref, weight_ref, part_ref, *refs):
@@ -364,7 +369,7 @@
             ],
         ),
         out_shape=[jax.ShapeDtypeStruct((rows, cols), jnp.bfloat16), grad, prior_grad],
-        cost_estimate=cost(2 * 20 * cols * span * rows, 4 * queries.size * 2),
+        cost_estimate=cost(4 * 20 * cols * span * rows, 4 * queries.size * 2),
         compiler_params=params(),
     )(c, place, start[0, ::QTILE], start, queries, d_out, own, prior, *image)
 
@@ -562,7 +567,7 @@
     y = trade(states, "mp", 2)
     low = trade(x[: image_rows // 2], "mp", 2)
     high = trade(y[image_rows // 2 :], "mp", 1)
-    part = project(m1, [states, x, y], weights)
+    part, *slabs = project(m1, d1, [states, x, y], weights)
 
     prior_text = shift(text_kv[0], "ctx", 1)
     docs = doc_ids[0]
@@ -578,21 +583,13 @@
         m1, c1, place, low, high, weights, part, ranks, capacity, per_shard, mixed
     )
 
-    half = feats // 2
-
-    def slab(head, side):
-        return lax.dynamic_slice_in_dim(weights_late, head * feats + side * half, half)
-
-    weights_late, _, _ = lax.optimization_barrier((weights, x, y))
-    slabs = [slab(m ^ s, d) for s in steps]
-    own_slabs = [slab(m, d), slab(m, 1 - d)]
-    *both, _ = lax.optimization_barrier((*slabs, *own_slabs, packed[0]))
-    slabs, own_slabs = both[: len(slabs)], both[len(slabs) :]
+    *slabs, _ = lax.optimization_barrier((*slabs, packed[0]))
+    slabs, own_slabs = slabs[:3], slabs[3:]
     last = trade(slabs[2], "mp", 3)
 
     if mixed:
-        kept, *moved = slices(m1, c1, [states, x, y, low, high], feats // mps)
-        moved[2], _ = lax.optimization_barrier((moved[2], packed[0]))
+        c2, _ = lax.optimization_barrier((c1, packed[0]))
+        kept, *moved = slices(m1, c2, [states, x, y, low, high], feats // mps)
         moved[2] = trade(moved[2], "ctx", 3)
         image = [trade(packed[s], "ctx", s) if s else packed[0] for s in range(ranks)]
         moved[0], moved[1], slabs[0], slabs[1], *image = lax.optimization_barrier(
@@ -616,6 +613,7 @@
     far = [own_slabs[1]] + [swap(w, "dp") for w in near]
     grad = own_grad + shift(prior_grad, "ctx", -1).astype(jnp.float32)
     grad = grad.astype(jnp.bfloat16)
+    grad, far[1], far[2] = lax.optimization_barrier((grad, far[1], far[2]))
     if mixed:
         gathered = [trade(grad, "ctx", s) if s else grad for s in range(ranks)]
         base = jnp.concatenate(moved, axis=0)

time: 132 us -> 132 us (level); the launches traced: 133 us -> 131 us
  starting transfers between devices: 43.8 us -> 42.1 us
  local copies, waits for them, and re-layouts: 10.5 us -> 9.14 us
    ppermute x23, waiting for transfers between devices: 46.1 us -> 51.4 us  [trade(): return lax.ppermute(block, axis, [(i, i ^ step) for i in range(count)])]
    dynamic_slice x1 -> x0, local copies, waits for them, and re-layouts: 2.89 us -> none  [slab(): lax.dynamic_slice_in_dim(weights_late, head * feats + side * half, half)]
    ppermute x2, waiting for transfers between devices: 6.59 us -> 4.04 us  [shift(): return lax.ppermute(block, axis, route)]
    unnamed x28 -> x44, local copies, waits for them, and re-layouts: 5.6 us -> 8.07 us
    ppermute x5, waiting for transfers between devices: 2.27 us -> 0.13 us  [swap(): return lax.ppermute(block, axis, [(i, count - 1 - i) for i in range(count)])]
    ppermute x23, starting transfers between devices: 37.5 us -> 35.9 us  [trade(): return lax.ppermute(block, axis, [(i, i ^ step) for i in range(count)])]
  transfers between devices with their start and end apart: 30 -> 30, of which waited for: 12 -> 11; matrix products, arithmetic and copies ran while one was open for 4% -> 2% of each run, Pallas kernels for 13% -> 13%
where the time goes in v8:
time: 132 us; the launch traced here: 131 us
  waiting for transfers between devices  55.6 us (42%)
  starting transfers between devices  42.1 us (32%)
  Pallas kernels  22 us (17%)
  local copies, waits for them, and re-layouts  9.14 us (7%)
    ppermute x23, waiting for transfers between devices, trade(): return lax.ppermute(block, axis, [(i, i ^ step) for i in range(count)])  51.4 us
    ppermute x23, starting transfers between devices, trade(): return lax.ppermute(block, axis, [(i, i ^ step) for i in range(count)])  35.9 us
    pallas_call x1, Pallas kernels, attention(): pl.pallas_call(functools.partial(attention_body, per_shard, images), grid...  10.2 us
    unnamed x44, local copies, waits for them, and re-layouts  8.07 us
    ppermute x2, starting transfers between devices, shift(): return lax.ppermute(block, axis, route)  5.09 us
    ppermute x2, waiting for transfers between devices, shift(): return lax.ppermute(block, axis, route)  4.04 us
    pallas_call x1, Pallas kernels, image_term(): pl.pallas_call(image_body, grid_spec=pltpu.PrefetchScalarGridSpec(num_sca...  2.91 us
  transfers between devices with their start and end apart: 30, of which 11 were waited for; matrix products, arithmetic and copies ran while one was open for 2% of the time, Pallas kernels for 13%

profile of v8, /device:TPU:0, one launch (start us, length us, event | category | flops | bytes accessed | tf_op | source)
XLA Modules:
  0.0 130.9 jit_solution(8379362367869901591)
XLA Ops:
  0.6 3.0 %collective-permute-start = (bf16[256,2048]{1,0:T(8,128)(2,1)}, bf16[256,2048]{1,0:T(8,128)(2,1)S(1)}, u32[]{:S(2)}, u32[]{:S(2)}) collective-permute-start(bf16[256,2048]{1,0:T(8,128)(2,1)} %bitcast.26), channel_id=1, source_target_pairs={{0,1},{1,0},{2,3},{3,2},{4,5},{5,4},{6,7},{7,6},{8,9},{9,8},{10,11... | collective-permute-start | bytes 3145736 | tf_op jit(solution)/shard_map/ppermute | solution.py:50
  3.6 1.5 %collective-permute-start.2 = (bf16[256,2048]{1,0:T(8,128)(2,1)}, bf16[256,2048]{1,0:T(8,128)(2,1)S(1)}, u32[]{:S(2)}, u32[]{:S(2)}) collective-permute-start(bf16[256,2048]{1,0:T(8,128)(2,1)} %bitcast.27), channel_id=1, source_target_pairs={{0,2},{1,3},{2,0},{3,1},{4,6},{5,7},{6,4},{7,5},{8,10},{9,11},{10,... | collective-permute-start | bytes 3145736 | tf_op jit(solution)/shard_map/ppermute | solution.py:50
  5.2 3.5 %collective-permute-start.4 = (bf16[512,256]{1,0:T(8,128)(2,1)}, bf16[512,256]{1,0:T(8,128)(2,1)S(1)}, u32[]{:S(2)}, u32[]{:S(2)}) collective-permute-start(bf16[512,256]{1,0:T(8,128)(2,1)} %bitcast.36), channel_id=1, source_target_pairs={{0,4},{4,8},{8,12},{1,5},{5,9},{9,13},{2,6},{6,10},{10,14},{3,7},{... | collective-permute-start | bytes 786440 | tf_op jit(solution)/shard_map/ppermute | solution.py:36
  10.3 16.7 %collective-permute-done.x_ref = bf16[256,2048]{1,0:T(8,128)(2,1)S(1)} collective-permute-done((bf16[256,2048]{1,0:T(8,128)(2,1)}, bf16[256,2048]{1,0:T(8,128)(2,1)S(1)}, u32[]{:S(2)}, u32[]{:S(2)}) %collective-permute-start) | collective-permute-done | bytes 1048608 | tf_op jit(solution)/shard_map/ppermute | solution.py:50
  27.1 1.8 %collective-permute-start.1 = (bf16[128,2048]{1,0:T(8,128)(2,1)S(1)}, bf16[128,2048]{1,0:T(8,128)(2,1)S(1)}, u32[]{:S(2)}, u32[]{:S(2)}) collective-permute-start(bf16[128,2048]{1,0:T(8,128)(2,1)S(1)} %slice.24), channel_id=1, source_target_pairs={{0,2},{1,3},{2,0},{3,1},{4,6},{5,7},{6,4},{7,5},{8,10},{9,11},{10,... | collective-permute-start | bytes 1572872 | tf_op jit(solution)/shard_map/ppermute | solution.py:50
  28.9 1.6 %collective-permute-start.3 = (bf16[128,2048]{1,0:T(8,128)(2,1)S(1)}, bf16[128,2048]{1,0:T(8,128)(2,1)S(1)}, u32[]{:S(2)}, u32[]{:S(2)}) collective-permute-start(bf16[128,2048]{1,0:T(8,128)(2,1)S(1)} %slice.25), channel_id=1, source_target_pairs={{0,1},{1,0},{2,3},{3,2},{4,5},{5,4},{6,7},{7,6},{8,9},{9,8},{10,11... | collective-permute-start | bytes 1572872 | tf_op jit(solution)/shard_map/ppermute | solution.py:50
  30.8 2.2 %copy-done = bf16[1,8192,256]{2,1,0:T(8,128)(2,1)S(1)} copy-done((bf16[1,8192,256]{2,1,0:T(8,128)(2,1)S(1)}, bf16[1,8192,256]{2,1,0:T(8,128)(2,1)}, u32[]{:S(2)}) %copy-start) | copy-done | bytes 4194328
  34.2 6.0 %collective-permute-done.1.low_ref = bf16[128,2048]{1,0:T(8,128)(2,1)S(1)} collective-permute-done((bf16[128,2048]{1,0:T(8,128)(2,1)S(1)}, bf16[128,2048]{1,0:T(8,128)(2,1)S(1)}, u32[]{:S(2)}, u32[]{:S(2)}) %collective-permute-start.1) | collective-permute-done | bytes 524320 | tf_op jit(solution)/shard_map/ppermute | solution.py:50
  41.5 2.0 %shard_map.95 = (bf16[2,64,256]{2,1,0:T(8,128)(2,1)S(1)}, bf16[2,64,256]{2,1,0:T(8,128)(2,1)}, bf16[2,64,256]{2,1,0:T(8,128)(2,1)}, bf16[2,64,256]{2,1,0:T(8,128)(2,1)S(1)}) custom-call(s32[1]{0:T(128)} %bitcast.10.m_ref, s32[1]{0:T(128)} %bitcast.c_ref, s32[64]{0:T(128)S(1)} %and_select_fusion.place_ref, ...), custom_call_target="tpu_custom_call" | custom-call | flops 268435456 | bytes 1048576 | tf_op jit(solution)/shard_map/pallas_call | solution.py:134
  46.9 3.6 %collective-permute-start.13 = (bf16[256,512]{1,0:T(8,128)(2,1)}, bf16[256,512]{1,0:T(8,128)(2,1)S(1)}, u32[]{:S(2)}, u32[]{:S(2)}) collective-permute-start(bf16[256,512]{1,0:T(8,128)(2,1)} %get-tuple-element.99), channel_id=1, source_target_pairs={{0,12},{4,8},{8,4},{12,0},{1,13},{5,9},{9,5},{13,1},{2,14},{6,10},... | collective-permute-start | bytes 786440 | tf_op jit(solution)/shard_map/ppermute | solution.py:50
  51.3 3.6 %collective-permute-start.7 = (bf16[2,64,256]{2,1,0:T(8,128)(2,1)S(1)}, bf16[2,64,256]{2,1,0:T(8,128)(2,1)S(1)}, u32[]{:S(2)}, u32[]{:S(2)}) collective-permute-start(bf16[2,64,256]{2,1,0:T(8,128)(2,1)S(1)} %get-tuple-element.87), channel_id=1, source_target_pairs={{0,12},{4,8},{8,4},{12,0},{1,13},{5,9},{9,5},{13,1},{2,14},{6,10},... | collective-permute-start | bytes 196616 | tf_op jit(solution)/shard_map/ppermute | solution.py:50
  57.6 7.0 %collective-permute-done.6.refs_2_ = bf16[2,64,256]{2,1,0:T(8,128)(2,1)S(1)} collective-permute-done((bf16[2,64,256]{2,1,0:T(8,128)(2,1)}, bf16[2,64,256]{2,1,0:T(8,128)(2,1)S(1)}, u32[]{:S(2)}, u32[]{:S(2)}) %collective-permute-start.6) | collective-permute-done | bytes 65568 | tf_op jit(solution)/shard_map/ppermute | solution.py:50
  64.6 1.5 %collective-permute-start.8 = (bf16[1024,256]{1,0:T(8,128)(2,1)}, bf16[1024,256]{1,0:T(8,128)(2,1)S(1)}, u32[]{:S(2)}, u32[]{:S(2)}) collective-permute-start(bf16[1024,256]{1,0:T(8,128)(2,1)} %copy-done.12), channel_id=1, source_target_pairs={{0,1},{1,0},{2,3},{3,2},{4,5},{5,4},{6,7},{7,6},{8,9},{9,8},{10,11... | collective-permute-start | bytes 1572872 | tf_op jit(solution)/shard_map/ppermute | solution.py:50
  67.9 1.8 %collective-permute-start.12 = (bf16[256,512]{1,0:T(8,128)(2,1)}, bf16[256,512]{1,0:T(8,128)(2,1)S(1)}, u32[]{:S(2)}, u32[]{:S(2)}) collective-permute-start(bf16[256,512]{1,0:T(8,128)(2,1)} %copy-done.17), channel_id=1, source_target_pairs={{0,8},{4,12},{8,0},{12,4},{1,9},{5,13},{9,1},{13,5},{2,10},{6,14},... | collective-permute-start | bytes 786440 | tf_op jit(solution)/shard_map/ppermute | solution.py:50
  73.1 10.2 %shard_map.97 = (bf16[512,1024]{1,0:T(8,128)(2,1)}, f32[256,256]{1,0:T(8,128)S(1)}, bf16[256,256]{1,0:T(8,128)(2,1)S(1)}) custom-call(s32[1]{0:T(128)} %bitcast.c_ref, s32[64]{0:T(128)S(1)} %and_select_fusion.place_ref, s32[4]{0:T(128)S(1)} %bitcast.38, s32[1,512]{1,0:T(1,128)S(1)} %bitcast.33, bf16[512,1024]{1,0:T(8,128)(2,1)S(1)} %bitcast.34, ...), custom_call_target="tpu_custom_call" | custom-call | flops 26843545600 | bytes 4194304 | tf_op jit(solution)/shard_map/pallas_call | solution.py:349
  83.4 1.6 %collective-permute-start.16 = (bf16[256,256]{1,0:T(8,128)(2,1)S(1)}, bf16[256,256]{1,0:T(8,128)(2,1)S(1)}, u32[]{:S(2)}, u32[]{:S(2)}) collective-permute-start(bf16[256,256]{1,0:T(8,128)(2,1)S(1)} %get-tuple-element.105), channel_id=1, source_target_pairs={{4,0},{8,4},{12,8},{5,1},{9,5},{13,9},{6,2},{10,6},{14,10},{7,3},{... | collective-permute-start | bytes 393224 | tf_op jit(solution)/shard_map/ppermute | solution.py:36
  87.7 4.0 %collective-permute-done.16 = bf16[256,256]{1,0:T(8,128)(2,1)S(1)} collective-permute-done((bf16[256,256]{1,0:T(8,128)(2,1)S(1)}, bf16[256,256]{1,0:T(8,128)(2,1)S(1)}, u32[]{:S(2)}, u32[]{:S(2)}) %collective-permute-start.16) | collective-permute-done | bytes 131104 | tf_op jit(solution)/shard_map/ppermute | solution.py:36
  91.8 2.1 %collective-permute-start.20 = (bf16[256,256]{1,0:T(8,128)(2,1)S(1)}, bf16[256,256]{1,0:T(8,128)(2,1)S(1)}, u32[]{:S(2)}, u32[]{:S(2)}) collective-permute-start(bf16[256,256]{1,0:T(8,128)(2,1)S(1)} %add_convert_fusion.refs_0_), channel_id=1, source_target_pairs={{0,4},{4,0},{8,12},{12,8},{1,5},{5,1},{9,13},{13,9},{2,6},{6,2},{1... | collective-permute-start | bytes 393224 | tf_op jit(solution)/shard_map/ppermute | solution.py:50
  93.9 3.4 %collective-permute-start.21 = (bf16[256,256]{1,0:T(8,128)(2,1)S(1)}, bf16[256,256]{1,0:T(8,128)(2,1)S(1)}, u32[]{:S(2)}, u32[]{:S(2)}) collective-permute-start(bf16[256,256]{1,0:T(8,128)(2,1)S(1)} %add_convert_fusion.refs_0_), channel_id=1, source_target_pairs={{0,8},{4,12},{8,0},{12,4},{1,9},{5,13},{9,1},{13,5},{2,10},{6,14},... | collective-permute-start | bytes 393224 | tf_op jit(solution)/shard_map/ppermute | solution.py:50
  98.0 9.2 %collective-permute-done.21.refs_2_ = bf16[256,256]{1,0:T(8,128)(2,1)S(1)} collective-permute-done((bf16[256,256]{1,0:T(8,128)(2,1)S(1)}, bf16[256,256]{1,0:T(8,128)(2,1)S(1)}, u32[]{:S(2)}, u32[]{:S(2)}) %collective-permute-start.21) | collective-permute-done | bytes 131104 | tf_op jit(solution)/shard_map/ppermute | solution.py:50
  109.5 1.7 %shard_map.98 = (bf16[1024,256]{1,0:T(8,128)(2,1)S(1)}, bf16[256,256]{1,0:T(8,128)(2,1)S(1)}) custom-call(s32[1]{0:T(128)} %bitcast.c_ref, s32[64]{0:T(128)S(1)} %and_select_fusion.place_ref, bf16[256,256]{1,0:T(8,128)(2,1)S(1)} %add_convert_fusion.refs_0_, bf16[256,256]{1,0:T(8,128)(2,1)S(1)} %collective-permute-done.20.refs_1_, ...), custom_call_target="tpu_custom_call" | custom-call | bytes 2097152 | tf_op jit(solution)/shard_map/pallas_call | solution.py:407
  114.7 8.0 %collective-permute-done.25.refs_1_ = bf16[256,256]{1,0:T(8,128)(2,1)S(1)} collective-permute-done((bf16[256,256]{1,0:T(8,128)(2,1)S(1)}, bf16[256,256]{1,0:T(8,128)(2,1)S(1)}, u32[]{:S(2)}, u32[]{:S(2)}) %collective-permute-start.25) | collective-permute-done | bytes 131104 | tf_op jit(solution)/shard_map/ppermute | solution.py:50
  126.3 2.9 %shard_map.99 = bf16[256,2048]{1,0:T(8,128)(2,1)} custom-call(s32[1]{0:T(128)} %bitcast.12.d_ref, bf16[256,256]{1,0:T(8,128)(2,1)S(1)} %get-tuple-element.120.refs_0_, bf16[256,256]{1,0:T(8,128)(2,1)S(1)} %collective-permute-done.25.refs_1_, bf16[256,256]{1,0:T(8,128)(2,1)S(1)} %collective-permute-done.26.refs_2_, ...), custom_call_target="tpu_custom_call" | custom-call | flops 1073741824 | bytes 8388608 | tf_op jit(solution)/shard_map/pallas_call | solution.py:530
  129.4 1.5 %shard_map.102 = f32[2048,256]{1,0:T(8,128)} custom-call(s32[1]{0:T(128)} %bitcast.10.m_ref, f32[3,512,256]{2,1,0:T(8,128)S(1)} %shard_map.100.refs_0_, f32[1,512,256]{2,1,0:T(8,128)S(1)} %shard_map.101.refs_1_, f32[3,512,256]{2,1,0:T(8,128)S(1)} %collective-permute-done.28.refs_2_, f32[1,512,256]{2,1,0:T(8,128)S(1)} %collective-permute-done.29.refs_3_), custom_call_target="tpu_custom_call" | custom-call | bytes 6291456 | tf_op jit(solution)/shard_map/pallas_call | solution.py:497
  (101 shorter events, 29.4 us)
Async XLA Ops:
  0.6 26.4 %collective-permute-start = (bf16[256,2048]{1,0:T(8,128)(2,1)}, bf16[256,2048]{1,0:T(8,128)(2,1)S(1)}, u32[]{:S(2)}, u32[]{:S(2)}) collective-permute-start(bf16[256,2048]{1,0:T(8,128)(2,1)} %bitcast.26), channel_id=1, source_target_pairs={{0,1},{1,0},{2,3},{3,2},{4,5},{5,4},{6,7},{7,6},{8,9},{9,8},{10,11... | collective-permute-start | bytes 3145736 | tf_op jit(solution)/shard_map/ppermute | solution.py:50
  3.6 25.2 %collective-permute-start.2 = (bf16[256,2048]{1,0:T(8,128)(2,1)}, bf16[256,2048]{1,0:T(8,128)(2,1)S(1)}, u32[]{:S(2)}, u32[]{:S(2)}) collective-permute-start(bf16[256,2048]{1,0:T(8,128)(2,1)} %bitcast.27), channel_id=1, source_target_pairs={{0,2},{1,3},{2,0},{3,1},{4,6},{5,7},{6,4},{7,5},{8,10},{9,11},{10,... | collective-permute-start | bytes 3145736 | tf_op jit(solution)/shard_map/ppermute | solution.py:50
  5.2 29.0 %collective-permute-start.4 = (bf16[512,256]{1,0:T(8,128)(2,1)}, bf16[512,256]{1,0:T(8,128)(2,1)S(1)}, u32[]{:S(2)}, u32[]{:S(2)}) collective-permute-start(bf16[512,256]{1,0:T(8,128)(2,1)} %bitcast.36), channel_id=1, source_target_pairs={{0,4},{4,8},{8,12},{1,5},{5,9},{9,13},{2,6},{6,10},{10,14},{3,7},{... | collective-permute-start | bytes 786440 | tf_op jit(solution)/shard_map/ppermute | solution.py:36
  27.1 13.2 %collective-permute-start.1 = (bf16[128,2048]{1,0:T(8,128)(2,1)S(1)}, bf16[128,2048]{1,0:T(8,128)(2,1)S(1)}, u32[]{:S(2)}, u32[]{:S(2)}) collective-permute-start(bf16[128,2048]{1,0:T(8,128)(2,1)S(1)} %slice.24), channel_id=1, source_target_pairs={{0,2},{1,3},{2,0},{3,1},{4,6},{5,7},{6,4},{7,5},{8,10},{9,11},{10,... | collective-permute-start | bytes 1572872 | tf_op jit(solution)/shard_map/ppermute | solution.py:50
  28.9 12.6 %collective-permute-start.3 = (bf16[128,2048]{1,0:T(8,128)(2,1)S(1)}, bf16[128,2048]{1,0:T(8,128)(2,1)S(1)}, u32[]{:S(2)}, u32[]{:S(2)}) collective-permute-start(bf16[128,2048]{1,0:T(8,128)(2,1)S(1)} %slice.25), channel_id=1, source_target_pairs={{0,1},{1,0},{2,3},{3,2},{4,5},{5,4},{6,7},{7,6},{8,9},{9,8},{10,11... | collective-permute-start | bytes 1572872 | tf_op jit(solution)/shard_map/ppermute | solution.py:50
  46.9 21.0 %collective-permute-start.13 = (bf16[256,512]{1,0:T(8,128)(2,1)}, bf16[256,512]{1,0:T(8,128)(2,1)S(1)}, u32[]{:S(2)}, u32[]{:S(2)}) collective-permute-start(bf16[256,512]{1,0:T(8,128)(2,1)} %get-tuple-element.99), channel_id=1, source_target_pairs={{0,12},{4,8},{8,4},{12,0},{1,13},{5,9},{9,5},{13,1},{2,14},{6,10},... | collective-permute-start | bytes 786440 | tf_op jit(solution)/shard_map/ppermute | solution.py:50
  50.5 7.1 %collective-permute-start.5 = (bf16[2,64,256]{2,1,0:T(8,128)(2,1)}, bf16[2,64,256]{2,1,0:T(8,128)(2,1)S(1)}, u32[]{:S(2)}, u32[]{:S(2)}) collective-permute-start(bf16[2,64,256]{2,1,0:T(8,128)(2,1)} %get-tuple-element.85), channel_id=1, source_target_pairs={{0,4},{4,0},{8,12},{12,8},{1,5},{5,1},{9,13},{13,9},{2,6},{6,2},{1... | collective-permute-start | bytes 196616 | tf_op jit(solution)/shard_map/ppermute | solution.py:50
  50.5 14.1 %collective-permute-start.6 = (bf16[2,64,256]{2,1,0:T(8,128)(2,1)}, bf16[2,64,256]{2,1,0:T(8,128)(2,1)S(1)}, u32[]{:S(2)}, u32[]{:S(2)}) collective-permute-start(bf16[2,64,256]{2,1,0:T(8,128)(2,1)} %get-tuple-element.86), channel_id=1, source_target_pairs={{0,8},{4,12},{8,0},{12,4},{1,9},{5,13},{9,1},{13,5},{2,10},{6,14},... | collective-permute-start | bytes 196616 | tf_op jit(solution)/shard_map/ppermute | solution.py:50
  51.3 13.3 %collective-permute-start.7 = (bf16[2,64,256]{2,1,0:T(8,128)(2,1)S(1)}, bf16[2,64,256]{2,1,0:T(8,128)(2,1)S(1)}, u32[]{:S(2)}, u32[]{:S(2)}) collective-permute-start(bf16[2,64,256]{2,1,0:T(8,128)(2,1)S(1)} %get-tuple-element.87), channel_id=1, source_target_pairs={{0,12},{4,8},{8,4},{12,0},{1,13},{5,9},{9,5},{13,1},{2,14},{6,10},... | collective-permute-start | bytes 196616 | tf_op jit(solution)/shard_map/ppermute | solution.py:50
  55.0 28.3 %collective-permute-start.10 = (bf16[1024,256]{1,0:T(8,128)(2,1)}, bf16[1024,256]{1,0:T(8,128)(2,1)S(1)}, u32[]{:S(2)}, u32[]{:S(2)}) collective-permute-start(bf16[1024,256]{1,0:T(8,128)(2,1)} %copy-done.13), channel_id=1, source_target_pairs={{0,3},{1,2},{2,1},{3,0},{4,7},{5,6},{6,5},{7,4},{8,11},{9,10},{10,... | collective-permute-start | bytes 1572872 | tf_op jit(solution)/shard_map/ppermute | solution.py:50
  64.6 18.7 %collective-permute-start.8 = (bf16[1024,256]{1,0:T(8,128)(2,1)}, bf16[1024,256]{1,0:T(8,128)(2,1)S(1)}, u32[]{:S(2)}, u32[]{:S(2)}) collective-permute-start(bf16[1024,256]{1,0:T(8,128)(2,1)} %copy-done.12), channel_id=1, source_target_pairs={{0,1},{1,0},{2,3},{3,2},{4,5},{5,4},{6,7},{7,6},{8,9},{9,8},{10,11... | collective-permute-start | bytes 1572872 | tf_op jit(solution)/shard_map/ppermute | solution.py:50
  66.1 17.2 %collective-permute-start.9 = (bf16[1024,256]{1,0:T(8,128)(2,1)}, bf16[1024,256]{1,0:T(8,128)(2,1)S(1)}, u32[]{:S(2)}, u32[]{:S(2)}) collective-permute-start(bf16[1024,256]{1,0:T(8,128)(2,1)} %copy-done.11), channel_id=1, source_target_pairs={{0,2},{1,3},{2,0},{3,1},{4,6},{5,7},{6,4},{7,5},{8,10},{9,11},{10,... | collective-permute-start | bytes 1572872 | tf_op jit(solution)/shard_map/ppermute | solution.py:50
  66.6 16.7 %collective-permute-start.11 = (bf16[256,512]{1,0:T(8,128)(2,1)}, bf16[256,512]{1,0:T(8,128)(2,1)S(1)}, u32[]{:S(2)}, u32[]{:S(2)}) collective-permute-start(bf16[256,512]{1,0:T(8,128)(2,1)} %copy-done.18), channel_id=1, source_target_pairs={{0,4},{4,0},{8,12},{12,8},{1,5},{5,1},{9,13},{13,9},{2,6},{6,2},{1... | collective-permute-start | bytes 786440 | tf_op jit(solution)/shard_map/ppermute | solution.py:50
  67.9 15.4 %collective-permute-start.12 = (bf16[256,512]{1,0:T(8,128)(2,1)}, bf16[256,512]{1,0:T(8,128)(2,1)S(1)}, u32[]{:S(2)}, u32[]{:S(2)}) collective-permute-start(bf16[256,512]{1,0:T(8,128)(2,1)} %copy-done.17), channel_id=1, source_target_pairs={{0,8},{4,12},{8,0},{12,4},{1,9},{5,13},{9,1},{13,5},{2,10},{6,14},... | collective-permute-start | bytes 786440 | tf_op jit(solution)/shard_map/ppermute | solution.py:50
  83.4 8.3 %collective-permute-start.16 = (bf16[256,256]{1,0:T(8,128)(2,1)S(1)}, bf16[256,256]{1,0:T(8,128)(2,1)S(1)}, u32[]{:S(2)}, u32[]{:S(2)}) collective-permute-start(bf16[256,256]{1,0:T(8,128)(2,1)S(1)} %get-tuple-element.105), channel_id=1, source_target_pairs={{4,0},{8,4},{12,8},{5,1},{9,5},{13,9},{6,2},{10,6},{14,10},{7,3},{... | collective-permute-start | bytes 393224 | tf_op jit(solution)/shard_map/ppermute | solution.py:36
  85.0 22.2 %collective-permute-start.14 = (bf16[768,512]{1,0:T(8,128)(2,1)S(1)}, bf16[768,512]{1,0:T(8,128)(2,1)S(1)}, u32[]{:S(2)}, u32[]{:S(2)}) collective-permute-start(bf16[768,512]{1,0:T(8,128)(2,1)S(1)} %constant_dynamic-update-slice_fusion.refs_0_), channel_id=1, source_target_pairs={{0,1},{1,0},{2,3},{3,2},{4,5},{5,4},{6,7},{7,6},{8,9},{9,8},{10,11... | collective-permute-start | bytes 2359304 | tf_op jit(solution)/shard_map/ppermute | solution.py:50
  86.2 21.1 %collective-permute-start.15 = (bf16[768,512]{1,0:T(8,128)(2,1)S(1)}, bf16[768,512]{1,0:T(8,128)(2,1)S(1)}, u32[]{:S(2)}, u32[]{:S(2)}) collective-permute-start(bf16[768,512]{1,0:T(8,128)(2,1)S(1)} %constant_dynamic-update-slice_fusion.refs_0_), channel_id=1, source_target_pairs={{0,2},{1,3},{2,0},{3,1},{4,6},{5,7},{6,4},{7,5},{8,10},{9,11},{10,... | collective-permute-start | bytes 2359304 | tf_op jit(solution)/shard_map/ppermute | solution.py:50
  93.9 13.4 %collective-permute-start.21 = (bf16[256,256]{1,0:T(8,128)(2,1)S(1)}, bf16[256,256]{1,0:T(8,128)(2,1)S(1)}, u32[]{:S(2)}, u32[]{:S(2)}) collective-permute-start(bf16[256,256]{1,0:T(8,128)(2,1)S(1)} %add_convert_fusion.refs_0_), channel_id=1, source_target_pairs={{0,8},{4,12},{8,0},{12,4},{1,9},{5,13},{9,1},{13,5},{2,10},{6,14},... | collective-permute-start | bytes 393224 | tf_op jit(solution)/shard_map/ppermute | solution.py:50
  97.3 9.9 %collective-permute-start.22 = (bf16[256,256]{1,0:T(8,128)(2,1)S(1)}, bf16[256,256]{1,0:T(8,128)(2,1)S(1)}, u32[]{:S(2)}, u32[]{:S(2)}) collective-permute-start(bf16[256,256]{1,0:T(8,128)(2,1)S(1)} %add_convert_fusion.refs_0_), channel_id=1, source_target_pairs={{0,12},{4,8},{8,4},{12,0},{1,13},{5,9},{9,5},{13,1},{2,14},{6,10},... | collective-permute-start | bytes 393224 | tf_op jit(solution)/shard_map/ppermute | solution.py:50
  107.3 16.8 %collective-permute-start.23 = (bf16[384,512]{1,0:T(8,128)(2,1)S(1)}, bf16[384,512]{1,0:T(8,128)(2,1)S(1)}, u32[]{:S(2)}, u32[]{:S(2)}) collective-permute-start(bf16[384,512]{1,0:T(8,128)(2,1)S(1)} %slice.22), channel_id=1, source_target_pairs={{0,2},{1,3},{2,0},{3,1},{4,6},{5,7},{6,4},{7,5},{8,10},{9,11},{10,... | collective-permute-start | bytes 1179656 | tf_op jit(solution)/shard_map/ppermute | solution.py:50
  108.4 15.6 %collective-permute-start.24 = (bf16[384,512]{1,0:T(8,128)(2,1)S(1)}, bf16[384,512]{1,0:T(8,128)(2,1)S(1)}, u32[]{:S(2)}, u32[]{:S(2)}) collective-permute-start(bf16[384,512]{1,0:T(8,128)(2,1)S(1)} %slice.23), channel_id=1, source_target_pairs={{0,1},{1,0},{2,3},{3,2},{4,5},{5,4},{6,7},{7,6},{8,9},{9,8},{10,11... | collective-permute-start | bytes 1179656 | tf_op jit(solution)/shard_map/ppermute | solution.py:50
  111.1 11.6 %collective-permute-start.25 = (bf16[256,256]{1,0:T(8,128)(2,1)S(1)}, bf16[256,256]{1,0:T(8,128)(2,1)S(1)}, u32[]{:S(2)}, u32[]{:S(2)}) collective-permute-start(bf16[256,256]{1,0:T(8,128)(2,1)S(1)} %get-tuple-element.120.refs_0_), channel_id=1, source_target_pairs={{0,1},{1,0},{2,3},{3,2},{4,5},{5,4},{6,7},{7,6},{8,9},{9,8},{10,11... | collective-permute-start | bytes 393224 | tf_op jit(solution)/shard_map/ppermute | solution.py:50
  112.3 10.5 %collective-permute-start.26 = (bf16[256,256]{1,0:T(8,128)(2,1)S(1)}, bf16[256,256]{1,0:T(8,128)(2,1)S(1)}, u32[]{:S(2)}, u32[]{:S(2)}) collective-permute-start(bf16[256,256]{1,0:T(8,128)(2,1)S(1)} %get-tuple-element.120.refs_0_), channel_id=1, source_target_pairs={{0,2},{1,3},{2,0},{3,1},{4,6},{5,7},{6,4},{7,5},{8,10},{9,11},{10,... | collective-permute-start | bytes 393224 | tf_op jit(solution)/shard_map/ppermute | solution.py:50
  113.2 10.8 %collective-permute-start.27 = (bf16[256,256]{1,0:T(8,128)(2,1)S(1)}, bf16[256,256]{1,0:T(8,128)(2,1)S(1)}, u32[]{:S(2)}, u32[]{:S(2)}) collective-permute-start(bf16[256,256]{1,0:T(8,128)(2,1)S(1)} %get-tuple-element.120.refs_0_), channel_id=1, source_target_pairs={{0,3},{1,2},{2,1},{3,0},{4,7},{5,6},{6,5},{7,4},{8,11},{9,10},{10,... | collective-permute-start | bytes 393224 | tf_op jit(solution)/shard_map/ppermute | solution.py:50
  (27 other events, 214.7 us)

commit v9 on v8

--- a/solution.py
+++ b/solution.py
@@ -197,7 +197,6 @@
     images,
     c_ref,
     place_ref,
-    first_ref,
     start_ref,
     q_ref,
     g_ref,
@@ -302,7 +301,7 @@
         total[pl.ds(base, span), hd:] += dot(probs[:span, :], stack(g_ref, 0, heads), NN)
 
     full = rows + QTILE
-    need = full - (first_ref[t] - first)
+    need = full - (jnp.min(start_ref[...]) - first)
     below = 0
     for span in sorted({min(b * QTILE, full) for b in SPANS} | {full}):
         lower, below = below, span
@@ -349,7 +348,7 @@
     return pl.pallas_call(
         functools.partial(attention_body, per_shard, images),
         grid_spec=pltpu.PrefetchScalarGridSpec(
-            num_scalar_prefetch=3,
+            num_scalar_prefetch=2,
             grid=(tiles,),
             in_specs=[
                 pl.BlockSpec((1, QTILE), lambda t, *_: (0, t)),
@@ -369,9 +368,9 @@
             ],
         ),
         out_shape=[jax.ShapeDtypeStruct((rows, cols), jnp.bfloat16), grad, prior_grad],
-        cost_estimate=cost(4 * 20 * cols * span * rows, 4 * queries.size * 2),
-        compiler_params=params(),
-    )(c, place, start[0, ::QTILE], start, queries, d_out, own, prior, *image)
+        cost_estimate=cost(2 * 20 * cols * span * rows, 4 * queries.size * 2),
+        compiler_params=params(),
+    )(c, place, start, queries, d_out, own, prior, *image)
 
 
 def reorder_body(per_shard, images, c_ref, place_ref, *refs):
@@ -585,35 +584,36 @@
 
     *slabs, _ = lax.optimization_barrier((*slabs, packed[0]))
     slabs, own_slabs = slabs[:3], slabs[3:]
-    last = trade(slabs[2], "mp", 3)
+    near = [trade(slabs[0], "mp", 1), None, trade(slabs[2], "mp", 3)]
 
     if mixed:
         c2, _ = lax.optimization_barrier((c1, packed[0]))
         kept, *moved = slices(m1, c2, [states, x, y, low, high], feats // mps)
-        moved[2] = trade(moved[2], "ctx", 3)
         image = [trade(packed[s], "ctx", s) if s else packed[0] for s in range(ranks)]
-        moved[0], moved[1], slabs[0], slabs[1], *image = lax.optimization_barrier(
-            (moved[0], moved[1], slabs[0], slabs[1], *image)
-        )
-        moved = [trade(moved[0], "ctx", 1), trade(moved[1], "ctx", 2), moved[2]]
+        both = lax.optimization_barrier((*moved, *image))
+        moved, image = both[: len(moved)], both[len(moved) :]
+        moved = [trade(moved[s - 1], "ctx", s) for s in range(1, ranks)]
     else:
         image = [exchange(packed[0], "ctx")]
         whole = lax.all_gather(states, "mp", axis=1, tiled=True)
         moved = whole.reshape(image_rows, ranks, mps, -1)
         moved = lax.dynamic_index_in_dim(moved, m, axis=2, keepdims=False).transpose(1, 0, 2)
         moved = [exchange(moved, "ctx").reshape(ranks * image_rows, -1)]
-    near = [trade(slabs[0], "mp", 1), trade(slabs[1], "mp", 2), last]
 
     attn_out, own_grad, prior_grad = attention(
         c1, place, start, queries[0], d_out[0], text_kv[0], prior_text, image,
         images, per_shard, image_rows,
     )
-    prior_grad, *both = lax.optimization_barrier((prior_grad, *near, *moved))
-    near, moved = both[: len(near)], both[len(near) :]
-    far = [own_slabs[1]] + [swap(w, "dp") for w in near]
+    early = ranks // 2 if mixed else 1
+    prior_grad, slabs[1], near[0], near[2], *both = lax.optimization_barrier(
+        (prior_grad, slabs[1], near[0], near[2], *moved[:early])
+    )
+    moved = both + list(moved[early:])
+    near[1] = trade(slabs[1], "mp", 2)
+    far = [own_slabs[1], swap(near[0], "dp"), None, swap(near[2], "dp")]
     grad = own_grad + shift(prior_grad, "ctx", -1).astype(jnp.float32)
     grad = grad.astype(jnp.bfloat16)
-    grad, far[1], far[2] = lax.optimization_barrier((grad, far[1], far[2]))
+    grad, far[1], far[3] = lax.optimization_barrier((grad, far[1], far[3]))
     if mixed:
         gathered = [trade(grad, "ctx", s) if s else grad for s in range(ranks)]
         base = jnp.concatenate(moved, axis=0)
@@ -623,16 +623,15 @@
     else:
         gathered = [exchange(jnp.broadcast_to(grad, (ranks,) + grad.shape), "ctx")]
         all_states = lax.all_gather(moved[0], "mp", axis=0)
-        base_x = base_y = all_states
-    base_x, base_y, *both = lax.optimization_barrier((base_x, base_y, *far, *gathered))
-    far, gathered = both[: len(far)], both[len(far) :]
+    near[1], *gathered = lax.optimization_barrier((near[1], *gathered))
+    far[2] = swap(near[1], "dp")
     by_rank, mine = reorder(c1, place, gathered, per_shard, images, ranks)
     head_grad = [mine] + [trade(mine, "mp", s) for s in steps]
     if mixed:
         base_low = trade(base_x[:cut], "mp", 2)
         base_high = trade(base_y[cut:], "mp", 1)
-        by_rank, base_low, base_high, *head_grad = lax.optimization_barrier(
-            (by_rank, base_low, base_high, *head_grad)
+        by_rank, base_low, base_high, far[2], *head_grad = lax.optimization_barrier(
+            (by_rank, base_low, base_high, far[2], *head_grad)
         )
     near = [own_slabs[0]] + list(near)
     image_grad = image_term(d1, head_grad, near, far)

time: 132 us -> 134 us (1.015)
  waiting for transfers between devices: 55.6 us -> 71.8 us
  starting transfers between devices: 42.1 us -> 34.6 us
  local copies, waits for them, and re-layouts: 9.14 us -> 3.21 us
    ppermute x23, waiting for transfers between devices: 51.4 us -> 69.1 us  [trade(): return lax.ppermute(block, axis, [(i, i ^ step) for i in range(count)])]
    ppermute x23, starting transfers between devices: 35.9 us -> 28.5 us  [trade(): return lax.ppermute(block, axis, [(i, i ^ step) for i in range(count)])]
    unnamed x44 -> x14, local copies, waits for them, and re-layouts: 8.07 us -> 2.24 us
    ppermute x2, waiting for transfers between devices: 4.04 us -> 2.65 us  [shift(): return lax.ppermute(block, axis, route)]
  transfers between devices with their start and end apart: 30 -> 30, of which waited for: 11 -> 13; matrix products, arithmetic and copies ran while one was open for 2% -> 2% of each run, Pallas kernels for 13% -> 13%
where the time goes in v9:
time: 134 us
  waiting for transfers between devices  71.8 us (54%)
  starting transfers between devices  34.6 us (26%)
  Pallas kernels  22 us (16%)
  local copies, waits for them, and re-layouts  3.21 us (2%)
    ppermute x23, waiting for transfers between devices, trade(): return lax.ppermute(block, axis, [(i, i ^ step) for i in range(count)])  69.1 us
    ppermute x23, starting transfers between devices, trade(): return lax.ppermute(block, axis, [(i, i ^ step) for i in range(count)])  28.5 us
    pallas_call x1, Pallas kernels, attention(): pl.pallas_call(functools.partial(attention_body, per_shard, images), grid...  11.5 us
    ppermute x2, starting transfers between devices, shift(): return lax.ppermute(block, axis, route)  4.95 us
    pallas_call x1, Pallas kernels, image_term(): pl.pallas_call(image_body, grid_spec=pltpu.PrefetchScalarGridSpec(num_sca...  2.92 us
  transfers between devices with their start and end apart: 30, of which 13 were waited for; matrix products, arithmetic and copies ran while one was open for 2% of the time, Pallas kernels for 13%

profile of v9, /device:TPU:0, one launch (start us, length us, event | category | flops | bytes accessed | tf_op | source)
XLA Modules:
  0.0 133.6 jit_solution(779703003978965171)
XLA Ops:
  0.6 3.0 %collective-permute-start = (bf16[256,2048]{1,0:T(8,128)(2,1)}, bf16[256,2048]{1,0:T(8,128)(2,1)S(1)}, u32[]{:S(2)}, u32[]{:S(2)}) collective-permute-start(bf16[256,2048]{1,0:T(8,128)(2,1)} %bitcast.25), channel_id=1, source_target_pairs={{0,1},{1,0},{2,3},{3,2},{4,5},{5,4},{6,7},{7,6},{8,9},{9,8},{10,11... | collective-permute-start | bytes 3145736 | tf_op jit(solution)/shard_map/ppermute | solution.py:50
  5.2 3.5 %collective-permute-start.4 = (bf16[512,256]{1,0:T(8,128)(2,1)}, bf16[512,256]{1,0:T(8,128)(2,1)S(1)}, u32[]{:S(2)}, u32[]{:S(2)}) collective-permute-start(bf16[512,256]{1,0:T(8,128)(2,1)} %bitcast.34), channel_id=1, source_target_pairs={{0,4},{4,8},{8,12},{1,5},{5,9},{9,13},{2,6},{6,10},{10,14},{3,7},{... | collective-permute-start | bytes 786440 | tf_op jit(solution)/shard_map/ppermute | solution.py:36
  10.3 16.7 %collective-permute-done.x_ref = bf16[256,2048]{1,0:T(8,128)(2,1)S(1)} collective-permute-done((bf16[256,2048]{1,0:T(8,128)(2,1)}, bf16[256,2048]{1,0:T(8,128)(2,1)S(1)}, u32[]{:S(2)}, u32[]{:S(2)}) %collective-permute-start) | collective-permute-done | bytes 1048608 | tf_op jit(solution)/shard_map/ppermute | solution.py:50
  27.1 1.8 %collective-permute-start.1 = (bf16[128,2048]{1,0:T(8,128)(2,1)S(1)}, bf16[128,2048]{1,0:T(8,128)(2,1)S(1)}, u32[]{:S(2)}, u32[]{:S(2)}) collective-permute-start(bf16[128,2048]{1,0:T(8,128)(2,1)S(1)} %slice.20), channel_id=1, source_target_pairs={{0,2},{1,3},{2,0},{3,1},{4,6},{5,7},{6,4},{7,5},{8,10},{9,11},{10,... | collective-permute-start | bytes 1572872 | tf_op jit(solution)/shard_map/ppermute | solution.py:50
  28.9 1.6 %collective-permute-start.3 = (bf16[128,2048]{1,0:T(8,128)(2,1)S(1)}, bf16[128,2048]{1,0:T(8,128)(2,1)S(1)}, u32[]{:S(2)}, u32[]{:S(2)}) collective-permute-start(bf16[128,2048]{1,0:T(8,128)(2,1)S(1)} %slice.21), channel_id=1, source_target_pairs={{0,1},{1,0},{2,3},{3,2},{4,5},{5,4},{6,7},{7,6},{8,9},{9,8},{10,11... | collective-permute-start | bytes 1572872 | tf_op jit(solution)/shard_map/ppermute | solution.py:50
  30.8 2.2 %copy-done = bf16[1,8192,256]{2,1,0:T(8,128)(2,1)S(1)} copy-done((bf16[1,8192,256]{2,1,0:T(8,128)(2,1)S(1)}, bf16[1,8192,256]{2,1,0:T(8,128)(2,1)}, u32[]{:S(2)}) %copy-start) | copy-done | bytes 4194328
  34.2 6.0 %collective-permute-done.1.low_ref = bf16[128,2048]{1,0:T(8,128)(2,1)S(1)} collective-permute-done((bf16[128,2048]{1,0:T(8,128)(2,1)S(1)}, bf16[128,2048]{1,0:T(8,128)(2,1)S(1)}, u32[]{:S(2)}, u32[]{:S(2)}) %collective-permute-start.1) | collective-permute-done | bytes 524320 | tf_op jit(solution)/shard_map/ppermute | solution.py:50
  42.9 1.6 %collective-permute-start.5 = (bf16[2,64,256]{2,1,0:T(8,128)(2,1)S(1)}, bf16[2,64,256]{2,1,0:T(8,128)(2,1)S(1)}, u32[]{:S(2)}, u32[]{:S(2)}) collective-permute-start(bf16[2,64,256]{2,1,0:T(8,128)(2,1)S(1)} %get-tuple-element.73), channel_id=1, source_target_pairs={{0,4},{4,0},{8,12},{12,8},{1,5},{5,1},{9,13},{13,9},{2,6},{6,2},{1... | collective-permute-start | bytes 196616 | tf_op jit(solution)/shard_map/ppermute | solution.py:50
  44.5 2.6 %collective-permute-start.6 = (bf16[2,64,256]{2,1,0:T(8,128)(2,1)S(1)}, bf16[2,64,256]{2,1,0:T(8,128)(2,1)S(1)}, u32[]{:S(2)}, u32[]{:S(2)}) collective-permute-start(bf16[2,64,256]{2,1,0:T(8,128)(2,1)S(1)} %get-tuple-element.74), channel_id=1, source_target_pairs={{0,8},{4,12},{8,0},{12,4},{1,9},{5,13},{9,1},{13,5},{2,10},{6,14},... | collective-permute-start | bytes 196616 | tf_op jit(solution)/shard_map/ppermute | solution.py:50
  51.0 3.0 %collective-permute-done.7.refs_3_ = bf16[2,64,256]{2,1,0:T(8,128)(2,1)S(1)} collective-permute-done((bf16[2,64,256]{2,1,0:T(8,128)(2,1)S(1)}, bf16[2,64,256]{2,1,0:T(8,128)(2,1)S(1)}, u32[]{:S(2)}, u32[]{:S(2)}) %collective-permute-start.7) | collective-permute-done | bytes 65568 | tf_op jit(solution)/shard_map/ppermute | solution.py:50
  54.6 3.7 %collective-permute-start.19 = (bf16[256,512]{1,0:T(8,128)(2,1)S(1)}, bf16[256,512]{1,0:T(8,128)(2,1)S(1)}, u32[]{:S(2)}, u32[]{:S(2)}) collective-permute-start(bf16[256,512]{1,0:T(8,128)(2,1)S(1)} %get-tuple-element.105), channel_id=1, source_target_pairs={{0,12},{4,8},{8,4},{12,0},{1,13},{5,9},{9,5},{13,1},{2,14},{6,10},... | collective-permute-start | bytes 786440 | tf_op jit(solution)/shard_map/ppermute | solution.py:50
  58.3 11.5 %shard_map.97 = (bf16[512,1024]{1,0:T(8,128)(2,1)}, f32[256,256]{1,0:T(8,128)S(1)}, bf16[256,256]{1,0:T(8,128)(2,1)S(1)}) custom-call(s32[1]{0:T(128)} %bitcast.c_ref, s32[64]{0:T(128)S(1)} %and_select_fusion.place_ref, s32[1,512]{1,0:T(1,128)S(1)} %bitcast.31, bf16[512,1024]{1,0:T(8,128)(2,1)S(1)} %bitcast.32, bf16[512,1024]{1,0:T(8,128)(2,1)S(1)} %bitcast.33, ...), custom_call_target="tpu_custom_call" | custom-call | flops 13421772800 | bytes 4194304 | tf_op jit(solution)/shard_map/pallas_call | solution.py:348
  69.9 3.5 %collective-permute-done.11 = bf16[256,512]{1,0:T(8,128)(2,1)S(1)} collective-permute-done((bf16[256,512]{1,0:T(8,128)(2,1)S(1)}, bf16[256,512]{1,0:T(8,128)(2,1)S(1)}, u32[]{:S(2)}, u32[]{:S(2)}) %collective-permute-start.11) | collective-permute-done | bytes 262176 | tf_op jit(solution)/shard_map/ppermute | solution.py:50
  75.5 1.6 %collective-permute-start.20 = (bf16[768,512]{1,0:T(8,128)(2,1)S(1)}, bf16[768,512]{1,0:T(8,128)(2,1)S(1)}, u32[]{:S(2)}, u32[]{:S(2)}) collective-permute-start(bf16[768,512]{1,0:T(8,128)(2,1)S(1)} %constant_dynamic-update-slice_fusion.refs_0_), channel_id=1, source_target_pairs={{0,1},{1,0},{2,3},{3,2},{4,5},{5,4},{6,7},{7,6},{8,9},{9,8},{10,11... | collective-permute-start | bytes 2359304 | tf_op jit(solution)/shard_map/ppermute | solution.py:50
  77.6 2.6 %collective-permute-done.13 = bf16[256,256]{1,0:T(8,128)(2,1)S(1)} collective-permute-done((bf16[256,256]{1,0:T(8,128)(2,1)S(1)}, bf16[256,256]{1,0:T(8,128)(2,1)S(1)}, u32[]{:S(2)}, u32[]{:S(2)}) %collective-permute-start.13) | collective-permute-done | bytes 131104 | tf_op jit(solution)/shard_map/ppermute | solution.py:36
  81.9 9.9 %collective-permute-done.12.refs_6_ = bf16[1024,256]{1,0:T(8,128)(2,1)S(1)} collective-permute-done((bf16[1024,256]{1,0:T(8,128)(2,1)S(1)}, bf16[1024,256]{1,0:T(8,128)(2,1)S(1)}, u32[]{:S(2)}, u32[]{:S(2)}) %collective-permute-start.12) | collective-permute-done | bytes 524320 | tf_op jit(solution)/shard_map/ppermute | solution.py:50
  91.9 1.6 %collective-permute-start.18 = (bf16[256,256]{1,0:T(8,128)(2,1)S(1)}, bf16[256,256]{1,0:T(8,128)(2,1)S(1)}, u32[]{:S(2)}, u32[]{:S(2)}) collective-permute-start(bf16[256,256]{1,0:T(8,128)(2,1)S(1)} %add_convert_fusion.refs_0_), channel_id=1, source_target_pairs={{0,12},{4,8},{8,4},{12,0},{1,13},{5,9},{9,5},{13,1},{2,14},{6,10},... | collective-permute-start | bytes 393224 | tf_op jit(solution)/shard_map/ppermute | solution.py:50
  93.5 5.2 %collective-permute-done.18.refs_3_ = bf16[256,256]{1,0:T(8,128)(2,1)S(1)} collective-permute-done((bf16[256,256]{1,0:T(8,128)(2,1)S(1)}, bf16[256,256]{1,0:T(8,128)(2,1)S(1)}, u32[]{:S(2)}, u32[]{:S(2)}) %collective-permute-start.18) | collective-permute-done | bytes 131104 | tf_op jit(solution)/shard_map/ppermute | solution.py:50
  99.3 9.4 %collective-permute-done.22.refs_2_ = bf16[768,512]{1,0:T(8,128)(2,1)S(1)} collective-permute-done((bf16[768,512]{1,0:T(8,128)(2,1)S(1)}, bf16[768,512]{1,0:T(8,128)(2,1)S(1)}, u32[]{:S(2)}, u32[]{:S(2)}) %collective-permute-start.22) | collective-permute-done | bytes 786464 | tf_op jit(solution)/shard_map/ppermute | solution.py:50
  109.3 1.7 %shard_map.98 = (bf16[1024,256]{1,0:T(8,128)(2,1)S(1)}, bf16[256,256]{1,0:T(8,128)(2,1)S(1)}) custom-call(s32[1]{0:T(128)} %bitcast.c_ref, s32[64]{0:T(128)S(1)} %and_select_fusion.place_ref, bf16[256,256]{1,0:T(8,128)(2,1)S(1)} %add_convert_fusion.refs_0_, bf16[256,256]{1,0:T(8,128)(2,1)S(1)} %collective-permute-done.16.refs_1_, ...), custom_call_target="tpu_custom_call" | custom-call | bytes 2097152 | tf_op jit(solution)/shard_map/pallas_call | solution.py:406
  111.0 1.6 %collective-permute-start.25 = (bf16[256,256]{1,0:T(8,128)(2,1)S(1)}, bf16[256,256]{1,0:T(8,128)(2,1)S(1)}, u32[]{:S(2)}, u32[]{:S(2)}) collective-permute-start(bf16[256,256]{1,0:T(8,128)(2,1)S(1)} %get-tuple-element.108.refs_0_), channel_id=1, source_target_pairs={{0,1},{1,0},{2,3},{3,2},{4,5},{5,4},{6,7},{7,6},{8,9},{9,8},{10,11... | collective-permute-start | bytes 393224 | tf_op jit(solution)/shard_map/ppermute | solution.py:50
  113.1 7.9 %collective-permute-done.25.refs_1_ = bf16[256,256]{1,0:T(8,128)(2,1)S(1)} collective-permute-done((bf16[256,256]{1,0:T(8,128)(2,1)S(1)}, bf16[256,256]{1,0:T(8,128)(2,1)S(1)}, u32[]{:S(2)}, u32[]{:S(2)}) %collective-permute-start.25) | collective-permute-done | bytes 131104 | tf_op jit(solution)/shard_map/ppermute | solution.py:50
  121.6 5.3 %collective-permute-done.27.refs_3_ = bf16[256,256]{1,0:T(8,128)(2,1)S(1)} collective-permute-done((bf16[256,256]{1,0:T(8,128)(2,1)S(1)}, bf16[256,256]{1,0:T(8,128)(2,1)S(1)}, u32[]{:S(2)}, u32[]{:S(2)}) %collective-permute-start.27) | collective-permute-done | bytes 131104 | tf_op jit(solution)/shard_map/ppermute | solution.py:50
  129.1 2.9 %shard_map.99 = bf16[256,2048]{1,0:T(8,128)(2,1)} custom-call(s32[1]{0:T(128)} %bitcast.11.d_ref, bf16[256,256]{1,0:T(8,128)(2,1)S(1)} %get-tuple-element.108.refs_0_, bf16[256,256]{1,0:T(8,128)(2,1)S(1)} %collective-permute-done.25.refs_1_, bf16[256,256]{1,0:T(8,128)(2,1)S(1)} %collective-permute-done.26.refs_2_, ...), custom_call_target="tpu_custom_call" | custom-call | flops 1073741824 | bytes 8388608 | tf_op jit(solution)/shard_map/pallas_call | solution.py:529
  (70 shorter events, 22.4 us)
Async XLA Ops:
  0.6 26.4 %collective-permute-start = (bf16[256,2048]{1,0:T(8,128)(2,1)}, bf16[256,2048]{1,0:T(8,128)(2,1)S(1)}, u32[]{:S(2)}, u32[]{:S(2)}) collective-permute-start(bf16[256,2048]{1,0:T(8,128)(2,1)} %bitcast.25), channel_id=1, source_target_pairs={{0,1},{1,0},{2,3},{3,2},{4,5},{5,4},{6,7},{7,6},{8,9},{9,8},{10,11... | collective-permute-start | bytes 3145736 | tf_op jit(solution)/shard_map/ppermute | solution.py:50
  3.6 25.2 %collective-permute-start.2 = (bf16[256,2048]{1,0:T(8,128)(2,1)}, bf16[256,2048]{1,0:T(8,128)(2,1)S(1)}, u32[]{:S(2)}, u32[]{:S(2)}) collective-permute-start(bf16[256,2048]{1,0:T(8,128)(2,1)} %bitcast.26), channel_id=1, source_target_pairs={{0,2},{1,3},{2,0},{3,1},{4,6},{5,7},{6,4},{7,5},{8,10},{9,11},{10,... | collective-permute-start | bytes 3145736 | tf_op jit(solution)/shard_map/ppermute | solution.py:50
  5.2 29.0 %collective-permute-start.4 = (bf16[512,256]{1,0:T(8,128)(2,1)}, bf16[512,256]{1,0:T(8,128)(2,1)S(1)}, u32[]{:S(2)}, u32[]{:S(2)}) collective-permute-start(bf16[512,256]{1,0:T(8,128)(2,1)} %bitcast.34), channel_id=1, source_target_pairs={{0,4},{4,8},{8,12},{1,5},{5,9},{9,13},{2,6},{6,10},{10,14},{3,7},{... | collective-permute-start | bytes 786440 | tf_op jit(solution)/shard_map/ppermute | solution.py:36
  27.1 13.2 %collective-permute-start.1 = (bf16[128,2048]{1,0:T(8,128)(2,1)S(1)}, bf16[128,2048]{1,0:T(8,128)(2,1)S(1)}, u32[]{:S(2)}, u32[]{:S(2)}) collective-permute-start(bf16[128,2048]{1,0:T(8,128)(2,1)S(1)} %slice.20), channel_id=1, source_target_pairs={{0,2},{1,3},{2,0},{3,1},{4,6},{5,7},{6,4},{7,5},{8,10},{9,11},{10,... | collective-permute-start | bytes 1572872 | tf_op jit(solution)/shard_map/ppermute | solution.py:50
  28.9 12.6 %collective-permute-start.3 = (bf16[128,2048]{1,0:T(8,128)(2,1)S(1)}, bf16[128,2048]{1,0:T(8,128)(2,1)S(1)}, u32[]{:S(2)}, u32[]{:S(2)}) collective-permute-start(bf16[128,2048]{1,0:T(8,128)(2,1)S(1)} %slice.21), channel_id=1, source_target_pairs={{0,1},{1,0},{2,3},{3,2},{4,5},{5,4},{6,7},{7,6},{8,9},{9,8},{10,11... | collective-permute-start | bytes 1572872 | tf_op jit(solution)/shard_map/ppermute | solution.py:50
  42.9 7.2 %collective-permute-start.5 = (bf16[2,64,256]{2,1,0:T(8,128)(2,1)S(1)}, bf16[2,64,256]{2,1,0:T(8,128)(2,1)S(1)}, u32[]{:S(2)}, u32[]{:S(2)}) collective-permute-start(bf16[2,64,256]{2,1,0:T(8,128)(2,1)S(1)} %get-tuple-element.73), channel_id=1, source_target_pairs={{0,4},{4,0},{8,12},{12,8},{1,5},{5,1},{9,13},{13,9},{2,6},{6,2},{1... | collective-permute-start | bytes 196616 | tf_op jit(solution)/shard_map/ppermute | solution.py:50
  47.1 6.8 %collective-permute-start.7 = (bf16[2,64,256]{2,1,0:T(8,128)(2,1)S(1)}, bf16[2,64,256]{2,1,0:T(8,128)(2,1)S(1)}, u32[]{:S(2)}, u32[]{:S(2)}) collective-permute-start(bf16[2,64,256]{2,1,0:T(8,128)(2,1)S(1)} %get-tuple-element.75), channel_id=1, source_target_pairs={{0,12},{4,8},{8,4},{12,0},{1,13},{5,9},{9,5},{13,1},{2,14},{6,10},... | collective-permute-start | bytes 196616 | tf_op jit(solution)/shard_map/ppermute | solution.py:50
  47.4 26.0 %collective-permute-start.8 = (bf16[1024,256]{1,0:T(8,128)(2,1)S(1)}, bf16[1024,256]{1,0:T(8,128)(2,1)S(1)}, u32[]{:S(2)}, u32[]{:S(2)}) collective-permute-start(bf16[1024,256]{1,0:T(8,128)(2,1)S(1)} %get-tuple-element.88), channel_id=1, source_target_pairs={{0,1},{1,0},{2,3},{3,2},{4,5},{5,4},{6,7},{7,6},{8,9},{9,8},{10,11... | collective-permute-start | bytes 1572872 | tf_op jit(solution)/shard_map/ppermute | solution.py:50
  48.9 24.5 %collective-permute-start.9 = (bf16[1024,256]{1,0:T(8,128)(2,1)S(1)}, bf16[1024,256]{1,0:T(8,128)(2,1)S(1)}, u32[]{:S(2)}, u32[]{:S(2)}) collective-permute-start(bf16[1024,256]{1,0:T(8,128)(2,1)S(1)} %get-tuple-element.89), channel_id=1, source_target_pairs={{0,3},{1,2},{2,1},{3,0},{4,7},{5,6},{6,5},{7,4},{8,11},{9,10},{10,... | collective-permute-start | bytes 1572872 | tf_op jit(solution)/shard_map/ppermute | solution.py:50
  53.9 15.9 %collective-permute-start.10 = (bf16[256,512]{1,0:T(8,128)(2,1)S(1)}, bf16[256,512]{1,0:T(8,128)(2,1)S(1)}, u32[]{:S(2)}, u32[]{:S(2)}) collective-permute-start(bf16[256,512]{1,0:T(8,128)(2,1)S(1)} %get-tuple-element.90), channel_id=1, source_target_pairs={{0,4},{4,0},{8,12},{12,8},{1,5},{5,1},{9,13},{13,9},{2,6},{6,2},{1... | collective-permute-start | bytes 786440 | tf_op jit(solution)/shard_map/ppermute | solution.py:50
  53.9 19.4 %collective-permute-start.11 = (bf16[256,512]{1,0:T(8,128)(2,1)S(1)}, bf16[256,512]{1,0:T(8,128)(2,1)S(1)}, u32[]{:S(2)}, u32[]{:S(2)}) collective-permute-start(bf16[256,512]{1,0:T(8,128)(2,1)S(1)} %get-tuple-element.91), channel_id=1, source_target_pairs={{0,8},{4,12},{8,0},{12,4},{1,9},{5,13},{9,1},{13,5},{2,10},{6,14},... | collective-permute-start | bytes 786440 | tf_op jit(solution)/shard_map/ppermute | solution.py:50
  54.6 20.8 %collective-permute-start.19 = (bf16[256,512]{1,0:T(8,128)(2,1)S(1)}, bf16[256,512]{1,0:T(8,128)(2,1)S(1)}, u32[]{:S(2)}, u32[]{:S(2)}) collective-permute-start(bf16[256,512]{1,0:T(8,128)(2,1)S(1)} %get-tuple-element.105), channel_id=1, source_target_pairs={{0,12},{4,8},{8,4},{12,0},{1,13},{5,9},{9,5},{13,1},{2,14},{6,10},... | collective-permute-start | bytes 786440 | tf_op jit(solution)/shard_map/ppermute | solution.py:50
  73.3 6.9 %collective-permute-start.13 = (bf16[256,256]{1,0:T(8,128)(2,1)S(1)}, bf16[256,256]{1,0:T(8,128)(2,1)S(1)}, u32[]{:S(2)}, u32[]{:S(2)}) collective-permute-start(bf16[256,256]{1,0:T(8,128)(2,1)S(1)} %get-tuple-element.94), channel_id=1, source_target_pairs={{4,0},{8,4},{12,8},{5,1},{9,5},{13,9},{6,2},{10,6},{14,10},{7,3},{... | collective-permute-start | bytes 393224 | tf_op jit(solution)/shard_map/ppermute | solution.py:36
  75.5 23.3 %collective-permute-start.20 = (bf16[768,512]{1,0:T(8,128)(2,1)S(1)}, bf16[768,512]{1,0:T(8,128)(2,1)S(1)}, u32[]{:S(2)}, u32[]{:S(2)}) collective-permute-start(bf16[768,512]{1,0:T(8,128)(2,1)S(1)} %constant_dynamic-update-slice_fusion.refs_0_), channel_id=1, source_target_pairs={{0,1},{1,0},{2,3},{3,2},{4,5},{5,4},{6,7},{7,6},{8,9},{9,8},{10,11... | collective-permute-start | bytes 2359304 | tf_op jit(solution)/shard_map/ppermute | solution.py:50
  77.0 14.8 %collective-permute-start.12 = (bf16[1024,256]{1,0:T(8,128)(2,1)S(1)}, bf16[1024,256]{1,0:T(8,128)(2,1)S(1)}, u32[]{:S(2)}, u32[]{:S(2)}) collective-permute-start(bf16[1024,256]{1,0:T(8,128)(2,1)S(1)} %get-tuple-element.92), channel_id=1, source_target_pairs={{0,2},{1,3},{2,0},{3,1},{4,6},{5,7},{6,4},{7,5},{8,10},{9,11},{10,... | collective-permute-start | bytes 1572872 | tf_op jit(solution)/shard_map/ppermute | solution.py:50
  80.2 28.5 %collective-permute-start.22 = (bf16[768,512]{1,0:T(8,128)(2,1)S(1)}, bf16[768,512]{1,0:T(8,128)(2,1)S(1)}, u32[]{:S(2)}, u32[]{:S(2)}) collective-permute-start(bf16[768,512]{1,0:T(8,128)(2,1)S(1)} %constant_dynamic-update-slice_fusion.refs_0_), channel_id=1, source_target_pairs={{0,2},{1,3},{2,0},{3,1},{4,6},{5,7},{6,4},{7,5},{8,10},{9,11},{10,... | collective-permute-start | bytes 2359304 | tf_op jit(solution)/shard_map/ppermute | solution.py:50
  81.3 12.2 %collective-permute-start.16 = (bf16[256,256]{1,0:T(8,128)(2,1)S(1)}, bf16[256,256]{1,0:T(8,128)(2,1)S(1)}, u32[]{:S(2)}, u32[]{:S(2)}) collective-permute-start(bf16[256,256]{1,0:T(8,128)(2,1)S(1)} %add_convert_fusion.refs_0_), channel_id=1, source_target_pairs={{0,4},{4,0},{8,12},{12,8},{1,5},{5,1},{9,13},{13,9},{2,6},{6,2},{1... | collective-permute-start | bytes 393224 | tf_op jit(solution)/shard_map/ppermute | solution.py:50
  81.9 11.6 %collective-permute-start.17 = (bf16[256,256]{1,0:T(8,128)(2,1)S(1)}, bf16[256,256]{1,0:T(8,128)(2,1)S(1)}, u32[]{:S(2)}, u32[]{:S(2)}) collective-permute-start(bf16[256,256]{1,0:T(8,128)(2,1)S(1)} %add_convert_fusion.refs_0_), channel_id=1, source_target_pairs={{0,8},{4,12},{8,0},{12,4},{1,9},{5,13},{9,1},{13,5},{2,10},{6,14},... | collective-permute-start | bytes 393224 | tf_op jit(solution)/shard_map/ppermute | solution.py:50
  91.9 6.9 %collective-permute-start.18 = (bf16[256,256]{1,0:T(8,128)(2,1)S(1)}, bf16[256,256]{1,0:T(8,128)(2,1)S(1)}, u32[]{:S(2)}, u32[]{:S(2)}) collective-permute-start(bf16[256,256]{1,0:T(8,128)(2,1)S(1)} %add_convert_fusion.refs_0_), channel_id=1, source_target_pairs={{0,12},{4,8},{8,4},{12,0},{1,13},{5,9},{9,5},{13,1},{2,14},{6,10},... | collective-permute-start | bytes 393224 | tf_op jit(solution)/shard_map/ppermute | solution.py:50
  98.7 28.1 %collective-permute-start.24 = (bf16[1024,256]{1,0:T(8,128)(2,1)S(1)}, bf16[1024,256]{1,0:T(8,128)(2,1)S(1)}, u32[]{:S(2)}, u32[]{:S(2)}) collective-permute-start(bf16[1024,256]{1,0:T(8,128)(2,1)S(1)} %collective-permute-done.12.refs_6_), channel_id=1, source_target_pairs={{0,16},{16,0},{1,17},{17,1},{2,18},{18,2},{3,19},{19,3},{4,20},{20... | collective-permute-start | bytes 1572872 | tf_op jit(solution)/shard_map/ppermute | solution.py:41
  98.8 28.0 %collective-permute-start.21 = (bf16[384,512]{1,0:T(8,128)(2,1)S(1)}, bf16[384,512]{1,0:T(8,128)(2,1)S(1)}, u32[]{:S(2)}, u32[]{:S(2)}) collective-permute-start(bf16[384,512]{1,0:T(8,128)(2,1)S(1)} %slice.22), channel_id=1, source_target_pairs={{0,2},{1,3},{2,0},{3,1},{4,6},{5,7},{6,4},{7,5},{8,10},{9,11},{10,... | collective-permute-start | bytes 1179656 | tf_op jit(solution)/shard_map/ppermute | solution.py:50
  108.7 18.1 %collective-permute-start.23 = (bf16[384,512]{1,0:T(8,128)(2,1)S(1)}, bf16[384,512]{1,0:T(8,128)(2,1)S(1)}, u32[]{:S(2)}, u32[]{:S(2)}) collective-permute-start(bf16[384,512]{1,0:T(8,128)(2,1)S(1)} %slice.23), channel_id=1, source_target_pairs={{0,1},{1,0},{2,3},{3,2},{4,5},{5,4},{6,7},{7,6},{8,9},{9,8},{10,11... | collective-permute-start | bytes 1179656 | tf_op jit(solution)/shard_map/ppermute | solution.py:50
  111.0 9.9 %collective-permute-start.25 = (bf16[256,256]{1,0:T(8,128)(2,1)S(1)}, bf16[256,256]{1,0:T(8,128)(2,1)S(1)}, u32[]{:S(2)}, u32[]{:S(2)}) collective-permute-start(bf16[256,256]{1,0:T(8,128)(2,1)S(1)} %get-tuple-element.108.refs_0_), channel_id=1, source_target_pairs={{0,1},{1,0},{2,3},{3,2},{4,5},{5,4},{6,7},{7,6},{8,9},{9,8},{10,11... | collective-permute-start | bytes 393224 | tf_op jit(solution)/shard_map/ppermute | solution.py:50
  112.6 9.0 %collective-permute-start.26 = (bf16[256,256]{1,0:T(8,128)(2,1)S(1)}, bf16[256,256]{1,0:T(8,128)(2,1)S(1)}, u32[]{:S(2)}, u32[]{:S(2)}) collective-permute-start(bf16[256,256]{1,0:T(8,128)(2,1)S(1)} %get-tuple-element.108.refs_0_), channel_id=1, source_target_pairs={{0,2},{1,3},{2,0},{3,1},{4,6},{5,7},{6,4},{7,5},{8,10},{9,11},{10,... | collective-permute-start | bytes 393224 | tf_op jit(solution)/shard_map/ppermute | solution.py:50
  (12 other events, 106.8 us)

commit v10 on v9

--- a/solution.py
+++ b/solution.py
@@ -604,16 +604,12 @@
         c1, place, start, queries[0], d_out[0], text_kv[0], prior_text, image,
         images, per_shard, image_rows,
     )
-    early = ranks // 2 if mixed else 1
-    prior_grad, slabs[1], near[0], near[2], *both = lax.optimization_barrier(
-        (prior_grad, slabs[1], near[0], near[2], *moved[:early])
+    prior_grad, near[0], near[2], *moved = lax.optimization_barrier(
+        (prior_grad, near[0], near[2], *moved)
     )
-    moved = both + list(moved[early:])
-    near[1] = trade(slabs[1], "mp", 2)
     far = [own_slabs[1], swap(near[0], "dp"), None, swap(near[2], "dp")]
     grad = own_grad + shift(prior_grad, "ctx", -1).astype(jnp.float32)
     grad = grad.astype(jnp.bfloat16)
-    grad, far[1], far[3] = lax.optimization_barrier((grad, far[1], far[3]))
     if mixed:
         gathered = [trade(grad, "ctx", s) if s else grad for s in range(ranks)]
         base = jnp.concatenate(moved, axis=0)
@@ -623,16 +619,20 @@
     else:
         gathered = [exchange(jnp.broadcast_to(grad, (ranks,) + grad.shape), "ctx")]
         all_states = lax.all_gather(moved[0], "mp", axis=0)
-    near[1], *gathered = lax.optimization_barrier((near[1], *gathered))
-    far[2] = swap(near[1], "dp")
+        base_x = base_y = all_states
+    slabs[1], base_x, base_y, *gathered = lax.optimization_barrier(
+        (slabs[1], base_x, base_y, *gathered)
+    )
+    near[1] = trade(slabs[1], "mp", 2)
     by_rank, mine = reorder(c1, place, gathered, per_shard, images, ranks)
     head_grad = [mine] + [trade(mine, "mp", s) for s in steps]
     if mixed:
         base_low = trade(base_x[:cut], "mp", 2)
         base_high = trade(base_y[cut:], "mp", 1)
-        by_rank, base_low, base_high, far[2], *head_grad = lax.optimization_barrier(
-            (by_rank, base_low, base_high, far[2], *head_grad)
+        by_rank, base_low, base_high, near[1], *head_grad = lax.optimization_barrier(
+            (by_rank, base_low, base_high, near[1], *head_grad)
         )
+    far[2] = swap(near[1], "dp")
     near = [own_slabs[0]] + list(near)
     image_grad = image_term(d1, head_grad, near, far)
     if mixed:

time: 134 us -> 129 us (0.963)
  waiting for transfers between devices: 71.8 us -> 62.1 us
  starting transfers between devices: 34.6 us -> 39.3 us
    ppermute x23, waiting for transfers between devices: 69.1 us -> 50.3 us  [trade(): return lax.ppermute(block, axis, [(i, i ^ step) for i in range(count)])]
    ppermute x2, waiting for transfers between devices: 2.65 us -> 7.87 us  [shift(): return lax.ppermute(block, axis, route)]
    ppermute x23, starting transfers between devices: 28.5 us -> 33.1 us  [trade(): return lax.ppermute(block, axis, [(i, i ^ step) for i in range(count)])]
    ppermute x5, waiting for transfers between devices: 0.13 us -> 3.95 us  [swap(): return lax.ppermute(block, axis, [(i, count - 1 - i) for i in range(count)])]
  transfers between devices with their start and end apart: 30 -> 30, of which waited for: 13 -> 14; matrix products, arithmetic and copies ran while one was open for 2% -> 2% of each run, Pallas kernels for 13% -> 14%
where the time goes in v10:
time: 129 us
  waiting for transfers between devices  62.1 us (48%)
  starting transfers between devices  39.3 us (30%)
  Pallas kernels  22 us (17%)
  local copies, waits for them, and re-layouts  3.21 us (2%)
    ppermute x23, waiting for transfers between devices, trade(): return lax.ppermute(block, axis, [(i, i ^ step) for i in range(count)])  50.3 us
    ppermute x23, starting transfers between devices, trade(): return lax.ppermute(block, axis, [(i, i ^ step) for i in range(count)])  33.1 us
    pallas_call x1, Pallas kernels, attention(): pl.pallas_call(functools.partial(attention_body, per_shard, images), grid...  11.5 us
    ppermute x2, waiting for transfers between devices, shift(): return lax.ppermute(block, axis, route)  7.87 us
    ppermute x2, starting transfers between devices, shift(): return lax.ppermute(block, axis, route)  4.95 us
    ppermute x5, waiting for transfers between devices, swap(): return lax.ppermute(block, axis, [(i, count - 1 - i) for i in range(count)])  3.95 us
    pallas_call x1, Pallas kernels, image_term(): pl.pallas_call(image_body, grid_spec=pltpu.PrefetchScalarGridSpec(num_sca...  2.92 us
  transfers between devices with their start and end apart: 30, of which 14 were waited for; matrix products, arithmetic and copies ran while one was open for 2% of the time, Pallas kernels for 14%

profile of v10, /device:TPU:0, one launch (start us, length us, event | category | flops | bytes accessed | tf_op | source)
XLA Modules:
  0.0 128.5 jit_solution(15987779324729395783)
XLA Ops:
  0.6 3.0 %collective-permute-start = (bf16[256,2048]{1,0:T(8,128)(2,1)}, bf16[256,2048]{1,0:T(8,128)(2,1)S(1)}, u32[]{:S(2)}, u32[]{:S(2)}) collective-permute-start(bf16[256,2048]{1,0:T(8,128)(2,1)} %bitcast.25), channel_id=1, source_target_pairs={{0,1},{1,0},{2,3},{3,2},{4,5},{5,4},{6,7},{7,6},{8,9},{9,8},{10,11... | collective-permute-start | bytes 3145736 | tf_op jit(solution)/shard_map/ppermute | solution.py:50
  5.2 3.5 %collective-permute-start.4 = (bf16[512,256]{1,0:T(8,128)(2,1)}, bf16[512,256]{1,0:T(8,128)(2,1)S(1)}, u32[]{:S(2)}, u32[]{:S(2)}) collective-permute-start(bf16[512,256]{1,0:T(8,128)(2,1)} %bitcast.34), channel_id=1, source_target_pairs={{0,4},{4,8},{8,12},{1,5},{5,9},{9,13},{2,6},{6,10},{10,14},{3,7},{... | collective-permute-start | bytes 786440 | tf_op jit(solution)/shard_map/ppermute | solution.py:36
  10.3 16.7 %collective-permute-done.x_ref = bf16[256,2048]{1,0:T(8,128)(2,1)S(1)} collective-permute-done((bf16[256,2048]{1,0:T(8,128)(2,1)}, bf16[256,2048]{1,0:T(8,128)(2,1)S(1)}, u32[]{:S(2)}, u32[]{:S(2)}) %collective-permute-start) | collective-permute-done | bytes 1048608 | tf_op jit(solution)/shard_map/ppermute | solution.py:50
  27.1 1.8 %collective-permute-start.1 = (bf16[128,2048]{1,0:T(8,128)(2,1)S(1)}, bf16[128,2048]{1,0:T(8,128)(2,1)S(1)}, u32[]{:S(2)}, u32[]{:S(2)}) collective-permute-start(bf16[128,2048]{1,0:T(8,128)(2,1)S(1)} %slice.20), channel_id=1, source_target_pairs={{0,2},{1,3},{2,0},{3,1},{4,6},{5,7},{6,4},{7,5},{8,10},{9,11},{10,... | collective-permute-start | bytes 1572872 | tf_op jit(solution)/shard_map/ppermute | solution.py:50
  28.9 1.6 %collective-permute-start.3 = (bf16[128,2048]{1,0:T(8,128)(2,1)S(1)}, bf16[128,2048]{1,0:T(8,128)(2,1)S(1)}, u32[]{:S(2)}, u32[]{:S(2)}) collective-permute-start(bf16[128,2048]{1,0:T(8,128)(2,1)S(1)} %slice.21), channel_id=1, source_target_pairs={{0,1},{1,0},{2,3},{3,2},{4,5},{5,4},{6,7},{7,6},{8,9},{9,8},{10,11... | collective-permute-start | bytes 1572872 | tf_op jit(solution)/shard_map/ppermute | solution.py:50
  30.8 2.2 %copy-done = bf16[1,8192,256]{2,1,0:T(8,128)(2,1)S(1)} copy-done((bf16[1,8192,256]{2,1,0:T(8,128)(2,1)S(1)}, bf16[1,8192,256]{2,1,0:T(8,128)(2,1)}, u32[]{:S(2)}) %copy-start) | copy-done | bytes 4194328
  34.2 6.0 %collective-permute-done.1.low_ref = bf16[128,2048]{1,0:T(8,128)(2,1)S(1)} collective-permute-done((bf16[128,2048]{1,0:T(8,128)(2,1)S(1)}, bf16[128,2048]{1,0:T(8,128)(2,1)S(1)}, u32[]{:S(2)}, u32[]{:S(2)}) %collective-permute-start.1) | collective-permute-done | bytes 524320 | tf_op jit(solution)/shard_map/ppermute | solution.py:50
  42.9 1.6 %collective-permute-start.5 = (bf16[2,64,256]{2,1,0:T(8,128)(2,1)S(1)}, bf16[2,64,256]{2,1,0:T(8,128)(2,1)S(1)}, u32[]{:S(2)}, u32[]{:S(2)}) collective-permute-start(bf16[2,64,256]{2,1,0:T(8,128)(2,1)S(1)} %get-tuple-element.72), channel_id=1, source_target_pairs={{0,4},{4,0},{8,12},{12,8},{1,5},{5,1},{9,13},{13,9},{2,6},{6,2},{1... | collective-permute-start | bytes 196616 | tf_op jit(solution)/shard_map/ppermute | solution.py:50
  44.5 2.6 %collective-permute-start.6 = (bf16[2,64,256]{2,1,0:T(8,128)(2,1)S(1)}, bf16[2,64,256]{2,1,0:T(8,128)(2,1)S(1)}, u32[]{:S(2)}, u32[]{:S(2)}) collective-permute-start(bf16[2,64,256]{2,1,0:T(8,128)(2,1)S(1)} %get-tuple-element.73), channel_id=1, source_target_pairs={{0,8},{4,12},{8,0},{12,4},{1,9},{5,13},{9,1},{13,5},{2,10},{6,14},... | collective-permute-start | bytes 196616 | tf_op jit(solution)/shard_map/ppermute | solution.py:50
  51.0 3.0 %collective-permute-done.7.refs_3_ = bf16[2,64,256]{2,1,0:T(8,128)(2,1)S(1)} collective-permute-done((bf16[2,64,256]{2,1,0:T(8,128)(2,1)S(1)}, bf16[2,64,256]{2,1,0:T(8,128)(2,1)S(1)}, u32[]{:S(2)}, u32[]{:S(2)}) %collective-permute-start.7) | collective-permute-done | bytes 65568 | tf_op jit(solution)/shard_map/ppermute | solution.py:50
  54.6 3.7 %collective-permute-start.12 = (bf16[256,512]{1,0:T(8,128)(2,1)S(1)}, bf16[256,512]{1,0:T(8,128)(2,1)S(1)}, u32[]{:S(2)}, u32[]{:S(2)}) collective-permute-start(bf16[256,512]{1,0:T(8,128)(2,1)S(1)} %get-tuple-element.91), channel_id=1, source_target_pairs={{0,12},{4,8},{8,4},{12,0},{1,13},{5,9},{9,5},{13,1},{2,14},{6,10},... | collective-permute-start | bytes 786440 | tf_op jit(solution)/shard_map/ppermute | solution.py:50
  58.3 11.5 %shard_map.97 = (bf16[512,1024]{1,0:T(8,128)(2,1)}, f32[256,256]{1,0:T(8,128)S(1)}, bf16[256,256]{1,0:T(8,128)(2,1)S(1)}) custom-call(s32[1]{0:T(128)} %bitcast.c_ref, s32[64]{0:T(128)S(1)} %and_select_fusion.place_ref, s32[1,512]{1,0:T(1,128)S(1)} %bitcast.31, bf16[512,1024]{1,0:T(8,128)(2,1)S(1)} %bitcast.32, bf16[512,1024]{1,0:T(8,128)(2,1)S(1)} %bitcast.33, ...), custom_call_target="tpu_custom_call" | custom-call | flops 13421772800 | bytes 4194304 | tf_op jit(solution)/shard_map/pallas_call | solution.py:348
  69.9 3.5 %collective-permute-done.11 = bf16[256,512]{1,0:T(8,128)(2,1)S(1)} collective-permute-done((bf16[256,512]{1,0:T(8,128)(2,1)S(1)}, bf16[256,512]{1,0:T(8,128)(2,1)S(1)}, u32[]{:S(2)}, u32[]{:S(2)}) %collective-permute-start.11) | collective-permute-done | bytes 262176 | tf_op jit(solution)/shard_map/ppermute | solution.py:50
  73.4 1.6 %collective-permute-start.13 = (bf16[768,512]{1,0:T(8,128)(2,1)S(1)}, bf16[768,512]{1,0:T(8,128)(2,1)S(1)}, u32[]{:S(2)}, u32[]{:S(2)}) collective-permute-start(bf16[768,512]{1,0:T(8,128)(2,1)S(1)} %constant_dynamic-update-slice_fusion.refs_0_), channel_id=1, source_target_pairs={{0,1},{1,0},{2,3},{3,2},{4,5},{5,4},{6,7},{7,6},{8,9},{9,8},{10,11... | collective-permute-start | bytes 2359304 | tf_op jit(solution)/shard_map/ppermute | solution.py:50
  77.0 7.9 %collective-permute-done.15 = bf16[256,256]{1,0:T(8,128)(2,1)S(1)} collective-permute-done((bf16[256,256]{1,0:T(8,128)(2,1)S(1)}, bf16[256,256]{1,0:T(8,128)(2,1)S(1)}, u32[]{:S(2)}, u32[]{:S(2)}) %collective-permute-start.15) | collective-permute-done | bytes 131104 | tf_op jit(solution)/shard_map/ppermute | solution.py:36
  87.2 2.1 %collective-permute-start.18 = (bf16[256,256]{1,0:T(8,128)(2,1)S(1)}, bf16[256,256]{1,0:T(8,128)(2,1)S(1)}, u32[]{:S(2)}, u32[]{:S(2)}) collective-permute-start(bf16[256,256]{1,0:T(8,128)(2,1)S(1)} %add_convert_fusion.refs_0_), channel_id=1, source_target_pairs={{0,12},{4,8},{8,4},{12,0},{1,13},{5,9},{9,5},{13,1},{2,14},{6,10},... | collective-permute-start | bytes 393224 | tf_op jit(solution)/shard_map/ppermute | solution.py:50
  89.3 1.8 %collective-permute-done.16.refs_1_ = bf16[256,256]{1,0:T(8,128)(2,1)S(1)} collective-permute-done((bf16[256,256]{1,0:T(8,128)(2,1)S(1)}, bf16[256,256]{1,0:T(8,128)(2,1)S(1)}, u32[]{:S(2)}, u32[]{:S(2)}) %collective-permute-start.16) | collective-permute-done | bytes 131104 | tf_op jit(solution)/shard_map/ppermute | solution.py:50
  91.1 3.9 %collective-permute-done.17.refs_2_ = bf16[256,256]{1,0:T(8,128)(2,1)S(1)} collective-permute-done((bf16[256,256]{1,0:T(8,128)(2,1)S(1)}, bf16[256,256]{1,0:T(8,128)(2,1)S(1)}, u32[]{:S(2)}, u32[]{:S(2)}) %collective-permute-start.17) | collective-permute-done | bytes 131104 | tf_op jit(solution)/shard_map/ppermute | solution.py:50
  95.0 1.6 %collective-permute-start.21 = (bf16[1024,256]{1,0:T(8,128)(2,1)S(1)}, bf16[1024,256]{1,0:T(8,128)(2,1)S(1)}, u32[]{:S(2)}, u32[]{:S(2)}) collective-permute-start(bf16[1024,256]{1,0:T(8,128)(2,1)S(1)} %get-tuple-element.104), channel_id=1, source_target_pairs={{0,2},{1,3},{2,0},{3,1},{4,6},{5,7},{6,4},{7,5},{8,10},{9,11},{10,... | collective-permute-start | bytes 1572872 | tf_op jit(solution)/shard_map/ppermute | solution.py:50
  98.4 1.7 %shard_map.98 = (bf16[1024,256]{1,0:T(8,128)(2,1)S(1)}, bf16[256,256]{1,0:T(8,128)(2,1)S(1)}) custom-call(s32[1]{0:T(128)} %bitcast.c_ref, s32[64]{0:T(128)S(1)} %and_select_fusion.place_ref, bf16[256,256]{1,0:T(8,128)(2,1)S(1)} %add_convert_fusion.refs_0_, bf16[256,256]{1,0:T(8,128)(2,1)S(1)} %collective-permute-done.16.refs_1_, ...), custom_call_target="tpu_custom_call" | custom-call | bytes 2097152 | tf_op jit(solution)/shard_map/pallas_call | solution.py:406
  102.6 5.3 %collective-permute-done.22.refs_1_ = bf16[256,256]{1,0:T(8,128)(2,1)S(1)} collective-permute-done((bf16[256,256]{1,0:T(8,128)(2,1)S(1)}, bf16[256,256]{1,0:T(8,128)(2,1)S(1)}, u32[]{:S(2)}, u32[]{:S(2)}) %collective-permute-start.22) | collective-permute-done | bytes 131104 | tf_op jit(solution)/shard_map/ppermute | solution.py:50
  109.4 7.9 %collective-permute-done.23.refs_2_ = bf16[256,256]{1,0:T(8,128)(2,1)S(1)} collective-permute-done((bf16[256,256]{1,0:T(8,128)(2,1)S(1)}, bf16[256,256]{1,0:T(8,128)(2,1)S(1)}, u32[]{:S(2)}, u32[]{:S(2)}) %collective-permute-start.23) | collective-permute-done | bytes 131104 | tf_op jit(solution)/shard_map/ppermute | solution.py:50
  120.1 2.4 %collective-permute-done.25.refs_9_ = bf16[1024,256]{1,0:T(8,128)(2,1)S(1)} collective-permute-done((bf16[1024,256]{1,0:T(8,128)(2,1)S(1)}, bf16[1024,256]{1,0:T(8,128)(2,1)S(1)}, u32[]{:S(2)}, u32[]{:S(2)}) %collective-permute-start.25) | collective-permute-done | bytes 524320 | tf_op jit(solution)/shard_map/ppermute | solution.py:41
  124.1 2.9 %shard_map.99 = bf16[256,2048]{1,0:T(8,128)(2,1)} custom-call(s32[1]{0:T(128)} %bitcast.11.d_ref, bf16[256,256]{1,0:T(8,128)(2,1)S(1)} %get-tuple-element.106.refs_0_, bf16[256,256]{1,0:T(8,128)(2,1)S(1)} %collective-permute-done.22.refs_1_, bf16[256,256]{1,0:T(8,128)(2,1)S(1)} %collective-permute-done.23.refs_2_, ...), custom_call_target="tpu_custom_call" | custom-call | flops 1073741824 | bytes 8388608 | tf_op jit(solution)/shard_map/pallas_call | solution.py:529
  (70 shorter events, 27.9 us)
Async XLA Ops:
  0.6 26.4 %collective-permute-start = (bf16[256,2048]{1,0:T(8,128)(2,1)}, bf16[256,2048]{1,0:T(8,128)(2,1)S(1)}, u32[]{:S(2)}, u32[]{:S(2)}) collective-permute-start(bf16[256,2048]{1,0:T(8,128)(2,1)} %bitcast.25), channel_id=1, source_target_pairs={{0,1},{1,0},{2,3},{3,2},{4,5},{5,4},{6,7},{7,6},{8,9},{9,8},{10,11... | collective-permute-start | bytes 3145736 | tf_op jit(solution)/shard_map/ppermute | solution.py:50
  3.6 25.2 %collective-permute-start.2 = (bf16[256,2048]{1,0:T(8,128)(2,1)}, bf16[256,2048]{1,0:T(8,128)(2,1)S(1)}, u32[]{:S(2)}, u32[]{:S(2)}) collective-permute-start(bf16[256,2048]{1,0:T(8,128)(2,1)} %bitcast.26), channel_id=1, source_target_pairs={{0,2},{1,3},{2,0},{3,1},{4,6},{5,7},{6,4},{7,5},{8,10},{9,11},{10,... | collective-permute-start | bytes 3145736 | tf_op jit(solution)/shard_map/ppermute | solution.py:50
  5.2 29.0 %collective-permute-start.4 = (bf16[512,256]{1,0:T(8,128)(2,1)}, bf16[512,256]{1,0:T(8,128)(2,1)S(1)}, u32[]{:S(2)}, u32[]{:S(2)}) collective-permute-start(bf16[512,256]{1,0:T(8,128)(2,1)} %bitcast.34), channel_id=1, source_target_pairs={{0,4},{4,8},{8,12},{1,5},{5,9},{9,13},{2,6},{6,10},{10,14},{3,7},{... | collective-permute-start | bytes 786440 | tf_op jit(solution)/shard_map/ppermute | solution.py:36
  27.1 13.2 %collective-permute-start.1 = (bf16[128,2048]{1,0:T(8,128)(2,1)S(1)}, bf16[128,2048]{1,0:T(8,128)(2,1)S(1)}, u32[]{:S(2)}, u32[]{:S(2)}) collective-permute-start(bf16[128,2048]{1,0:T(8,128)(2,1)S(1)} %slice.20), channel_id=1, source_target_pairs={{0,2},{1,3},{2,0},{3,1},{4,6},{5,7},{6,4},{7,5},{8,10},{9,11},{10,... | collective-permute-start | bytes 1572872 | tf_op jit(solution)/shard_map/ppermute | solution.py:50
  28.9 12.6 %collective-permute-start.3 = (bf16[128,2048]{1,0:T(8,128)(2,1)S(1)}, bf16[128,2048]{1,0:T(8,128)(2,1)S(1)}, u32[]{:S(2)}, u32[]{:S(2)}) collective-permute-start(bf16[128,2048]{1,0:T(8,128)(2,1)S(1)} %slice.21), channel_id=1, source_target_pairs={{0,1},{1,0},{2,3},{3,2},{4,5},{5,4},{6,7},{7,6},{8,9},{9,8},{10,11... | collective-permute-start | bytes 1572872 | tf_op jit(solution)/shard_map/ppermute | solution.py:50
  42.9 7.2 %collective-permute-start.5 = (bf16[2,64,256]{2,1,0:T(8,128)(2,1)S(1)}, bf16[2,64,256]{2,1,0:T(8,128)(2,1)S(1)}, u32[]{:S(2)}, u32[]{:S(2)}) collective-permute-start(bf16[2,64,256]{2,1,0:T(8,128)(2,1)S(1)} %get-tuple-element.72), channel_id=1, source_target_pairs={{0,4},{4,0},{8,12},{12,8},{1,5},{5,1},{9,13},{13,9},{2,6},{6,2},{1... | collective-permute-start | bytes 196616 | tf_op jit(solution)/shard_map/ppermute | solution.py:50
  47.4 26.0 %collective-permute-start.8 = (bf16[1024,256]{1,0:T(8,128)(2,1)S(1)}, bf16[1024,256]{1,0:T(8,128)(2,1)S(1)}, u32[]{:S(2)}, u32[]{:S(2)}) collective-permute-start(bf16[1024,256]{1,0:T(8,128)(2,1)S(1)} %get-tuple-element.87), channel_id=1, source_target_pairs={{0,1},{1,0},{2,3},{3,2},{4,5},{5,4},{6,7},{7,6},{8,9},{9,8},{10,11... | collective-permute-start | bytes 1572872 | tf_op jit(solution)/shard_map/ppermute | solution.py:50
  48.9 24.5 %collective-permute-start.9 = (bf16[1024,256]{1,0:T(8,128)(2,1)S(1)}, bf16[1024,256]{1,0:T(8,128)(2,1)S(1)}, u32[]{:S(2)}, u32[]{:S(2)}) collective-permute-start(bf16[1024,256]{1,0:T(8,128)(2,1)S(1)} %get-tuple-element.88), channel_id=1, source_target_pairs={{0,3},{1,2},{2,1},{3,0},{4,7},{5,6},{6,5},{7,4},{8,11},{9,10},{10,... | collective-permute-start | bytes 1572872 | tf_op jit(solution)/shard_map/ppermute | solution.py:50
  53.9 15.9 %collective-permute-start.10 = (bf16[256,512]{1,0:T(8,128)(2,1)S(1)}, bf16[256,512]{1,0:T(8,128)(2,1)S(1)}, u32[]{:S(2)}, u32[]{:S(2)}) collective-permute-start(bf16[256,512]{1,0:T(8,128)(2,1)S(1)} %get-tuple-element.89), channel_id=1, source_target_pairs={{0,4},{4,0},{8,12},{12,8},{1,5},{5,1},{9,13},{13,9},{2,6},{6,2},{1... | collective-permute-start | bytes 786440 | tf_op jit(solution)/shard_map/ppermute | solution.py:50
  53.9 19.4 %collective-permute-start.11 = (bf16[256,512]{1,0:T(8,128)(2,1)S(1)}, bf16[256,512]{1,0:T(8,128)(2,1)S(1)}, u32[]{:S(2)}, u32[]{:S(2)}) collective-permute-start(bf16[256,512]{1,0:T(8,128)(2,1)S(1)} %get-tuple-element.90), channel_id=1, source_target_pairs={{0,8},{4,12},{8,0},{12,4},{1,9},{5,13},{9,1},{13,5},{2,10},{6,14},... | collective-permute-start | bytes 786440 | tf_op jit(solution)/shard_map/ppermute | solution.py:50
  54.6 18.7 %collective-permute-start.12 = (bf16[256,512]{1,0:T(8,128)(2,1)S(1)}, bf16[256,512]{1,0:T(8,128)(2,1)S(1)}, u32[]{:S(2)}, u32[]{:S(2)}) collective-permute-start(bf16[256,512]{1,0:T(8,128)(2,1)S(1)} %get-tuple-element.91), channel_id=1, source_target_pairs={{0,12},{4,8},{8,4},{12,0},{1,13},{5,9},{9,5},{13,1},{2,14},{6,10},... | collective-permute-start | bytes 786440 | tf_op jit(solution)/shard_map/ppermute | solution.py:50
  73.4 21.6 %collective-permute-start.13 = (bf16[768,512]{1,0:T(8,128)(2,1)S(1)}, bf16[768,512]{1,0:T(8,128)(2,1)S(1)}, u32[]{:S(2)}, u32[]{:S(2)}) collective-permute-start(bf16[768,512]{1,0:T(8,128)(2,1)S(1)} %constant_dynamic-update-slice_fusion.refs_0_), channel_id=1, source_target_pairs={{0,1},{1,0},{2,3},{3,2},{4,5},{5,4},{6,7},{7,6},{8,9},{9,8},{10,11... | collective-permute-start | bytes 2359304 | tf_op jit(solution)/shard_map/ppermute | solution.py:50
  75.0 20.1 %collective-permute-start.14 = (bf16[768,512]{1,0:T(8,128)(2,1)S(1)}, bf16[768,512]{1,0:T(8,128)(2,1)S(1)}, u32[]{:S(2)}, u32[]{:S(2)}) collective-permute-start(bf16[768,512]{1,0:T(8,128)(2,1)S(1)} %constant_dynamic-update-slice_fusion.refs_0_), channel_id=1, source_target_pairs={{0,2},{1,3},{2,0},{3,1},{4,6},{5,7},{6,4},{7,5},{8,10},{9,11},{10,... | collective-permute-start | bytes 2359304 | tf_op jit(solution)/shard_map/ppermute | solution.py:50
  75.5 9.3 %collective-permute-start.15 = (bf16[256,256]{1,0:T(8,128)(2,1)S(1)}, bf16[256,256]{1,0:T(8,128)(2,1)S(1)}, u32[]{:S(2)}, u32[]{:S(2)}) collective-permute-start(bf16[256,256]{1,0:T(8,128)(2,1)S(1)} %get-tuple-element.96), channel_id=1, source_target_pairs={{4,0},{8,4},{12,8},{5,1},{9,5},{13,9},{6,2},{10,6},{14,10},{7,3},{... | collective-permute-start | bytes 393224 | tf_op jit(solution)/shard_map/ppermute | solution.py:36
  86.0 9.0 %collective-permute-start.17 = (bf16[256,256]{1,0:T(8,128)(2,1)S(1)}, bf16[256,256]{1,0:T(8,128)(2,1)S(1)}, u32[]{:S(2)}, u32[]{:S(2)}) collective-permute-start(bf16[256,256]{1,0:T(8,128)(2,1)S(1)} %add_convert_fusion.refs_0_), channel_id=1, source_target_pairs={{0,8},{4,12},{8,0},{12,4},{1,9},{5,13},{9,1},{13,5},{2,10},{6,14},... | collective-permute-start | bytes 393224 | tf_op jit(solution)/shard_map/ppermute | solution.py:50
  87.2 7.8 %collective-permute-start.18 = (bf16[256,256]{1,0:T(8,128)(2,1)S(1)}, bf16[256,256]{1,0:T(8,128)(2,1)S(1)}, u32[]{:S(2)}, u32[]{:S(2)}) collective-permute-start(bf16[256,256]{1,0:T(8,128)(2,1)S(1)} %add_convert_fusion.refs_0_), channel_id=1, source_target_pairs={{0,12},{4,8},{8,4},{12,0},{1,13},{5,9},{9,5},{13,1},{2,14},{6,10},... | collective-permute-start | bytes 393224 | tf_op jit(solution)/shard_map/ppermute | solution.py:50
  95.0 22.3 %collective-permute-start.21 = (bf16[1024,256]{1,0:T(8,128)(2,1)S(1)}, bf16[1024,256]{1,0:T(8,128)(2,1)S(1)}, u32[]{:S(2)}, u32[]{:S(2)}) collective-permute-start(bf16[1024,256]{1,0:T(8,128)(2,1)S(1)} %get-tuple-element.104), channel_id=1, source_target_pairs={{0,2},{1,3},{2,0},{3,1},{4,6},{5,7},{6,4},{7,5},{8,10},{9,11},{10,... | collective-permute-start | bytes 1572872 | tf_op jit(solution)/shard_map/ppermute | solution.py:50
  96.7 20.6 %collective-permute-start.19 = (bf16[384,512]{1,0:T(8,128)(2,1)S(1)}, bf16[384,512]{1,0:T(8,128)(2,1)S(1)}, u32[]{:S(2)}, u32[]{:S(2)}) collective-permute-start(bf16[384,512]{1,0:T(8,128)(2,1)S(1)} %slice.18), channel_id=1, source_target_pairs={{0,2},{1,3},{2,0},{3,1},{4,6},{5,7},{6,4},{7,5},{8,10},{9,11},{10,... | collective-permute-start | bytes 1179656 | tf_op jit(solution)/shard_map/ppermute | solution.py:50
  97.3 20.0 %collective-permute-start.20 = (bf16[384,512]{1,0:T(8,128)(2,1)S(1)}, bf16[384,512]{1,0:T(8,128)(2,1)S(1)}, u32[]{:S(2)}, u32[]{:S(2)}) collective-permute-start(bf16[384,512]{1,0:T(8,128)(2,1)S(1)} %slice.19), channel_id=1, source_target_pairs={{0,1},{1,0},{2,3},{3,2},{4,5},{5,4},{6,7},{7,6},{8,9},{9,8},{10,11... | collective-permute-start | bytes 1179656 | tf_op jit(solution)/shard_map/ppermute | solution.py:50
  100.1 7.8 %collective-permute-start.22 = (bf16[256,256]{1,0:T(8,128)(2,1)S(1)}, bf16[256,256]{1,0:T(8,128)(2,1)S(1)}, u32[]{:S(2)}, u32[]{:S(2)}) collective-permute-start(bf16[256,256]{1,0:T(8,128)(2,1)S(1)} %get-tuple-element.106.refs_0_), channel_id=1, source_target_pairs={{0,1},{1,0},{2,3},{3,2},{4,5},{5,4},{6,7},{7,6},{8,9},{9,8},{10,11... | collective-permute-start | bytes 393224 | tf_op jit(solution)/shard_map/ppermute | solution.py:50
  101.1 16.2 %collective-permute-start.23 = (bf16[256,256]{1,0:T(8,128)(2,1)S(1)}, bf16[256,256]{1,0:T(8,128)(2,1)S(1)}, u32[]{:S(2)}, u32[]{:S(2)}) collective-permute-start(bf16[256,256]{1,0:T(8,128)(2,1)S(1)} %get-tuple-element.106.refs_0_), channel_id=1, source_target_pairs={{0,2},{1,3},{2,0},{3,1},{4,6},{5,7},{6,4},{7,5},{8,10},{9,11},{10,... | collective-permute-start | bytes 393224 | tf_op jit(solution)/shard_map/ppermute | solution.py:50
  107.9 9.4 %collective-permute-start.24 = (bf16[256,256]{1,0:T(8,128)(2,1)S(1)}, bf16[256,256]{1,0:T(8,128)(2,1)S(1)}, u32[]{:S(2)}, u32[]{:S(2)}) collective-permute-start(bf16[256,256]{1,0:T(8,128)(2,1)S(1)} %get-tuple-element.106.refs_0_), channel_id=1, source_target_pairs={{0,3},{1,2},{2,1},{3,0},{4,7},{5,6},{6,5},{7,4},{8,11},{9,10},{10,... | collective-permute-start | bytes 393224 | tf_op jit(solution)/shard_map/ppermute | solution.py:50
  118.4 8.7 %collective-permute-start.28 = (f32[3,512,256]{2,1,0:T(8,128)S(1)}, f32[3,512,256]{2,1,0:T(8,128)S(1)}, u32[]{:S(2)}, u32[]{:S(2)}) collective-permute-start(f32[3,512,256]{2,1,0:T(8,128)S(1)} %shard_map.100.refs_0_), channel_id=1, source_target_pairs={{0,16},{16,0},{1,17},{17,1},{2,18},{18,2},{3,19},{19,3},{4,20},{20... | collective-permute-start | bytes 4718600 | tf_op jit(solution)/shard_map/ppermute | solution.py:41
  120.0 7.0 %collective-permute-start.29 = (f32[1,512,256]{2,1,0:T(8,128)S(1)}, f32[1,512,256]{2,1,0:T(8,128)S(1)}, u32[]{:S(2)}, u32[]{:S(2)}) collective-permute-start(f32[1,512,256]{2,1,0:T(8,128)S(1)} %shard_map.101.refs_1_), channel_id=1, source_target_pairs={{0,16},{16,0},{1,17},{17,1},{2,18},{18,2},{3,19},{19,3},{4,20},{20... | collective-permute-start | bytes 1572872 | tf_op jit(solution)/shard_map/ppermute | solution.py:41
  (12 other events, 106.8 us)

commit v11 on v10

--- a/solution.py
+++ b/solution.py
@@ -58,7 +58,7 @@
     m = m_ref[0]
     d = d_ref[0]
     feats = own_ref.shape[1]
-    half = slab_refs[0].shape[0]
+    half = slab_refs[1].shape[0]
 
     def rows(k, at, count):
         return pl.ds(pl.multiple_of((m ^ k) * feats + at, half), count)
@@ -67,8 +67,8 @@
     for k, ref in ((1, x_ref), (2, y_ref)):
         total = total + dot(ref[...], weight_ref[rows(k, 0, feats), :], NN)
     out_ref[...] = total
-    for k, side, ref in zip((1, 2, 3, 0, 0), (d, d, d, d, 1 - d), slab_refs):
-        ref[...] = weight_ref[rows(k, side * half, half), :]
+    for k, at, ref in zip((1 + d, 3, 0), (0, d * half, 0), slab_refs):
+        ref[...] = weight_ref[rows(k, at, ref.shape[0]), :]
 
 
 def project(m, d, blocks, weights):
@@ -76,12 +76,12 @@
     width = weights.shape[1]
     smem = pl.BlockSpec(memory_space=pltpu.SMEM)
     vmem = pl.BlockSpec(memory_space=pltpu.VMEM)
-    slab = jax.ShapeDtypeStruct((feats // 2, width), weights.dtype)
+    slabs = [jax.ShapeDtypeStruct((r, width), weights.dtype) for r in (feats, feats // 2, feats)]
     return pl.pallas_call(
         project_body,
         in_specs=[smem, smem] + [vmem] * 4,
-        out_specs=[vmem] * 6,
-        out_shape=[jax.ShapeDtypeStruct((rows, width), jnp.float32)] + [slab] * 5,
+        out_specs=[vmem] * 4,
+        out_shape=[jax.ShapeDtypeStruct((rows, width), jnp.float32)] + slabs,
         cost_estimate=cost(6 * rows * feats * width, 4 * weights.size),
         compiler_params=params(),
     )(m, d, *blocks, weights)
@@ -503,41 +503,33 @@
     )(m, *own, *other)
 
 
-def image_body(d_ref, *refs):
-    out_ref = refs[-1]
-    heads = (len(refs) - 1) // 3
-    grads, near, far = refs[:heads], refs[heads : 2 * heads], refs[2 * heads : -1]
-    j = pl.program_id(0)
-    cols = near[0].shape[0]
-    half = out_ref.shape[1] // 2
+def image_body(d_ref, g0, g1, g2, g3, own_ref, first_ref, second_ref, near_ref, far_ref, out_ref):
+    half = near_ref.shape[0]
+    tile = half // 4
     d = d_ref[0]
-    for weights, side in ((near, d), (far, 1 - d)):
-        total = dot(grads[0][...], weights[0][...], NT)
-        for h in range(1, heads):
-            total = total + dot(grads[h][...], weights[h][...], NT)
-        at = pl.multiple_of(side * half + j * cols, cols)
-        out_ref[:, pl.ds(at, cols)] = total.astype(out_ref.dtype)
-
-
-def image_term(d, grads, near, far):
-    heads = len(near)
-    half, width = near[0].shape
+    first = jnp.where(d == 0, g1[...], g2[...])
+    second = jnp.where(d == 0, g2[...], g1[...])
+    for ref, side in ((near_ref, d), (far_ref, 1 - d)):
+        for j in range(0, half, tile):
+            at = pl.ds(pl.multiple_of(side * half + j, tile), tile)
+            total = dot(g0[...], own_ref[at, :], NT) + dot(first, first_ref[at, :], NT)
+            total = total + dot(second, second_ref[at, :], NT)
+            total = total + dot(g3[...], ref[j : j + tile, :], NT)
+            out_ref[:, at] = total.astype(out_ref.dtype)
+
+
+def image_term(d, grads, weights):
+    feats, width = weights[0].shape
     rows = grads[0].shape[0]
-    tiles = 4
-    side = pl.BlockSpec((half // tiles, width), lambda j, d: (j, 0))
-    grad = pl.BlockSpec((rows, width), lambda j, d: (0, 0))
+    vmem = pl.BlockSpec(memory_space=pltpu.VMEM)
     return pl.pallas_call(
         image_body,
-        grid_spec=pltpu.PrefetchScalarGridSpec(
-            num_scalar_prefetch=1,
-            grid=(tiles,),
-            in_specs=[grad] * heads + [side] * (2 * heads),
-            out_specs=pl.BlockSpec((rows, 2 * half), lambda j, d: (0, 0)),
-        ),
-        out_shape=jax.ShapeDtypeStruct((rows, 2 * half), jnp.bfloat16),
-        cost_estimate=cost(4 * heads * half * width * rows, 4 * heads * half * width * 2),
-        compiler_params=params(),
-    )(d, *grads, *near, *far)
+        in_specs=[pl.BlockSpec(memory_space=pltpu.SMEM)] + [vmem] * 9,
+        out_specs=vmem,
+        out_shape=jax.ShapeDtypeStruct((rows, feats), jnp.bfloat16),
+        cost_estimate=cost(8 * feats * width * rows, 8 * feats * width),
+        compiler_params=params(),
+    )(d, *grads, *weights)
 
 
 def per_device(image_states, place_index, doc_ids, queries, text_kv, kv_weight, d_out):
@@ -582,9 +574,12 @@
         m1, c1, place, low, high, weights, part, ranks, capacity, per_shard, mixed
     )
 
-    *slabs, _ = lax.optimization_barrier((*slabs, packed[0]))
-    slabs, own_slabs = slabs[:3], slabs[3:]
-    near = [trade(slabs[0], "mp", 1), None, trade(slabs[2], "mp", 3)]
+    *slabs, own_slab, _ = lax.optimization_barrier((*slabs, packed[0]))
+    cores = lax.axis_size("dp")
+    route = [
+        (i * mps + j, i * mps + (j ^ (1 + i))) for i in range(cores) for j in range(mps)
+    ]
+    near = [lax.ppermute(slabs[0], ("dp", "mp"), route), trade(slabs[1], "mp", 3)]
 
     if mixed:
         c2, _ = lax.optimization_barrier((c1, packed[0]))
@@ -604,10 +599,10 @@
         c1, place, start, queries[0], d_out[0], text_kv[0], prior_text, image,
         images, per_shard, image_rows,
     )
-    prior_grad, near[0], near[2], *moved = lax.optimization_barrier(
-        (prior_grad, near[0], near[2], *moved)
+    prior_grad, near[0], near[1], *moved = lax.optimization_barrier(
+        (prior_grad, near[0], near[1], *moved)
     )
-    far = [own_slabs[1], swap(near[0], "dp"), None, swap(near[2], "dp")]
+    far = [swap(w, "dp") for w in near]
     grad = own_grad + shift(prior_grad, "ctx", -1).astype(jnp.float32)
     grad = grad.astype(jnp.bfloat16)
     if mixed:
@@ -620,21 +615,16 @@
         gathered = [exchange(jnp.broadcast_to(grad, (ranks,) + grad.shape), "ctx")]
         all_states = lax.all_gather(moved[0], "mp", axis=0)
         base_x = base_y = all_states
-    slabs[1], base_x, base_y, *gathered = lax.optimization_barrier(
-        (slabs[1], base_x, base_y, *gathered)
-    )
-    near[1] = trade(slabs[1], "mp", 2)
+    base_x, base_y, *gathered = lax.optimization_barrier((base_x, base_y, *gathered))
     by_rank, mine = reorder(c1, place, gathered, per_shard, images, ranks)
     head_grad = [mine] + [trade(mine, "mp", s) for s in steps]
     if mixed:
         base_low = trade(base_x[:cut], "mp", 2)
         base_high = trade(base_y[cut:], "mp", 1)
-        by_rank, base_low, base_high, near[1], *head_grad = lax.optimization_barrier(
-            (by_rank, base_low, base_high, near[1], *head_grad)
+        by_rank, base_low, base_high, *head_grad = lax.optimization_barrier(
+            (by_rank, base_low, base_high, *head_grad)
         )
-    far[2] = swap(near[1], "dp")
-    near = [own_slabs[0]] + list(near)
-    image_grad = image_term(d1, head_grad, near, far)
+    image_grad = image_term(d1, head_grad, [own_slab, near[0], far[0], near[1], far[1]])
     if mixed:
         by_rank = by_rank.reshape(ranks, image_rows, width)
         terms = [

time: 129 us -> 118 us (0.915)
  waiting for transfers between devices: 62.1 us -> 53.4 us
    ppermute x23 -> x21, waiting for transfers between devices: 50.3 us -> 42.2 us  [trade(): return lax.ppermute(block, axis, [(i, i ^ step) for i in range(count)])]
    ppermute x23 -> x21, starting transfers between devices: 33.1 us -> 30.6 us  [trade(): return lax.ppermute(block, axis, [(i, i ^ step) for i in range(count)])]
    ppermute x0 -> x1, starting transfers between devices: none -> 1.5 us  [per_device(): lax.ppermute(slabs[0], ('dp', 'mp'), route)]
    ppermute x5 -> x4, waiting for transfers between devices: 3.95 us -> 4.03 us  [swap(): return lax.ppermute(block, axis, [(i, count - 1 - i) for i in range(count)])]
  transfers between devices with their start and end apart: 30 -> 28, of which waited for: 14 -> 13; matrix products, arithmetic and copies ran while one was open for 2% -> 2% of each run, Pallas kernels for 14% -> 15%
where the time goes in v11:
time: 118 us
  waiting for transfers between devices  53.4 us (45%)
  starting transfers between devices  38.2 us (32%)
  Pallas kernels  21.3 us (18%)
  local copies, waits for them, and re-layouts  3.22 us (3%)
    ppermute x21, waiting for transfers between devices, trade(): return lax.ppermute(block, axis, [(i, i ^ step) for i in range(count)])  42.2 us
    ppermute x21, starting transfers between devices, trade(): return lax.ppermute(block, axis, [(i, i ^ step) for i in range(count)])  30.6 us
    pallas_call x1, Pallas kernels, attention(): pl.pallas_call(functools.partial(attention_body, per_shard, images), grid...  11.5 us
    ppermute x2, waiting for transfers between devices, shift(): return lax.ppermute(block, axis, route)  7.14 us
    ppermute x2, starting transfers between devices, shift(): return lax.ppermute(block, axis, route)  4.95 us
    ppermute x4, waiting for transfers between devices, swap(): return lax.ppermute(block, axis, [(i, count - 1 - i) for i in range(count)])  4.03 us
  transfers between devices with their start and end apart: 28, of which 13 were waited for; matrix products, arithmetic and copies ran while one was open for 2% of the time, Pallas kernels for 15%

profile of v11, /device:TPU:0, one launch (start us, length us, event | category | flops | bytes accessed | tf_op | source)
XLA Modules:
  0.0 118.1 jit_solution(10210840080258924397)
XLA Ops:
  0.6 3.0 %collective-permute-start = (bf16[256,2048]{1,0:T(8,128)(2,1)}, bf16[256,2048]{1,0:T(8,128)(2,1)S(1)}, u32[]{:S(2)}, u32[]{:S(2)}) collective-permute-start(bf16[256,2048]{1,0:T(8,128)(2,1)} %bitcast.25), channel_id=1, source_target_pairs={{0,1},{1,0},{2,3},{3,2},{4,5},{5,4},{6,7},{7,6},{8,9},{9,8},{10,11... | collective-permute-start | bytes 3145736 | tf_op jit(solution)/shard_map/ppermute | solution.py:50
  5.2 3.5 %collective-permute-start.4 = (bf16[512,256]{1,0:T(8,128)(2,1)}, bf16[512,256]{1,0:T(8,128)(2,1)S(1)}, u32[]{:S(2)}, u32[]{:S(2)}) collective-permute-start(bf16[512,256]{1,0:T(8,128)(2,1)} %bitcast.34), channel_id=1, source_target_pairs={{0,4},{4,8},{8,12},{1,5},{5,9},{9,13},{2,6},{6,10},{10,14},{3,7},{... | collective-permute-start | bytes 786440 | tf_op jit(solution)/shard_map/ppermute | solution.py:36
  10.3 16.7 %collective-permute-done.x_ref = bf16[256,2048]{1,0:T(8,128)(2,1)S(1)} collective-permute-done((bf16[256,2048]{1,0:T(8,128)(2,1)}, bf16[256,2048]{1,0:T(8,128)(2,1)S(1)}, u32[]{:S(2)}, u32[]{:S(2)}) %collective-permute-start) | collective-permute-done | bytes 1048608 | tf_op jit(solution)/shard_map/ppermute | solution.py:50
  27.1 1.8 %collective-permute-start.1 = (bf16[128,2048]{1,0:T(8,128)(2,1)S(1)}, bf16[128,2048]{1,0:T(8,128)(2,1)S(1)}, u32[]{:S(2)}, u32[]{:S(2)}) collective-permute-start(bf16[128,2048]{1,0:T(8,128)(2,1)S(1)} %slice.20), channel_id=1, source_target_pairs={{0,2},{1,3},{2,0},{3,1},{4,6},{5,7},{6,4},{7,5},{8,10},{9,11},{10,... | collective-permute-start | bytes 1572872 | tf_op jit(solution)/shard_map/ppermute | solution.py:50
  28.9 1.6 %collective-permute-start.3 = (bf16[128,2048]{1,0:T(8,128)(2,1)S(1)}, bf16[128,2048]{1,0:T(8,128)(2,1)S(1)}, u32[]{:S(2)}, u32[]{:S(2)}) collective-permute-start(bf16[128,2048]{1,0:T(8,128)(2,1)S(1)} %slice.21), channel_id=1, source_target_pairs={{0,1},{1,0},{2,3},{3,2},{4,5},{5,4},{6,7},{7,6},{8,9},{9,8},{10,11... | collective-permute-start | bytes 1572872 | tf_op jit(solution)/shard_map/ppermute | solution.py:50
  30.8 2.2 %copy-done = bf16[1,8192,256]{2,1,0:T(8,128)(2,1)S(1)} copy-done((bf16[1,8192,256]{2,1,0:T(8,128)(2,1)S(1)}, bf16[1,8192,256]{2,1,0:T(8,128)(2,1)}, u32[]{:S(2)}) %copy-start) | copy-done | bytes 4194328
  34.2 6.1 %collective-permute-done.1.low_ref = bf16[128,2048]{1,0:T(8,128)(2,1)S(1)} collective-permute-done((bf16[128,2048]{1,0:T(8,128)(2,1)S(1)}, bf16[128,2048]{1,0:T(8,128)(2,1)S(1)}, u32[]{:S(2)}, u32[]{:S(2)}) %collective-permute-start.1) | collective-permute-done | bytes 524320 | tf_op jit(solution)/shard_map/ppermute | solution.py:50
  42.9 1.6 %collective-permute-start.5 = (bf16[2,64,256]{2,1,0:T(8,128)(2,1)S(1)}, bf16[2,64,256]{2,1,0:T(8,128)(2,1)S(1)}, u32[]{:S(2)}, u32[]{:S(2)}) collective-permute-start(bf16[2,64,256]{2,1,0:T(8,128)(2,1)S(1)} %get-tuple-element.66), channel_id=1, source_target_pairs={{0,4},{4,0},{8,12},{12,8},{1,5},{5,1},{9,13},{13,9},{2,6},{6,2},{1... | collective-permute-start | bytes 196616 | tf_op jit(solution)/shard_map/ppermute | solution.py:50
  44.5 2.6 %collective-permute-start.6 = (bf16[2,64,256]{2,1,0:T(8,128)(2,1)S(1)}, bf16[2,64,256]{2,1,0:T(8,128)(2,1)S(1)}, u32[]{:S(2)}, u32[]{:S(2)}) collective-permute-start(bf16[2,64,256]{2,1,0:T(8,128)(2,1)S(1)} %get-tuple-element.67), channel_id=1, source_target_pairs={{0,8},{4,12},{8,0},{12,4},{1,9},{5,13},{9,1},{13,5},{2,10},{6,14},... | collective-permute-start | bytes 196616 | tf_op jit(solution)/shard_map/ppermute | solution.py:50
  51.0 3.0 %collective-permute-done.7.refs_3_ = bf16[2,64,256]{2,1,0:T(8,128)(2,1)S(1)} collective-permute-done((bf16[2,64,256]{2,1,0:T(8,128)(2,1)S(1)}, bf16[2,64,256]{2,1,0:T(8,128)(2,1)S(1)}, u32[]{:S(2)}, u32[]{:S(2)}) %collective-permute-start.7) | collective-permute-done | bytes 65568 | tf_op jit(solution)/shard_map/ppermute | solution.py:50
  54.6 3.7 %collective-permute-start.12 = (bf16[256,512]{1,0:T(8,128)(2,1)S(1)}, bf16[256,512]{1,0:T(8,128)(2,1)S(1)}, u32[]{:S(2)}, u32[]{:S(2)}) collective-permute-start(bf16[256,512]{1,0:T(8,128)(2,1)S(1)} %get-tuple-element.82), channel_id=1, source_target_pairs={{0,12},{4,8},{8,4},{12,0},{1,13},{5,9},{9,5},{13,1},{2,14},{6,10},... | collective-permute-start | bytes 786440 | tf_op jit(solution)/shard_map/ppermute | solution.py:50
  58.3 11.5 %shard_map.97 = (bf16[512,1024]{1,0:T(8,128)(2,1)}, f32[256,256]{1,0:T(8,128)S(1)}, bf16[256,256]{1,0:T(8,128)(2,1)S(1)}) custom-call(s32[1]{0:T(128)} %bitcast.c_ref, s32[64]{0:T(128)S(1)} %and_select_fusion.place_ref, s32[1,512]{1,0:T(1,128)S(1)} %bitcast.31, bf16[512,1024]{1,0:T(8,128)(2,1)S(1)} %bitcast.32, bf16[512,1024]{1,0:T(8,128)(2,1)S(1)} %bitcast.33, ...), custom_call_target="tpu_custom_call" | custom-call | flops 13421772800 | bytes 4194304 | tf_op jit(solution)/shard_map/pallas_call | solution.py:348
  69.9 3.5 %collective-permute-done.11 = bf16[256,512]{1,0:T(8,128)(2,1)S(1)} collective-permute-done((bf16[256,512]{1,0:T(8,128)(2,1)S(1)}, bf16[256,512]{1,0:T(8,128)(2,1)S(1)}, u32[]{:S(2)}, u32[]{:S(2)}) %collective-permute-start.11) | collective-permute-done | bytes 262176 | tf_op jit(solution)/shard_map/ppermute | solution.py:50
  77.7 7.1 %collective-permute-done.15 = bf16[256,256]{1,0:T(8,128)(2,1)S(1)} collective-permute-done((bf16[256,256]{1,0:T(8,128)(2,1)S(1)}, bf16[256,256]{1,0:T(8,128)(2,1)S(1)}, u32[]{:S(2)}, u32[]{:S(2)}) %collective-permute-start.15) | collective-permute-done | bytes 131104 | tf_op jit(solution)/shard_map/ppermute | solution.py:36
  87.2 2.1 %collective-permute-start.18 = (bf16[256,256]{1,0:T(8,128)(2,1)S(1)}, bf16[256,256]{1,0:T(8,128)(2,1)S(1)}, u32[]{:S(2)}, u32[]{:S(2)}) collective-permute-start(bf16[256,256]{1,0:T(8,128)(2,1)S(1)} %add_convert_fusion.refs_0_), channel_id=1, source_target_pairs={{0,12},{4,8},{8,4},{12,0},{1,13},{5,9},{9,5},{13,1},{2,14},{6,10},... | collective-permute-start | bytes 393224 | tf_op jit(solution)/shard_map/ppermute | solution.py:50
  89.3 1.8 %collective-permute-done.16.refs_1_ = bf16[256,256]{1,0:T(8,128)(2,1)S(1)} collective-permute-done((bf16[256,256]{1,0:T(8,128)(2,1)S(1)}, bf16[256,256]{1,0:T(8,128)(2,1)S(1)}, u32[]{:S(2)}, u32[]{:S(2)}) %collective-permute-start.16) | collective-permute-done | bytes 131104 | tf_op jit(solution)/shard_map/ppermute | solution.py:50
  91.1 3.9 %collective-permute-done.17.refs_2_ = bf16[256,256]{1,0:T(8,128)(2,1)S(1)} collective-permute-done((bf16[256,256]{1,0:T(8,128)(2,1)S(1)}, bf16[256,256]{1,0:T(8,128)(2,1)S(1)}, u32[]{:S(2)}, u32[]{:S(2)}) %collective-permute-start.17) | collective-permute-done | bytes 131104 | tf_op jit(solution)/shard_map/ppermute | solution.py:50
  95.1 1.6 %collective-permute-start.19 = (bf16[384,512]{1,0:T(8,128)(2,1)S(1)}, bf16[384,512]{1,0:T(8,128)(2,1)S(1)}, u32[]{:S(2)}, u32[]{:S(2)}) collective-permute-start(bf16[384,512]{1,0:T(8,128)(2,1)S(1)} %slice.18), channel_id=1, source_target_pairs={{0,2},{1,3},{2,0},{3,1},{4,6},{5,7},{6,4},{7,5},{8,10},{9,11},{10,... | collective-permute-start | bytes 1179656 | tf_op jit(solution)/shard_map/ppermute | solution.py:50
  97.3 1.7 %shard_map.98 = (bf16[1024,256]{1,0:T(8,128)(2,1)S(1)}, bf16[256,256]{1,0:T(8,128)(2,1)S(1)}) custom-call(s32[1]{0:T(128)} %bitcast.c_ref, s32[64]{0:T(128)S(1)} %and_select_fusion.place_ref, bf16[256,256]{1,0:T(8,128)(2,1)S(1)} %add_convert_fusion.refs_0_, bf16[256,256]{1,0:T(8,128)(2,1)S(1)} %collective-permute-done.16.refs_1_, ...), custom_call_target="tpu_custom_call" | custom-call | bytes 2097152 | tf_op jit(solution)/shard_map/pallas_call | solution.py:406
  99.0 1.6 %collective-permute-start.21 = (bf16[256,256]{1,0:T(8,128)(2,1)S(1)}, bf16[256,256]{1,0:T(8,128)(2,1)S(1)}, u32[]{:S(2)}, u32[]{:S(2)}) collective-permute-start(bf16[256,256]{1,0:T(8,128)(2,1)S(1)} %get-tuple-element.96.g0), channel_id=1, source_target_pairs={{0,1},{1,0},{2,3},{3,2},{4,5},{5,4},{6,7},{7,6},{8,9},{9,8},{10,11... | collective-permute-start | bytes 393224 | tf_op jit(solution)/shard_map/ppermute | solution.py:50
  102.5 3.5 %collective-permute-done.21.g1 = bf16[256,256]{1,0:T(8,128)(2,1)S(1)} collective-permute-done((bf16[256,256]{1,0:T(8,128)(2,1)S(1)}, bf16[256,256]{1,0:T(8,128)(2,1)S(1)}, u32[]{:S(2)}, u32[]{:S(2)}) %collective-permute-start.21) | collective-permute-done | bytes 131104 | tf_op jit(solution)/shard_map/ppermute | solution.py:50
  110.2 4.0 %collective-permute-done.25.far_ref = bf16[1024,256]{1,0:T(8,128)(2,1)S(1)} collective-permute-done((bf16[1024,256]{1,0:T(8,128)(2,1)S(1)}, bf16[1024,256]{1,0:T(8,128)(2,1)S(1)}, u32[]{:S(2)}, u32[]{:S(2)}) %collective-permute-start.25) | collective-permute-done | bytes 524320 | tf_op jit(solution)/shard_map/ppermute | solution.py:41
  114.2 2.3 %shard_map.99 = bf16[256,2048]{1,0:T(8,128)(2,1)} custom-call(s32[1]{0:T(128)} %bitcast.11.d_ref, bf16[256,256]{1,0:T(8,128)(2,1)S(1)} %get-tuple-element.96.g0, bf16[256,256]{1,0:T(8,128)(2,1)S(1)} %collective-permute-done.21.g1, bf16[256,256]{1,0:T(8,128)(2,1)S(1)} %collective-permute-done.22.g2, bf16[256,256]{1,0:T(8,128)(2,1)S(1)} %collective-permute-done.23.g3, ...), custom_call_target="tpu_custom_call" | custom-call | flops 1073741824 | bytes 4194304 | tf_op jit(solution)/shard_map/pallas_call | solution.py:525
  116.5 1.5 %shard_map.102 = f32[2048,256]{1,0:T(8,128)} custom-call(s32[1]{0:T(128)} %bitcast.9.m_ref, f32[3,512,256]{2,1,0:T(8,128)S(1)} %shard_map.100.refs_0_, f32[1,512,256]{2,1,0:T(8,128)S(1)} %shard_map.101.refs_1_, f32[3,512,256]{2,1,0:T(8,128)S(1)} %collective-permute-done.26.refs_2_, f32[1,512,256]{2,1,0:T(8,128)S(1)} %collective-permute-done.27.refs_3_), custom_call_target="tpu_custom_call" | custom-call | bytes 6291456 | tf_op jit(solution)/shard_map/pallas_call | solution.py:496
  (66 shorter events, 25.3 us)
Async XLA Ops:
  0.6 26.4 %collective-permute-start = (bf16[256,2048]{1,0:T(8,128)(2,1)}, bf16[256,2048]{1,0:T(8,128)(2,1)S(1)}, u32[]{:S(2)}, u32[]{:S(2)}) collective-permute-start(bf16[256,2048]{1,0:T(8,128)(2,1)} %bitcast.25), channel_id=1, source_target_pairs={{0,1},{1,0},{2,3},{3,2},{4,5},{5,4},{6,7},{7,6},{8,9},{9,8},{10,11... | collective-permute-start | bytes 3145736 | tf_op jit(solution)/shard_map/ppermute | solution.py:50
  3.6 25.2 %collective-permute-start.2 = (bf16[256,2048]{1,0:T(8,128)(2,1)}, bf16[256,2048]{1,0:T(8,128)(2,1)S(1)}, u32[]{:S(2)}, u32[]{:S(2)}) collective-permute-start(bf16[256,2048]{1,0:T(8,128)(2,1)} %bitcast.26), channel_id=1, source_target_pairs={{0,2},{1,3},{2,0},{3,1},{4,6},{5,7},{6,4},{7,5},{8,10},{9,11},{10,... | collective-permute-start | bytes 3145736 | tf_op jit(solution)/shard_map/ppermute | solution.py:50
  5.2 29.0 %collective-permute-start.4 = (bf16[512,256]{1,0:T(8,128)(2,1)}, bf16[512,256]{1,0:T(8,128)(2,1)S(1)}, u32[]{:S(2)}, u32[]{:S(2)}) collective-permute-start(bf16[512,256]{1,0:T(8,128)(2,1)} %bitcast.34), channel_id=1, source_target_pairs={{0,4},{4,8},{8,12},{1,5},{5,9},{9,13},{2,6},{6,10},{10,14},{3,7},{... | collective-permute-start | bytes 786440 | tf_op jit(solution)/shard_map/ppermute | solution.py:36
  27.1 13.2 %collective-permute-start.1 = (bf16[128,2048]{1,0:T(8,128)(2,1)S(1)}, bf16[128,2048]{1,0:T(8,128)(2,1)S(1)}, u32[]{:S(2)}, u32[]{:S(2)}) collective-permute-start(bf16[128,2048]{1,0:T(8,128)(2,1)S(1)} %slice.20), channel_id=1, source_target_pairs={{0,2},{1,3},{2,0},{3,1},{4,6},{5,7},{6,4},{7,5},{8,10},{9,11},{10,... | collective-permute-start | bytes 1572872 | tf_op jit(solution)/shard_map/ppermute | solution.py:50
  28.9 12.6 %collective-permute-start.3 = (bf16[128,2048]{1,0:T(8,128)(2,1)S(1)}, bf16[128,2048]{1,0:T(8,128)(2,1)S(1)}, u32[]{:S(2)}, u32[]{:S(2)}) collective-permute-start(bf16[128,2048]{1,0:T(8,128)(2,1)S(1)} %slice.21), channel_id=1, source_target_pairs={{0,1},{1,0},{2,3},{3,2},{4,5},{5,4},{6,7},{7,6},{8,9},{9,8},{10,11... | collective-permute-start | bytes 1572872 | tf_op jit(solution)/shard_map/ppermute | solution.py:50
  42.9 7.2 %collective-permute-start.5 = (bf16[2,64,256]{2,1,0:T(8,128)(2,1)S(1)}, bf16[2,64,256]{2,1,0:T(8,128)(2,1)S(1)}, u32[]{:S(2)}, u32[]{:S(2)}) collective-permute-start(bf16[2,64,256]{2,1,0:T(8,128)(2,1)S(1)} %get-tuple-element.66), channel_id=1, source_target_pairs={{0,4},{4,0},{8,12},{12,8},{1,5},{5,1},{9,13},{13,9},{2,6},{6,2},{1... | collective-permute-start | bytes 196616 | tf_op jit(solution)/shard_map/ppermute | solution.py:50
  44.5 6.4 %collective-permute-start.6 = (bf16[2,64,256]{2,1,0:T(8,128)(2,1)S(1)}, bf16[2,64,256]{2,1,0:T(8,128)(2,1)S(1)}, u32[]{:S(2)}, u32[]{:S(2)}) collective-permute-start(bf16[2,64,256]{2,1,0:T(8,128)(2,1)S(1)} %get-tuple-element.67), channel_id=1, source_target_pairs={{0,8},{4,12},{8,0},{12,4},{1,9},{5,13},{9,1},{13,5},{2,10},{6,14},... | collective-permute-start | bytes 196616 | tf_op jit(solution)/shard_map/ppermute | solution.py:50
  47.1 6.8 %collective-permute-start.7 = (bf16[2,64,256]{2,1,0:T(8,128)(2,1)S(1)}, bf16[2,64,256]{2,1,0:T(8,128)(2,1)S(1)}, u32[]{:S(2)}, u32[]{:S(2)}) collective-permute-start(bf16[2,64,256]{2,1,0:T(8,128)(2,1)S(1)} %get-tuple-element.68), channel_id=1, source_target_pairs={{0,12},{4,8},{8,4},{12,0},{1,13},{5,9},{9,5},{13,1},{2,14},{6,10},... | collective-permute-start | bytes 196616 | tf_op jit(solution)/shard_map/ppermute | solution.py:50
  47.4 26.2 %collective-permute-start.8 = (bf16[2048,256]{1,0:T(8,128)(2,1)S(1)}, bf16[2048,256]{1,0:T(8,128)(2,1)S(1)}, u32[]{:S(2)}, u32[]{:S(2)}) collective-permute-start(bf16[2048,256]{1,0:T(8,128)(2,1)S(1)} %get-tuple-element.78), channel_id=1, source_target_pairs={{0,1},{1,0},{2,3},{3,2},{16,18},{17,19},{18,16},{19,17},{4,5},{5,4... | collective-permute-start | bytes 3145736 | tf_op jit(solution)/shard_map/ppermute | solution.py:582
  48.9 24.7 %collective-permute-start.9 = (bf16[1024,256]{1,0:T(8,128)(2,1)S(1)}, bf16[1024,256]{1,0:T(8,128)(2,1)S(1)}, u32[]{:S(2)}, u32[]{:S(2)}) collective-permute-start(bf16[1024,256]{1,0:T(8,128)(2,1)S(1)} %get-tuple-element.79), channel_id=1, source_target_pairs={{0,3},{1,2},{2,1},{3,0},{4,7},{5,6},{6,5},{7,4},{8,11},{9,10},{10,... | collective-permute-start | bytes 1572872 | tf_op jit(solution)/shard_map/ppermute | solution.py:50
  53.9 15.9 %collective-permute-start.10 = (bf16[256,512]{1,0:T(8,128)(2,1)S(1)}, bf16[256,512]{1,0:T(8,128)(2,1)S(1)}, u32[]{:S(2)}, u32[]{:S(2)}) collective-permute-start(bf16[256,512]{1,0:T(8,128)(2,1)S(1)} %get-tuple-element.80), channel_id=1, source_target_pairs={{0,4},{4,0},{8,12},{12,8},{1,5},{5,1},{9,13},{13,9},{2,6},{6,2},{1... | collective-permute-start | bytes 786440 | tf_op jit(solution)/shard_map/ppermute | solution.py:50
  53.9 19.4 %collective-permute-start.11 = (bf16[256,512]{1,0:T(8,128)(2,1)S(1)}, bf16[256,512]{1,0:T(8,128)(2,1)S(1)}, u32[]{:S(2)}, u32[]{:S(2)}) collective-permute-start(bf16[256,512]{1,0:T(8,128)(2,1)S(1)} %get-tuple-element.81), channel_id=1, source_target_pairs={{0,8},{4,12},{8,0},{12,4},{1,9},{5,13},{9,1},{13,5},{2,10},{6,14},... | collective-permute-start | bytes 786440 | tf_op jit(solution)/shard_map/ppermute | solution.py:50
  54.6 18.7 %collective-permute-start.12 = (bf16[256,512]{1,0:T(8,128)(2,1)S(1)}, bf16[256,512]{1,0:T(8,128)(2,1)S(1)}, u32[]{:S(2)}, u32[]{:S(2)}) collective-permute-start(bf16[256,512]{1,0:T(8,128)(2,1)S(1)} %get-tuple-element.82), channel_id=1, source_target_pairs={{0,12},{4,8},{8,4},{12,0},{1,13},{5,9},{9,5},{13,1},{2,14},{6,10},... | collective-permute-start | bytes 786440 | tf_op jit(solution)/shard_map/ppermute | solution.py:50
  73.6 21.4 %collective-permute-start.13 = (bf16[768,512]{1,0:T(8,128)(2,1)S(1)}, bf16[768,512]{1,0:T(8,128)(2,1)S(1)}, u32[]{:S(2)}, u32[]{:S(2)}) collective-permute-start(bf16[768,512]{1,0:T(8,128)(2,1)S(1)} %constant_dynamic-update-slice_fusion.refs_0_), channel_id=1, source_target_pairs={{0,1},{1,0},{2,3},{3,2},{4,5},{5,4},{6,7},{7,6},{8,9},{9,8},{10,11... | collective-permute-start | bytes 2359304 | tf_op jit(solution)/shard_map/ppermute | solution.py:50
  75.0 20.1 %collective-permute-start.14 = (bf16[768,512]{1,0:T(8,128)(2,1)S(1)}, bf16[768,512]{1,0:T(8,128)(2,1)S(1)}, u32[]{:S(2)}, u32[]{:S(2)}) collective-permute-start(bf16[768,512]{1,0:T(8,128)(2,1)S(1)} %constant_dynamic-update-slice_fusion.refs_0_), channel_id=1, source_target_pairs={{0,2},{1,3},{2,0},{3,1},{4,6},{5,7},{6,4},{7,5},{8,10},{9,11},{10,... | collective-permute-start | bytes 2359304 | tf_op jit(solution)/shard_map/ppermute | solution.py:50
  76.2 8.6 %collective-permute-start.15 = (bf16[256,256]{1,0:T(8,128)(2,1)S(1)}, bf16[256,256]{1,0:T(8,128)(2,1)S(1)}, u32[]{:S(2)}, u32[]{:S(2)}) collective-permute-start(bf16[256,256]{1,0:T(8,128)(2,1)S(1)} %get-tuple-element.87), channel_id=1, source_target_pairs={{4,0},{8,4},{12,8},{5,1},{9,5},{13,9},{6,2},{10,6},{14,10},{7,3},{... | collective-permute-start | bytes 393224 | tf_op jit(solution)/shard_map/ppermute | solution.py:36
  86.0 9.0 %collective-permute-start.17 = (bf16[256,256]{1,0:T(8,128)(2,1)S(1)}, bf16[256,256]{1,0:T(8,128)(2,1)S(1)}, u32[]{:S(2)}, u32[]{:S(2)}) collective-permute-start(bf16[256,256]{1,0:T(8,128)(2,1)S(1)} %add_convert_fusion.refs_0_), channel_id=1, source_target_pairs={{0,8},{4,12},{8,0},{12,4},{1,9},{5,13},{9,1},{13,5},{2,10},{6,14},... | collective-permute-start | bytes 393224 | tf_op jit(solution)/shard_map/ppermute | solution.py:50
  87.2 7.8 %collective-permute-start.18 = (bf16[256,256]{1,0:T(8,128)(2,1)S(1)}, bf16[256,256]{1,0:T(8,128)(2,1)S(1)}, u32[]{:S(2)}, u32[]{:S(2)}) collective-permute-start(bf16[256,256]{1,0:T(8,128)(2,1)S(1)} %add_convert_fusion.refs_0_), channel_id=1, source_target_pairs={{0,12},{4,8},{8,4},{12,0},{1,13},{5,9},{9,5},{13,1},{2,14},{6,10},... | collective-permute-start | bytes 393224 | tf_op jit(solution)/shard_map/ppermute | solution.py:50
  95.1 12.3 %collective-permute-start.19 = (bf16[384,512]{1,0:T(8,128)(2,1)S(1)}, bf16[384,512]{1,0:T(8,128)(2,1)S(1)}, u32[]{:S(2)}, u32[]{:S(2)}) collective-permute-start(bf16[384,512]{1,0:T(8,128)(2,1)S(1)} %slice.18), channel_id=1, source_target_pairs={{0,2},{1,3},{2,0},{3,1},{4,6},{5,7},{6,4},{7,5},{8,10},{9,11},{10,... | collective-permute-start | bytes 1179656 | tf_op jit(solution)/shard_map/ppermute | solution.py:50
  96.7 10.7 %collective-permute-start.20 = (bf16[384,512]{1,0:T(8,128)(2,1)S(1)}, bf16[384,512]{1,0:T(8,128)(2,1)S(1)}, u32[]{:S(2)}, u32[]{:S(2)}) collective-permute-start(bf16[384,512]{1,0:T(8,128)(2,1)S(1)} %slice.19), channel_id=1, source_target_pairs={{0,1},{1,0},{2,3},{3,2},{4,5},{5,4},{6,7},{7,6},{8,9},{9,8},{10,11... | collective-permute-start | bytes 1179656 | tf_op jit(solution)/shard_map/ppermute | solution.py:50
  99.0 7.1 %collective-permute-start.21 = (bf16[256,256]{1,0:T(8,128)(2,1)S(1)}, bf16[256,256]{1,0:T(8,128)(2,1)S(1)}, u32[]{:S(2)}, u32[]{:S(2)}) collective-permute-start(bf16[256,256]{1,0:T(8,128)(2,1)S(1)} %get-tuple-element.96.g0), channel_id=1, source_target_pairs={{0,1},{1,0},{2,3},{3,2},{4,5},{5,4},{6,7},{7,6},{8,9},{9,8},{10,11... | collective-permute-start | bytes 393224 | tf_op jit(solution)/shard_map/ppermute | solution.py:50
  101.0 6.4 %collective-permute-start.23 = (bf16[256,256]{1,0:T(8,128)(2,1)S(1)}, bf16[256,256]{1,0:T(8,128)(2,1)S(1)}, u32[]{:S(2)}, u32[]{:S(2)}) collective-permute-start(bf16[256,256]{1,0:T(8,128)(2,1)S(1)} %get-tuple-element.96.g0), channel_id=1, source_target_pairs={{0,3},{1,2},{2,1},{3,0},{4,7},{5,6},{6,5},{7,4},{8,11},{9,10},{10,... | collective-permute-start | bytes 393224 | tf_op jit(solution)/shard_map/ppermute | solution.py:50
  108.5 8.1 %collective-permute-start.26 = (f32[3,512,256]{2,1,0:T(8,128)S(1)}, f32[3,512,256]{2,1,0:T(8,128)S(1)}, u32[]{:S(2)}, u32[]{:S(2)}) collective-permute-start(f32[3,512,256]{2,1,0:T(8,128)S(1)} %shard_map.100.refs_0_), channel_id=1, source_target_pairs={{0,16},{16,0},{1,17},{17,1},{2,18},{18,2},{3,19},{19,3},{4,20},{20... | collective-permute-start | bytes 4718600 | tf_op jit(solution)/shard_map/ppermute | solution.py:41
  109.7 6.9 %collective-permute-start.27 = (f32[1,512,256]{2,1,0:T(8,128)S(1)}, f32[1,512,256]{2,1,0:T(8,128)S(1)}, u32[]{:S(2)}, u32[]{:S(2)}) collective-permute-start(f32[1,512,256]{2,1,0:T(8,128)S(1)} %shard_map.101.refs_1_), channel_id=1, source_target_pairs={{0,16},{16,0},{1,17},{17,1},{2,18},{18,2},{3,19},{19,3},{4,20},{20... | collective-permute-start | bytes 1572872 | tf_op jit(solution)/shard_map/ppermute | solution.py:41
  (10 other events, 96.4 us)

commit v12 on v11

--- a/solution.py
+++ b/solution.py
@@ -9,7 +9,7 @@
 
 IMGTOK = 16
 QTILE = 128
-SPANS = (2, 3)
+SPANS = (2, 3, 4)
 LOG2E = 1.4426950408889634
 VMEM = 24 * 1024 * 1024
 
@@ -602,9 +602,10 @@
     prior_grad, near[0], near[1], *moved = lax.optimization_barrier(
         (prior_grad, near[0], near[1], *moved)
     )
-    far = [swap(w, "dp") for w in near]
     grad = own_grad + shift(prior_grad, "ctx", -1).astype(jnp.float32)
     grad = grad.astype(jnp.bfloat16)
+    far = [swap(w, "dp") for w in near]
+    grad, far[0] = lax.optimization_barrier((grad, far[0]))
     if mixed:
         gathered = [trade(grad, "ctx", s) if s else grad for s in range(ranks)]
         base = jnp.concatenate(moved, axis=0)

time: 118 us -> 124 us (1.051)
  waiting for transfers between devices: 53.4 us -> 59.3 us
    ppermute x21, waiting for transfers between devices: 42.2 us -> 49 us  [trade(): return lax.ppermute(block, axis, [(i, i ^ step) for i in range(count)])]
  transfers between devices with their start and end apart: 28 -> 28, of which waited for: 13 -> 13; matrix products, arithmetic and copies ran while one was open for 2% -> 2% of each run, Pallas kernels for 15% -> 14%
where the time goes in v12:
time: 124 us; the launch traced here: 123 us
  waiting for transfers between devices  59.3 us (48%)
  starting transfers between devices  37.3 us (30%)
  Pallas kernels  21.6 us (17%)
  local copies, waits for them, and re-layouts  3.22 us (3%)
    ppermute x21, waiting for transfers between devices, trade(): return lax.ppermute(block, axis, [(i, i ^ step) for i in range(count)])  49 us
    ppermute x21, starting transfers between devices, trade(): return lax.ppermute(block, axis, [(i, i ^ step) for i in range(count)])  30 us
    pallas_call x1, Pallas kernels, attention(): pl.pallas_call(functools.partial(attention_body, per_shard, images), grid...  11.6 us
    ppermute x2, waiting for transfers between devices, shift(): return lax.ppermute(block, axis, route)  7.35 us
    ppermute x2, starting transfers between devices, shift(): return lax.ppermute(block, axis, route)  4.99 us
    ppermute x4, waiting for transfers between devices, swap(): return lax.ppermute(block, axis, [(i, count - 1 - i) for i in range(count)])  2.97 us
  transfers between devices with their start and end apart: 28, of which 13 were waited for; matrix products, arithmetic and copies ran while one was open for 2% of the time, Pallas kernels for 14%

profile of v12, /device:TPU:0, one launch (start us, length us, event | category | flops | bytes accessed | tf_op | source)
XLA Modules:
  0.0 123.4 jit_solution(12099016191407665797)
XLA Ops:
  0.6 3.0 %collective-permute-start = (bf16[256,2048]{1,0:T(8,128)(2,1)}, bf16[256,2048]{1,0:T(8,128)(2,1)S(1)}, u32[]{:S(2)}, u32[]{:S(2)}) collective-permute-start(bf16[256,2048]{1,0:T(8,128)(2,1)} %bitcast.25), channel_id=1, source_target_pairs={{0,1},{1,0},{2,3},{3,2},{4,5},{5,4},{6,7},{7,6},{8,9},{9,8},{10,11... | collective-permute-start | bytes 3145736 | tf_op jit(solution)/shard_map/ppermute | solution.py:50
  5.2 3.5 %collective-permute-start.4 = (bf16[512,256]{1,0:T(8,128)(2,1)}, bf16[512,256]{1,0:T(8,128)(2,1)S(1)}, u32[]{:S(2)}, u32[]{:S(2)}) collective-permute-start(bf16[512,256]{1,0:T(8,128)(2,1)} %bitcast.34), channel_id=1, source_target_pairs={{0,4},{4,8},{8,12},{1,5},{5,9},{9,13},{2,6},{6,10},{10,14},{3,7},{... | collective-permute-start | bytes 786440 | tf_op jit(solution)/shard_map/ppermute | solution.py:36
  10.3 16.7 %collective-permute-done.x_ref = bf16[256,2048]{1,0:T(8,128)(2,1)S(1)} collective-permute-done((bf16[256,2048]{1,0:T(8,128)(2,1)}, bf16[256,2048]{1,0:T(8,128)(2,1)S(1)}, u32[]{:S(2)}, u32[]{:S(2)}) %collective-permute-start) | collective-permute-done | bytes 1048608 | tf_op jit(solution)/shard_map/ppermute | solution.py:50
  27.1 1.8 %collective-permute-start.1 = (bf16[128,2048]{1,0:T(8,128)(2,1)S(1)}, bf16[128,2048]{1,0:T(8,128)(2,1)S(1)}, u32[]{:S(2)}, u32[]{:S(2)}) collective-permute-start(bf16[128,2048]{1,0:T(8,128)(2,1)S(1)} %slice.20), channel_id=1, source_target_pairs={{0,2},{1,3},{2,0},{3,1},{4,6},{5,7},{6,4},{7,5},{8,10},{9,11},{10,... | collective-permute-start | bytes 1572872 | tf_op jit(solution)/shard_map/ppermute | solution.py:50
  28.9 1.6 %collective-permute-start.3 = (bf16[128,2048]{1,0:T(8,128)(2,1)S(1)}, bf16[128,2048]{1,0:T(8,128)(2,1)S(1)}, u32[]{:S(2)}, u32[]{:S(2)}) collective-permute-start(bf16[128,2048]{1,0:T(8,128)(2,1)S(1)} %slice.21), channel_id=1, source_target_pairs={{0,1},{1,0},{2,3},{3,2},{4,5},{5,4},{6,7},{7,6},{8,9},{9,8},{10,11... | collective-permute-start | bytes 1572872 | tf_op jit(solution)/shard_map/ppermute | solution.py:50
  30.8 2.2 %copy-done = bf16[1,8192,256]{2,1,0:T(8,128)(2,1)S(1)} copy-done((bf16[1,8192,256]{2,1,0:T(8,128)(2,1)S(1)}, bf16[1,8192,256]{2,1,0:T(8,128)(2,1)}, u32[]{:S(2)}) %copy-start) | copy-done | bytes 4194328
  34.2 6.1 %collective-permute-done.1.low_ref = bf16[128,2048]{1,0:T(8,128)(2,1)S(1)} collective-permute-done((bf16[128,2048]{1,0:T(8,128)(2,1)S(1)}, bf16[128,2048]{1,0:T(8,128)(2,1)S(1)}, u32[]{:S(2)}, u32[]{:S(2)}) %collective-permute-start.1) | collective-permute-done | bytes 524320 | tf_op jit(solution)/shard_map/ppermute | solution.py:50
  42.9 1.6 %collective-permute-start.5 = (bf16[2,64,256]{2,1,0:T(8,128)(2,1)S(1)}, bf16[2,64,256]{2,1,0:T(8,128)(2,1)S(1)}, u32[]{:S(2)}, u32[]{:S(2)}) collective-permute-start(bf16[2,64,256]{2,1,0:T(8,128)(2,1)S(1)} %get-tuple-element.68), channel_id=1, source_target_pairs={{0,4},{4,0},{8,12},{12,8},{1,5},{5,1},{9,13},{13,9},{2,6},{6,2},{1... | collective-permute-start | bytes 196616 | tf_op jit(solution)/shard_map/ppermute | solution.py:50
  44.5 2.6 %collective-permute-start.6 = (bf16[2,64,256]{2,1,0:T(8,128)(2,1)S(1)}, bf16[2,64,256]{2,1,0:T(8,128)(2,1)S(1)}, u32[]{:S(2)}, u32[]{:S(2)}) collective-permute-start(bf16[2,64,256]{2,1,0:T(8,128)(2,1)S(1)} %get-tuple-element.69), channel_id=1, source_target_pairs={{0,8},{4,12},{8,0},{12,4},{1,9},{5,13},{9,1},{13,5},{2,10},{6,14},... | collective-permute-start | bytes 196616 | tf_op jit(solution)/shard_map/ppermute | solution.py:50
  51.0 3.0 %collective-permute-done.7.refs_3_ = bf16[2,64,256]{2,1,0:T(8,128)(2,1)S(1)} collective-permute-done((bf16[2,64,256]{2,1,0:T(8,128)(2,1)S(1)}, bf16[2,64,256]{2,1,0:T(8,128)(2,1)S(1)}, u32[]{:S(2)}, u32[]{:S(2)}) %collective-permute-start.7) | collective-permute-done | bytes 65568 | tf_op jit(solution)/shard_map/ppermute | solution.py:50
  54.6 3.7 %collective-permute-start.12 = (bf16[256,512]{1,0:T(8,128)(2,1)S(1)}, bf16[256,512]{1,0:T(8,128)(2,1)S(1)}, u32[]{:S(2)}, u32[]{:S(2)}) collective-permute-start(bf16[256,512]{1,0:T(8,128)(2,1)S(1)} %get-tuple-element.84), channel_id=1, source_target_pairs={{0,12},{4,8},{8,4},{12,0},{1,13},{5,9},{9,5},{13,1},{2,14},{6,10},... | collective-permute-start | bytes 786440 | tf_op jit(solution)/shard_map/ppermute | solution.py:50
  58.3 11.6 %shard_map.97 = (bf16[512,1024]{1,0:T(8,128)(2,1)}, f32[256,256]{1,0:T(8,128)S(1)}, bf16[256,256]{1,0:T(8,128)(2,1)S(1)}) custom-call(s32[1]{0:T(128)} %bitcast.c_ref, s32[64]{0:T(128)S(1)} %and_select_fusion.place_ref, s32[1,512]{1,0:T(1,128)S(1)} %bitcast.31, bf16[512,1024]{1,0:T(8,128)(2,1)S(1)} %bitcast.32, bf16[512,1024]{1,0:T(8,128)(2,1)S(1)} %bitcast.33, ...), custom_call_target="tpu_custom_call" | custom-call | flops 13421772800 | bytes 4194304 | tf_op jit(solution)/shard_map/pallas_call | solution.py:348
  69.9 3.5 %collective-permute-done.11 = bf16[256,512]{1,0:T(8,128)(2,1)S(1)} collective-permute-done((bf16[256,512]{1,0:T(8,128)(2,1)S(1)}, bf16[256,512]{1,0:T(8,128)(2,1)S(1)}, u32[]{:S(2)}, u32[]{:S(2)}) %collective-permute-start.11) | collective-permute-done | bytes 262176 | tf_op jit(solution)/shard_map/ppermute | solution.py:50
  77.1 7.3 %collective-permute-done.15 = bf16[256,256]{1,0:T(8,128)(2,1)S(1)} collective-permute-done((bf16[256,256]{1,0:T(8,128)(2,1)S(1)}, bf16[256,256]{1,0:T(8,128)(2,1)S(1)}, u32[]{:S(2)}, u32[]{:S(2)}) %collective-permute-start.15) | collective-permute-done | bytes 131104 | tf_op jit(solution)/shard_map/ppermute | solution.py:36
  84.5 1.8 %collective-permute-start.17 = (bf16[256,256]{1,0:T(8,128)(2,1)S(1)}, bf16[256,256]{1,0:T(8,128)(2,1)S(1)}, u32[]{:S(2)}, u32[]{:S(2)}) collective-permute-start(bf16[256,256]{1,0:T(8,128)(2,1)S(1)} %add_convert_fusion.refs_0_), channel_id=1, source_target_pairs={{0,4},{4,0},{8,12},{12,8},{1,5},{5,1},{9,13},{13,9},{2,6},{6,2},{1... | collective-permute-start | bytes 393224 | tf_op jit(solution)/shard_map/ppermute | solution.py:50
  86.3 2.7 %collective-permute-start.19 = (bf16[256,256]{1,0:T(8,128)(2,1)S(1)}, bf16[256,256]{1,0:T(8,128)(2,1)S(1)}, u32[]{:S(2)}, u32[]{:S(2)}) collective-permute-start(bf16[256,256]{1,0:T(8,128)(2,1)S(1)} %add_convert_fusion.refs_0_), channel_id=1, source_target_pairs={{0,12},{4,8},{8,4},{12,0},{1,13},{5,9},{9,5},{13,1},{2,14},{6,10},... | collective-permute-start | bytes 393224 | tf_op jit(solution)/shard_map/ppermute | solution.py:50
  88.9 4.6 %collective-permute-done.13.refs_1_ = bf16[768,512]{1,0:T(8,128)(2,1)S(1)} collective-permute-done((bf16[768,512]{1,0:T(8,128)(2,1)S(1)}, bf16[768,512]{1,0:T(8,128)(2,1)S(1)}, u32[]{:S(2)}, u32[]{:S(2)}) %collective-permute-start.13) | collective-permute-done | bytes 786464 | tf_op jit(solution)/shard_map/ppermute | solution.py:50
  94.7 3.2 %collective-permute-done.18.refs_2_ = bf16[256,256]{1,0:T(8,128)(2,1)S(1)} collective-permute-done((bf16[256,256]{1,0:T(8,128)(2,1)S(1)}, bf16[256,256]{1,0:T(8,128)(2,1)S(1)}, u32[]{:S(2)}, u32[]{:S(2)}) %collective-permute-start.18) | collective-permute-done | bytes 131104 | tf_op jit(solution)/shard_map/ppermute | solution.py:50
  97.9 1.6 %collective-permute-start.20 = (bf16[384,512]{1,0:T(8,128)(2,1)S(1)}, bf16[384,512]{1,0:T(8,128)(2,1)S(1)}, u32[]{:S(2)}, u32[]{:S(2)}) collective-permute-start(bf16[384,512]{1,0:T(8,128)(2,1)S(1)} %slice.18), channel_id=1, source_target_pairs={{0,2},{1,3},{2,0},{3,1},{4,6},{5,7},{6,4},{7,5},{8,10},{9,11},{10,... | collective-permute-start | bytes 1179656 | tf_op jit(solution)/shard_map/ppermute | solution.py:50
  100.1 1.7 %shard_map.98 = (bf16[1024,256]{1,0:T(8,128)(2,1)S(1)}, bf16[256,256]{1,0:T(8,128)(2,1)S(1)}) custom-call(s32[1]{0:T(128)} %bitcast.c_ref, s32[64]{0:T(128)S(1)} %and_select_fusion.place_ref, bf16[256,256]{1,0:T(8,128)(2,1)S(1)} %add_convert_fusion.refs_0_, bf16[256,256]{1,0:T(8,128)(2,1)S(1)} %collective-permute-done.17.refs_1_, ...), custom_call_target="tpu_custom_call" | custom-call | bytes 2097152 | tf_op jit(solution)/shard_map/pallas_call | solution.py:406
  101.8 1.6 %collective-permute-start.22 = (bf16[256,256]{1,0:T(8,128)(2,1)S(1)}, bf16[256,256]{1,0:T(8,128)(2,1)S(1)}, u32[]{:S(2)}, u32[]{:S(2)}) collective-permute-start(bf16[256,256]{1,0:T(8,128)(2,1)S(1)} %get-tuple-element.100.g0), channel_id=1, source_target_pairs={{0,1},{1,0},{2,3},{3,2},{4,5},{5,4},{6,7},{7,6},{8,9},{9,8},{10,11... | collective-permute-start | bytes 393224 | tf_op jit(solution)/shard_map/ppermute | solution.py:50
  105.4 7.5 %collective-permute-done.22.g1 = bf16[256,256]{1,0:T(8,128)(2,1)S(1)} collective-permute-done((bf16[256,256]{1,0:T(8,128)(2,1)S(1)}, bf16[256,256]{1,0:T(8,128)(2,1)S(1)}, u32[]{:S(2)}, u32[]{:S(2)}) %collective-permute-start.22) | collective-permute-done | bytes 131104 | tf_op jit(solution)/shard_map/ppermute | solution.py:50
  116.5 3.0 %collective-permute-done.25.far_ref = bf16[1024,256]{1,0:T(8,128)(2,1)S(1)} collective-permute-done((bf16[1024,256]{1,0:T(8,128)(2,1)S(1)}, bf16[1024,256]{1,0:T(8,128)(2,1)S(1)}, u32[]{:S(2)}, u32[]{:S(2)}) %collective-permute-start.25) | collective-permute-done | bytes 524320 | tf_op jit(solution)/shard_map/ppermute | solution.py:41
  119.5 2.3 %shard_map.99 = bf16[256,2048]{1,0:T(8,128)(2,1)} custom-call(s32[1]{0:T(128)} %bitcast.11.d_ref, bf16[256,256]{1,0:T(8,128)(2,1)S(1)} %get-tuple-element.100.g0, bf16[256,256]{1,0:T(8,128)(2,1)S(1)} %collective-permute-done.22.g1, bf16[256,256]{1,0:T(8,128)(2,1)S(1)} %collective-permute-done.23.g2, bf16[256,256]{1,0:T(8,128)(2,1)S(1)} %collective-permute-done.24.g3, ...), custom_call_target="tpu_custom_call" | custom-call | flops 1073741824 | bytes 4194304 | tf_op jit(solution)/shard_map/pallas_call | solution.py:525
  (66 shorter events, 24.6 us)
Async XLA Ops:
  0.6 26.4 %collective-permute-start = (bf16[256,2048]{1,0:T(8,128)(2,1)}, bf16[256,2048]{1,0:T(8,128)(2,1)S(1)}, u32[]{:S(2)}, u32[]{:S(2)}) collective-permute-start(bf16[256,2048]{1,0:T(8,128)(2,1)} %bitcast.25), channel_id=1, source_target_pairs={{0,1},{1,0},{2,3},{3,2},{4,5},{5,4},{6,7},{7,6},{8,9},{9,8},{10,11... | collective-permute-start | bytes 3145736 | tf_op jit(solution)/shard_map/ppermute | solution.py:50
  3.6 25.2 %collective-permute-start.2 = (bf16[256,2048]{1,0:T(8,128)(2,1)}, bf16[256,2048]{1,0:T(8,128)(2,1)S(1)}, u32[]{:S(2)}, u32[]{:S(2)}) collective-permute-start(bf16[256,2048]{1,0:T(8,128)(2,1)} %bitcast.26), channel_id=1, source_target_pairs={{0,2},{1,3},{2,0},{3,1},{4,6},{5,7},{6,4},{7,5},{8,10},{9,11},{10,... | collective-permute-start | bytes 3145736 | tf_op jit(solution)/shard_map/ppermute | solution.py:50
  5.2 29.0 %collective-permute-start.4 = (bf16[512,256]{1,0:T(8,128)(2,1)}, bf16[512,256]{1,0:T(8,128)(2,1)S(1)}, u32[]{:S(2)}, u32[]{:S(2)}) collective-permute-start(bf16[512,256]{1,0:T(8,128)(2,1)} %bitcast.34), channel_id=1, source_target_pairs={{0,4},{4,8},{8,12},{1,5},{5,9},{9,13},{2,6},{6,10},{10,14},{3,7},{... | collective-permute-start | bytes 786440 | tf_op jit(solution)/shard_map/ppermute | solution.py:36
  27.1 13.2 %collective-permute-start.1 = (bf16[128,2048]{1,0:T(8,128)(2,1)S(1)}, bf16[128,2048]{1,0:T(8,128)(2,1)S(1)}, u32[]{:S(2)}, u32[]{:S(2)}) collective-permute-start(bf16[128,2048]{1,0:T(8,128)(2,1)S(1)} %slice.20), channel_id=1, source_target_pairs={{0,2},{1,3},{2,0},{3,1},{4,6},{5,7},{6,4},{7,5},{8,10},{9,11},{10,... | collective-permute-start | bytes 1572872 | tf_op jit(solution)/shard_map/ppermute | solution.py:50
  28.9 12.6 %collective-permute-start.3 = (bf16[128,2048]{1,0:T(8,128)(2,1)S(1)}, bf16[128,2048]{1,0:T(8,128)(2,1)S(1)}, u32[]{:S(2)}, u32[]{:S(2)}) collective-permute-start(bf16[128,2048]{1,0:T(8,128)(2,1)S(1)} %slice.21), channel_id=1, source_target_pairs={{0,1},{1,0},{2,3},{3,2},{4,5},{5,4},{6,7},{7,6},{8,9},{9,8},{10,11... | collective-permute-start | bytes 1572872 | tf_op jit(solution)/shard_map/ppermute | solution.py:50
  42.9 7.4 %collective-permute-start.5 = (bf16[2,64,256]{2,1,0:T(8,128)(2,1)S(1)}, bf16[2,64,256]{2,1,0:T(8,128)(2,1)S(1)}, u32[]{:S(2)}, u32[]{:S(2)}) collective-permute-start(bf16[2,64,256]{2,1,0:T(8,128)(2,1)S(1)} %get-tuple-element.68), channel_id=1, source_target_pairs={{0,4},{4,0},{8,12},{12,8},{1,5},{5,1},{9,13},{13,9},{2,6},{6,2},{1... | collective-permute-start | bytes 196616 | tf_op jit(solution)/shard_map/ppermute | solution.py:50
  47.1 6.8 %collective-permute-start.7 = (bf16[2,64,256]{2,1,0:T(8,128)(2,1)S(1)}, bf16[2,64,256]{2,1,0:T(8,128)(2,1)S(1)}, u32[]{:S(2)}, u32[]{:S(2)}) collective-permute-start(bf16[2,64,256]{2,1,0:T(8,128)(2,1)S(1)} %get-tuple-element.70), channel_id=1, source_target_pairs={{0,12},{4,8},{8,4},{12,0},{1,13},{5,9},{9,5},{13,1},{2,14},{6,10},... | collective-permute-start | bytes 196616 | tf_op jit(solution)/shard_map/ppermute | solution.py:50
  47.4 26.0 %collective-permute-start.8 = (bf16[2048,256]{1,0:T(8,128)(2,1)S(1)}, bf16[2048,256]{1,0:T(8,128)(2,1)S(1)}, u32[]{:S(2)}, u32[]{:S(2)}) collective-permute-start(bf16[2048,256]{1,0:T(8,128)(2,1)S(1)} %get-tuple-element.80), channel_id=1, source_target_pairs={{0,1},{1,0},{2,3},{3,2},{16,18},{17,19},{18,16},{19,17},{4,5},{5,4... | collective-permute-start | bytes 3145736 | tf_op jit(solution)/shard_map/ppermute | solution.py:582
  48.9 24.5 %collective-permute-start.9 = (bf16[1024,256]{1,0:T(8,128)(2,1)S(1)}, bf16[1024,256]{1,0:T(8,128)(2,1)S(1)}, u32[]{:S(2)}, u32[]{:S(2)}) collective-permute-start(bf16[1024,256]{1,0:T(8,128)(2,1)S(1)} %get-tuple-element.81), channel_id=1, source_target_pairs={{0,3},{1,2},{2,1},{3,0},{4,7},{5,6},{6,5},{7,4},{8,11},{9,10},{10,... | collective-permute-start | bytes 1572872 | tf_op jit(solution)/shard_map/ppermute | solution.py:50
  53.9 16.0 %collective-permute-start.10 = (bf16[256,512]{1,0:T(8,128)(2,1)S(1)}, bf16[256,512]{1,0:T(8,128)(2,1)S(1)}, u32[]{:S(2)}, u32[]{:S(2)}) collective-permute-start(bf16[256,512]{1,0:T(8,128)(2,1)S(1)} %get-tuple-element.82), channel_id=1, source_target_pairs={{0,4},{4,0},{8,12},{12,8},{1,5},{5,1},{9,13},{13,9},{2,6},{6,2},{1... | collective-permute-start | bytes 786440 | tf_op jit(solution)/shard_map/ppermute | solution.py:50
  53.9 19.4 %collective-permute-start.11 = (bf16[256,512]{1,0:T(8,128)(2,1)S(1)}, bf16[256,512]{1,0:T(8,128)(2,1)S(1)}, u32[]{:S(2)}, u32[]{:S(2)}) collective-permute-start(bf16[256,512]{1,0:T(8,128)(2,1)S(1)} %get-tuple-element.83), channel_id=1, source_target_pairs={{0,8},{4,12},{8,0},{12,4},{1,9},{5,13},{9,1},{13,5},{2,10},{6,14},... | collective-permute-start | bytes 786440 | tf_op jit(solution)/shard_map/ppermute | solution.py:50
  54.6 18.7 %collective-permute-start.12 = (bf16[256,512]{1,0:T(8,128)(2,1)S(1)}, bf16[256,512]{1,0:T(8,128)(2,1)S(1)}, u32[]{:S(2)}, u32[]{:S(2)}) collective-permute-start(bf16[256,512]{1,0:T(8,128)(2,1)S(1)} %get-tuple-element.84), channel_id=1, source_target_pairs={{0,12},{4,8},{8,4},{12,0},{1,13},{5,9},{9,5},{13,1},{2,14},{6,10},... | collective-permute-start | bytes 786440 | tf_op jit(solution)/shard_map/ppermute | solution.py:50
  73.4 11.1 %collective-permute-start.16 = (bf16[2048,256]{1,0:T(8,128)(2,1)S(1)}, bf16[2048,256]{1,0:T(8,128)(2,1)S(1)}, u32[]{:S(2)}, u32[]{:S(2)}) collective-permute-start(bf16[2048,256]{1,0:T(8,128)(2,1)S(1)} %collective-permute-done.8.first_ref), channel_id=1, source_target_pairs={{0,16},{16,0},{1,17},{17,1},{2,18},{18,2},{3,19},{19,3},{4,20},{20... | collective-permute-start | bytes 3145736 | tf_op jit(solution)/shard_map/ppermute | solution.py:41
  73.5 20.0 %collective-permute-start.13 = (bf16[768,512]{1,0:T(8,128)(2,1)S(1)}, bf16[768,512]{1,0:T(8,128)(2,1)S(1)}, u32[]{:S(2)}, u32[]{:S(2)}) collective-permute-start(bf16[768,512]{1,0:T(8,128)(2,1)S(1)} %constant_dynamic-update-slice_fusion.refs_0_), channel_id=1, source_target_pairs={{0,1},{1,0},{2,3},{3,2},{4,5},{5,4},{6,7},{7,6},{8,9},{9,8},{10,11... | collective-permute-start | bytes 2359304 | tf_op jit(solution)/shard_map/ppermute | solution.py:50
  75.1 19.7 %collective-permute-start.14 = (bf16[768,512]{1,0:T(8,128)(2,1)S(1)}, bf16[768,512]{1,0:T(8,128)(2,1)S(1)}, u32[]{:S(2)}, u32[]{:S(2)}) collective-permute-start(bf16[768,512]{1,0:T(8,128)(2,1)S(1)} %constant_dynamic-update-slice_fusion.refs_0_), channel_id=1, source_target_pairs={{0,2},{1,3},{2,0},{3,1},{4,6},{5,7},{6,4},{7,5},{8,10},{9,11},{10,... | collective-permute-start | bytes 2359304 | tf_op jit(solution)/shard_map/ppermute | solution.py:50
  75.6 8.9 %collective-permute-start.15 = (bf16[256,256]{1,0:T(8,128)(2,1)S(1)}, bf16[256,256]{1,0:T(8,128)(2,1)S(1)}, u32[]{:S(2)}, u32[]{:S(2)}) collective-permute-start(bf16[256,256]{1,0:T(8,128)(2,1)S(1)} %get-tuple-element.89), channel_id=1, source_target_pairs={{4,0},{8,4},{12,8},{5,1},{9,5},{13,9},{6,2},{10,6},{14,10},{7,3},{... | collective-permute-start | bytes 393224 | tf_op jit(solution)/shard_map/ppermute | solution.py:36
  84.5 10.3 %collective-permute-start.17 = (bf16[256,256]{1,0:T(8,128)(2,1)S(1)}, bf16[256,256]{1,0:T(8,128)(2,1)S(1)}, u32[]{:S(2)}, u32[]{:S(2)}) collective-permute-start(bf16[256,256]{1,0:T(8,128)(2,1)S(1)} %add_convert_fusion.refs_0_), channel_id=1, source_target_pairs={{0,4},{4,0},{8,12},{12,8},{1,5},{5,1},{9,13},{13,9},{2,6},{6,2},{1... | collective-permute-start | bytes 393224 | tf_op jit(solution)/shard_map/ppermute | solution.py:50
  86.3 11.6 %collective-permute-start.18 = (bf16[256,256]{1,0:T(8,128)(2,1)S(1)}, bf16[256,256]{1,0:T(8,128)(2,1)S(1)}, u32[]{:S(2)}, u32[]{:S(2)}) collective-permute-start(bf16[256,256]{1,0:T(8,128)(2,1)S(1)} %add_convert_fusion.refs_0_), channel_id=1, source_target_pairs={{0,8},{4,12},{8,0},{12,4},{1,9},{5,13},{9,1},{13,5},{2,10},{6,14},... | collective-permute-start | bytes 393224 | tf_op jit(solution)/shard_map/ppermute | solution.py:50
  86.3 11.6 %collective-permute-start.19 = (bf16[256,256]{1,0:T(8,128)(2,1)S(1)}, bf16[256,256]{1,0:T(8,128)(2,1)S(1)}, u32[]{:S(2)}, u32[]{:S(2)}) collective-permute-start(bf16[256,256]{1,0:T(8,128)(2,1)S(1)} %add_convert_fusion.refs_0_), channel_id=1, source_target_pairs={{0,12},{4,8},{8,4},{12,0},{1,13},{5,9},{9,5},{13,1},{2,14},{6,10},... | collective-permute-start | bytes 393224 | tf_op jit(solution)/shard_map/ppermute | solution.py:50
  97.9 16.3 %collective-permute-start.20 = (bf16[384,512]{1,0:T(8,128)(2,1)S(1)}, bf16[384,512]{1,0:T(8,128)(2,1)S(1)}, u32[]{:S(2)}, u32[]{:S(2)}) collective-permute-start(bf16[384,512]{1,0:T(8,128)(2,1)S(1)} %slice.18), channel_id=1, source_target_pairs={{0,2},{1,3},{2,0},{3,1},{4,6},{5,7},{6,4},{7,5},{8,10},{9,11},{10,... | collective-permute-start | bytes 1179656 | tf_op jit(solution)/shard_map/ppermute | solution.py:50
  99.5 14.7 %collective-permute-start.21 = (bf16[384,512]{1,0:T(8,128)(2,1)S(1)}, bf16[384,512]{1,0:T(8,128)(2,1)S(1)}, u32[]{:S(2)}, u32[]{:S(2)}) collective-permute-start(bf16[384,512]{1,0:T(8,128)(2,1)S(1)} %slice.19), channel_id=1, source_target_pairs={{0,1},{1,0},{2,3},{3,2},{4,5},{5,4},{6,7},{7,6},{8,9},{9,8},{10,11... | collective-permute-start | bytes 1179656 | tf_op jit(solution)/shard_map/ppermute | solution.py:50
  101.8 11.0 %collective-permute-start.22 = (bf16[256,256]{1,0:T(8,128)(2,1)S(1)}, bf16[256,256]{1,0:T(8,128)(2,1)S(1)}, u32[]{:S(2)}, u32[]{:S(2)}) collective-permute-start(bf16[256,256]{1,0:T(8,128)(2,1)S(1)} %get-tuple-element.100.g0), channel_id=1, source_target_pairs={{0,1},{1,0},{2,3},{3,2},{4,5},{5,4},{6,7},{7,6},{8,9},{9,8},{10,11... | collective-permute-start | bytes 393224 | tf_op jit(solution)/shard_map/ppermute | solution.py:50
  103.4 9.5 %collective-permute-start.23 = (bf16[256,256]{1,0:T(8,128)(2,1)S(1)}, bf16[256,256]{1,0:T(8,128)(2,1)S(1)}, u32[]{:S(2)}, u32[]{:S(2)}) collective-permute-start(bf16[256,256]{1,0:T(8,128)(2,1)S(1)} %get-tuple-element.100.g0), channel_id=1, source_target_pairs={{0,2},{1,3},{2,0},{3,1},{4,6},{5,7},{6,4},{7,5},{8,10},{9,11},{10,... | collective-permute-start | bytes 393224 | tf_op jit(solution)/shard_map/ppermute | solution.py:50
  103.9 10.3 %collective-permute-start.24 = (bf16[256,256]{1,0:T(8,128)(2,1)S(1)}, bf16[256,256]{1,0:T(8,128)(2,1)S(1)}, u32[]{:S(2)}, u32[]{:S(2)}) collective-permute-start(bf16[256,256]{1,0:T(8,128)(2,1)S(1)} %get-tuple-element.100.g0), channel_id=1, source_target_pairs={{0,3},{1,2},{2,1},{3,0},{4,7},{5,6},{6,5},{7,4},{8,11},{9,10},{10,... | collective-permute-start | bytes 393224 | tf_op jit(solution)/shard_map/ppermute | solution.py:50
  (10 other events, 96.4 us)

commit v13 on v11

--- a/solution.py
+++ b/solution.py
@@ -9,7 +9,7 @@
 
 IMGTOK = 16
 QTILE = 128
-SPANS = (2, 3)
+SPANS = (2, 3, 4)
 LOG2E = 1.4426950408889634
 VMEM = 24 * 1024 * 1024
 

time: 118 us -> 118 us (level)
  transfers between devices with their start and end apart: 28 -> 28, of which waited for: 13 -> 12; matrix products, arithmetic and copies ran while one was open for 2% -> 2% of each run, Pallas kernels for 15% -> 14%
where the time goes in v13:
time: 118 us
  waiting for transfers between devices  54.2 us (46%)
  starting transfers between devices  37.7 us (32%)
  Pallas kernels  21.1 us (18%)
  local copies, waits for them, and re-layouts  3.22 us (3%)
    ppermute x21, waiting for transfers between devices, trade(): return lax.ppermute(block, axis, [(i, i ^ step) for i in range(count)])  42.3 us
    ppermute x21, starting transfers between devices, trade(): return lax.ppermute(block, axis, [(i, i ^ step) for i in range(count)])  30 us
    pallas_call x1, Pallas kernels, attention(): pl.pallas_call(functools.partial(attention_body, per_shard, images), grid...  11.1 us
    ppermute x2, waiting for transfers between devices, shift(): return lax.ppermute(block, axis, route)  7.83 us
    ppermute x2, starting transfers between devices, shift(): return lax.ppermute(block, axis, route)  4.99 us
    ppermute x4, waiting for transfers between devices, swap(): return lax.ppermute(block, axis, [(i, count - 1 - i) for i in range(count)])  4.03 us
  transfers between devices with their start and end apart: 28, of which 12 were waited for; matrix products, arithmetic and copies ran while one was open for 2% of the time, Pallas kernels for 14%

profile of v13, /device:TPU:0, one launch (start us, length us, event | category | flops | bytes accessed | tf_op | source)
XLA Modules:
  0.0 118.1 jit_solution(427690134181684861)
XLA Ops:
  0.6 3.0 %collective-permute-start = (bf16[256,2048]{1,0:T(8,128)(2,1)}, bf16[256,2048]{1,0:T(8,128)(2,1)S(1)}, u32[]{:S(2)}, u32[]{:S(2)}) collective-permute-start(bf16[256,2048]{1,0:T(8,128)(2,1)} %bitcast.25), channel_id=1, source_target_pairs={{0,1},{1,0},{2,3},{3,2},{4,5},{5,4},{6,7},{7,6},{8,9},{9,8},{10,11... | collective-permute-start | bytes 3145736 | tf_op jit(solution)/shard_map/ppermute | solution.py:50
  5.2 3.5 %collective-permute-start.4 = (bf16[512,256]{1,0:T(8,128)(2,1)}, bf16[512,256]{1,0:T(8,128)(2,1)S(1)}, u32[]{:S(2)}, u32[]{:S(2)}) collective-permute-start(bf16[512,256]{1,0:T(8,128)(2,1)} %bitcast.34), channel_id=1, source_target_pairs={{0,4},{4,8},{8,12},{1,5},{5,9},{9,13},{2,6},{6,10},{10,14},{3,7},{... | collective-permute-start | bytes 786440 | tf_op jit(solution)/shard_map/ppermute | solution.py:36
  10.3 16.7 %collective-permute-done.x_ref = bf16[256,2048]{1,0:T(8,128)(2,1)S(1)} collective-permute-done((bf16[256,2048]{1,0:T(8,128)(2,1)}, bf16[256,2048]{1,0:T(8,128)(2,1)S(1)}, u32[]{:S(2)}, u32[]{:S(2)}) %collective-permute-start) | collective-permute-done | bytes 1048608 | tf_op jit(solution)/shard_map/ppermute | solution.py:50
  27.1 1.8 %collective-permute-start.1 = (bf16[128,2048]{1,0:T(8,128)(2,1)S(1)}, bf16[128,2048]{1,0:T(8,128)(2,1)S(1)}, u32[]{:S(2)}, u32[]{:S(2)}) collective-permute-start(bf16[128,2048]{1,0:T(8,128)(2,1)S(1)} %slice.20), channel_id=1, source_target_pairs={{0,2},{1,3},{2,0},{3,1},{4,6},{5,7},{6,4},{7,5},{8,10},{9,11},{10,... | collective-permute-start | bytes 1572872 | tf_op jit(solution)/shard_map/ppermute | solution.py:50
  28.9 1.6 %collective-permute-start.3 = (bf16[128,2048]{1,0:T(8,128)(2,1)S(1)}, bf16[128,2048]{1,0:T(8,128)(2,1)S(1)}, u32[]{:S(2)}, u32[]{:S(2)}) collective-permute-start(bf16[128,2048]{1,0:T(8,128)(2,1)S(1)} %slice.21), channel_id=1, source_target_pairs={{0,1},{1,0},{2,3},{3,2},{4,5},{5,4},{6,7},{7,6},{8,9},{9,8},{10,11... | collective-permute-start | bytes 1572872 | tf_op jit(solution)/shard_map/ppermute | solution.py:50
  30.8 2.2 %copy-done = bf16[1,8192,256]{2,1,0:T(8,128)(2,1)S(1)} copy-done((bf16[1,8192,256]{2,1,0:T(8,128)(2,1)S(1)}, bf16[1,8192,256]{2,1,0:T(8,128)(2,1)}, u32[]{:S(2)}) %copy-start) | copy-done | bytes 4194328
  34.2 6.1 %collective-permute-done.1.low_ref = bf16[128,2048]{1,0:T(8,128)(2,1)S(1)} collective-permute-done((bf16[128,2048]{1,0:T(8,128)(2,1)S(1)}, bf16[128,2048]{1,0:T(8,128)(2,1)S(1)}, u32[]{:S(2)}, u32[]{:S(2)}) %collective-permute-start.1) | collective-permute-done | bytes 524320 | tf_op jit(solution)/shard_map/ppermute | solution.py:50
  42.9 1.6 %collective-permute-start.5 = (bf16[2,64,256]{2,1,0:T(8,128)(2,1)S(1)}, bf16[2,64,256]{2,1,0:T(8,128)(2,1)S(1)}, u32[]{:S(2)}, u32[]{:S(2)}) collective-permute-start(bf16[2,64,256]{2,1,0:T(8,128)(2,1)S(1)} %get-tuple-element.66), channel_id=1, source_target_pairs={{0,4},{4,0},{8,12},{12,8},{1,5},{5,1},{9,13},{13,9},{2,6},{6,2},{1... | collective-permute-start | bytes 196616 | tf_op jit(solution)/shard_map/ppermute | solution.py:50
  44.5 2.6 %collective-permute-start.6 = (bf16[2,64,256]{2,1,0:T(8,128)(2,1)S(1)}, bf16[2,64,256]{2,1,0:T(8,128)(2,1)S(1)}, u32[]{:S(2)}, u32[]{:S(2)}) collective-permute-start(bf16[2,64,256]{2,1,0:T(8,128)(2,1)S(1)} %get-tuple-element.67), channel_id=1, source_target_pairs={{0,8},{4,12},{8,0},{12,4},{1,9},{5,13},{9,1},{13,5},{2,10},{6,14},... | collective-permute-start | bytes 196616 | tf_op jit(solution)/shard_map/ppermute | solution.py:50
  51.0 3.0 %collective-permute-done.7.refs_3_ = bf16[2,64,256]{2,1,0:T(8,128)(2,1)S(1)} collective-permute-done((bf16[2,64,256]{2,1,0:T(8,128)(2,1)S(1)}, bf16[2,64,256]{2,1,0:T(8,128)(2,1)S(1)}, u32[]{:S(2)}, u32[]{:S(2)}) %collective-permute-start.7) | collective-permute-done | bytes 65568 | tf_op jit(solution)/shard_map/ppermute | solution.py:50
  54.6 3.7 %collective-permute-start.12 = (bf16[256,512]{1,0:T(8,128)(2,1)S(1)}, bf16[256,512]{1,0:T(8,128)(2,1)S(1)}, u32[]{:S(2)}, u32[]{:S(2)}) collective-permute-start(bf16[256,512]{1,0:T(8,128)(2,1)S(1)} %get-tuple-element.82), channel_id=1, source_target_pairs={{0,12},{4,8},{8,4},{12,0},{1,13},{5,9},{9,5},{13,1},{2,14},{6,10},... | collective-permute-start | bytes 786440 | tf_op jit(solution)/shard_map/ppermute | solution.py:50
  58.3 11.1 %shard_map.97 = (bf16[512,1024]{1,0:T(8,128)(2,1)}, f32[256,256]{1,0:T(8,128)S(1)}, bf16[256,256]{1,0:T(8,128)(2,1)S(1)}) custom-call(s32[1]{0:T(128)} %bitcast.c_ref, s32[64]{0:T(128)S(1)} %and_select_fusion.place_ref, s32[1,512]{1,0:T(1,128)S(1)} %bitcast.31, bf16[512,1024]{1,0:T(8,128)(2,1)S(1)} %bitcast.32, bf16[512,1024]{1,0:T(8,128)(2,1)S(1)} %bitcast.33, ...), custom_call_target="tpu_custom_call" | custom-call | flops 13421772800 | bytes 4194304 | tf_op jit(solution)/shard_map/pallas_call | solution.py:348
  69.4 3.9 %collective-permute-done.11 = bf16[256,512]{1,0:T(8,128)(2,1)S(1)} collective-permute-done((bf16[256,512]{1,0:T(8,128)(2,1)S(1)}, bf16[256,512]{1,0:T(8,128)(2,1)S(1)}, u32[]{:S(2)}, u32[]{:S(2)}) %collective-permute-start.11) | collective-permute-done | bytes 262176 | tf_op jit(solution)/shard_map/ppermute | solution.py:50
  73.4 1.6 %collective-permute-start.13 = (bf16[768,512]{1,0:T(8,128)(2,1)S(1)}, bf16[768,512]{1,0:T(8,128)(2,1)S(1)}, u32[]{:S(2)}, u32[]{:S(2)}) collective-permute-start(bf16[768,512]{1,0:T(8,128)(2,1)S(1)} %constant_dynamic-update-slice_fusion.refs_0_), channel_id=1, source_target_pairs={{0,1},{1,0},{2,3},{3,2},{4,5},{5,4},{6,7},{7,6},{8,9},{9,8},{10,11... | collective-permute-start | bytes 2359304 | tf_op jit(solution)/shard_map/ppermute | solution.py:50
  77.0 7.8 %collective-permute-done.15 = bf16[256,256]{1,0:T(8,128)(2,1)S(1)} collective-permute-done((bf16[256,256]{1,0:T(8,128)(2,1)S(1)}, bf16[256,256]{1,0:T(8,128)(2,1)S(1)}, u32[]{:S(2)}, u32[]{:S(2)}) %collective-permute-start.15) | collective-permute-done | bytes 131104 | tf_op jit(solution)/shard_map/ppermute | solution.py:36
  87.5 1.8 %collective-permute-start.18 = (bf16[256,256]{1,0:T(8,128)(2,1)S(1)}, bf16[256,256]{1,0:T(8,128)(2,1)S(1)}, u32[]{:S(2)}, u32[]{:S(2)}) collective-permute-start(bf16[256,256]{1,0:T(8,128)(2,1)S(1)} %add_convert_fusion.refs_0_), channel_id=1, source_target_pairs={{0,12},{4,8},{8,4},{12,0},{1,13},{5,9},{9,5},{13,1},{2,14},{6,10},... | collective-permute-start | bytes 393224 | tf_op jit(solution)/shard_map/ppermute | solution.py:50
  89.3 1.8 %collective-permute-done.16.refs_1_ = bf16[256,256]{1,0:T(8,128)(2,1)S(1)} collective-permute-done((bf16[256,256]{1,0:T(8,128)(2,1)S(1)}, bf16[256,256]{1,0:T(8,128)(2,1)S(1)}, u32[]{:S(2)}, u32[]{:S(2)}) %collective-permute-start.16) | collective-permute-done | bytes 131104 | tf_op jit(solution)/shard_map/ppermute | solution.py:50
  91.1 3.9 %collective-permute-done.17.refs_2_ = bf16[256,256]{1,0:T(8,128)(2,1)S(1)} collective-permute-done((bf16[256,256]{1,0:T(8,128)(2,1)S(1)}, bf16[256,256]{1,0:T(8,128)(2,1)S(1)}, u32[]{:S(2)}, u32[]{:S(2)}) %collective-permute-start.17) | collective-permute-done | bytes 131104 | tf_op jit(solution)/shard_map/ppermute | solution.py:50
  95.1 1.6 %collective-permute-start.19 = (bf16[384,512]{1,0:T(8,128)(2,1)S(1)}, bf16[384,512]{1,0:T(8,128)(2,1)S(1)}, u32[]{:S(2)}, u32[]{:S(2)}) collective-permute-start(bf16[384,512]{1,0:T(8,128)(2,1)S(1)} %slice.18), channel_id=1, source_target_pairs={{0,2},{1,3},{2,0},{3,1},{4,6},{5,7},{6,4},{7,5},{8,10},{9,11},{10,... | collective-permute-start | bytes 1179656 | tf_op jit(solution)/shard_map/ppermute | solution.py:50
  97.3 1.7 %shard_map.98 = (bf16[1024,256]{1,0:T(8,128)(2,1)S(1)}, bf16[256,256]{1,0:T(8,128)(2,1)S(1)}) custom-call(s32[1]{0:T(128)} %bitcast.c_ref, s32[64]{0:T(128)S(1)} %and_select_fusion.place_ref, bf16[256,256]{1,0:T(8,128)(2,1)S(1)} %add_convert_fusion.refs_0_, bf16[256,256]{1,0:T(8,128)(2,1)S(1)} %collective-permute-done.16.refs_1_, ...), custom_call_target="tpu_custom_call" | custom-call | bytes 2097152 | tf_op jit(solution)/shard_map/pallas_call | solution.py:406
  99.0 1.6 %collective-permute-start.21 = (bf16[256,256]{1,0:T(8,128)(2,1)S(1)}, bf16[256,256]{1,0:T(8,128)(2,1)S(1)}, u32[]{:S(2)}, u32[]{:S(2)}) collective-permute-start(bf16[256,256]{1,0:T(8,128)(2,1)S(1)} %get-tuple-element.96.g0), channel_id=1, source_target_pairs={{0,1},{1,0},{2,3},{3,2},{4,5},{5,4},{6,7},{7,6},{8,9},{9,8},{10,11... | collective-permute-start | bytes 393224 | tf_op jit(solution)/shard_map/ppermute | solution.py:50
  102.5 3.5 %collective-permute-done.21.g1 = bf16[256,256]{1,0:T(8,128)(2,1)S(1)} collective-permute-done((bf16[256,256]{1,0:T(8,128)(2,1)S(1)}, bf16[256,256]{1,0:T(8,128)(2,1)S(1)}, u32[]{:S(2)}, u32[]{:S(2)}) %collective-permute-start.21) | collective-permute-done | bytes 131104 | tf_op jit(solution)/shard_map/ppermute | solution.py:50
  110.2 4.0 %collective-permute-done.25.far_ref = bf16[1024,256]{1,0:T(8,128)(2,1)S(1)} collective-permute-done((bf16[1024,256]{1,0:T(8,128)(2,1)S(1)}, bf16[1024,256]{1,0:T(8,128)(2,1)S(1)}, u32[]{:S(2)}, u32[]{:S(2)}) %collective-permute-start.25) | collective-permute-done | bytes 524320 | tf_op jit(solution)/shard_map/ppermute | solution.py:41
  114.2 2.3 %shard_map.99 = bf16[256,2048]{1,0:T(8,128)(2,1)} custom-call(s32[1]{0:T(128)} %bitcast.11.d_ref, bf16[256,256]{1,0:T(8,128)(2,1)S(1)} %get-tuple-element.96.g0, bf16[256,256]{1,0:T(8,128)(2,1)S(1)} %collective-permute-done.21.g1, bf16[256,256]{1,0:T(8,128)(2,1)S(1)} %collective-permute-done.22.g2, bf16[256,256]{1,0:T(8,128)(2,1)S(1)} %collective-permute-done.23.g3, ...), custom_call_target="tpu_custom_call" | custom-call | flops 1073741824 | bytes 4194304 | tf_op jit(solution)/shard_map/pallas_call | solution.py:525
  (66 shorter events, 24.9 us)
Async XLA Ops:
  0.6 26.4 %collective-permute-start = (bf16[256,2048]{1,0:T(8,128)(2,1)}, bf16[256,2048]{1,0:T(8,128)(2,1)S(1)}, u32[]{:S(2)}, u32[]{:S(2)}) collective-permute-start(bf16[256,2048]{1,0:T(8,128)(2,1)} %bitcast.25), channel_id=1, source_target_pairs={{0,1},{1,0},{2,3},{3,2},{4,5},{5,4},{6,7},{7,6},{8,9},{9,8},{10,11... | collective-permute-start | bytes 3145736 | tf_op jit(solution)/shard_map/ppermute | solution.py:50
  3.6 25.2 %collective-permute-start.2 = (bf16[256,2048]{1,0:T(8,128)(2,1)}, bf16[256,2048]{1,0:T(8,128)(2,1)S(1)}, u32[]{:S(2)}, u32[]{:S(2)}) collective-permute-start(bf16[256,2048]{1,0:T(8,128)(2,1)} %bitcast.26), channel_id=1, source_target_pairs={{0,2},{1,3},{2,0},{3,1},{4,6},{5,7},{6,4},{7,5},{8,10},{9,11},{10,... | collective-permute-start | bytes 3145736 | tf_op jit(solution)/shard_map/ppermute | solution.py:50
  5.2 29.0 %collective-permute-start.4 = (bf16[512,256]{1,0:T(8,128)(2,1)}, bf16[512,256]{1,0:T(8,128)(2,1)S(1)}, u32[]{:S(2)}, u32[]{:S(2)}) collective-permute-start(bf16[512,256]{1,0:T(8,128)(2,1)} %bitcast.34), channel_id=1, source_target_pairs={{0,4},{4,8},{8,12},{1,5},{5,9},{9,13},{2,6},{6,10},{10,14},{3,7},{... | collective-permute-start | bytes 786440 | tf_op jit(solution)/shard_map/ppermute | solution.py:36
  27.1 13.2 %collective-permute-start.1 = (bf16[128,2048]{1,0:T(8,128)(2,1)S(1)}, bf16[128,2048]{1,0:T(8,128)(2,1)S(1)}, u32[]{:S(2)}, u32[]{:S(2)}) collective-permute-start(bf16[128,2048]{1,0:T(8,128)(2,1)S(1)} %slice.20), channel_id=1, source_target_pairs={{0,2},{1,3},{2,0},{3,1},{4,6},{5,7},{6,4},{7,5},{8,10},{9,11},{10,... | collective-permute-start | bytes 1572872 | tf_op jit(solution)/shard_map/ppermute | solution.py:50
  28.9 12.6 %collective-permute-start.3 = (bf16[128,2048]{1,0:T(8,128)(2,1)S(1)}, bf16[128,2048]{1,0:T(8,128)(2,1)S(1)}, u32[]{:S(2)}, u32[]{:S(2)}) collective-permute-start(bf16[128,2048]{1,0:T(8,128)(2,1)S(1)} %slice.21), channel_id=1, source_target_pairs={{0,1},{1,0},{2,3},{3,2},{4,5},{5,4},{6,7},{7,6},{8,9},{9,8},{10,11... | collective-permute-start | bytes 1572872 | tf_op jit(solution)/shard_map/ppermute | solution.py:50
  42.9 7.4 %collective-permute-start.5 = (bf16[2,64,256]{2,1,0:T(8,128)(2,1)S(1)}, bf16[2,64,256]{2,1,0:T(8,128)(2,1)S(1)}, u32[]{:S(2)}, u32[]{:S(2)}) collective-permute-start(bf16[2,64,256]{2,1,0:T(8,128)(2,1)S(1)} %get-tuple-element.66), channel_id=1, source_target_pairs={{0,4},{4,0},{8,12},{12,8},{1,5},{5,1},{9,13},{13,9},{2,6},{6,2},{1... | collective-permute-start | bytes 196616 | tf_op jit(solution)/shard_map/ppermute | solution.py:50
  44.5 6.4 %collective-permute-start.6 = (bf16[2,64,256]{2,1,0:T(8,128)(2,1)S(1)}, bf16[2,64,256]{2,1,0:T(8,128)(2,1)S(1)}, u32[]{:S(2)}, u32[]{:S(2)}) collective-permute-start(bf16[2,64,256]{2,1,0:T(8,128)(2,1)S(1)} %get-tuple-element.67), channel_id=1, source_target_pairs={{0,8},{4,12},{8,0},{12,4},{1,9},{5,13},{9,1},{13,5},{2,10},{6,14},... | collective-permute-start | bytes 196616 | tf_op jit(solution)/shard_map/ppermute | solution.py:50
  47.1 6.8 %collective-permute-start.7 = (bf16[2,64,256]{2,1,0:T(8,128)(2,1)S(1)}, bf16[2,64,256]{2,1,0:T(8,128)(2,1)S(1)}, u32[]{:S(2)}, u32[]{:S(2)}) collective-permute-start(bf16[2,64,256]{2,1,0:T(8,128)(2,1)S(1)} %get-tuple-element.68), channel_id=1, source_target_pairs={{0,12},{4,8},{8,4},{12,0},{1,13},{5,9},{9,5},{13,1},{2,14},{6,10},... | collective-permute-start | bytes 196616 | tf_op jit(solution)/shard_map/ppermute | solution.py:50
  47.4 26.0 %collective-permute-start.8 = (bf16[2048,256]{1,0:T(8,128)(2,1)S(1)}, bf16[2048,256]{1,0:T(8,128)(2,1)S(1)}, u32[]{:S(2)}, u32[]{:S(2)}) collective-permute-start(bf16[2048,256]{1,0:T(8,128)(2,1)S(1)} %get-tuple-element.78), channel_id=1, source_target_pairs={{0,1},{1,0},{2,3},{3,2},{16,18},{17,19},{18,16},{19,17},{4,5},{5,4... | collective-permute-start | bytes 3145736 | tf_op jit(solution)/shard_map/ppermute | solution.py:582
  48.9 24.5 %collective-permute-start.9 = (bf16[1024,256]{1,0:T(8,128)(2,1)S(1)}, bf16[1024,256]{1,0:T(8,128)(2,1)S(1)}, u32[]{:S(2)}, u32[]{:S(2)}) collective-permute-start(bf16[1024,256]{1,0:T(8,128)(2,1)S(1)} %get-tuple-element.79), channel_id=1, source_target_pairs={{0,3},{1,2},{2,1},{3,0},{4,7},{5,6},{6,5},{7,4},{8,11},{9,10},{10,... | collective-permute-start | bytes 1572872 | tf_op jit(solution)/shard_map/ppermute | solution.py:50
  53.9 15.5 %collective-permute-start.10 = (bf16[256,512]{1,0:T(8,128)(2,1)S(1)}, bf16[256,512]{1,0:T(8,128)(2,1)S(1)}, u32[]{:S(2)}, u32[]{:S(2)}) collective-permute-start(bf16[256,512]{1,0:T(8,128)(2,1)S(1)} %get-tuple-element.80), channel_id=1, source_target_pairs={{0,4},{4,0},{8,12},{12,8},{1,5},{5,1},{9,13},{13,9},{2,6},{6,2},{1... | collective-permute-start | bytes 786440 | tf_op jit(solution)/shard_map/ppermute | solution.py:50
  53.9 19.4 %collective-permute-start.11 = (bf16[256,512]{1,0:T(8,128)(2,1)S(1)}, bf16[256,512]{1,0:T(8,128)(2,1)S(1)}, u32[]{:S(2)}, u32[]{:S(2)}) collective-permute-start(bf16[256,512]{1,0:T(8,128)(2,1)S(1)} %get-tuple-element.81), channel_id=1, source_target_pairs={{0,8},{4,12},{8,0},{12,4},{1,9},{5,13},{9,1},{13,5},{2,10},{6,14},... | collective-permute-start | bytes 786440 | tf_op jit(solution)/shard_map/ppermute | solution.py:50
  54.6 18.7 %collective-permute-start.12 = (bf16[256,512]{1,0:T(8,128)(2,1)S(1)}, bf16[256,512]{1,0:T(8,128)(2,1)S(1)}, u32[]{:S(2)}, u32[]{:S(2)}) collective-permute-start(bf16[256,512]{1,0:T(8,128)(2,1)S(1)} %get-tuple-element.82), channel_id=1, source_target_pairs={{0,12},{4,8},{8,4},{12,0},{1,13},{5,9},{9,5},{13,1},{2,14},{6,10},... | collective-permute-start | bytes 786440 | tf_op jit(solution)/shard_map/ppermute | solution.py:50
  73.4 21.6 %collective-permute-start.13 = (bf16[768,512]{1,0:T(8,128)(2,1)S(1)}, bf16[768,512]{1,0:T(8,128)(2,1)S(1)}, u32[]{:S(2)}, u32[]{:S(2)}) collective-permute-start(bf16[768,512]{1,0:T(8,128)(2,1)S(1)} %constant_dynamic-update-slice_fusion.refs_0_), channel_id=1, source_target_pairs={{0,1},{1,0},{2,3},{3,2},{4,5},{5,4},{6,7},{7,6},{8,9},{9,8},{10,11... | collective-permute-start | bytes 2359304 | tf_op jit(solution)/shard_map/ppermute | solution.py:50
  75.0 20.1 %collective-permute-start.14 = (bf16[768,512]{1,0:T(8,128)(2,1)S(1)}, bf16[768,512]{1,0:T(8,128)(2,1)S(1)}, u32[]{:S(2)}, u32[]{:S(2)}) collective-permute-start(bf16[768,512]{1,0:T(8,128)(2,1)S(1)} %constant_dynamic-update-slice_fusion.refs_0_), channel_id=1, source_target_pairs={{0,2},{1,3},{2,0},{3,1},{4,6},{5,7},{6,4},{7,5},{8,10},{9,11},{10,... | collective-permute-start | bytes 2359304 | tf_op jit(solution)/shard_map/ppermute | solution.py:50
  75.5 9.3 %collective-permute-start.15 = (bf16[256,256]{1,0:T(8,128)(2,1)S(1)}, bf16[256,256]{1,0:T(8,128)(2,1)S(1)}, u32[]{:S(2)}, u32[]{:S(2)}) collective-permute-start(bf16[256,256]{1,0:T(8,128)(2,1)S(1)} %get-tuple-element.87), channel_id=1, source_target_pairs={{4,0},{8,4},{12,8},{5,1},{9,5},{13,9},{6,2},{10,6},{14,10},{7,3},{... | collective-permute-start | bytes 393224 | tf_op jit(solution)/shard_map/ppermute | solution.py:36
  86.0 9.0 %collective-permute-start.17 = (bf16[256,256]{1,0:T(8,128)(2,1)S(1)}, bf16[256,256]{1,0:T(8,128)(2,1)S(1)}, u32[]{:S(2)}, u32[]{:S(2)}) collective-permute-start(bf16[256,256]{1,0:T(8,128)(2,1)S(1)} %add_convert_fusion.refs_0_), channel_id=1, source_target_pairs={{0,8},{4,12},{8,0},{12,4},{1,9},{5,13},{9,1},{13,5},{2,10},{6,14},... | collective-permute-start | bytes 393224 | tf_op jit(solution)/shard_map/ppermute | solution.py:50
  87.5 7.5 %collective-permute-start.18 = (bf16[256,256]{1,0:T(8,128)(2,1)S(1)}, bf16[256,256]{1,0:T(8,128)(2,1)S(1)}, u32[]{:S(2)}, u32[]{:S(2)}) collective-permute-start(bf16[256,256]{1,0:T(8,128)(2,1)S(1)} %add_convert_fusion.refs_0_), channel_id=1, source_target_pairs={{0,12},{4,8},{8,4},{12,0},{1,13},{5,9},{9,5},{13,1},{2,14},{6,10},... | collective-permute-start | bytes 393224 | tf_op jit(solution)/shard_map/ppermute | solution.py:50
  95.1 12.3 %collective-permute-start.19 = (bf16[384,512]{1,0:T(8,128)(2,1)S(1)}, bf16[384,512]{1,0:T(8,128)(2,1)S(1)}, u32[]{:S(2)}, u32[]{:S(2)}) collective-permute-start(bf16[384,512]{1,0:T(8,128)(2,1)S(1)} %slice.18), channel_id=1, source_target_pairs={{0,2},{1,3},{2,0},{3,1},{4,6},{5,7},{6,4},{7,5},{8,10},{9,11},{10,... | collective-permute-start | bytes 1179656 | tf_op jit(solution)/shard_map/ppermute | solution.py:50
  96.7 10.7 %collective-permute-start.20 = (bf16[384,512]{1,0:T(8,128)(2,1)S(1)}, bf16[384,512]{1,0:T(8,128)(2,1)S(1)}, u32[]{:S(2)}, u32[]{:S(2)}) collective-permute-start(bf16[384,512]{1,0:T(8,128)(2,1)S(1)} %slice.19), channel_id=1, source_target_pairs={{0,1},{1,0},{2,3},{3,2},{4,5},{5,4},{6,7},{7,6},{8,9},{9,8},{10,11... | collective-permute-start | bytes 1179656 | tf_op jit(solution)/shard_map/ppermute | solution.py:50
  99.0 7.1 %collective-permute-start.21 = (bf16[256,256]{1,0:T(8,128)(2,1)S(1)}, bf16[256,256]{1,0:T(8,128)(2,1)S(1)}, u32[]{:S(2)}, u32[]{:S(2)}) collective-permute-start(bf16[256,256]{1,0:T(8,128)(2,1)S(1)} %get-tuple-element.96.g0), channel_id=1, source_target_pairs={{0,1},{1,0},{2,3},{3,2},{4,5},{5,4},{6,7},{7,6},{8,9},{9,8},{10,11... | collective-permute-start | bytes 393224 | tf_op jit(solution)/shard_map/ppermute | solution.py:50
  101.0 6.4 %collective-permute-start.23 = (bf16[256,256]{1,0:T(8,128)(2,1)S(1)}, bf16[256,256]{1,0:T(8,128)(2,1)S(1)}, u32[]{:S(2)}, u32[]{:S(2)}) collective-permute-start(bf16[256,256]{1,0:T(8,128)(2,1)S(1)} %get-tuple-element.96.g0), channel_id=1, source_target_pairs={{0,3},{1,2},{2,1},{3,0},{4,7},{5,6},{6,5},{7,4},{8,11},{9,10},{10,... | collective-permute-start | bytes 393224 | tf_op jit(solution)/shard_map/ppermute | solution.py:50
  108.5 8.1 %collective-permute-start.26 = (f32[3,512,256]{2,1,0:T(8,128)S(1)}, f32[3,512,256]{2,1,0:T(8,128)S(1)}, u32[]{:S(2)}, u32[]{:S(2)}) collective-permute-start(f32[3,512,256]{2,1,0:T(8,128)S(1)} %shard_map.100.refs_0_), channel_id=1, source_target_pairs={{0,16},{16,0},{1,17},{17,1},{2,18},{18,2},{3,19},{19,3},{4,20},{20... | collective-permute-start | bytes 4718600 | tf_op jit(solution)/shard_map/ppermute | solution.py:41
  109.7 6.9 %collective-permute-start.27 = (f32[1,512,256]{2,1,0:T(8,128)S(1)}, f32[1,512,256]{2,1,0:T(8,128)S(1)}, u32[]{:S(2)}, u32[]{:S(2)}) collective-permute-start(f32[1,512,256]{2,1,0:T(8,128)S(1)} %shard_map.101.refs_1_), channel_id=1, source_target_pairs={{0,16},{16,0},{1,17},{17,1},{2,18},{18,2},{3,19},{19,3},{4,20},{20... | collective-permute-start | bytes 1572872 | tf_op jit(solution)/shard_map/ppermute | solution.py:41
  (10 other events, 96.4 us)
